TPU v7x, 32 devices: a whole 2x2x4 slice. The times are simulated.
32 devices in a mesh: groups: 1, ep: 32 (over z, y, x, core), tp: 1.
Axes of the slice: x: 2, y: 2, z: 4, core: 2. Of those that a mesh axis runs over, the one named last changes fastest.
Arguments:
- query_latent: bfloat16 [32, 128, 576], P(('groups', 'ep')), may hold values from -40 to 40
- latent_cache: bfloat16 [32, 1024, 576], P(('groups', 'ep'), 'tp'), may hold values from -5 to 5
- cache_length: int32 [32], P(('groups', 'ep')), may hold values from 1 to 1024, 16384 in all
- prefill_latent: bfloat16 [32, 32, 4, 576], P(('groups', 'ep'), 'tp'), may hold values from -5 to 5
- block_owner: int32 [32, 32, 1], P(('groups', 'ep'), 'tp'), may hold values from 0 to 31; in each aligned block of 32 rows (0 to 31, 32 to 63, ..., all dimensions but the last counted through in order) at most 2 rows name the same one
- tokens: bfloat16 [1024, 3584], P(('groups', 'ep')), may hold values from -6 to 6
- expert_ids: int32 [1024, 8], P(('groups', 'ep')), may hold values from 0 to 15, all different within a row; in each aligned block of 32 rows (0 to 31, 32 to 63, ...) at most 32 rows name the same one
- route_weight: float32 [1024, 8], P(('groups', 'ep')), may hold values from 0.1 to 1
- gate_weight: bfloat16 [32, 3584, 512], P('ep', None, 'tp'), may hold values from -0.09375 to 0.09375
- up_weight: bfloat16 [32, 3584, 512], P('ep', None, 'tp'), may hold values from -0.09375 to 0.09375
- down_weight: bfloat16 [32, 512, 3584], P('ep', None, 'tp'), may hold values from -0.1875 to 0.1875
Outputs:
- attn_out: bfloat16 [32, 128, 512], P(('groups', 'ep'))
- moe_out: bfloat16 [1024, 3584], P(('groups', 'ep'), 'tp')
Inputs may be any that keep to these rules, and one draw needn't show every extreme that they name: `expert_ids`: each row names 8 different experts; the 32 rows of one device name one expert at most 32 times. `block_owner`: the 32 blocks of one device name one request at most 2 times.
All inputs are finite; a program needn't handle non-finite values. No bound on the sum of `cache_length` on one device may be relied on, other than what follows from the above.
Results may differ from a plain program's by a relative error of at most 0.00235.
The roundings to bfloat16 on the way count: a program that leaves them out, or rounds other values in their place, can miss the bound.
Values may be sent and summed in bfloat16 or wider, within the bound.
No kernel may reach another device: no remote copies, remote signals or barrier semaphores. Data moves between devices by JAX's collectives and lax.ppermute only.
A program may use at most 128 MiB of HBM per device.

v0:
```python
import jax
import jax.numpy as jnp
from jax import lax
from jax.sharding import PartitionSpec as P

VAL = 512


SCALE = 192.0 ** (-0.5)
NEG = -1e30


def combined_all(x, axis, combine):
    everything = jax.tree.map(lambda part: lax.all_gather(part, axis), x)
    leading = jax.tree.map(lambda part: part[0], everything)

    def lap(k, so_far):
        return combine(so_far, jax.tree.map(lambda part: part[k], everything))

    return lax.fori_loop(1, lax.axis_size(axis), lap, leading)


def attend_keys(query, keys, valid, value_width):
    scores = (
        lax.dot_general(query, keys, (((1,), (1,)), ((), ())), preferred_element_type=jnp.float32)
        * SCALE
    )
    scores = jnp.where(valid[None, :], scores, NEG)
    peak = jnp.max(scores, axis=1)
    expo = jnp.where(valid[None, :], jnp.exp(scores - peak[:, None]), 0.0)
    total = jnp.sum(expo, axis=1)
    mixed = jnp.dot(
        expo.astype(jnp.bfloat16), keys[:, :value_width], preferred_element_type=jnp.float32
    )
    return (peak, total, mixed)


def join_parts(first, second):
    peak = jnp.maximum(first[0], second[0])
    left = jnp.exp(first[0] - peak)
    right = jnp.exp(second[0] - peak)
    return (
        peak,
        first[1] * left + second[1] * right,
        first[2] * left[:, None] + second[2] * right[:, None],
    )


def place_rows(targets, count, tok_rows, top_k):
    hits = (jnp.arange(count, dtype=jnp.int32)[:, None] == targets[None, :]).astype(jnp.float32)
    return jnp.sum(hits.reshape(count, tok_rows, top_k), axis=2)


def weigh_rows(targets, weights, count, tok_rows, top_k):
    hits = (jnp.arange(count, dtype=jnp.int32)[None, :] == targets[:, None]).astype(
        jnp.float32
    ) * weights[:, None]
    return jnp.sum(hits.reshape(tok_rows, top_k, count), axis=1)


def per_device(
    query_latent,
    latent_cache,
    cache_length,
    prefill_latent,
    block_owner,
    tokens,
    expert_ids,
    route_weight,
    gate_weight,
    up_weight,
    down_weight,
):
    peers = lax.axis_size("ep")
    blocks = prefill_latent.shape[1]
    block_len = prefill_latent.shape[2]
    latent = prefill_latent.shape[3]
    owner = block_owner.reshape(blocks)
    same = owner[:, None] == owner[None, :]
    earlier = jnp.arange(blocks)[None, :] < jnp.arange(blocks)[:, None]
    order_in = jnp.sum(jnp.logical_and(same, earlier).astype(jnp.int32), axis=1)
    target = owner * 2 + order_in
    chosen = jnp.arange(2 * peers, dtype=jnp.int32)[:, None] == target[None, :]
    packed = jnp.dot(
        chosen.astype(jnp.bfloat16),
        prefill_latent.reshape(blocks, block_len * latent),
        preferred_element_type=jnp.float32,
    ).astype(jnp.bfloat16)
    filled = jnp.sum(chosen.astype(jnp.int32), axis=1)
    arrived, present = (
        lax.all_to_all(
            packed.reshape(peers, 2 * block_len, latent),
            "ep",
            split_axis=0,
            concat_axis=0,
            tiled=True,
        ),
        lax.all_to_all(filled.reshape(peers, 2), "ep", split_axis=0, concat_axis=0, tiled=True),
    )
    shard_len = latent_cache.shape[1]
    positions = lax.axis_index("tp") * shard_len + jnp.arange(shard_len, dtype=jnp.int32)
    keys = jnp.concatenate(
        [latent_cache[0], arrived.reshape(peers * 2 * block_len, latent)], axis=0
    )
    valid = jnp.concatenate(
        [positions < cache_length[0], jnp.repeat(present.reshape(peers * 2) > 0, block_len)]
    )
    peak, total, mixed = attend_keys(query_latent[0], keys, valid, VAL)
    peak, total, mixed = combined_all((peak, total, mixed), "tp", join_parts)
    attn_out = (mixed / total[:, None]).astype(jnp.bfloat16)[None]
    tok_rows, top_k = expert_ids.shape
    experts = peers // 2
    capacity = min(tok_rows, 2 * tok_rows * top_k // experts)
    flat = expert_ids.reshape(tok_rows * top_k)
    weights = route_weight.reshape(tok_rows * top_k)
    hits = (flat[:, None] == jnp.arange(experts, dtype=jnp.int32)[None, :]).astype(jnp.int32)
    slots = jnp.sum((jnp.cumsum(hits, axis=0) - hits) * hits, axis=1)
    first = 2 * flat * capacity + slots
    second = (2 * flat + 1) * capacity + slots
    placing = place_rows(first, peers * capacity, tok_rows, top_k) + place_rows(
        second, peers * capacity, tok_rows, top_k
    )
    mixing = weigh_rows(first, weights, peers * capacity, tok_rows, top_k) + weigh_rows(
        second, weights, peers * capacity, tok_rows, top_k
    )
    outgoing = jnp.dot(
        placing.astype(jnp.bfloat16), tokens, preferred_element_type=jnp.float32
    ).astype(jnp.bfloat16)
    incoming = lax.all_to_all(
        outgoing.reshape(peers, capacity, tokens.shape[1]),
        "ep",
        split_axis=0,
        concat_axis=0,
        tiled=True,
    )
    rows = incoming.reshape(peers * capacity, tokens.shape[1])
    gate_local = gate_weight[0]
    up_local = up_weight[0]
    down_local = down_weight[0]
    gate = jnp.dot(rows, gate_local, preferred_element_type=jnp.float32)
    upper = jnp.dot(rows, up_local, preferred_element_type=jnp.float32)
    hidden = (jax.nn.silu(gate) * upper).astype(jnp.bfloat16)
    out_width = down_local.shape[1]
    partial_out = jnp.dot(
        lax.all_gather(hidden, "tp", axis=1, tiled=True),
        down_local,
        preferred_element_type=jnp.float32,
    )
    back = lax.all_to_all(
        partial_out.reshape(peers, capacity, out_width),
        "ep",
        split_axis=0,
        concat_axis=0,
        tiled=True,
    )
    combined = jnp.dot(
        mixing,
        back.reshape(peers * capacity, out_width),
        precision=lax.Precision.HIGHEST,
        preferred_element_type=jnp.float32,
    )
    moe_out = combined.astype(jnp.bfloat16)
    return (attn_out, moe_out)


def solution(mesh):
    in_specs = (
        P(("groups", "ep"), None, None),
        P(("groups", "ep"), "tp", None),
        P(("groups", "ep")),
        P(("groups", "ep"), "tp", None, None),
        P(("groups", "ep"), "tp", None),
        P(("groups", "ep"), None),
        P(("groups", "ep"), None),
        P(("groups", "ep"), None),
        P("ep", None, "tp"),
        P("ep", None, "tp"),
        P("ep", None, "tp"),
    )
    out_specs = (P(("groups", "ep"), None, None), P(("groups", "ep"), "tp"))
    return jax.shard_map(
        per_device, mesh=mesh, in_specs=in_specs, out_specs=out_specs, check_vma=False
    )
```

profile of v0, /device:TPU:0, one launch (start us, length us, event | category | flops | bytes accessed | tf_op | source)
XLA Modules:
  0.0 556.6 jit_solution(16441585966629181008)
XLA Ops:
  0.6 0.8 copy.36
  1.4 0.1 eq.118
  1.5 0.1 eq.114
  1.6 0.6 reduce-window.6
  2.2 0.2 slice_reduce_fusion
  2.5 0.1 fusion.35
  2.7 0.7 convert_reduce_fusion
  3.4 5.1 convolution_convert_fusion
  8.5 7.4 %all-to-all-start.2 = ((bf16[32,32,3584]{2,1,0:T(8,128)(2,1)}), bf16[32,32,3584]{2,1,0:T(8,128)(2,1)}, u32[]{:S(2)}, u32[]{:S(2)}) async-start(bf16[32,32,3584]{2,1,0:T(8,128)(2,1)} %bitcast.55), calls=%async_computation.2 | async-start | bytes 14680064 | tf_op jit(solution)/shard_map/all_to_all | solution.py:129
  15.9 0.2 convert_reduce_fusion.3
  16.1 0.1 convert_reduce_fusion.2
  16.2 0.7 all_to_all.15
  16.9 0.2 reshape.162
  17.1 0.3 convolution_convert_fusion.2
  17.4 1.1 reshape.163
  18.6 160.4 %all-to-all-done.2 = bf16[32,32,3584]{2,1,0:T(8,128)(2,1)} async-done(((bf16[32,32,3584]{2,1,0:T(8,128)(2,1)}), bf16[32,32,3584]{2,1,0:T(8,128)(2,1)}, u32[]{:S(2)}, u32[]{:S(2)}) %all-to-all-start.2) | async-done | bytes 7340064 | tf_op jit(solution)/shard_map/all_to_all | solution.py:129
  179.0 2.5 all-to-all-start
  181.6 7.4 %fusion.2 = f32[1024,512]{1,0:T(8,128)S(1)} fusion(bf16[1024,3584]{1,0:T(8,128)(2,1)} %bitcast.9, bf16[1,3584,512]{2,1,0:T(8,128)(2,1)} %param.20), kind=kOutput, calls=%fused_computation.4 | convolution fusion | flops 3758096384 | bytes 13107200 | tf_op jit(solution)/shard_map/dot_general | solution.py:141
  189.0 7.3 %multiply_convert_fusion = bf16[1024,512]{1,0:T(8,128)(2,1)S(1)} fusion(f32[1024,512]{1,0:T(8,128)S(1)} %fusion.2, bf16[1024,3584]{1,0:T(8,128)(2,1)} %bitcast.9, bf16[1,3584,512]{2,1,0:T(8,128)(2,1)S(1)} %copy-done.3), kind=kOutput, calls=%fused_computation.11 | convolution fusion | flops 3761242112 | bytes 14155776 | tf_op jit(solution)/shard_map/dot_general | solution.py:140
  196.3 5.8 %all-to-all-start.1 = ((bf16[32,8,576]{2,1,0:T(8,128)(2,1)}), bf16[32,8,576]{2,1,0:T(8,128)(2,1)S(1)}, u32[]{:S(2)}, u32[]{:S(2)}) async-start(bf16[32,8,576]{2,1,0:T(8,128)(2,1)} %reshape.163), calls=%async_computation.1 | async-start | bytes 655360 | tf_op jit(solution)/shard_map/all_to_all | solution.py:91
  202.2 9.3 %fusion = f32[32,32,3584]{2,1,0:T(8,128)} fusion(bf16[32,32,512]{2,1,0:T(8,128)(2,1)S(1)} %bitcast.60, bf16[1,512,3584]{2,1,0:T(8,128)(2,1)} %param.21), kind=kOutput, calls=%fused_computation.2 | convolution fusion | flops 3758096384 | bytes 19398656 | tf_op jit(solution)/shard_map/dot_general | solution.py:144
  211.5 2.7 all-to-all-done.1
  214.2 4.0 all-to-all-start.3
  218.9 0.9 select_reduce_fusion
  220.0 0.1 gt.11
  220.1 0.1 reshape.161
  220.3 0.2 copy.35
  220.5 0.7 fusion.42
  221.2 0.3 fusion.25
  221.5 1.5 fusion.22
  223.0 321.2 %all-to-all-done.3 = f32[32,32,3584]{2,1,0:T(8,128)} async-done(((f32[32,32,3584]{2,1,0:T(8,128)}), f32[32,32,3584]{2,1,0:T(8,128)}, u32[]{:S(2)}, u32[]{:S(2)}) %all-to-all-start.3) | async-done | bytes 14680096 | tf_op jit(solution)/shard_map/all_to_all | solution.py:149
  544.2 12.3 %convolution_convert_fusion.1 = bf16[32,3584]{1,0:T(8,128)(2,1)} fusion(f32[1024,3584]{1,0:T(8,128)} %bitcast.15, f32[32,1024]{1,0:T(8,128)S(1)} %get-tuple-element.3, f32[32,1024]{1,0:T(8,128)S(1)} %get-tuple-element.2), kind=kOutput, calls=%fused_computation.1 | convolution fusion | flops 1409433600 | bytes 15171584 | tf_op jit(solution)/shard_map/dot_general | solution.py:156
  (26 shorter events, 0.4 us)
Async XLA Ops:
  0.6 2.7 copy-start
  8.5 7.4 %copy-start.6 = (s32[1,32,1]{1,2,0:T(1,128)S(1)}, s32[1,32,1]{1,2,0:T(1,128)}, u32[]{:S(2)}) copy-start(s32[1,32,1]{1,2,0:T(1,128)} %param.15) | copy-start | bytes 388
  8.5 8.4 %copy-start.1 = (bf16[1,32,4,576]{3,2,1,0:T(4,128)(2,1)S(1)}, bf16[1,32,4,576]{3,2,1,0:T(4,128)(2,1)}, u32[]{:S(2)}) copy-start(bf16[1,32,4,576]{3,2,1,0:T(4,128)(2,1)} %param.14) | copy-start | bytes 442372
  8.5 170.5 %all-to-all-start.2 = ((bf16[32,32,3584]{2,1,0:T(8,128)(2,1)}), bf16[32,32,3584]{2,1,0:T(8,128)(2,1)}, u32[]{:S(2)}, u32[]{:S(2)}) async-start(bf16[32,32,3584]{2,1,0:T(8,128)(2,1)} %bitcast.55), calls=%async_computation.2 | async-start | bytes 14680064 | tf_op jit(solution)/shard_map/all_to_all | solution.py:129
  179.0 17.3 %all-to-all-start = ((s32[32,1,2]{2,1,0:T(1,128)}), s32[32,1,2]{2,1,0:T(1,128)S(1)}, u32[]{:S(2)}, u32[]{:S(2)}) async-start(s32[32,1,2]{2,1,0:T(1,128)} %bitcast.2), calls=%async_computation | async-start | bytes 32768 | tf_op jit(solution)/shard_map/all_to_all | solution.py:98
  181.5 7.5 %copy-start.3 = (bf16[1,3584,512]{2,1,0:T(8,128)(2,1)S(1)}, bf16[1,3584,512]{2,1,0:T(8,128)(2,1)}, u32[]{:S(2)}) copy-start(bf16[1,3584,512]{2,1,0:T(8,128)(2,1)} %param.19) | copy-start | bytes 11010052
  196.3 17.8 %all-to-all-start.1 = ((bf16[32,8,576]{2,1,0:T(8,128)(2,1)}), bf16[32,8,576]{2,1,0:T(8,128)(2,1)S(1)}, u32[]{:S(2)}, u32[]{:S(2)}) async-start(bf16[32,8,576]{2,1,0:T(8,128)(2,1)} %reshape.163), calls=%async_computation.1 | async-start | bytes 655360 | tf_op jit(solution)/shard_map/all_to_all | solution.py:91
  211.5 6.7 %copy-start.2 = (f32[32,8]{0,1:T(8,128)S(1)}, f32[32,8]{0,1:T(8,128)}, u32[]{:S(2)}) copy-start(f32[32,8]{0,1:T(8,128)} %param.18) | copy-start | bytes 3076
  211.5 8.9 %copy-start.4 = (bf16[1,1024,576]{1,2,0:T(8,128)(2,1)S(1)}, bf16[1,1024,576]{1,2,0:T(8,128)(2,1)}, u32[]{:S(2)}) copy-start(bf16[1,1024,576]{1,2,0:T(8,128)(2,1)} %param.12) | copy-start | bytes 3538948
  211.5 8.9 %copy-start.5 = (bf16[1,128,576]{1,2,0:T(8,128)(2,1)S(1)}, bf16[1,128,576]{1,2,0:T(8,128)(2,1)}, u32[]{:S(2)}) copy-start(bf16[1,128,576]{1,2,0:T(8,128)(2,1)} %param.11) | copy-start | bytes 442372
  214.2 330.1 %all-to-all-start.3 = ((f32[32,32,3584]{2,1,0:T(8,128)}), f32[32,32,3584]{2,1,0:T(8,128)}, u32[]{:S(2)}, u32[]{:S(2)}) async-start(f32[32,32,3584]{2,1,0:T(8,128)} %fusion), calls=%async_computation.3 | async-start | bytes 29360128 | tf_op jit(solution)/shard_map/all_to_all | solution.py:149
where the time goes:
time: 557 us
  waiting for transfers between devices  484 us (87%)
  matrix products  44.1 us (8%)
  starting transfers between devices  19.8 us (4%)
    all_to_all x1, waiting for transfers between devices, per_device(): lax.all_to_all(partial_out.reshape(peers, capacity, out_width), 'ep', spl...  321 us
    all_to_all x1, waiting for transfers between devices, per_device(): lax.all_to_all(outgoing.reshape(peers, capacity, tokens.shape[1]), 'ep',...  160 us
    dot_general x1, matrix products, per_device(): jnp.dot(mixing, back.reshape(peers * capacity, out_width), precision=lax....  12.3 us
  transfers between devices with their start and end apart: 4, of which 3 were waited for; matrix products, arithmetic and copies ran while one was open for 5% of the time, Pallas kernels for 0%

commit v1 on v0

v1 whole, which is shorter than its diff:
```python
import jax
import jax.numpy as jnp
from jax import lax
from jax.sharding import PartitionSpec as P

VAL = 512


SCALE = 192.0 ** (-0.5)
NEG = -1e30


def combined_all(x, axis, combine):
    if lax.axis_size(axis) == 1:
        return x
    everything = jax.tree.map(lambda part: lax.all_gather(part, axis), x)
    leading = jax.tree.map(lambda part: part[0], everything)

    def lap(k, so_far):
        return combine(so_far, jax.tree.map(lambda part: part[k], everything))

    return lax.fori_loop(1, lax.axis_size(axis), lap, leading)


def attend_keys(query, keys, valid, value_width):
    scores = (
        lax.dot_general(query, keys, (((1,), (1,)), ((), ())), preferred_element_type=jnp.float32)
        * SCALE
    )
    scores = jnp.where(valid[None, :], scores, NEG)
    peak = jnp.max(scores, axis=1)
    expo = jnp.where(valid[None, :], jnp.exp(scores - peak[:, None]), 0.0)
    total = jnp.sum(expo, axis=1)
    mixed = jnp.dot(
        expo.astype(jnp.bfloat16), keys[:, :value_width], preferred_element_type=jnp.float32
    )
    return (peak, total, mixed)


def join_parts(first, second):
    peak = jnp.maximum(first[0], second[0])
    left = jnp.exp(first[0] - peak)
    right = jnp.exp(second[0] - peak)
    return (
        peak,
        first[1] * left + second[1] * right,
        first[2] * left[:, None] + second[2] * right[:, None],
    )


def per_device(
    query_latent,
    latent_cache,
    cache_length,
    prefill_latent,
    block_owner,
    tokens,
    expert_ids,
    route_weight,
    gate_weight,
    up_weight,
    down_weight,
):
    peers = lax.axis_size("ep")
    blocks = prefill_latent.shape[1]
    block_len = prefill_latent.shape[2]
    latent = prefill_latent.shape[3]
    tok_rows, top_k = expert_ids.shape

    rows = lax.all_gather(tokens, "ep", axis=0, tiled=True)

    owner = block_owner.reshape(blocks)
    same = owner[:, None] == owner[None, :]
    earlier = jnp.arange(blocks)[None, :] < jnp.arange(blocks)[:, None]
    order_in = jnp.sum(jnp.logical_and(same, earlier).astype(jnp.int32), axis=1)
    target = owner * 2 + order_in
    chosen = jnp.arange(2 * peers, dtype=jnp.int32)[:, None] == target[None, :]
    filled = jnp.sum(chosen.astype(jnp.float32), axis=1)
    expert_of = jnp.arange(peers, dtype=jnp.int32) // 2
    named = expert_ids[None, :, :] == expert_of[:, None, None]
    share = jnp.sum(jnp.where(named, route_weight[None, :, :], 0.0), axis=2)
    small = lax.all_to_all(
        jnp.concatenate([share, filled.reshape(peers, 2)], axis=1),
        "ep",
        split_axis=0,
        concat_axis=0,
        tiled=True,
    )
    scale_rows = small[:, :tok_rows].reshape(peers * tok_rows)
    present = small[:, tok_rows:].reshape(peers * 2)

    packed = jnp.dot(
        chosen.astype(jnp.bfloat16),
        prefill_latent.reshape(blocks, block_len * latent),
        preferred_element_type=jnp.float32,
    ).astype(jnp.bfloat16)
    arrived = lax.all_to_all(
        packed.reshape(peers, 2 * block_len, latent),
        "ep",
        split_axis=0,
        concat_axis=0,
        tiled=True,
    )
    shard_len = latent_cache.shape[1]
    positions = lax.axis_index("tp") * shard_len + jnp.arange(shard_len, dtype=jnp.int32)
    keys = jnp.concatenate(
        [latent_cache[0], arrived.reshape(peers * 2 * block_len, latent)], axis=0
    )
    valid = jnp.concatenate([positions < cache_length[0], jnp.repeat(present > 0, block_len)])
    peak, total, mixed = attend_keys(query_latent[0], keys, valid, VAL)
    peak, total, mixed = combined_all((peak, total, mixed), "tp", join_parts)
    attn_out = (mixed / total[:, None]).astype(jnp.bfloat16)[None]

    gate = jnp.dot(rows, gate_weight[0], preferred_element_type=jnp.float32)
    upper = jnp.dot(rows, up_weight[0], preferred_element_type=jnp.float32)
    hidden = (jax.nn.silu(gate) * upper).astype(jnp.bfloat16)
    if lax.axis_size("tp") > 1:
        hidden = lax.all_gather(hidden, "tp", axis=1, tiled=True)
    partial_out = (
        jnp.dot(hidden, down_weight[0], preferred_element_type=jnp.float32) * scale_rows[:, None]
    )
    combined = lax.psum_scatter(partial_out, "ep", scatter_dimension=0, tiled=True)
    moe_out = combined.astype(jnp.bfloat16)
    return (attn_out, moe_out)


def solution(mesh):
    in_specs = (
        P(("groups", "ep"), None, None),
        P(("groups", "ep"), "tp", None),
        P(("groups", "ep")),
        P(("groups", "ep"), "tp", None, None),
        P(("groups", "ep"), "tp", None),
        P(("groups", "ep"), None),
        P(("groups", "ep"), None),
        P(("groups", "ep"), None),
        P("ep", None, "tp"),
        P("ep", None, "tp"),
        P("ep", None, "tp"),
    )
    out_specs = (P(("groups", "ep"), None, None), P(("groups", "ep"), "tp"))
    return jax.shard_map(
        per_device, mesh=mesh, in_specs=in_specs, out_specs=out_specs, check_vma=False
    )
```

time: 557 us -> 284 us (0.51)
  waiting for transfers between devices: 484 us -> 218 us
  matrix products: 44.1 us -> 25.4 us
  starting transfers between devices: 19.8 us -> 3.23 us
  blocking collectives: 0 us -> 14.2 us
  between operations: 1.49 us -> 14.8 us
    all_to_all x3 -> x0, waiting for transfers between devices: 482 us -> none  [the longest x1 321 us: per_device(): lax.all_to_all(partial_out.reshape(peers, capacity, out_width), 'ep', spl...]
    reduce_scatter x0 -> x1, waiting for transfers between devices: none -> 138 us  [per_device(): lax.psum_scatter(partial_out, 'ep', scatter_dimension=0, tiled=True)]
    all_gather x0 -> x1, waiting for transfers between devices: none -> 62.1 us  [per_device(): rows = lax.all_gather(tokens, 'ep', axis=0, tiled=True)]
    dot_general x5 -> x2, matrix products: 41.5 us -> 22.8 us  [the longest x1 15.5 us: per_device(): jnp.dot(hidden, down_weight[0], preferred_element_type=jnp.float32)]
    all_to_all x1, waiting for transfers between devices: 2.66 us -> 17 us  [per_device(): lax.all_to_all(packed.reshape(peers, 2 * block_len, latent), 'ep', split_...]
    all_to_all x0 -> x1, blocking collectives: none -> 14.2 us  [per_device(): lax.all_to_all(jnp.concatenate([share, filled.reshape(peers, 2)], axis=1)...]
    all_to_all x3 -> x0, starting transfers between devices: 14 us -> none  [the longest x1 7.4 us: per_device(): lax.all_to_all(outgoing.reshape(peers, capacity, tokens.shape[1]), 'ep',...]
  transfers between devices with their start and end apart: 4 -> 3, of which waited for: 3 -> 3; matrix products, arithmetic and copies ran while one was open for 5% -> 3% of each run, Pallas kernels for 0% -> 0%
where the time goes in v1:
time: 284 us; the launch traced here: 283 us
  waiting for transfers between devices  218 us (77%)
  matrix products  25.4 us (9%)
  between operations  14.8 us (5%)
  blocking collectives  14.2 us (5%)
  other arithmetic  4.64 us (2%)
  starting transfers between devices  3.23 us (1%)
    reduce_scatter x1, waiting for transfers between devices, per_device(): lax.psum_scatter(partial_out, 'ep', scatter_dimension=0, tiled=True)  138 us
    all_gather x1, waiting for transfers between devices, per_device(): rows = lax.all_gather(tokens, 'ep', axis=0, tiled=True)  62.1 us
    all_to_all x1, waiting for transfers between devices, per_device(): lax.all_to_all(packed.reshape(peers, 2 * block_len, latent), 'ep', split_...  17 us
    dot_general x1, matrix products, per_device(): jnp.dot(hidden, down_weight[0], preferred_element_type=jnp.float32)  15.5 us
    all_to_all x1, blocking collectives, per_device(): lax.all_to_all(jnp.concatenate([share, filled.reshape(peers, 2)], axis=1)...  14.2 us
    dot_general x1, matrix products, per_device(): upper = jnp.dot(rows, up_weight[0], preferred_element_type=jnp.float32)  7.28 us
  transfers between devices with their start and end apart: 3, of which 3 were waited for; matrix products, arithmetic and copies ran while one was open for 3% of the time, Pallas kernels for 0%

profile of v1, /device:TPU:0, one launch (start us, length us, event | category | flops | bytes accessed | tf_op | source)
XLA Modules:
  0.0 283.3 jit_solution(5194868378086051490)
XLA Ops:
  7.2 0.0 copy-start
  7.2 0.0 all-gather.2.cloned.1.call-start
  7.2 0.7 all-gather.2.cloned.1.call-update
  7.9 0.0 reduce-scatter.2.cloned.1.call-start
  8.0 0.9 convert_reduce_fusion.1
  8.9 0.7 multiply_add_fusion
  9.5 0.1 convert_reduce_fusion
  9.6 0.1 reshape.57
  9.7 0.8 select_reduce_fusion
  10.6 0.1 pad_maximum_fusion
  10.6 14.2 %all_to_all.17 = f32[32,1,34]{2,1,0:T(1,128)S(1)} all-to-all(f32[32,1,34]{2,1,0:T(1,128)S(1)} %bitcast.37), channel_id=1, replica_groups=mesh['groups'=1,'ep'=32,'tp'=1] {'ep'}, dimensions={0} | all-to-all | bytes 8704 | tf_op jit(solution)/shard_map/all_to_all | solution.py:82
  24.9 0.1 mul.38
  25.0 62.1 %all-gather.2.cloned.1.call-done = bf16[1024,3584]{1,0:T(8,128)(2,1)} async-done(((bf16[32,3584]{1,0:T(8,128)(2,1)}), bf16[1024,3584]{1,0:T(8,128)(2,1)}) %all-gather.2.cloned.1.call-update) | async-done | bytes 7340048 | tf_op jit(solution)/shard_map/all_gather | solution.py:70
  87.1 7.3 %fusion.1 = f32[1024,512]{1,0:T(8,128)S(1)} fusion(bf16[1024,3584]{1,0:T(8,128)(2,1)} %all-gather.2.cloned.1.call-done, bf16[1,3584,512]{2,1,0:T(8,128)(2,1)} %param.20), kind=kOutput, calls=%fused_computation.2 | convolution fusion | flops 3758096384 | bytes 13107200 | tf_op jit(solution)/shard_map/dot_general | solution.py:115
  94.4 15.5 %convolution_multiply_fusion = f32[1024,3584]{1,0:T(8,128)} fusion(f32[1024]{0:T(1024)S(1)} %mul.38, bf16[1,512,3584]{2,1,0:T(8,128)(2,1)} %param.21, f32[1024,512]{1,0:T(8,128)S(1)} %fusion.1, bf16[1024,3584]{1,0:T(8,128)(2,1)} %all-gather.2.cloned.1.call-done, bf16[1,3584,512]{2,1,0:T(8,128)(2,1)} %param.19), kind=kOutput, calls=%fused_computation | convolution fusion | flops 7523008512 | bytes 31461376 | tf_op jit(solution)/shard_map/dot_general | solution.py:120
  109.9 0.0 reduce-scatter.2.cloned.1.call-update
  109.9 0.9 copy-done.1
  110.8 0.2 reshape.59
  111.0 0.3 convolution_convert_fusion
  111.3 1.1 reshape.60
  112.5 3.2 %all-to-all-start.1 = ((bf16[32,8,576]{2,1,0:T(8,128)(2,1)}), bf16[32,8,576]{2,1,0:T(8,128)(2,1)S(1)}, u32[]{:S(2)}, u32[]{:S(2)}) async-start(bf16[32,8,576]{2,1,0:T(8,128)(2,1)} %reshape.60), calls=%async_computation.1 | async-start | bytes 655360 | tf_op jit(solution)/shard_map/all_to_all | solution.py:97
  116.3 0.1 slice_compare_fusion
  116.4 0.1 gt.11
  116.5 0.1 broadcast_in_dim.51
  116.6 0.1 reshape.58
  116.7 17.0 %all-to-all-done.1 = bf16[32,8,576]{2,1,0:T(8,128)(2,1)S(1)} async-done(((bf16[32,8,576]{2,1,0:T(8,128)(2,1)}), bf16[32,8,576]{2,1,0:T(8,128)(2,1)S(1)}, u32[]{:S(2)}, u32[]{:S(2)}) %all-to-all-start.1) | async-done | bytes 294944 | tf_op jit(solution)/shard_map/all_to_all | solution.py:97
  133.7 0.2 copy.23
  133.9 0.7 fusion.40
  134.6 0.3 fusion.27
  134.8 1.5 fusion.23
  136.4 138.3 %reduce-scatter.2.cloned.1.call-done = f32[32,3584]{1,0:T(8,128)} async-done(((f32[1024,3584]{1,0:T(8,128)}), f32[32,3584]{1,0:T(8,128)}) %reduce-scatter.2.cloned.1.call-update) | async-done | bytes 458768 | tf_op jit(solution)/shard_map/reduce_scatter | solution.py:122
  274.7 1.7 convert_element_type.28
  (7 shorter events, 0.0 us)
Async XLA Ops:
  7.2 126.7 %copy-start = (bf16[1,128,576]{1,2,0:T(8,128)(2,1)S(1)}, bf16[1,128,576]{1,2,0:T(8,128)(2,1)}, u32[]{:S(2)}) copy-start(bf16[1,128,576]{1,2,0:T(8,128)(2,1)} %param.11) | copy-start | bytes 442372
  7.2 79.9 %all-gather.2.cloned.1.call-start = ((), (), s32[]{:S(2)}) async-start(), calls=%async_computation.3 | async-start | bytes 7569408 | tf_op jit(solution)/shard_map/all_gather | solution.py:70
  7.9 266.8 %reduce-scatter.2.cloned.1.call-start = ((), (), s32[]{:S(2)}) async-start(), calls=%async_computation.4 | async-start | bytes 15138816 | tf_op jit(solution)/shard_map/reduce_scatter | solution.py:122
  109.9 0.9 copy-start.1
  109.9 23.9 %copy-start.2 = (bf16[1,1024,576]{1,2,0:T(8,128)(2,1)S(1)}, bf16[1,1024,576]{1,2,0:T(8,128)(2,1)}, u32[]{:S(2)}) copy-start(bf16[1,1024,576]{1,2,0:T(8,128)(2,1)} %param.12) | copy-start | bytes 3538948
  112.5 21.2 %all-to-all-start.1 = ((bf16[32,8,576]{2,1,0:T(8,128)(2,1)}), bf16[32,8,576]{2,1,0:T(8,128)(2,1)S(1)}, u32[]{:S(2)}, u32[]{:S(2)}) async-start(bf16[32,8,576]{2,1,0:T(8,128)(2,1)} %reshape.60), calls=%async_computation.1 | async-start | bytes 655360 | tf_op jit(solution)/shard_map/all_to_all | solution.py:97
Sparse Core Ops, SparseCore 0:
  10.8 76.1 all-gather.1
  110.0 164.6 reduce-scatter.1

commit v2 on v1

--- a/solution.py
+++ b/solution.py
@@ -46,6 +46,78 @@
         first[1] * left + second[1] * right,
         first[2] * left[:, None] + second[2] * right[:, None],
     )
+
+
+def ring_experts(tokens, scale_rows, gate_weight, up_weight, down_weight):
+    rows = lax.all_gather(tokens, "ep", axis=0, tiled=True)
+    gate = jnp.dot(rows, gate_weight[0], preferred_element_type=jnp.float32)
+    upper = jnp.dot(rows, up_weight[0], preferred_element_type=jnp.float32)
+    hidden = (jax.nn.silu(gate) * upper).astype(jnp.bfloat16)
+    if lax.axis_size("tp") > 1:
+        hidden = lax.all_gather(hidden, "tp", axis=1, tiled=True)
+    partial_out = (
+        jnp.dot(hidden, down_weight[0], preferred_element_type=jnp.float32) * scale_rows[:, None]
+    )
+    return lax.psum_scatter(partial_out, "ep", scatter_dimension=0, tiled=True)
+
+
+def grid_experts(tokens, share, gate_weight, up_weight, down_weight):
+    peers = lax.axis_size("ep")
+    chips = peers // 2
+    planes = chips // 4
+
+    def flip(value, chip_bits):
+        return lax.ppermute(value, "ep", [(i, i ^ (2 * chip_bits)) for i in range(peers)])
+
+    def swap(value):
+        return lax.ppermute(value, "ep", [(i, i ^ 1) for i in range(peers)])
+
+    gate_both = jnp.concatenate([gate_weight[0], swap(gate_weight[0])], axis=1)
+    up_both = jnp.concatenate([up_weight[0], swap(up_weight[0])], axis=1)
+    down_both = jnp.concatenate([down_weight[0], swap(down_weight[0])], axis=0)
+
+    held = {}
+    for plane in range(planes):
+        held[plane, 0] = tokens if plane == 0 else flip(tokens, 4 * plane)
+    for plane in range(planes):
+        held[plane, 1] = flip(held[plane, 0], 1)
+        held[plane, 2] = flip(held[plane, 0], 2)
+        if plane % 2 == 0:
+            held[plane, 3] = flip(held[plane, 2], 1)
+        else:
+            held[plane, 3] = flip(held[plane, 1], 2)
+
+    tok_rows = tokens.shape[0]
+    me = lax.axis_index("ep")
+    slots = jnp.bitwise_xor(me, 2 * jnp.arange(chips, dtype=jnp.int32))
+    picks = slots[:, None] == jnp.arange(peers, dtype=jnp.int32)[None, :]
+    scales = jnp.sum(jnp.where(picks[:, :, None], share[None, :, :], 0.0), axis=1)
+
+    partial_of = {}
+    for first in range(planes - 2, -1, -2):
+        keys = [(plane, kind) for plane in (first, first + 1) for kind in range(4)]
+        rows = jnp.concatenate([held[key] for key in keys], axis=0)
+        gate = jnp.dot(rows, gate_both, preferred_element_type=jnp.float32)
+        upper = jnp.dot(rows, up_both, preferred_element_type=jnp.float32)
+        hidden = (jax.nn.silu(gate) * upper).astype(jnp.bfloat16)
+        scale = scales[4 * first : 4 * first + 8].reshape(8 * tok_rows)
+        outs = jnp.dot(hidden, down_both, preferred_element_type=jnp.float32) * scale[:, None]
+        for at, key in enumerate(keys):
+            partial_of[key] = outs[at * tok_rows : (at + 1) * tok_rows]
+
+    total = None
+    for plane in range(planes - 1, -1, -1):
+        if plane % 2 == 0:
+            via_x = partial_of[plane, 1]
+            via_y = partial_of[plane, 2] + flip(partial_of[plane, 3], 1)
+        else:
+            via_x = partial_of[plane, 1] + flip(partial_of[plane, 3], 2)
+            via_y = partial_of[plane, 2]
+        mine = partial_of[plane, 0] + flip(via_x, 1) + flip(via_y, 2)
+        if plane > 0:
+            mine = flip(mine, 4 * plane)
+        total = mine if total is None else total + mine
+    return total
 
 
 def per_device(
@@ -66,29 +138,28 @@
     block_len = prefill_latent.shape[2]
     latent = prefill_latent.shape[3]
     tok_rows, top_k = expert_ids.shape
-
-    rows = lax.all_gather(tokens, "ep", axis=0, tiled=True)
+    experts = peers // 2
 
     owner = block_owner.reshape(blocks)
+    named = expert_ids[:, :, None] == jnp.arange(experts, dtype=jnp.int32)[None, None, :]
+    share = jnp.sum(jnp.where(named, route_weight[:, :, None], 0.0), axis=1)
+    routing = lax.all_gather(
+        jnp.concatenate([share.reshape(tok_rows * experts), owner.astype(jnp.float32)]), "ep"
+    )
+    me = lax.axis_index("ep")
+    share_all = routing[:, : tok_rows * experts].reshape(peers, tok_rows, experts)
+    my_expert = jnp.arange(experts, dtype=jnp.int32) == me // 2
+    share_mine = jnp.sum(jnp.where(my_expert[None, None, :], share_all, 0.0), axis=2)
+    sent_here = jnp.sum(
+        (routing[:, tok_rows * experts :] == me.astype(jnp.float32)).astype(jnp.int32), axis=1
+    )
+    present = (jnp.arange(2)[None, :] < sent_here[:, None]).reshape(peers * 2)
+
     same = owner[:, None] == owner[None, :]
     earlier = jnp.arange(blocks)[None, :] < jnp.arange(blocks)[:, None]
     order_in = jnp.sum(jnp.logical_and(same, earlier).astype(jnp.int32), axis=1)
     target = owner * 2 + order_in
     chosen = jnp.arange(2 * peers, dtype=jnp.int32)[:, None] == target[None, :]
-    filled = jnp.sum(chosen.astype(jnp.float32), axis=1)
-    expert_of = jnp.arange(peers, dtype=jnp.int32) // 2
-    named = expert_ids[None, :, :] == expert_of[:, None, None]
-    share = jnp.sum(jnp.where(named, route_weight[None, :, :], 0.0), axis=2)
-    small = lax.all_to_all(
-        jnp.concatenate([share, filled.reshape(peers, 2)], axis=1),
-        "ep",
-        split_axis=0,
-        concat_axis=0,
-        tiled=True,
-    )
-    scale_rows = small[:, :tok_rows].reshape(peers * tok_rows)
-    present = small[:, tok_rows:].reshape(peers * 2)
-
     packed = jnp.dot(
         chosen.astype(jnp.bfloat16),
         prefill_latent.reshape(blocks, block_len * latent),
@@ -106,20 +177,17 @@
     keys = jnp.concatenate(
         [latent_cache[0], arrived.reshape(peers * 2 * block_len, latent)], axis=0
     )
-    valid = jnp.concatenate([positions < cache_length[0], jnp.repeat(present > 0, block_len)])
+    valid = jnp.concatenate([positions < cache_length[0], jnp.repeat(present, block_len)])
     peak, total, mixed = attend_keys(query_latent[0], keys, valid, VAL)
     peak, total, mixed = combined_all((peak, total, mixed), "tp", join_parts)
     attn_out = (mixed / total[:, None]).astype(jnp.bfloat16)[None]
 
-    gate = jnp.dot(rows, gate_weight[0], preferred_element_type=jnp.float32)
-    upper = jnp.dot(rows, up_weight[0], preferred_element_type=jnp.float32)
-    hidden = (jax.nn.silu(gate) * upper).astype(jnp.bfloat16)
-    if lax.axis_size("tp") > 1:
-        hidden = lax.all_gather(hidden, "tp", axis=1, tiled=True)
-    partial_out = (
-        jnp.dot(hidden, down_weight[0], preferred_element_type=jnp.float32) * scale_rows[:, None]
-    )
-    combined = lax.psum_scatter(partial_out, "ep", scatter_dimension=0, tiled=True)
+    if peers == 32 and lax.axis_size("tp") == 1:
+        combined = grid_experts(tokens, share_mine, gate_weight, up_weight, down_weight)
+    else:
+        combined = ring_experts(
+            tokens, share_mine.reshape(peers * tok_rows), gate_weight, up_weight, down_weight
+        )
     moe_out = combined.astype(jnp.bfloat16)
     return (attn_out, moe_out)
 

time: 284 us -> 327 us (1.15)
  the two profiles are of different devices: /device:TPU:0 before, /device:TPU:8 now
where the time goes in v2:
time: 327 us
  waiting for transfers between devices  206 us (63%)
  starting transfers between devices  42.1 us (13%)
  matrix products  39.4 us (12%)
  local copies, waits for them, and re-layouts  17.5 us (5%)
  between operations  15 us (5%)
  other arithmetic  7.48 us (2%)
    unnamed x2, waiting for transfers between devices  113 us
    ppermute x30, waiting for transfers between devices, flip(): lax.ppermute(value, 'ep', [(i, i ^ 2 * chip_bits) for i in range(peers)])  92.2 us
    ppermute x30, starting transfers between devices, flip(): lax.ppermute(value, 'ep', [(i, i ^ 2 * chip_bits) for i in range(peers)])  38.1 us
    dot_general x2, matrix products, grid_experts(): jnp.dot(hidden, down_both, preferred_element_type=jnp.float32)  23.3 us
    dot_general x2, matrix products, grid_experts(): upper = jnp.dot(rows, up_both, preferred_element_type=jnp.float32)  13.6 us
    unnamed x29, local copies, waits for them, and re-layouts  9.4 us
  transfers between devices with their start and end apart: 35, of which 18 were waited for; matrix products, arithmetic and copies ran while one was open for 15% of the time, Pallas kernels for 0%

profile of v2, /device:TPU:8, one launch (start us, length us, event | category | flops | bytes accessed | tf_op | source)
XLA Modules:
  0.0 326.9 jit_solution(18079644955798112441)
XLA Ops:
  7.2 2.7 collective-permute-start
  9.9 1.5 collective-permute-start.20
  12.9 1.8 collective-permute-start.22
  21.0 3.3 all-to-all-start
  24.3 1.6 constant_dynamic-update-slice_fusion.15
  26.7 113.3 %all-reduce.3.cloned.1.call-done = f32[17408]{0:T(1024)} async-done(((f32[17408]{0:T(1024)}), f32[17408]{0:T(1024)}) %all-reduce.3.cloned.1.call-update) | async-done | bytes 69648
  145.8 5.4 %collective-permute-done.1 = bf16[32,3584]{1,0:T(8,128)(2,1)S(1)} collective-permute-done((bf16[32,3584]{1,0:T(8,128)(2,1)S(1)}, bf16[32,3584]{1,0:T(8,128)(2,1)S(1)}, u32[]{:S(2)}, u32[]{:S(2)}) %collective-permute-start.1) | collective-permute-done | bytes 229408 | tf_op jit(solution)/shard_map/ppermute | solution.py:70
  152.6 5.2 %collective-permute-done.21 = bf16[32,3584]{1,0:T(8,128)(2,1)S(1)} collective-permute-done((bf16[32,3584]{1,0:T(8,128)(2,1)S(1)}, bf16[32,3584]{1,0:T(8,128)(2,1)S(1)}, u32[]{:S(2)}, u32[]{:S(2)}) %collective-permute-start.21) | collective-permute-done | bytes 229408 | tf_op jit(solution)/shard_map/ppermute | solution.py:70
  160.7 5.9 %collective-permute-done.2 = bf16[32,3584]{1,0:T(8,128)(2,1)S(1)} collective-permute-done((bf16[32,3584]{1,0:T(8,128)(2,1)S(1)}, bf16[32,3584]{1,0:T(8,128)(2,1)S(1)}, u32[]{:S(2)}, u32[]{:S(2)}) %collective-permute-start.2) | collective-permute-done | bytes 229408 | tf_op jit(solution)/shard_map/ppermute | solution.py:70
  168.1 1.5 collective-permute-start.24
  169.6 4.2 %collective-permute-done.23 = bf16[32,3584]{1,0:T(8,128)(2,1)S(1)} collective-permute-done((bf16[32,3584]{1,0:T(8,128)(2,1)S(1)}, bf16[32,3584]{1,0:T(8,128)(2,1)S(1)}, u32[]{:S(2)}, u32[]{:S(2)}) %collective-permute-start.23) | collective-permute-done | bytes 229408 | tf_op jit(solution)/shard_map/ppermute | solution.py:70
  177.4 4.9 %collective-permute-done.5 = bf16[32,3584]{1,0:T(8,128)(2,1)S(1)} collective-permute-done((bf16[32,3584]{1,0:T(8,128)(2,1)S(1)}, bf16[32,3584]{1,0:T(8,128)(2,1)S(1)}, u32[]{:S(2)}, u32[]{:S(2)}) %collective-permute-start.5) | collective-permute-done | bytes 229408 | tf_op jit(solution)/shard_map/ppermute | solution.py:70
  188.7 2.2 collective-permute-done.6
  193.0 2.4 collective-permute-done.7
  196.1 1.7 collective-permute-done.25
  198.6 6.8 %fusion.1 = f32[256,1024]{1,0:T(8,128)} fusion(bf16[256,3584]{1,0:T(8,128)(2,1)} %constant_dynamic-update-slice_fusion, bf16[3584,512]{1,0:T(8,128)(2,1)} %collective-permute-done.9, bf16[3584,512]{1,0:T(8,128)(2,1)} %bitcast.26), kind=kOutput, calls=%fused_computation.6 | convolution fusion | flops 1893728256 | bytes 10223616 | tf_op jit(solution)/shard_map/dot_general | solution.py:101
  205.4 11.4 %convolution_multiply_fusion.1 = f32[256,3584]{1,0:T(8,128)} fusion(bf16[512,3584]{1,0:T(8,128)(2,1)} %collective-permute-done.10, bf16[512,3584]{1,0:T(8,128)(2,1)} %bitcast.29, f32[256]{0:T(256)S(1)} %mul.65, f32[256,1024]{1,0:T(8,128)} %fusion.1, bf16[256,3584]{1,0:T(8,128)(2,1)S(1)} %copy-done.5, bf16[3584,512]{1,0:T(8,128)(2,1)} %collective-permute-done.8, ...), kind=kOutput, calls=%fused_computation.4 | convolution fusion | flops 3789946880 | bytes 21234688 | tf_op jit(solution)/shard_map/dot_general | solution.py:104
  218.1 1.5 collective-permute-start.16
  220.2 6.7 %fusion = f32[256,1024]{1,0:T(8,128)} fusion(bf16[256,3584]{1,0:T(8,128)(2,1)} %constant_dynamic-update-slice_fusion.8, bf16[3584,512]{1,0:T(8,128)(2,1)} %collective-permute-done.9, bf16[3584,512]{1,0:T(8,128)(2,1)} %bitcast.27), kind=kOutput, calls=%fused_computation.5 | convolution fusion | flops 1893728256 | bytes 10223616 | tf_op jit(solution)/shard_map/dot_general | solution.py:101
  226.9 11.9 %convolution_multiply_fusion = f32[256,3584]{1,0:T(8,128)} fusion(bf16[512,3584]{1,0:T(8,128)(2,1)} %collective-permute-done.10, bf16[512,3584]{1,0:T(8,128)(2,1)} %bitcast.30, f32[256]{0:T(256)S(1)} %mul.70, f32[256,1024]{1,0:T(8,128)} %fusion, bf16[256,3584]{1,0:T(8,128)(2,1)} %constant_dynamic-update-slice_fusion.8, ...), kind=kOutput, calls=%fused_computation.3 | convolution fusion | flops 3789946880 | bytes 21234688 | tf_op jit(solution)/shard_map/dot_general | solution.py:104
  240.0 1.5 collective-permute-start.26
  243.5 10.0 %collective-permute-done.26 = f32[32,3584]{1,0:T(8,128)S(1)} collective-permute-done((f32[32,3584]{1,0:T(8,128)S(1)}, f32[32,3584]{1,0:T(8,128)S(1)}, u32[]{:S(2)}, u32[]{:S(2)}) %collective-permute-start.26) | collective-permute-done | bytes 458784 | tf_op jit(solution)/shard_map/ppermute | solution.py:70
  254.8 1.5 collective-permute-start.27
  257.7 5.6 %collective-permute-done.17 = f32[32,3584]{1,0:T(8,128)S(1)} collective-permute-done((f32[32,3584]{1,0:T(8,128)S(1)}, f32[32,3584]{1,0:T(8,128)S(1)}, u32[]{:S(2)}, u32[]{:S(2)}) %collective-permute-start.17) | collective-permute-done | bytes 458784 | tf_op jit(solution)/shard_map/ppermute | solution.py:70
  263.5 1.5 collective-permute-start.11
  267.0 6.2 %collective-permute-done.28 = f32[32,3584]{1,0:T(8,128)S(1)} collective-permute-done((f32[32,3584]{1,0:T(8,128)S(1)}, f32[32,3584]{1,0:T(8,128)S(1)}, u32[]{:S(2)}, u32[]{:S(2)}) %collective-permute-start.28) | collective-permute-done | bytes 458784 | tf_op jit(solution)/shard_map/ppermute | solution.py:70
  274.8 8.2 %collective-permute-done.11 = f32[32,3584]{1,0:T(8,128)S(1)} collective-permute-done((f32[32,3584]{1,0:T(8,128)S(1)}, f32[32,3584]{1,0:T(8,128)S(1)}, u32[]{:S(2)}, u32[]{:S(2)}) %collective-permute-start.11) | collective-permute-done | bytes 458784 | tf_op jit(solution)/shard_map/ppermute | solution.py:70
  284.5 2.0 collective-permute-done.31
  288.0 2.0 collective-permute-done.13
  291.5 10.0 %collective-permute-done.12 = f32[32,3584]{1,0:T(8,128)S(1)} collective-permute-done((f32[32,3584]{1,0:T(8,128)S(1)}, f32[32,3584]{1,0:T(8,128)S(1)}, u32[]{:S(2)}, u32[]{:S(2)}) %collective-permute-start.12) | collective-permute-done | bytes 458784 | tf_op jit(solution)/shard_map/ppermute | solution.py:70
  302.7 1.5 fusion.18
  304.3 15.0 %collective-permute-done.14 = f32[32,3584]{1,0:T(8,128)S(1)} collective-permute-done((f32[32,3584]{1,0:T(8,128)S(1)}, f32[32,3584]{1,0:T(8,128)S(1)}, u32[]{:S(2)}, u32[]{:S(2)}) %collective-permute-start.14) | collective-permute-done | bytes 458784 | tf_op jit(solution)/shard_map/ppermute | solution.py:70
  (117 shorter events, 50.8 us)
Async XLA Ops:
  7.2 132.9 %all-reduce.3.cloned.1.call-start = ((), (), s32[]{:S(2)}) async-start(), calls=%async_computation.1 | async-start | bytes 139264
  7.2 135.0 %collective-permute-start = (bf16[32,3584]{1,0:T(8,128)(2,1)}, bf16[32,3584]{1,0:T(8,128)(2,1)S(1)}, u32[]{:S(2)}, u32[]{:S(2)}) collective-permute-start(bf16[32,3584]{1,0:T(8,128)(2,1)} %param.16), channel_id=1, source_target_pairs={{0,16},{1,17},{2,18},{3,19},{4,20},{5,21},{6,22},{7,23},{8,24},{9,... | collective-permute-start | bytes 688136 | tf_op jit(solution)/shard_map/ppermute | solution.py:70
  9.9 158.2 %collective-permute-start.4 = (bf16[32,3584]{1,0:T(8,128)(2,1)}, bf16[32,3584]{1,0:T(8,128)(2,1)S(1)}, u32[]{:S(2)}, u32[]{:S(2)}) collective-permute-start(bf16[32,3584]{1,0:T(8,128)(2,1)} %param.16), channel_id=1, source_target_pairs={{0,24},{1,25},{2,26},{3,27},{4,28},{5,29},{6,30},{7,31},{8,16},{9,... | collective-permute-start | bytes 688136 | tf_op jit(solution)/shard_map/ppermute | solution.py:70
  9.9 133.8 %collective-permute-start.20 = (bf16[32,3584]{1,0:T(8,128)(2,1)}, bf16[32,3584]{1,0:T(8,128)(2,1)S(1)}, u32[]{:S(2)}, u32[]{:S(2)}) collective-permute-start(bf16[32,3584]{1,0:T(8,128)(2,1)} %param.16), channel_id=1, source_target_pairs={{0,4},{1,5},{2,6},{3,7},{4,0},{5,1},{6,2},{7,3},{8,12},{9,13},{10,... | collective-permute-start | bytes 688136 | tf_op jit(solution)/shard_map/ppermute | solution.py:70
  11.4 131.0 %collective-permute-start.19 = (bf16[32,3584]{1,0:T(8,128)(2,1)}, bf16[32,3584]{1,0:T(8,128)(2,1)S(1)}, u32[]{:S(2)}, u32[]{:S(2)}) collective-permute-start(bf16[32,3584]{1,0:T(8,128)(2,1)} %param.16), channel_id=1, source_target_pairs={{0,2},{1,3},{2,0},{3,1},{4,6},{5,7},{6,4},{7,5},{8,10},{9,11},{10,... | collective-permute-start | bytes 688136 | tf_op jit(solution)/shard_map/ppermute | solution.py:70
  12.9 145.7 %collective-permute-start.22 = (bf16[32,3584]{1,0:T(8,128)(2,1)}, bf16[32,3584]{1,0:T(8,128)(2,1)S(1)}, u32[]{:S(2)}, u32[]{:S(2)}) collective-permute-start(bf16[32,3584]{1,0:T(8,128)(2,1)} %param.16), channel_id=1, source_target_pairs={{0,8},{1,9},{2,10},{3,11},{4,12},{5,13},{6,14},{7,15},{8,0},{9,1},... | collective-permute-start | bytes 688136 | tf_op jit(solution)/shard_map/ppermute | solution.py:70
  21.0 156.2 %all-to-all-start = ((bf16[32,8,576]{2,1,0:T(8,128)(2,1)}), bf16[32,8,576]{2,1,0:T(8,128)(2,1)S(1)}, u32[]{:S(2)}, u32[]{:S(2)}) async-start(bf16[32,8,576]{2,1,0:T(8,128)(2,1)} %reshape.81), calls=%async_computation | async-start | bytes 655360 | tf_op jit(solution)/shard_map/all_to_all | solution.py:168
  142.3 56.3 %collective-permute-start.9 = (bf16[3584,512]{1,0:T(8,128)(2,1)}, bf16[3584,512]{1,0:T(8,128)(2,1)}, u32[]{:S(2)}, u32[]{:S(2)}) collective-permute-start(bf16[3584,512]{1,0:T(8,128)(2,1)} %bitcast.25), channel_id=1, source_target_pairs={{0,1},{1,0},{2,3},{3,2},{4,5},{5,4},{6,7},{7,6},{8,9},{9,8},{10,11... | collective-permute-start | bytes 11010056 | tf_op jit(solution)/shard_map/ppermute | solution.py:73
  142.4 63.0 %collective-permute-start.10 = (bf16[512,3584]{1,0:T(8,128)(2,1)}, bf16[512,3584]{1,0:T(8,128)(2,1)}, u32[]{:S(2)}, u32[]{:S(2)}) collective-permute-start(bf16[512,3584]{1,0:T(8,128)(2,1)} %bitcast.28), channel_id=1, source_target_pairs={{0,1},{1,0},{2,3},{3,2},{4,5},{5,4},{6,7},{7,6},{8,9},{9,8},{10,11... | collective-permute-start | bytes 11010056 | tf_op jit(solution)/shard_map/ppermute | solution.py:73
  143.6 7.5 %collective-permute-start.1 = (bf16[32,3584]{1,0:T(8,128)(2,1)S(1)}, bf16[32,3584]{1,0:T(8,128)(2,1)S(1)}, u32[]{:S(2)}, u32[]{:S(2)}) collective-permute-start(bf16[32,3584]{1,0:T(8,128)(2,1)S(1)} %collective-permute-done), channel_id=1, source_target_pairs={{0,2},{1,3},{2,0},{3,1},{4,6},{5,7},{6,4},{7,5},{8,10},{9,11},{10,... | collective-permute-start | bytes 688136 | tf_op jit(solution)/shard_map/ppermute | solution.py:70
  157.9 47.6 %collective-permute-start.8 = (bf16[3584,512]{1,0:T(8,128)(2,1)}, bf16[3584,512]{1,0:T(8,128)(2,1)}, u32[]{:S(2)}, u32[]{:S(2)}) collective-permute-start(bf16[3584,512]{1,0:T(8,128)(2,1)} %bitcast.31), channel_id=1, source_target_pairs={{0,1},{1,0},{2,3},{3,2},{4,5},{5,4},{6,7},{7,6},{8,9},{9,8},{10,11... | collective-permute-start | bytes 11010056 | tf_op jit(solution)/shard_map/ppermute | solution.py:73
  158.6 8.0 %collective-permute-start.2 = (bf16[32,3584]{1,0:T(8,128)(2,1)S(1)}, bf16[32,3584]{1,0:T(8,128)(2,1)S(1)}, u32[]{:S(2)}, u32[]{:S(2)}) collective-permute-start(bf16[32,3584]{1,0:T(8,128)(2,1)S(1)} %collective-permute-done), channel_id=1, source_target_pairs={{0,4},{1,5},{2,6},{3,7},{4,0},{5,1},{6,2},{7,3},{8,12},{9,13},{10,... | collective-permute-start | bytes 688136 | tf_op jit(solution)/shard_map/ppermute | solution.py:70
  168.1 7.9 %collective-permute-start.24 = (bf16[32,3584]{1,0:T(8,128)(2,1)S(1)}, bf16[32,3584]{1,0:T(8,128)(2,1)S(1)}, u32[]{:S(2)}, u32[]{:S(2)}) collective-permute-start(bf16[32,3584]{1,0:T(8,128)(2,1)S(1)} %collective-permute-done.22), channel_id=1, source_target_pairs={{0,4},{1,5},{2,6},{3,7},{4,0},{5,1},{6,2},{7,3},{8,12},{9,13},{10,... | collective-permute-start | bytes 688136 | tf_op jit(solution)/shard_map/ppermute | solution.py:70
  173.8 8.5 %collective-permute-start.5 = (bf16[32,3584]{1,0:T(8,128)(2,1)S(1)}, bf16[32,3584]{1,0:T(8,128)(2,1)S(1)}, u32[]{:S(2)}, u32[]{:S(2)}) collective-permute-start(bf16[32,3584]{1,0:T(8,128)(2,1)S(1)} %collective-permute-done.4), channel_id=1, source_target_pairs={{0,2},{1,3},{2,0},{3,1},{4,6},{5,7},{6,4},{7,5},{8,10},{9,11},{10,... | collective-permute-start | bytes 688136 | tf_op jit(solution)/shard_map/ppermute | solution.py:70
  176.0 9.1 %collective-permute-start.3 = (bf16[32,3584]{1,0:T(8,128)(2,1)S(1)}, bf16[32,3584]{1,0:T(8,128)(2,1)S(1)}, u32[]{:S(2)}, u32[]{:S(2)}) collective-permute-start(bf16[32,3584]{1,0:T(8,128)(2,1)S(1)} %collective-permute-done.2), channel_id=1, source_target_pairs={{0,2},{1,3},{2,0},{3,1},{4,6},{5,7},{6,4},{7,5},{8,10},{9,11},{10,... | collective-permute-start | bytes 688136 | tf_op jit(solution)/shard_map/ppermute | solution.py:70
  182.3 8.5 %collective-permute-start.6 = (bf16[32,3584]{1,0:T(8,128)(2,1)S(1)}, bf16[32,3584]{1,0:T(8,128)(2,1)S(1)}, u32[]{:S(2)}, u32[]{:S(2)}) collective-permute-start(bf16[32,3584]{1,0:T(8,128)(2,1)S(1)} %collective-permute-done.4), channel_id=1, source_target_pairs={{0,4},{1,5},{2,6},{3,7},{4,0},{5,1},{6,2},{7,3},{8,12},{9,13},{10,... | collective-permute-start | bytes 688136 | tf_op jit(solution)/shard_map/ppermute | solution.py:70
  185.1 10.3 %collective-permute-start.7 = (bf16[32,3584]{1,0:T(8,128)(2,1)S(1)}, bf16[32,3584]{1,0:T(8,128)(2,1)S(1)}, u32[]{:S(2)}, u32[]{:S(2)}) collective-permute-start(bf16[32,3584]{1,0:T(8,128)(2,1)S(1)} %collective-permute-done.5), channel_id=1, source_target_pairs={{0,4},{1,5},{2,6},{3,7},{4,0},{5,1},{6,2},{7,3},{8,12},{9,13},{10,... | collective-permute-start | bytes 688136 | tf_op jit(solution)/shard_map/ppermute | solution.py:70
  218.1 23.4 %collective-permute-start.16 = (f32[32,3584]{1,0:T(8,128)S(1)}, f32[32,3584]{1,0:T(8,128)S(1)}, u32[]{:S(2)}, u32[]{:S(2)}) collective-permute-start(f32[32,3584]{1,0:T(8,128)S(1)} %get-tuple-element.6), channel_id=1, source_target_pairs={{0,2},{1,3},{2,0},{3,1},{4,6},{5,7},{6,4},{7,5},{8,10},{9,11},{10,... | collective-permute-start | bytes 1376264 | tf_op jit(solution)/shard_map/ppermute | solution.py:70
  219.6 38.1 %collective-permute-start.15 = (f32[32,3584]{1,0:T(8,128)S(1)}, f32[32,3584]{1,0:T(8,128)S(1)}, u32[]{:S(2)}, u32[]{:S(2)}) collective-permute-start(f32[32,3584]{1,0:T(8,128)S(1)} %get-tuple-element.5), channel_id=1, source_target_pairs={{0,2},{1,3},{2,0},{3,1},{4,6},{5,7},{6,4},{7,5},{8,10},{9,11},{10,... | collective-permute-start | bytes 1376264 | tf_op jit(solution)/shard_map/ppermute | solution.py:70
  240.0 13.5 %collective-permute-start.26 = (f32[32,3584]{1,0:T(8,128)S(1)}, f32[32,3584]{1,0:T(8,128)S(1)}, u32[]{:S(2)}, u32[]{:S(2)}) collective-permute-start(f32[32,3584]{1,0:T(8,128)S(1)} %slice.98), channel_id=1, source_target_pairs={{0,4},{1,5},{2,6},{3,7},{4,0},{5,1},{6,2},{7,3},{8,12},{9,13},{10,... | collective-permute-start | bytes 1376264 | tf_op jit(solution)/shard_map/ppermute | solution.py:70
  242.6 20.8 %collective-permute-start.17 = (f32[32,3584]{1,0:T(8,128)S(1)}, f32[32,3584]{1,0:T(8,128)S(1)}, u32[]{:S(2)}, u32[]{:S(2)}) collective-permute-start(f32[32,3584]{1,0:T(8,128)S(1)} %slice_add_fusion.4), channel_id=1, source_target_pairs={{0,4},{1,5},{2,6},{3,7},{4,0},{5,1},{6,2},{7,3},{8,12},{9,13},{10,... | collective-permute-start | bytes 1376264 | tf_op jit(solution)/shard_map/ppermute | solution.py:70
  254.8 12.2 %collective-permute-start.27 = (f32[32,3584]{1,0:T(8,128)S(1)}, f32[32,3584]{1,0:T(8,128)S(1)}, u32[]{:S(2)}, u32[]{:S(2)}) collective-permute-start(f32[32,3584]{1,0:T(8,128)S(1)} %get-tuple-element.10), channel_id=1, source_target_pairs={{0,2},{1,3},{2,0},{3,1},{4,6},{5,7},{6,4},{7,5},{8,10},{9,11},{10,... | collective-permute-start | bytes 1376264 | tf_op jit(solution)/shard_map/ppermute | solution.py:70
  256.3 16.9 %collective-permute-start.28 = (f32[32,3584]{1,0:T(8,128)S(1)}, f32[32,3584]{1,0:T(8,128)S(1)}, u32[]{:S(2)}, u32[]{:S(2)}) collective-permute-start(f32[32,3584]{1,0:T(8,128)S(1)} %get-tuple-element.11), channel_id=1, source_target_pairs={{0,4},{1,5},{2,6},{3,7},{4,0},{5,1},{6,2},{7,3},{8,12},{9,13},{10,... | collective-permute-start | bytes 1376264 | tf_op jit(solution)/shard_map/ppermute | solution.py:70
  263.5 19.5 %collective-permute-start.11 = (f32[32,3584]{1,0:T(8,128)S(1)}, f32[32,3584]{1,0:T(8,128)S(1)}, u32[]{:S(2)}, u32[]{:S(2)}) collective-permute-start(f32[32,3584]{1,0:T(8,128)S(1)} %get-tuple-element.4), channel_id=1, source_target_pairs={{0,4},{1,5},{2,6},{3,7},{4,0},{5,1},{6,2},{7,3},{8,12},{9,13},{10,... | collective-permute-start | bytes 1376264 | tf_op jit(solution)/shard_map/ppermute | solution.py:70
  265.0 25.0 %collective-permute-start.13 = (f32[32,3584]{1,0:T(8,128)S(1)}, f32[32,3584]{1,0:T(8,128)S(1)}, u32[]{:S(2)}, u32[]{:S(2)}) collective-permute-start(f32[32,3584]{1,0:T(8,128)S(1)} %get-tuple-element.3), channel_id=1, source_target_pairs={{0,4},{1,5},{2,6},{3,7},{4,0},{5,1},{6,2},{7,3},{8,12},{9,13},{10,... | collective-permute-start | bytes 1376264 | tf_op jit(solution)/shard_map/ppermute | solution.py:70
  265.6 38.7 %collective-permute-start.18 = (f32[32,3584]{1,0:T(8,128)S(1)}, f32[32,3584]{1,0:T(8,128)S(1)}, u32[]{:S(2)}, u32[]{:S(2)}) collective-permute-start(f32[32,3584]{1,0:T(8,128)S(1)} %get-tuple-element.2), channel_id=1, source_target_pairs={{0,16},{1,17},{2,18},{3,19},{4,20},{5,21},{6,22},{7,23},{8,24},{9,... | collective-permute-start | bytes 1376264 | tf_op jit(solution)/shard_map/ppermute | solution.py:70
  273.3 13.2 %collective-permute-start.31 = (f32[32,3584]{1,0:T(8,128)S(1)}, f32[32,3584]{1,0:T(8,128)S(1)}, u32[]{:S(2)}, u32[]{:S(2)}) collective-permute-start(f32[32,3584]{1,0:T(8,128)S(1)} %get-tuple-element.8), channel_id=1, source_target_pairs={{0,2},{1,3},{2,0},{3,1},{4,6},{5,7},{6,4},{7,5},{8,10},{9,11},{10,... | collective-permute-start | bytes 1376264 | tf_op jit(solution)/shard_map/ppermute | solution.py:70
  274.8 29.4 %collective-permute-start.29 = (f32[32,3584]{1,0:T(8,128)S(1)}, f32[32,3584]{1,0:T(8,128)S(1)}, u32[]{:S(2)}, u32[]{:S(2)}) collective-permute-start(f32[32,3584]{1,0:T(8,128)S(1)} %get-tuple-element.7), channel_id=1, source_target_pairs={{0,8},{1,9},{2,10},{3,11},{4,12},{5,13},{6,14},{7,15},{8,0},{9,1},... | collective-permute-start | bytes 1376264 | tf_op jit(solution)/shard_map/ppermute | solution.py:70
  283.0 21.3 %collective-permute-start.30 = (f32[32,3584]{1,0:T(8,128)S(1)}, f32[32,3584]{1,0:T(8,128)S(1)}, u32[]{:S(2)}, u32[]{:S(2)}) collective-permute-start(f32[32,3584]{1,0:T(8,128)S(1)} %get-tuple-element.9), channel_id=1, source_target_pairs={{0,2},{1,3},{2,0},{3,1},{4,6},{5,7},{6,4},{7,5},{8,10},{9,11},{10,... | collective-permute-start | bytes 1376264 | tf_op jit(solution)/shard_map/ppermute | solution.py:70
  286.5 15.0 %collective-permute-start.12 = (f32[32,3584]{1,0:T(8,128)S(1)}, f32[32,3584]{1,0:T(8,128)S(1)}, u32[]{:S(2)}, u32[]{:S(2)}) collective-permute-start(f32[32,3584]{1,0:T(8,128)S(1)} %slice_add_fusion.6), channel_id=1, source_target_pairs={{0,2},{1,3},{2,0},{3,1},{4,6},{5,7},{6,4},{7,5},{8,10},{9,11},{10,... | collective-permute-start | bytes 1376264 | tf_op jit(solution)/shard_map/ppermute | solution.py:70
  290.1 14.2 %collective-permute-start.32 = (f32[32,3584]{1,0:T(8,128)S(1)}, f32[32,3584]{1,0:T(8,128)S(1)}, u32[]{:S(2)}, u32[]{:S(2)}) collective-permute-start(f32[32,3584]{1,0:T(8,128)S(1)} %slice_add_fusion), channel_id=1, source_target_pairs={{0,4},{1,5},{2,6},{3,7},{4,0},{5,1},{6,2},{7,3},{8,12},{9,13},{10,... | collective-permute-start | bytes 1376264 | tf_op jit(solution)/shard_map/ppermute | solution.py:70
  301.6 17.7 %collective-permute-start.14 = (f32[32,3584]{1,0:T(8,128)S(1)}, f32[32,3584]{1,0:T(8,128)S(1)}, u32[]{:S(2)}, u32[]{:S(2)}) collective-permute-start(f32[32,3584]{1,0:T(8,128)S(1)} %fusion.30), channel_id=1, source_target_pairs={{0,24},{1,25},{2,26},{3,27},{4,28},{5,29},{6,30},{7,31},{8,16},{9,... | collective-permute-start | bytes 1376264 | tf_op jit(solution)/shard_map/ppermute | solution.py:70
  (10 other events, 425.3 us)
Sparse Core Ops, SparseCore 0:
  17.1 122.9 all-reduce.2

commit v3 on v1

--- a/solution.py
+++ b/solution.py
@@ -1,6 +1,10 @@
+import functools
+
 import jax
 import jax.numpy as jnp
 from jax import lax
+from jax.experimental import pallas as pl
+from jax.experimental.pallas import tpu as pltpu
 from jax.sharding import PartitionSpec as P
 
 VAL = 512
@@ -46,6 +50,299 @@
         first[1] * left + second[1] * right,
         first[2] * left[:, None] + second[2] * right[:, None],
     )
+
+
+def ring_experts(tokens, share, gate_weight, up_weight, down_weight):
+    rows = lax.all_gather(tokens, "ep", axis=0, tiled=True)
+    gate = jnp.dot(rows, gate_weight[0], preferred_element_type=jnp.float32)
+    upper = jnp.dot(rows, up_weight[0], preferred_element_type=jnp.float32)
+    hidden = (jax.nn.silu(gate) * upper).astype(jnp.bfloat16)
+    if lax.axis_size("tp") > 1:
+        hidden = lax.all_gather(hidden, "tp", axis=1, tiled=True)
+    partial_out = jnp.dot(hidden, down_weight[0], preferred_element_type=jnp.float32)
+    scaled = partial_out * share.reshape(-1)[:, None]
+    return lax.psum_scatter(scaled, "ep", scatter_dimension=0, tiled=True).astype(jnp.bfloat16)
+
+
+MIB = 1024 * 1024
+
+
+def hidden_kernel(places, *refs):
+    sources = refs[: len(places)]
+    gate_ref, up_ref, gate_other_ref, up_other_ref, hidden_ref, rows_ref = refs[len(places) :]
+    step = pl.program_id(0)
+    own_steps = pl.num_programs(0) // 2
+
+    @pl.when(step == 0)
+    def _():
+        at = 0
+        for source, (start, stop) in zip(sources, places):
+            rows_ref[at : at + stop - start] = source[start:stop]
+            at += stop - start
+
+    def units(gate_tile, up_tile):
+        rows = rows_ref[...]
+        gate = jnp.dot(rows, gate_tile[...], preferred_element_type=jnp.float32)
+        upper = jnp.dot(rows, up_tile[...], preferred_element_type=jnp.float32)
+        hidden_ref[...] = (gate / (1.0 + jnp.exp(-gate)) * upper).astype(jnp.bfloat16)
+
+    @pl.when(step < own_steps)
+    def _():
+        units(gate_ref, up_ref)
+
+    @pl.when(step >= own_steps)
+    def _():
+        units(gate_other_ref, up_other_ref)
+
+
+def packed_weights(gate, up, down, after):
+    width, units = gate.shape
+    blocks = width // units
+
+    def kernel(gate_ref, up_ref, down_ref, after_ref, out_ref, sems):
+        copies = [
+            pltpu.make_async_copy(gate_ref, out_ref.at[pl.ds(0, width)], sems.at[0]),
+            pltpu.make_async_copy(up_ref, out_ref.at[pl.ds(width, width)], sems.at[1]),
+        ]
+        for at in range(blocks):
+            copies.append(
+                pltpu.make_async_copy(
+                    down_ref.at[:, pl.ds(at * units, units)],
+                    out_ref.at[pl.ds(2 * width + at * units, units)],
+                    sems.at[2 + at],
+                )
+            )
+        for copy in copies:
+            copy.start()
+        for copy in copies:
+            copy.wait()
+
+    return pl.pallas_call(
+        kernel,
+        in_specs=[pl.BlockSpec(memory_space=pl.ANY)] * 4,
+        out_specs=pl.BlockSpec(memory_space=pl.ANY),
+        out_shape=jax.ShapeDtypeStruct((3 * width, units), gate.dtype),
+        scratch_shapes=[pltpu.SemaphoreType.DMA((2 + blocks,))],
+        compiler_params=pltpu.CompilerParams(vmem_limit_bytes=56 * MIB),
+        cost_estimate=pl.CostEstimate(
+            flops=0, bytes_accessed=12 * width * units, transcendentals=0
+        ),
+        name="packed_weights",
+    )(gate, up, down, after)
+
+
+def expert_hidden(pieces, gate, up, other):
+    width, units = gate.shape
+    count = sum(stop - start for _, start, stop in pieces)
+    tile = 256
+    steps = units // tile
+    own = pl.BlockSpec((width, tile), lambda i: (0, jnp.minimum(i, steps - 1)))
+    gate_other = pl.BlockSpec((width, tile), lambda i: (0, jnp.maximum(i - steps, 0)))
+    up_other = pl.BlockSpec((width, tile), lambda i: (1, jnp.maximum(i - steps, 0)))
+    return pl.pallas_call(
+        functools.partial(hidden_kernel, [(start, stop) for _, start, stop in pieces]),
+        grid=(2 * steps,),
+        in_specs=[pl.BlockSpec(array.shape, lambda i: (0, 0)) for array, _, _ in pieces]
+        + [own, own, gate_other, up_other],
+        out_specs=pl.BlockSpec((count, tile), lambda i: (0, i)),
+        out_shape=jax.ShapeDtypeStruct((count, 2 * units), jnp.bfloat16),
+        scratch_shapes=[pltpu.VMEM((count, width), jnp.bfloat16)],
+        compiler_params=pltpu.CompilerParams(vmem_limit_bytes=52 * MIB),
+        cost_estimate=pl.CostEstimate(
+            flops=8 * count * width * units,
+            bytes_accessed=2 * (count * width + 4 * width * units + 2 * count * units),
+            transcendentals=2 * count * units,
+        ),
+        name="expert_hidden",
+    )(*[array for array, _, _ in pieces], gate, up, other, other)
+
+
+def output_kernel(scale_ref, hidden_ref, down_ref, down_other_ref, *out_refs):
+    units = down_ref.shape[0]
+    hidden = hidden_ref[...]
+    out = jnp.dot(hidden[:, :units], down_ref[...], preferred_element_type=jnp.float32)
+    out += jnp.dot(hidden[:, units:], down_other_ref[...], preferred_element_type=jnp.float32)
+    out = out * scale_ref[...]
+    unit = out_refs[0].shape[0]
+    for at, out_ref in enumerate(out_refs):
+        out_ref[...] = out[at * unit : (at + 1) * unit]
+
+
+def expert_output(plane, block, unit, scale, hidden, down, other):
+    units, width = down.shape
+    steps = width // units
+    slot = jax.ShapeDtypeStruct((unit, width), jnp.float32)
+    return pl.pallas_call(
+        output_kernel,
+        grid=(steps,),
+        in_specs=[
+            pl.BlockSpec((4 * unit, 1), lambda i: (plane, 0)),
+            pl.BlockSpec((4 * unit, 2 * units), lambda i: (block, 0)),
+            pl.BlockSpec((units, units), lambda i: (0, i)),
+            pl.BlockSpec((units, units), lambda i: (2 * steps + i, 0)),
+        ],
+        out_specs=[pl.BlockSpec((unit, units), lambda i: (0, i))] * 4,
+        out_shape=[slot] * 4,
+        compiler_params=pltpu.CompilerParams(vmem_limit_bytes=44 * MIB),
+        cost_estimate=pl.CostEstimate(
+            flops=16 * unit * width * units,
+            bytes_accessed=4 * width * units + 16 * unit * width,
+            transcendentals=0,
+        ),
+        name="expert_output",
+    )(scale, hidden, down, other)
+
+
+def whole_call(kernel, operands, out_shape, name):
+    return pl.pallas_call(
+        kernel,
+        in_specs=[pl.BlockSpec(memory_space=pltpu.VMEM)] * len(operands),
+        out_specs=[pl.BlockSpec(memory_space=pltpu.VMEM)] * len(out_shape),
+        out_shape=out_shape,
+        compiler_params=pltpu.CompilerParams(vmem_limit_bytes=12 * MIB),
+        cost_estimate=pl.CostEstimate(
+            flops=0,
+            bytes_accessed=sum(x.size * x.dtype.itemsize for x in list(operands) + list(out_shape)),
+            transcendentals=0,
+        ),
+        name=name,
+    )(*operands)
+
+
+def gather_round(unit, column, from_x, from_y, extra):
+    width = from_x.shape[1]
+    half = unit // 2
+    head = unit if column is not None else 0
+    operands = [x for x in (from_x, from_y, column, extra) if x is not None]
+    message = jax.ShapeDtypeStruct((head + half, width), from_x.dtype)
+    out_shape = [message, message] + ([extra] if extra is not None else [])
+
+    def kernel(x_ref, y_ref, *refs):
+        refs = list(refs)
+        column_ref = refs.pop(0) if column is not None else None
+        extra_ref = refs.pop(0) if extra is not None else None
+        if column is not None:
+            refs[0][:head] = column_ref[...]
+            refs[1][:head] = column_ref[...]
+        refs[0][head:] = y_ref[:half]
+        refs[1][head:] = x_ref[half:unit]
+        if extra is not None:
+            refs[2][...] = extra_ref[...]
+
+    return whole_call(kernel, operands, out_shape, "gather_round")
+
+
+def scatter_round(received, plane, following, finished, column, base=()):
+    unit, width = (plane or following or finished)[0].shape
+    half = unit // 2
+    operands = list(received) if received is not None else []
+    operands += [plane[1], plane[2]] if plane is not None else []
+    operands += [following[3]] if following is not None else []
+    operands += [finished[0]] if finished is not None else []
+    operands += list(column) + list(base)
+    length = (unit if plane is not None else 0) + (half if following is not None else 0)
+    out_shape = [jax.ShapeDtypeStruct((length, width), jnp.float32)] * 2 if length else []
+    if finished is not None:
+        out_shape = out_shape + [jax.ShapeDtypeStruct((unit, width), jnp.float32)]
+    if base:
+        out_shape = out_shape + [jax.ShapeDtypeStruct((unit, width), jnp.float32)]
+    head = unit if finished is not None else 0
+
+    def kernel(*refs):
+        refs = list(refs)
+        from_x, from_y = (refs.pop(0), refs.pop(0)) if received is not None else (None, None)
+        at = 0
+        slot_x, slot_y = (refs.pop(0), refs.pop(0)) if plane is not None else (None, None)
+        slot_d = refs.pop(0) if following is not None else None
+        own = refs.pop(0) if finished is not None else None
+        more = [refs.pop(0) for _ in column]
+        bases = [refs.pop(0) for _ in base]
+        if base:
+            refs.pop()[...] = bases[0][...] + bases[1][...]
+        if plane is not None:
+            refs[0][:half] = slot_x[:half]
+            refs[0][half:unit] = slot_x[half:] + from_y[head : head + half]
+            refs[1][:half] = slot_y[:half] + from_x[head : head + half]
+            refs[1][half:unit] = slot_y[half:]
+            at = unit
+        if following is not None:
+            refs[0][at : at + half] = slot_d[:half]
+            refs[1][at : at + half] = slot_d[half:]
+        if finished is not None:
+            total = own[...] + from_x[:head] + from_y[:head]
+            for part in more:
+                total = total + part[...]
+            refs[-1][...] = total
+
+    return list(whole_call(kernel, operands, out_shape, "scatter_round"))
+
+
+def grid_experts(tokens, share, gate_weight, up_weight, down_weight):
+    peers = lax.axis_size("ep")
+    chips = peers // 2
+    unit = tokens.shape[0]
+    half = unit // 2
+    me = lax.axis_index("ep")
+
+    def flip(value, chip_bits):
+        return lax.ppermute(value, "ep", [(i, i ^ (2 * chip_bits)) for i in range(peers)])
+
+    def swap(value):
+        return lax.ppermute(value, "ep", [(i, i ^ 1) for i in range(peers)])
+
+    gate, up, down = gate_weight[0], up_weight[0], down_weight[0]
+
+    column = {0: tokens, 1: flip(tokens, 4), 2: flip(tokens, 8)}
+    by_x, by_y = {0: flip(tokens, 1)}, {0: flip(tokens, 2)}
+    for plane in (1, 2, 3):
+        extra = tokens if plane == 1 else None
+        to_x, to_y, *passed = gather_round(
+            unit, column[plane], by_x[plane - 1], by_y[plane - 1], extra
+        )
+        by_x[plane], by_y[plane] = flip(to_x, 1), flip(to_y, 2)
+        if passed:
+            column[3] = flip(passed[0], 12)
+            other = swap(packed_weights(gate, up, down, to_x))
+    to_x, to_y = gather_round(unit, None, by_x[3], by_y[3], None)
+    by_x[4], by_y[4] = flip(to_x, 1), flip(to_y, 2)
+
+    slots = jnp.bitwise_xor(me, 2 * jnp.arange(chips, dtype=jnp.int32))
+    picks = slots[:, None] == jnp.arange(peers, dtype=jnp.int32)[None, :]
+    scale = jnp.sum(jnp.where(picks[:, :, None], share[None, :, :], 0.0), axis=1)
+    scale = scale.reshape(chips * unit, 1)
+
+    def plane_rows(plane):
+        tail = unit if plane < 3 else 0
+        return [
+            (column[plane], 0, unit),
+            (by_x[plane], 0, unit),
+            (by_y[plane], 0, unit),
+            (by_x[plane + 1], tail, tail + half),
+            (by_y[plane + 1], tail, tail + half),
+        ]
+
+    outs = {}
+    for planes in ((0, 1), (2,), (3,)):
+        pieces = [piece for plane in planes for piece in plane_rows(plane)]
+        hidden = expert_hidden(pieces, gate, up, other)
+        for block, plane in enumerate(planes):
+            outs[plane] = expert_output(plane, block, unit, scale, hidden, down, other)
+
+    order = [2, 3, 1, 0]
+    sums = []
+    received = None
+    for at in range(-1, len(order)):
+        plane = outs[order[at]] if at >= 0 else None
+        following = outs[order[at + 1]] if at + 1 < len(order) else None
+        finished = outs[order[at - 1]] if at >= 1 else None
+        base = (outs[0][0], sums[0]) if at == 3 else ()
+        results = scatter_round(received, plane, following, finished, [], base)
+        received = (flip(results[0], 1), flip(results[1], 2))
+        if finished is not None:
+            sums.append(flip(results[2], 4 * order[at - 1]))
+    own = (results[3],)
+    (total,) = scatter_round(received, None, None, own, sums[1:])
+    return total.astype(jnp.bfloat16)
 
 
 def per_device(
@@ -67,40 +364,41 @@
     latent = prefill_latent.shape[3]
     tok_rows, top_k = expert_ids.shape
 
-    rows = lax.all_gather(tokens, "ep", axis=0, tiled=True)
-
     owner = block_owner.reshape(blocks)
     same = owner[:, None] == owner[None, :]
     earlier = jnp.arange(blocks)[None, :] < jnp.arange(blocks)[:, None]
     order_in = jnp.sum(jnp.logical_and(same, earlier).astype(jnp.int32), axis=1)
     target = owner * 2 + order_in
     chosen = jnp.arange(2 * peers, dtype=jnp.int32)[:, None] == target[None, :]
-    filled = jnp.sum(chosen.astype(jnp.float32), axis=1)
-    expert_of = jnp.arange(peers, dtype=jnp.int32) // 2
-    named = expert_ids[None, :, :] == expert_of[:, None, None]
-    share = jnp.sum(jnp.where(named, route_weight[None, :, :], 0.0), axis=2)
-    small = lax.all_to_all(
-        jnp.concatenate([share, filled.reshape(peers, 2)], axis=1),
-        "ep",
-        split_axis=0,
-        concat_axis=0,
-        tiled=True,
-    )
-    scale_rows = small[:, :tok_rows].reshape(peers * tok_rows)
-    present = small[:, tok_rows:].reshape(peers * 2)
-
     packed = jnp.dot(
         chosen.astype(jnp.bfloat16),
         prefill_latent.reshape(blocks, block_len * latent),
         preferred_element_type=jnp.float32,
     ).astype(jnp.bfloat16)
+
+    expert_of = jnp.arange(peers, dtype=jnp.int32) // 2
+    named = expert_ids[None, :, :] == expert_of[:, None, None]
+    share = jnp.sum(jnp.where(named, route_weight[None, :, :], 0.0), axis=2)
+    high = lax.reduce_precision(share, 8, 7)
+    middle = lax.reduce_precision(share - high, 8, 7)
+    low = share - high - middle
+    filled = jnp.sum(chosen.astype(jnp.float32), axis=1).reshape(peers, 1, 2)
+    side = jnp.zeros((peers, 2 * block_len, max(tok_rows, 2)), jnp.float32)
+    side = side.at[:, :3, :tok_rows].set(jnp.stack([high, middle, low], axis=1))
+    side = side.at[:, 3:4, :2].set(filled)
     arrived = lax.all_to_all(
-        packed.reshape(peers, 2 * block_len, latent),
+        jnp.concatenate(
+            [packed.reshape(peers, 2 * block_len, latent), side.astype(jnp.bfloat16)], axis=2
+        ),
         "ep",
         split_axis=0,
         concat_axis=0,
         tiled=True,
     )
+    side_in = arrived[:, :, latent:].astype(jnp.float32)
+    share_in = side_in[:, 0, :tok_rows] + side_in[:, 1, :tok_rows] + side_in[:, 2, :tok_rows]
+    present = side_in[:, 3, :2].reshape(peers * 2)
+    arrived = arrived[:, :, :latent]
     shard_len = latent_cache.shape[1]
     positions = lax.axis_index("tp") * shard_len + jnp.arange(shard_len, dtype=jnp.int32)
     keys = jnp.concatenate(
@@ -111,16 +409,11 @@
     peak, total, mixed = combined_all((peak, total, mixed), "tp", join_parts)
     attn_out = (mixed / total[:, None]).astype(jnp.bfloat16)[None]
 
-    gate = jnp.dot(rows, gate_weight[0], preferred_element_type=jnp.float32)
-    upper = jnp.dot(rows, up_weight[0], preferred_element_type=jnp.float32)
-    hidden = (jax.nn.silu(gate) * upper).astype(jnp.bfloat16)
-    if lax.axis_size("tp") > 1:
-        hidden = lax.all_gather(hidden, "tp", axis=1, tiled=True)
-    partial_out = (
-        jnp.dot(hidden, down_weight[0], preferred_element_type=jnp.float32) * scale_rows[:, None]
-    )
-    combined = lax.psum_scatter(partial_out, "ep", scatter_dimension=0, tiled=True)
-    moe_out = combined.astype(jnp.bfloat16)
+    if peers == 32 and lax.axis_size("tp") == 1:
+        serve = grid_experts
+    else:
+        serve = ring_experts
+    moe_out = serve(tokens, share_in, gate_weight, up_weight, down_weight)
     return (attn_out, moe_out)
 
 

time: 284 us -> 515 us (1.81)
  Pallas kernels: 0 us -> 389 us
  waiting for transfers between devices: 218 us -> 68.8 us
  starting transfers between devices: 3.23 us -> 37.5 us
  matrix products: 25.4 us -> 2.61 us
  blocking collectives: 14.2 us -> 0 us
  between operations: 14.8 us -> 1.72 us
  local copies, waits for them, and re-layouts: 2.83 us -> 9.38 us
    pallas_call x0 -> x18, Pallas kernels: none -> 389 us  [the longest x1 335 us: packed_weights(): pl.pallas_call(kernel, in_specs=[pl.BlockSpec(memory_space=pl.ANY)] * 4,...]
    reduce_scatter x1 -> x0, waiting for transfers between devices: 138 us -> none  [per_device(): lax.psum_scatter(partial_out, 'ep', scatter_dimension=0, tiled=True)]
    ppermute x0 -> x27, waiting for transfers between devices: none -> 68.8 us  [the longest x26 68.8 us: flip(): lax.ppermute(value, 'ep', [(i, i ^ 2 * chip_bits) for i in range(peers)])]
    all_gather x1 -> x0, waiting for transfers between devices: 62.1 us -> none  [per_device(): rows = lax.all_gather(tokens, 'ep', axis=0, tiled=True)]
    ppermute x0 -> x27, starting transfers between devices: none -> 33.3 us  [the longest x26 33.3 us: flip(): lax.ppermute(value, 'ep', [(i, i ^ 2 * chip_bits) for i in range(peers)])]
    dot_general x2 -> x0, matrix products: 22.8 us -> none  [the longest x1 15.5 us: per_device(): jnp.dot(hidden, down_weight[0], preferred_element_type=jnp.float32)]
    all_to_all x1, waiting for transfers between devices: 17 us -> 0.01 us  [per_device(): lax.all_to_all(jnp.concatenate([packed.reshape(peers, 2 * block_len, late...]
    all_to_all x1 -> x0, blocking collectives: 14.2 us -> none  [per_device(): lax.all_to_all(jnp.concatenate([share, filled.reshape(peers, 2)], axis=1)...]
  transfers between devices with their start and end apart: 3 -> 28, of which waited for: 3 -> 14; matrix products, arithmetic and copies ran while one was open for 3% -> 2% of each run, Pallas kernels for 0% -> 10%
where the time goes in v3:
time: 515 us; the launch traced here: 514 us
  Pallas kernels  389 us (76%)
  waiting for transfers between devices  68.8 us (13%)
  starting transfers between devices  37.5 us (7%)
  local copies, waits for them, and re-layouts  9.38 us (2%)
    pallas_call x1, Pallas kernels, packed_weights(): pl.pallas_call(kernel, in_specs=[pl.BlockSpec(memory_space=pl.ANY)] * 4,...  335 us
    ppermute x26, waiting for transfers between devices, flip(): lax.ppermute(value, 'ep', [(i, i ^ 2 * chip_bits) for i in range(peers)])  68.8 us
    ppermute x26, starting transfers between devices, flip(): lax.ppermute(value, 'ep', [(i, i ^ 2 * chip_bits) for i in range(peers)])  33.3 us
    pallas_call x3, Pallas kernels, expert_hidden(): pl.pallas_call(functools.partial(hidden_kernel, [(start, stop) for _, sta...  26.1 us
    pallas_call x4, Pallas kernels, expert_output(): pl.pallas_call(output_kernel, grid=(steps,), in_specs=[pl.BlockSpec((4 *...  23 us
  transfers between devices with their start and end apart: 28, of which 14 were waited for; matrix products, arithmetic and copies ran while one was open for 2% of the time, Pallas kernels for 10%

profile of v3, /device:TPU:0, one launch (start us, length us, event | category | flops | bytes accessed | tf_op | source)
XLA Modules:
  0.0 513.7 jit_solution(1543349350477892331)
XLA Ops:
  0.6 3.0 collective-permute-start.1
  3.6 1.5 collective-permute-start.2
  5.2 1.6 collective-permute-start.3
  6.7 2.7 collective-permute-done.1.x_ref.refs_1_
  14.6 334.7 %packed_weights.1 = bf16[10752,512]{1,0:T(8,128)(2,1)} custom-call(bf16[3584,512]{1,0:T(8,128)(2,1)} %bitcast.37, bf16[3584,512]{1,0:T(8,128)(2,1)} %bitcast.41, bf16[512,3584]{1,0:T(8,128)(2,1)} %bitcast.32, bf16[48,3584]{1,0:T(8,128)(2,1)} %copy-done.10), custom_call_target="tpu_custom_call" | custom-call | bytes 22020096 | tf_op jit(solution)/shard_map/packed_weights/pallas_call | solution.py:120
  352.0 4.2 all-to-all-start
  356.2 1.8 collective-permute-start.4
  359.4 2.4 collective-permute-start
  363.2 18.8 %collective-permute-done.refs_0_ = bf16[32,3584]{1,0:T(8,128)(2,1)S(1)} collective-permute-done((bf16[32,3584]{1,0:T(8,128)(2,1)S(1)}, bf16[32,3584]{1,0:T(8,128)(2,1)S(1)}, u32[]{:S(2)}, u32[]{:S(2)}) %collective-permute-start) | collective-permute-done | bytes 229408 | tf_op jit(solution)/shard_map/ppermute | solution.py:288
  384.2 1.5 collective-permute-start.7
  386.7 5.1 collective-permute-done.6.x_ref.refs_1_.refs_8_
  396.5 5.6 %collective-permute-done.10.refs_4_.y_ref.refs_2_ = bf16[48,3584]{1,0:T(8,128)(2,1)S(1)} collective-permute-done((bf16[48,3584]{1,0:T(8,128)(2,1)}, bf16[48,3584]{1,0:T(8,128)(2,1)S(1)}, u32[]{:S(2)}, u32[]{:S(2)}) %collective-permute-start.10) | collective-permute-done | bytes 344096 | tf_op jit(solution)/shard_map/ppermute | solution.py:288
  402.2 1.7 collective-permute-done.9.refs_3_.x_ref.refs_1_
  406.0 7.8 %expert_hidden.3.hidden_ref = bf16[128,1024]{1,0:T(8,128)(2,1)S(1)} custom-call(bf16[32,3584]{1,0:T(8,128)(2,1)S(1)} %copy-done.9, bf16[48,3584]{1,0:T(8,128)(2,1)S(1)} %collective-permute-done.6.x_ref.refs_1_.refs_8_, bf16[48,3584]{1,0:T(8,128)(2,1)S(1)} %collective-permute-done.7.y_ref.refs_2_.refs_9_, ...), custom_call_target="tpu_custom_call" | custom-call | flops 1879048192 | bytes 15859712 | tf_op jit(solution)/shard_map/expert_hidden/pallas_call | solution.py:142
  413.8 5.8 %expert_output.4 = (f32[32,3584]{1,0:T(8,128)S(1)}, f32[32,3584]{1,0:T(8,128)S(1)}, f32[32,3584]{1,0:T(8,128)S(1)}, f32[32,3584]{1,0:T(8,128)S(1)}) custom-call(f32[512,1]{1,0:T(8,128)S(1)} %reshape.195.scale_ref, bf16[128,1024]{1,0:T(8,128)(2,1)S(1)} %expert_hidden.3.hidden_ref, bf16[512,3584]{1,0:T(8,128)(2,1)S(1)} %bitcast.33, ...), custom_call_target="tpu_custom_call" | custom-call | flops 939524096 | bytes 9175040 | tf_op jit(solution)/shard_map/expert_output/pallas_call | solution.py:175
  419.6 1.5 collective-permute-start.12
  421.2 1.5 collective-permute-start.13
  422.7 7.7 %expert_hidden.4.hidden_ref = bf16[128,1024]{1,0:T(8,128)(2,1)S(1)} custom-call(bf16[32,3584]{1,0:T(8,128)(2,1)S(1)} %copy-done.7, bf16[48,3584]{1,0:T(8,128)(2,1)S(1)} %collective-permute-done.9.refs_3_.x_ref.refs_1_, bf16[48,3584]{1,0:T(8,128)(2,1)S(1)} %collective-permute-done.10.refs_4_.y_ref.refs_2_, ...), custom_call_target="tpu_custom_call" | custom-call | flops 1879048192 | bytes 15859712 | tf_op jit(solution)/shard_map/expert_hidden/pallas_call | solution.py:142
  430.4 5.7 %expert_output.5 = (f32[32,3584]{1,0:T(8,128)S(1)}, f32[32,3584]{1,0:T(8,128)S(1)}, f32[32,3584]{1,0:T(8,128)S(1)}, f32[32,3584]{1,0:T(8,128)S(1)}) custom-call(f32[512,1]{1,0:T(8,128)S(1)} %reshape.195.scale_ref, bf16[128,1024]{1,0:T(8,128)(2,1)S(1)} %expert_hidden.4.hidden_ref, bf16[512,3584]{1,0:T(8,128)(2,1)S(1)} %bitcast.34, ...), custom_call_target="tpu_custom_call" | custom-call | flops 939524096 | bytes 9175040 | tf_op jit(solution)/shard_map/expert_output/pallas_call | solution.py:175
  437.4 10.6 %expert_hidden.5.hidden_ref = bf16[256,1024]{1,0:T(8,128)(2,1)} custom-call(bf16[32,3584]{1,0:T(8,128)(2,1)S(1)} %copy-done.5, bf16[32,3584]{1,0:T(8,128)(2,1)S(1)} %collective-permute-done.1.x_ref.refs_1_, bf16[32,3584]{1,0:T(8,128)(2,1)S(1)} %collective-permute-done.2.y_ref.refs_2_, bf16[48,3584]{1,0:T(8,128)(2,1)S(1)} %collective-permute-done.4.x_ref.refs_3_.refs_6_, ...), custom_call_target="tpu_custom_call" | custom-call | flops 3758096384 | bytes 17039360 | tf_op jit(solution)/shard_map/expert_hidden/pallas_call | solution.py:142
  449.0 5.7 %expert_output.6 = (f32[32,3584]{1,0:T(8,128)S(1)}, f32[32,3584]{1,0:T(8,128)S(1)}, f32[32,3584]{1,0:T(8,128)S(1)}, f32[32,3584]{1,0:T(8,128)S(1)}) custom-call(f32[512,1]{1,0:T(8,128)S(1)} %reshape.195.scale_ref, bf16[256,1024]{1,0:T(8,128)(2,1)S(1)} %copy-done.2, bf16[512,3584]{1,0:T(8,128)(2,1)S(1)} %bitcast.35, ...), custom_call_target="tpu_custom_call" | custom-call | flops 939524096 | bytes 9175040 | tf_op jit(solution)/shard_map/expert_output/pallas_call | solution.py:175
  457.2 1.5 collective-permute-start.19
  458.7 5.7 %expert_output.7 = (f32[32,3584]{1,0:T(8,128)S(1)}, f32[32,3584]{1,0:T(8,128)S(1)}, f32[32,3584]{1,0:T(8,128)S(1)}, f32[32,3584]{1,0:T(8,128)S(1)}) custom-call(f32[512,1]{1,0:T(8,128)S(1)} %reshape.195.scale_ref, bf16[256,1024]{1,0:T(8,128)(2,1)S(1)} %copy-done.2, bf16[512,3584]{1,0:T(8,128)(2,1)S(1)} %bitcast.36, ...), custom_call_target="tpu_custom_call" | custom-call | flops 939524096 | bytes 9175040 | tf_op jit(solution)/shard_map/expert_output/pallas_call | solution.py:175
  464.4 4.5 collective-permute-done.18.refs_0_
  468.9 1.6 collective-permute-done.19.refs_1_
  472.6 1.5 collective-permute-start.21
  476.1 1.7 slice_bitcast_fusion
  477.9 1.8 copy.26
  479.7 1.9 collective-permute-start.25
  481.6 19.5 %collective-permute-done.22.refs_6_ = f32[32,3584]{1,0:T(8,128)} collective-permute-done((f32[32,3584]{1,0:T(8,128)}, f32[32,3584]{1,0:T(8,128)}, u32[]{:S(2)}, u32[]{:S(2)}) %collective-permute-start.22) | collective-permute-done | bytes 458784 | tf_op jit(solution)/shard_map/ppermute | solution.py:288
  506.1 1.5 fusion.14
  507.6 4.3 collective-permute-done.23.refs_0_
  (114 shorter events, 35.3 us)
Async XLA Ops:
  0.6 504.5 %copy-start = (bf16[1,128,576]{1,2,0:T(8,128)(2,1)S(1)}, bf16[1,128,576]{1,2,0:T(8,128)(2,1)}, u32[]{:S(2)}) copy-start(bf16[1,128,576]{1,2,0:T(8,128)(2,1)} %param.15) | copy-start | bytes 442372
  0.6 8.8 %collective-permute-start.1 = (bf16[32,3584]{1,0:T(8,128)(2,1)}, bf16[32,3584]{1,0:T(8,128)(2,1)S(1)}, u32[]{:S(2)}, u32[]{:S(2)}) collective-permute-start(bf16[32,3584]{1,0:T(8,128)(2,1)} %refs_0_.1), channel_id=1, source_target_pairs={{0,2},{1,3},{2,0},{3,1},{4,6},{5,7},{6,4},{7,5},{8,10},{9,11},{10,... | collective-permute-start | bytes 688136 | tf_op jit(solution)/shard_map/ppermute | solution.py:288
  3.6 7.3 %collective-permute-start.2 = (bf16[32,3584]{1,0:T(8,128)(2,1)}, bf16[32,3584]{1,0:T(8,128)(2,1)S(1)}, u32[]{:S(2)}, u32[]{:S(2)}) collective-permute-start(bf16[32,3584]{1,0:T(8,128)(2,1)} %refs_0_.1), channel_id=1, source_target_pairs={{0,4},{1,5},{2,6},{3,7},{4,0},{5,1},{6,2},{7,3},{8,12},{9,13},{10,... | collective-permute-start | bytes 688136 | tf_op jit(solution)/shard_map/ppermute | solution.py:288
  5.2 7.0 %collective-permute-start.3 = (bf16[32,3584]{1,0:T(8,128)(2,1)}, bf16[32,3584]{1,0:T(8,128)(2,1)S(1)}, u32[]{:S(2)}, u32[]{:S(2)}) collective-permute-start(bf16[32,3584]{1,0:T(8,128)(2,1)} %refs_0_.1), channel_id=1, source_target_pairs={{0,8},{1,9},{2,10},{3,11},{4,12},{5,13},{6,14},{7,15},{8,0},{9,1},... | collective-permute-start | bytes 688136 | tf_op jit(solution)/shard_map/ppermute | solution.py:288
  14.6 335.2 %copy-start.16 = (f32[32,8]{0,1:T(8,128)S(1)}, f32[32,8]{0,1:T(8,128)}, u32[]{:S(2)}) copy-start(f32[32,8]{0,1:T(8,128)} %param.22) | copy-start | bytes 3076
  14.6 335.2 %copy-start.17 = (s32[32,8]{0,1:T(8,128)S(1)}, s32[32,8]{0,1:T(8,128)}, u32[]{:S(2)}) copy-start(s32[32,8]{0,1:T(8,128)} %param.21) | copy-start | bytes 3076
  14.6 335.6 %copy-start.15 = (bf16[1,32,4,576]{3,2,1,0:T(4,128)(2,1)S(1)}, bf16[1,32,4,576]{3,2,1,0:T(4,128)(2,1)}, u32[]{:S(2)}) copy-start(bf16[1,32,4,576]{3,2,1,0:T(4,128)(2,1)} %param.18) | copy-start | bytes 442372
  349.3 55.7 %collective-permute-start.11 = (bf16[10752,512]{1,0:T(8,128)(2,1)}, bf16[10752,512]{1,0:T(8,128)(2,1)}, u32[]{:S(2)}, u32[]{:S(2)}) collective-permute-start(bf16[10752,512]{1,0:T(8,128)(2,1)} %packed_weights.1), channel_id=1, source_target_pairs={{0,1},{1,0},{2,3},{3,2},{4,5},{5,4},{6,7},{7,6},{8,9},{9,8},{10,11... | collective-permute-start | bytes 33030152 | tf_op jit(solution)/shard_map/ppermute | solution.py:291
  352.0 33.8 %all-to-all-start = ((bf16[32,8,608]{2,1,0:T(8,128)(2,1)}), bf16[32,8,608]{2,1,0:T(8,128)(2,1)}, u32[]{:S(2)}, u32[]{:S(2)}) async-start(bf16[32,8,608]{2,1,0:T(8,128)(2,1)} %pad_maximum_fusion), calls=%async_computation | async-start | bytes 655360 | tf_op jit(solution)/shard_map/all_to_all | solution.py:389
  356.2 25.9 %collective-permute-start.4 = (bf16[48,3584]{1,0:T(8,128)(2,1)S(1)}, bf16[48,3584]{1,0:T(8,128)(2,1)S(1)}, u32[]{:S(2)}, u32[]{:S(2)}) collective-permute-start(bf16[48,3584]{1,0:T(8,128)(2,1)S(1)} %copy-done.11), channel_id=1, source_target_pairs={{0,2},{1,3},{2,0},{3,1},{4,6},{5,7},{6,4},{7,5},{8,10},{9,11},{10,... | collective-permute-start | bytes 1032200 | tf_op jit(solution)/shard_map/ppermute | solution.py:288
  357.9 24.1 %collective-permute-start.5 = (bf16[48,3584]{1,0:T(8,128)(2,1)S(1)}, bf16[48,3584]{1,0:T(8,128)(2,1)S(1)}, u32[]{:S(2)}, u32[]{:S(2)}) collective-permute-start(bf16[48,3584]{1,0:T(8,128)(2,1)S(1)} %get-tuple-element.66), channel_id=1, source_target_pairs={{0,4},{1,5},{2,6},{3,7},{4,0},{5,1},{6,2},{7,3},{8,12},{9,13},{10,... | collective-permute-start | bytes 1032200 | tf_op jit(solution)/shard_map/ppermute | solution.py:288
  359.4 22.6 %collective-permute-start = (bf16[32,3584]{1,0:T(8,128)(2,1)S(1)}, bf16[32,3584]{1,0:T(8,128)(2,1)S(1)}, u32[]{:S(2)}, u32[]{:S(2)}) collective-permute-start(bf16[32,3584]{1,0:T(8,128)(2,1)S(1)} %copy-done.5), channel_id=1, source_target_pairs={{0,16},{1,17},{2,18},{3,19},{4,20},{5,21},{6,22},{7,23},{8,24},{9,... | collective-permute-start | bytes 688136 | tf_op jit(solution)/shard_map/ppermute | solution.py:288
  361.8 24.9 %collective-permute-start.8 = (bf16[32,3584]{1,0:T(8,128)(2,1)}, bf16[32,3584]{1,0:T(8,128)(2,1)S(1)}, u32[]{:S(2)}, u32[]{:S(2)}) collective-permute-start(bf16[32,3584]{1,0:T(8,128)(2,1)} %get-tuple-element.69), channel_id=1, source_target_pairs={{0,24},{1,25},{2,26},{3,27},{4,28},{5,29},{6,30},{7,31},{8,16},{9,... | collective-permute-start | bytes 688136 | tf_op jit(solution)/shard_map/ppermute | solution.py:288
  382.7 9.1 %collective-permute-start.6 = (bf16[48,3584]{1,0:T(8,128)(2,1)S(1)}, bf16[48,3584]{1,0:T(8,128)(2,1)S(1)}, u32[]{:S(2)}, u32[]{:S(2)}) collective-permute-start(bf16[48,3584]{1,0:T(8,128)(2,1)S(1)} %get-tuple-element.67), channel_id=1, source_target_pairs={{0,2},{1,3},{2,0},{3,1},{4,6},{5,7},{6,4},{7,5},{8,10},{9,11},{10,... | collective-permute-start | bytes 1032200 | tf_op jit(solution)/shard_map/ppermute | solution.py:288
  384.2 8.9 %collective-permute-start.7 = (bf16[48,3584]{1,0:T(8,128)(2,1)S(1)}, bf16[48,3584]{1,0:T(8,128)(2,1)S(1)}, u32[]{:S(2)}, u32[]{:S(2)}) collective-permute-start(bf16[48,3584]{1,0:T(8,128)(2,1)S(1)} %get-tuple-element.68), channel_id=1, source_target_pairs={{0,4},{1,5},{2,6},{3,7},{4,0},{5,1},{6,2},{7,3},{8,12},{9,13},{10,... | collective-permute-start | bytes 1032200 | tf_op jit(solution)/shard_map/ppermute | solution.py:288
  394.0 8.1 %collective-permute-start.10 = (bf16[48,3584]{1,0:T(8,128)(2,1)}, bf16[48,3584]{1,0:T(8,128)(2,1)S(1)}, u32[]{:S(2)}, u32[]{:S(2)}) collective-permute-start(bf16[48,3584]{1,0:T(8,128)(2,1)} %get-tuple-element.71), channel_id=1, source_target_pairs={{0,4},{1,5},{2,6},{3,7},{4,0},{5,1},{6,2},{7,3},{8,12},{9,13},{10,... | collective-permute-start | bytes 1032200 | tf_op jit(solution)/shard_map/ppermute | solution.py:288
  395.5 8.3 %collective-permute-start.9 = (bf16[48,3584]{1,0:T(8,128)(2,1)}, bf16[48,3584]{1,0:T(8,128)(2,1)S(1)}, u32[]{:S(2)}, u32[]{:S(2)}) collective-permute-start(bf16[48,3584]{1,0:T(8,128)(2,1)} %get-tuple-element.70), channel_id=1, source_target_pairs={{0,2},{1,3},{2,0},{3,1},{4,6},{5,7},{6,4},{7,5},{8,10},{9,11},{10,... | collective-permute-start | bytes 1032200 | tf_op jit(solution)/shard_map/ppermute | solution.py:288
  403.9 18.8 %collective-permute-start.14 = (bf16[16,3584]{1,0:T(8,128)(2,1)S(1)}, bf16[16,3584]{1,0:T(8,128)(2,1)S(1)}, u32[]{:S(2)}, u32[]{:S(2)}) collective-permute-start(bf16[16,3584]{1,0:T(8,128)(2,1)S(1)} %get-tuple-element.77), channel_id=1, source_target_pairs={{0,2},{1,3},{2,0},{3,1},{4,6},{5,7},{6,4},{7,5},{8,10},{9,11},{10,... | collective-permute-start | bytes 344072 | tf_op jit(solution)/shard_map/ppermute | solution.py:288
  404.5 18.2 %collective-permute-start.15 = (bf16[16,3584]{1,0:T(8,128)(2,1)S(1)}, bf16[16,3584]{1,0:T(8,128)(2,1)S(1)}, u32[]{:S(2)}, u32[]{:S(2)}) collective-permute-start(bf16[16,3584]{1,0:T(8,128)(2,1)S(1)} %get-tuple-element.78), channel_id=1, source_target_pairs={{0,4},{1,5},{2,6},{3,7},{4,0},{5,1},{6,2},{7,3},{8,12},{9,13},{10,... | collective-permute-start | bytes 344072 | tf_op jit(solution)/shard_map/ppermute | solution.py:288
  419.6 16.5 %collective-permute-start.12 = (f32[16,3584]{1,0:T(8,128)S(1)}, f32[16,3584]{1,0:T(8,128)S(1)}, u32[]{:S(2)}, u32[]{:S(2)}) collective-permute-start(f32[16,3584]{1,0:T(8,128)S(1)} %get-tuple-element.73), channel_id=1, source_target_pairs={{0,2},{1,3},{2,0},{3,1},{4,6},{5,7},{6,4},{7,5},{8,10},{9,11},{10,... | collective-permute-start | bytes 688136 | tf_op jit(solution)/shard_map/ppermute | solution.py:288
  421.2 15.0 %collective-permute-start.13 = (f32[16,3584]{1,0:T(8,128)S(1)}, f32[16,3584]{1,0:T(8,128)S(1)}, u32[]{:S(2)}, u32[]{:S(2)}) collective-permute-start(f32[16,3584]{1,0:T(8,128)S(1)} %get-tuple-element.74), channel_id=1, source_target_pairs={{0,4},{1,5},{2,6},{3,7},{4,0},{5,1},{6,2},{7,3},{8,12},{9,13},{10,... | collective-permute-start | bytes 688136 | tf_op jit(solution)/shard_map/ppermute | solution.py:288
  436.3 18.5 %collective-permute-start.16 = (f32[48,3584]{1,0:T(8,128)S(1)}, f32[48,3584]{1,0:T(8,128)S(1)}, u32[]{:S(2)}, u32[]{:S(2)}) collective-permute-start(f32[48,3584]{1,0:T(8,128)S(1)} %get-tuple-element.80), channel_id=1, source_target_pairs={{0,2},{1,3},{2,0},{3,1},{4,6},{5,7},{6,4},{7,5},{8,10},{9,11},{10,... | collective-permute-start | bytes 2064392 | tf_op jit(solution)/shard_map/ppermute | solution.py:288
  436.9 17.9 %collective-permute-start.17 = (f32[48,3584]{1,0:T(8,128)S(1)}, f32[48,3584]{1,0:T(8,128)S(1)}, u32[]{:S(2)}, u32[]{:S(2)}) collective-permute-start(f32[48,3584]{1,0:T(8,128)S(1)} %get-tuple-element.81), channel_id=1, source_target_pairs={{0,4},{1,5},{2,6},{3,7},{4,0},{5,1},{6,2},{7,3},{8,12},{9,13},{10,... | collective-permute-start | bytes 2064392 | tf_op jit(solution)/shard_map/ppermute | solution.py:288
  455.7 13.2 %collective-permute-start.18 = (f32[48,3584]{1,0:T(8,128)S(1)}, f32[48,3584]{1,0:T(8,128)S(1)}, u32[]{:S(2)}, u32[]{:S(2)}) collective-permute-start(f32[48,3584]{1,0:T(8,128)S(1)} %get-tuple-element.86), channel_id=1, source_target_pairs={{0,2},{1,3},{2,0},{3,1},{4,6},{5,7},{6,4},{7,5},{8,10},{9,11},{10,... | collective-permute-start | bytes 2064392 | tf_op jit(solution)/shard_map/ppermute | solution.py:288
  457.2 13.3 %collective-permute-start.19 = (f32[48,3584]{1,0:T(8,128)S(1)}, f32[48,3584]{1,0:T(8,128)S(1)}, u32[]{:S(2)}, u32[]{:S(2)}) collective-permute-start(f32[48,3584]{1,0:T(8,128)S(1)} %get-tuple-element.87), channel_id=1, source_target_pairs={{0,4},{1,5},{2,6},{3,7},{4,0},{5,1},{6,2},{7,3},{8,12},{9,13},{10,... | collective-permute-start | bytes 2064392 | tf_op jit(solution)/shard_map/ppermute | solution.py:288
  471.8 29.3 %collective-permute-start.20 = (f32[48,3584]{1,0:T(8,128)}, f32[48,3584]{1,0:T(8,128)S(1)}, u32[]{:S(2)}, u32[]{:S(2)}) collective-permute-start(f32[48,3584]{1,0:T(8,128)} %get-tuple-element.92), channel_id=1, source_target_pairs={{0,2},{1,3},{2,0},{3,1},{4,6},{5,7},{6,4},{7,5},{8,10},{9,11},{10,... | collective-permute-start | bytes 2064392 | tf_op jit(solution)/shard_map/ppermute | solution.py:288
  472.6 28.5 %collective-permute-start.21 = (f32[48,3584]{1,0:T(8,128)}, f32[48,3584]{1,0:T(8,128)S(1)}, u32[]{:S(2)}, u32[]{:S(2)}) collective-permute-start(f32[48,3584]{1,0:T(8,128)} %get-tuple-element.93), channel_id=1, source_target_pairs={{0,4},{1,5},{2,6},{3,7},{4,0},{5,1},{6,2},{7,3},{8,12},{9,13},{10,... | collective-permute-start | bytes 2064392 | tf_op jit(solution)/shard_map/ppermute | solution.py:288
  474.7 26.4 %collective-permute-start.22 = (f32[32,3584]{1,0:T(8,128)}, f32[32,3584]{1,0:T(8,128)}, u32[]{:S(2)}, u32[]{:S(2)}) collective-permute-start(f32[32,3584]{1,0:T(8,128)} %get-tuple-element.98), channel_id=1, source_target_pairs={{0,16},{1,17},{2,18},{3,19},{4,20},{5,21},{6,22},{7,23},{8,24},{9,... | collective-permute-start | bytes 1376264 | tf_op jit(solution)/shard_map/ppermute | solution.py:288
  479.7 27.9 %collective-permute-start.25 = (f32[32,3584]{1,0:T(8,128)}, f32[32,3584]{1,0:T(8,128)S(1)}, u32[]{:S(2)}, u32[]{:S(2)}) collective-permute-start(f32[32,3584]{1,0:T(8,128)} %copy-done.12), channel_id=1, source_target_pairs={{0,24},{1,25},{2,26},{3,27},{4,28},{5,29},{6,30},{7,31},{8,16},{9,... | collective-permute-start | bytes 1376264 | tf_op jit(solution)/shard_map/ppermute | solution.py:288
  502.4 9.5 %collective-permute-start.23 = (f32[32,3584]{1,0:T(8,128)S(1)}, f32[32,3584]{1,0:T(8,128)S(1)}, u32[]{:S(2)}, u32[]{:S(2)}) collective-permute-start(f32[32,3584]{1,0:T(8,128)S(1)} %get-tuple-element.99), channel_id=1, source_target_pairs={{0,2},{1,3},{2,0},{3,1},{4,6},{5,7},{6,4},{7,5},{8,10},{9,11},{10,... | collective-permute-start | bytes 1376264 | tf_op jit(solution)/shard_map/ppermute | solution.py:288
  503.6 9.1 %collective-permute-start.24 = (f32[32,3584]{1,0:T(8,128)S(1)}, f32[32,3584]{1,0:T(8,128)S(1)}, u32[]{:S(2)}, u32[]{:S(2)}) collective-permute-start(f32[32,3584]{1,0:T(8,128)S(1)} %get-tuple-element.100), channel_id=1, source_target_pairs={{0,4},{1,5},{2,6},{3,7},{4,0},{5,1},{6,2},{7,3},{8,12},{9,13},{10,... | collective-permute-start | bytes 1376264 | tf_op jit(solution)/shard_map/ppermute | solution.py:288
  504.4 8.5 %collective-permute-start.26 = (f32[32,3584]{1,0:T(8,128)S(1)}, f32[32,3584]{1,0:T(8,128)S(1)}, u32[]{:S(2)}, u32[]{:S(2)}) collective-permute-start(f32[32,3584]{1,0:T(8,128)S(1)} %get-tuple-element.103), channel_id=1, source_target_pairs={{0,8},{1,9},{2,10},{3,11},{4,12},{5,13},{6,14},{7,15},{8,0},{9,1},... | collective-permute-start | bytes 1376264 | tf_op jit(solution)/shard_map/ppermute | solution.py:288
  (16 other events, 419.7 us)

commit v4 on v3

--- a/solution.py
+++ b/solution.py
@@ -95,40 +95,10 @@
         units(gate_other_ref, up_other_ref)
 
 
-def packed_weights(gate, up, down, after):
+def packed_weights(gate, up, down):
     width, units = gate.shape
-    blocks = width // units
-
-    def kernel(gate_ref, up_ref, down_ref, after_ref, out_ref, sems):
-        copies = [
-            pltpu.make_async_copy(gate_ref, out_ref.at[pl.ds(0, width)], sems.at[0]),
-            pltpu.make_async_copy(up_ref, out_ref.at[pl.ds(width, width)], sems.at[1]),
-        ]
-        for at in range(blocks):
-            copies.append(
-                pltpu.make_async_copy(
-                    down_ref.at[:, pl.ds(at * units, units)],
-                    out_ref.at[pl.ds(2 * width + at * units, units)],
-                    sems.at[2 + at],
-                )
-            )
-        for copy in copies:
-            copy.start()
-        for copy in copies:
-            copy.wait()
-
-    return pl.pallas_call(
-        kernel,
-        in_specs=[pl.BlockSpec(memory_space=pl.ANY)] * 4,
-        out_specs=pl.BlockSpec(memory_space=pl.ANY),
-        out_shape=jax.ShapeDtypeStruct((3 * width, units), gate.dtype),
-        scratch_shapes=[pltpu.SemaphoreType.DMA((2 + blocks,))],
-        compiler_params=pltpu.CompilerParams(vmem_limit_bytes=56 * MIB),
-        cost_estimate=pl.CostEstimate(
-            flops=0, bytes_accessed=12 * width * units, transcendentals=0
-        ),
-        name="packed_weights",
-    )(gate, up, down, after)
+    blocks = [down[:, at : at + units] for at in range(0, width, units)]
+    return jnp.concatenate([gate, up] + blocks, axis=0)
 
 
 def expert_hidden(pieces, gate, up, other):
@@ -168,35 +138,42 @@
         out_ref[...] = out[at * unit : (at + 1) * unit]
 
 
-def expert_output(plane, block, unit, scale, hidden, down, other):
+def expert_output(unit, scale, hidden, down, other):
     units, width = down.shape
+    count = hidden.shape[0]
+    slots = count // unit
     steps = width // units
-    slot = jax.ShapeDtypeStruct((unit, width), jnp.float32)
     return pl.pallas_call(
         output_kernel,
         grid=(steps,),
         in_specs=[
-            pl.BlockSpec((4 * unit, 1), lambda i: (plane, 0)),
-            pl.BlockSpec((4 * unit, 2 * units), lambda i: (block, 0)),
+            pl.BlockSpec((count, 1), lambda i: (0, 0)),
+            pl.BlockSpec((count, 2 * units), lambda i: (0, 0)),
             pl.BlockSpec((units, units), lambda i: (0, i)),
             pl.BlockSpec((units, units), lambda i: (2 * steps + i, 0)),
         ],
-        out_specs=[pl.BlockSpec((unit, units), lambda i: (0, i))] * 4,
-        out_shape=[slot] * 4,
+        out_specs=[pl.BlockSpec((unit, units), lambda i: (0, i))] * slots,
+        out_shape=[jax.ShapeDtypeStruct((unit, width), jnp.float32)] * slots,
         compiler_params=pltpu.CompilerParams(vmem_limit_bytes=44 * MIB),
         cost_estimate=pl.CostEstimate(
-            flops=16 * unit * width * units,
-            bytes_accessed=4 * width * units + 16 * unit * width,
+            flops=4 * count * width * units,
+            bytes_accessed=4 * width * units + 4 * count * width,
             transcendentals=0,
         ),
         name="expert_output",
     )(scale, hidden, down, other)
 
 
-def whole_call(kernel, operands, out_shape, name):
+def whole_call(kernel, operands, out_shape, name, after=()):
+    given = len(operands)
+
+    def body(*refs):
+        kernel(*refs[:given], *refs[given + len(after) :])
+
     return pl.pallas_call(
-        kernel,
-        in_specs=[pl.BlockSpec(memory_space=pltpu.VMEM)] * len(operands),
+        body,
+        in_specs=[pl.BlockSpec(memory_space=pltpu.VMEM)] * given
+        + [pl.BlockSpec(memory_space=pl.ANY)] * len(after),
         out_specs=[pl.BlockSpec(memory_space=pltpu.VMEM)] * len(out_shape),
         out_shape=out_shape,
         compiler_params=pltpu.CompilerParams(vmem_limit_bytes=12 * MIB),
@@ -206,10 +183,10 @@
             transcendentals=0,
         ),
         name=name,
-    )(*operands)
-
-
-def gather_round(unit, column, from_x, from_y, extra):
+    )(*operands, *after)
+
+
+def gather_round(unit, column, from_x, from_y, extra, after=()):
     width = from_x.shape[1]
     half = unit // 2
     head = unit if column is not None else 0
@@ -229,7 +206,7 @@
         if extra is not None:
             refs[2][...] = extra_ref[...]
 
-    return whole_call(kernel, operands, out_shape, "gather_round")
+    return whole_call(kernel, operands, out_shape, "gather_round", after)
 
 
 def scatter_round(received, plane, following, finished, column, base=()):
@@ -292,56 +269,62 @@
 
     gate, up, down = gate_weight[0], up_weight[0], down_weight[0]
 
-    column = {0: tokens, 1: flip(tokens, 4), 2: flip(tokens, 8)}
-    by_x, by_y = {0: flip(tokens, 1)}, {0: flip(tokens, 2)}
-    for plane in (1, 2, 3):
-        extra = tokens if plane == 1 else None
+    other = swap(packed_weights(gate, up, down))
+    gathered = [0, 2, 3, 1]
+    column = {0: tokens, 2: flip(tokens, 8)}
+    by_x, by_y = [flip(tokens, 1)], [flip(tokens, 2)]
+
+    def plane_rows(at):
+        tail = unit if at < 3 else 0
+        return [
+            (column[gathered[at]], 0, unit),
+            (by_x[at], 0, unit),
+            (by_y[at], 0, unit),
+            (by_x[at + 1], tail, tail + half),
+            (by_y[at + 1], tail, tail + half),
+        ]
+
+    hidden = []
+    for at in (1, 2, 3, 4):
+        plane = gathered[at] if at < 4 else None
+        extra = tokens if at < 3 else None
         to_x, to_y, *passed = gather_round(
-            unit, column[plane], by_x[plane - 1], by_y[plane - 1], extra
+            unit, column.get(plane), by_x[-1], by_y[-1], extra, hidden if at == 4 else ()
         )
-        by_x[plane], by_y[plane] = flip(to_x, 1), flip(to_y, 2)
+        by_x.append(flip(to_x, 1))
+        by_y.append(flip(to_y, 2))
         if passed:
-            column[3] = flip(passed[0], 12)
-            other = swap(packed_weights(gate, up, down, to_x))
-    to_x, to_y = gather_round(unit, None, by_x[3], by_y[3], None)
-    by_x[4], by_y[4] = flip(to_x, 1), flip(to_y, 2)
+            column[gathered[at + 1]] = flip(passed[0], 4 * gathered[at + 1])
+        if at in (2, 4):
+            rows = plane_rows(at - 2) + plane_rows(at - 1)
+            hidden.append(expert_hidden(rows, gate, up, other))
 
     slots = jnp.bitwise_xor(me, 2 * jnp.arange(chips, dtype=jnp.int32))
     picks = slots[:, None] == jnp.arange(peers, dtype=jnp.int32)[None, :]
     scale = jnp.sum(jnp.where(picks[:, :, None], share[None, :, :], 0.0), axis=1)
-    scale = scale.reshape(chips * unit, 1)
-
-    def plane_rows(plane):
-        tail = unit if plane < 3 else 0
-        return [
-            (column[plane], 0, unit),
-            (by_x[plane], 0, unit),
-            (by_y[plane], 0, unit),
-            (by_x[plane + 1], tail, tail + half),
-            (by_y[plane + 1], tail, tail + half),
-        ]
 
     outs = {}
-    for planes in ((0, 1), (2,), (3,)):
-        pieces = [piece for plane in planes for piece in plane_rows(plane)]
-        hidden = expert_hidden(pieces, gate, up, other)
-        for block, plane in enumerate(planes):
-            outs[plane] = expert_output(plane, block, unit, scale, hidden, down, other)
+    for units, planes in zip(hidden, (gathered[:2], gathered[2:])):
+        group_scale = jnp.concatenate([scale[4 * plane : 4 * plane + 4] for plane in planes])
+        results = expert_output(unit, group_scale.reshape(8 * unit, 1), units, down, other)
+        for place, plane in enumerate(planes):
+            outs[plane] = results[4 * place : 4 * place + 4]
 
     order = [2, 3, 1, 0]
-    sums = []
+    base, along_z = outs[0][0], None
     received = None
     for at in range(-1, len(order)):
         plane = outs[order[at]] if at >= 0 else None
         following = outs[order[at + 1]] if at + 1 < len(order) else None
         finished = outs[order[at - 1]] if at >= 1 else None
-        base = (outs[0][0], sums[0]) if at == 3 else ()
-        results = scatter_round(received, plane, following, finished, [], base)
+        bases = (base, along_z) if along_z is not None else ()
+        results = scatter_round(received, plane, following, finished, [], bases)
         received = (flip(results[0], 1), flip(results[1], 2))
+        if bases:
+            base = results[3]
         if finished is not None:
-            sums.append(flip(results[2], 4 * order[at - 1]))
-    own = (results[3],)
-    (total,) = scatter_round(received, None, None, own, sums[1:])
+            along_z = flip(results[2], 4 * order[at - 1])
+    (total,) = scatter_round(received, None, None, (base,), [along_z])
     return total.astype(jnp.bfloat16)
 
 

time: 515 us -> 185 us (0.36)
  Pallas kernels: 389 us -> 38 us
  local copies, waits for them, and re-layouts: 9.38 us -> 22.2 us
  starting transfers between devices: 37.5 us -> 43.6 us
    pallas_call x15 -> x12, Pallas kernels: 363 us -> 16.7 us  [the longest x2 12.7 us: expert_output(): pl.pallas_call(output_kernel, grid=(steps,), in_specs=[pl.BlockSpec((coun...]
    unnamed x40 -> x44, local copies, waits for them, and re-layouts: 4.4 us -> 16.4 us
    pallas_call x3 -> x2, Pallas kernels: 26.1 us -> 21.4 us  [expert_hidden(): pl.pallas_call(functools.partial(hidden_kernel, [(start, stop) for _, sta...]
  transfers between devices with their start and end apart: 28 -> 28, of which waited for: 14 -> 14; matrix products, arithmetic and copies ran while one was open for 2% -> 6% of each run, Pallas kernels for 10% -> 19%
where the time goes in v4:
time: 185 us; the launch traced here: 184 us
  waiting for transfers between devices  72 us (39%)
  starting transfers between devices  43.6 us (24%)
  Pallas kernels  38 us (21%)
  local copies, waits for them, and re-layouts  22.2 us (12%)
  other arithmetic  4.41 us (2%)
  matrix products  2.62 us (1%)
    ppermute x26, waiting for transfers between devices, flip(): lax.ppermute(value, 'ep', [(i, i ^ 2 * chip_bits) for i in range(peers)])  72 us
    ppermute x26, starting transfers between devices, flip(): lax.ppermute(value, 'ep', [(i, i ^ 2 * chip_bits) for i in range(peers)])  35.8 us
    pallas_call x2, Pallas kernels, expert_hidden(): pl.pallas_call(functools.partial(hidden_kernel, [(start, stop) for _, sta...  21.4 us
    unnamed x44, local copies, waits for them, and re-layouts  16.4 us
    pallas_call x2, Pallas kernels, expert_output(): pl.pallas_call(output_kernel, grid=(steps,), in_specs=[pl.BlockSpec((coun...  12.7 us
    all_to_all x1, starting transfers between devices, per_device(): lax.all_to_all(jnp.concatenate([packed.reshape(peers, 2 * block_len, late...  7.25 us
    pallas_call x10, Pallas kernels, whole_call(): pl.pallas_call(body, in_specs=[pl.BlockSpec(memory_space=pltpu.VMEM)] * g...  3.96 us
  transfers between devices with their start and end apart: 28, of which 14 were waited for; matrix products, arithmetic and copies ran while one was open for 6% of the time, Pallas kernels for 19%

profile of v4, /device:TPU:0, one launch (start us, length us, event | category | flops | bytes accessed | tf_op | source)
XLA Modules:
  0.0 184.4 jit_solution(1882506799224594671)
XLA Ops:
  0.7 4.3 %constant_dynamic-update-slice_fusion.1 = bf16[10752,512]{1,0:T(8,128)(2,1)} fusion(bf16[1,3584,512]{2,1,0:T(8,128)(2,1)} %param.23), kind=kLoop, calls=%fused_computation.37 | loop fusion | bytes 7340032
  5.0 2.1 %constant_dynamic-update-slice_fusion = bf16[10752,512]{1,0:T(8,128)(2,1)} fusion(bf16[10752,512]{1,0:T(8,128)(2,1)} %constant_dynamic-update-slice_fusion.1, bf16[1,3584,512]{2,1,0:T(8,128)(2,1)S(1)} %copy-done.10), kind=kLoop, calls=%fused_computation.36 | loop fusion | bytes 7340032
  17.3 7.3 %all-to-all-start = ((bf16[32,8,608]{2,1,0:T(8,128)(2,1)}), bf16[32,8,608]{2,1,0:T(8,128)(2,1)}, u32[]{:S(2)}, u32[]{:S(2)}) async-start(bf16[32,8,608]{2,1,0:T(8,128)(2,1)} %pad_maximum_fusion), calls=%async_computation | async-start | bytes 655360 | tf_op jit(solution)/shard_map/all_to_all | solution.py:372
  24.5 1.6 collective-permute-start
  26.1 1.5 collective-permute-start.1
  27.6 2.4 %collective-permute-start.2 = (bf16[32,3584]{1,0:T(8,128)(2,1)S(1)}, bf16[32,3584]{1,0:T(8,128)(2,1)S(1)}, u32[]{:S(2)}, u32[]{:S(2)}) collective-permute-start(bf16[32,3584]{1,0:T(8,128)(2,1)S(1)} %copy-done.9), channel_id=1, source_target_pairs={{0,16},{1,17},{2,18},{3,19},{4,20},{5,21},{6,22},{7,23},{8,24},{9,... | collective-permute-start | bytes 688136 | tf_op jit(solution)/shard_map/ppermute | solution.py:265
  30.0 5.4 %collective-permute-done.refs_0_.refs_1_ = bf16[32,3584]{1,0:T(8,128)(2,1)S(1)} collective-permute-done((bf16[32,3584]{1,0:T(8,128)(2,1)S(1)}, bf16[32,3584]{1,0:T(8,128)(2,1)S(1)}, u32[]{:S(2)}, u32[]{:S(2)}) %collective-permute-start) | collective-permute-done | bytes 229408 | tf_op jit(solution)/shard_map/ppermute | solution.py:265
  35.8 9.1 %collective-permute-done.2.refs_2_.refs_5_ = bf16[32,3584]{1,0:T(8,128)(2,1)S(1)} collective-permute-done((bf16[32,3584]{1,0:T(8,128)(2,1)S(1)}, bf16[32,3584]{1,0:T(8,128)(2,1)S(1)}, u32[]{:S(2)}, u32[]{:S(2)}) %collective-permute-start.2) | collective-permute-done | bytes 229408 | tf_op jit(solution)/shard_map/ppermute | solution.py:265
  44.9 1.5 collective-permute-start.3
  46.4 1.5 collective-permute-start.4
  49.4 7.0 %collective-permute-done.5.refs_2_.refs_0_ = bf16[32,3584]{1,0:T(8,128)(2,1)S(1)} collective-permute-done((bf16[32,3584]{1,0:T(8,128)(2,1)S(1)}, bf16[32,3584]{1,0:T(8,128)(2,1)S(1)}, u32[]{:S(2)}, u32[]{:S(2)}) %collective-permute-start.5) | collective-permute-done | bytes 229408 | tf_op jit(solution)/shard_map/ppermute | solution.py:265
  58.7 1.6 collective-permute-start.11
  62.1 2.8 %collective-permute-done.11.refs_2_.refs_5_ = bf16[32,3584]{1,0:T(8,128)(2,1)S(1)} collective-permute-done((bf16[32,3584]{1,0:T(8,128)(2,1)}, bf16[32,3584]{1,0:T(8,128)(2,1)S(1)}, u32[]{:S(2)}, u32[]{:S(2)}) %collective-permute-start.11) | collective-permute-done | bytes 229408 | tf_op jit(solution)/shard_map/ppermute | solution.py:265
  65.7 1.5 collective-permute-start.12
  68.4 10.7 %expert_hidden.2.hidden_ref.refs_2_ = bf16[256,1024]{1,0:T(8,128)(2,1)} custom-call(bf16[32,3584]{1,0:T(8,128)(2,1)S(1)} %copy-done.9, bf16[32,3584]{1,0:T(8,128)(2,1)S(1)} %collective-permute-done.refs_0_.refs_1_, bf16[32,3584]{1,0:T(8,128)(2,1)S(1)} %collective-permute-done.1.refs_1_.refs_2_, ...), custom_call_target="tpu_custom_call" | custom-call | flops 3758096384 | bytes 17039360 | tf_op jit(solution)/shard_map/expert_hidden/pallas_call | solution.py:112
  82.8 6.4 %expert_output.2 = (f32[32,3584]{1,0:T(8,128)S(1)}, f32[32,3584]{1,0:T(8,128)S(1)}, f32[32,3584]{1,0:T(8,128)S(1)}, f32[32,3584]{1,0:T(8,128)S(1)}, f32[32,3584]...) custom-call(f32[256,1]{1,0:T(8,128)S(1)} %reshape.199.scale_ref, ...), custom_call_target="tpu_custom_call" | custom-call | flops 1879048192 | bytes 11010048 | tf_op jit(solution)/shard_map/expert_output/pallas_call | solution.py:146
  91.9 10.6 %expert_hidden.3.hidden_ref = bf16[256,1024]{1,0:T(8,128)(2,1)} custom-call(bf16[32,3584]{1,0:T(8,128)(2,1)S(1)} %collective-permute-done.5.refs_2_.refs_0_, bf16[48,3584]{1,0:T(8,128)(2,1)S(1)} %collective-permute-done.6.refs_8_.refs_0_.refs_1_, bf16[48,3584]{1,0:T(8,128)(2,1)S(1)} %copy-done.6, ...), custom_call_target="tpu_custom_call" | custom-call | flops 3758096384 | bytes 17039360 | tf_op jit(solution)/shard_map/expert_hidden/pallas_call | solution.py:112
  103.5 6.3 %expert_output.3 = (f32[32,3584]{1,0:T(8,128)S(1)}, f32[32,3584]{1,0:T(8,128)S(1)}, f32[32,3584]{1,0:T(8,128)S(1)}, f32[32,3584]{1,0:T(8,128)S(1)}, f32[32,3584]...) custom-call(f32[256,1]{1,0:T(8,128)S(1)} %reshape.200.scale_ref, ...), custom_call_target="tpu_custom_call" | custom-call | flops 1879048192 | bytes 11010048 | tf_op jit(solution)/shard_map/expert_output/pallas_call | solution.py:146
  111.5 13.5 %collective-permute-done.16.refs_0_ = f32[48,3584]{1,0:T(8,128)S(1)} collective-permute-done((f32[48,3584]{1,0:T(8,128)S(1)}, f32[48,3584]{1,0:T(8,128)S(1)}, u32[]{:S(2)}, u32[]{:S(2)}) %collective-permute-start.16) | collective-permute-done | bytes 688160 | tf_op jit(solution)/shard_map/ppermute | solution.py:265
  125.4 1.6 collective-permute-start.18
  127.9 7.2 %collective-permute-start.20 = (f32[32,3584]{1,0:T(8,128)S(1)}, f32[32,3584]{1,0:T(8,128)S(1)}, u32[]{:S(2)}, u32[]{:S(2)}) collective-permute-start(f32[32,3584]{1,0:T(8,128)S(1)} %get-tuple-element.96), channel_id=1, source_target_pairs={{0,16},{1,17},{2,18},{3,19},{4,20},{5,21},{6,22},{7,23},{8,24},{9,... | collective-permute-start | bytes 1376264 | tf_op jit(solution)/shard_map/ppermute | solution.py:265
  135.1 19.6 %collective-permute-done.20.refs_7_ = f32[32,3584]{1,0:T(8,128)S(1)} collective-permute-done((f32[32,3584]{1,0:T(8,128)S(1)}, f32[32,3584]{1,0:T(8,128)S(1)}, u32[]{:S(2)}, u32[]{:S(2)}) %collective-permute-start.20) | collective-permute-done | bytes 458784 | tf_op jit(solution)/shard_map/ppermute | solution.py:265
  156.8 1.5 collective-permute-start.23
  159.6 1.7 slice_bitcast_fusion
  161.3 1.8 copy.24
  163.2 7.4 %collective-permute-done.23.refs_6_ = f32[32,3584]{1,0:T(8,128)} collective-permute-done((f32[32,3584]{1,0:T(8,128)}, f32[32,3584]{1,0:T(8,128)}, u32[]{:S(2)}, u32[]{:S(2)}) %collective-permute-start.23) | collective-permute-done | bytes 458784 | tf_op jit(solution)/shard_map/ppermute | solution.py:265
  171.7 1.7 collective-permute-start.24
  173.4 1.7 collective-permute-start.25
  176.2 1.5 fusion.14
  177.7 2.6 %collective-permute-done.24.refs_0_ = f32[32,3584]{1,0:T(8,128)S(1)} collective-permute-done((f32[32,3584]{1,0:T(8,128)S(1)}, f32[32,3584]{1,0:T(8,128)S(1)}, u32[]{:S(2)}, u32[]{:S(2)}) %collective-permute-start.24) | collective-permute-done | bytes 458784 | tf_op jit(solution)/shard_map/ppermute | solution.py:265
  180.3 1.6 collective-permute-done.25.refs_1_
  181.9 1.7 collective-permute-done.26.refs_3_
  (119 shorter events, 34.0 us)
Async XLA Ops:
  0.6 174.5 %copy-start = (bf16[1,128,576]{1,2,0:T(8,128)(2,1)S(1)}, bf16[1,128,576]{1,2,0:T(8,128)(2,1)}, u32[]{:S(2)}) copy-start(bf16[1,128,576]{1,2,0:T(8,128)(2,1)} %param.15) | copy-start | bytes 442372
  10.9 13.6 %copy-start.9 = (bf16[32,3584]{1,0:T(8,128)(2,1)S(1)}, bf16[32,3584]{1,0:T(8,128)(2,1)}, u32[]{:S(2)}) copy-start(bf16[32,3584]{1,0:T(8,128)(2,1)} %refs_0_.1) | copy-start | bytes 688132
  14.3 54.1 %collective-permute-start.8 = (bf16[10752,512]{1,0:T(8,128)(2,1)}, bf16[10752,512]{1,0:T(8,128)(2,1)}, u32[]{:S(2)}, u32[]{:S(2)}) collective-permute-start(bf16[10752,512]{1,0:T(8,128)(2,1)} %slice_dynamic-update-slice_fusion), channel_id=1, source_target_pairs={{0,1},{1,0},{2,3},{3,2},{4,5},{5,4},{6,7},{7,6},{8,9},{9,8},{10,11... | collective-permute-start | bytes 33030152 | tf_op jit(solution)/shard_map/ppermute | solution.py:268
  17.3 43.0 %all-to-all-start = ((bf16[32,8,608]{2,1,0:T(8,128)(2,1)}), bf16[32,8,608]{2,1,0:T(8,128)(2,1)}, u32[]{:S(2)}, u32[]{:S(2)}) async-start(bf16[32,8,608]{2,1,0:T(8,128)(2,1)} %pad_maximum_fusion), calls=%async_computation | async-start | bytes 655360 | tf_op jit(solution)/shard_map/all_to_all | solution.py:372
  24.5 10.9 %collective-permute-start = (bf16[32,3584]{1,0:T(8,128)(2,1)S(1)}, bf16[32,3584]{1,0:T(8,128)(2,1)S(1)}, u32[]{:S(2)}, u32[]{:S(2)}) collective-permute-start(bf16[32,3584]{1,0:T(8,128)(2,1)S(1)} %copy-done.9), channel_id=1, source_target_pairs={{0,2},{1,3},{2,0},{3,1},{4,6},{5,7},{6,4},{7,5},{8,10},{9,11},{10,... | collective-permute-start | bytes 688136 | tf_op jit(solution)/shard_map/ppermute | solution.py:265
  26.1 9.6 %collective-permute-start.1 = (bf16[32,3584]{1,0:T(8,128)(2,1)S(1)}, bf16[32,3584]{1,0:T(8,128)(2,1)S(1)}, u32[]{:S(2)}, u32[]{:S(2)}) collective-permute-start(bf16[32,3584]{1,0:T(8,128)(2,1)S(1)} %copy-done.9), channel_id=1, source_target_pairs={{0,4},{1,5},{2,6},{3,7},{4,0},{5,1},{6,2},{7,3},{8,12},{9,13},{10,... | collective-permute-start | bytes 688136 | tf_op jit(solution)/shard_map/ppermute | solution.py:265
  27.6 17.3 %collective-permute-start.2 = (bf16[32,3584]{1,0:T(8,128)(2,1)S(1)}, bf16[32,3584]{1,0:T(8,128)(2,1)S(1)}, u32[]{:S(2)}, u32[]{:S(2)}) collective-permute-start(bf16[32,3584]{1,0:T(8,128)(2,1)S(1)} %copy-done.9), channel_id=1, source_target_pairs={{0,16},{1,17},{2,18},{3,19},{4,20},{5,21},{6,22},{7,23},{8,24},{9,... | collective-permute-start | bytes 688136 | tf_op jit(solution)/shard_map/ppermute | solution.py:265
  44.9 11.5 %collective-permute-start.3 = (bf16[48,3584]{1,0:T(8,128)(2,1)S(1)}, bf16[48,3584]{1,0:T(8,128)(2,1)S(1)}, u32[]{:S(2)}, u32[]{:S(2)}) collective-permute-start(bf16[48,3584]{1,0:T(8,128)(2,1)S(1)} %get-tuple-element.67), channel_id=1, source_target_pairs={{0,2},{1,3},{2,0},{3,1},{4,6},{5,7},{6,4},{7,5},{8,10},{9,11},{10,... | collective-permute-start | bytes 1032200 | tf_op jit(solution)/shard_map/ppermute | solution.py:265
  46.4 10.0 %collective-permute-start.4 = (bf16[48,3584]{1,0:T(8,128)(2,1)S(1)}, bf16[48,3584]{1,0:T(8,128)(2,1)S(1)}, u32[]{:S(2)}, u32[]{:S(2)}) collective-permute-start(bf16[48,3584]{1,0:T(8,128)(2,1)S(1)} %get-tuple-element.68), channel_id=1, source_target_pairs={{0,4},{1,5},{2,6},{3,7},{4,0},{5,1},{6,2},{7,3},{8,12},{9,13},{10,... | collective-permute-start | bytes 1032200 | tf_op jit(solution)/shard_map/ppermute | solution.py:265
  47.9 8.5 %collective-permute-start.5 = (bf16[32,3584]{1,0:T(8,128)(2,1)S(1)}, bf16[32,3584]{1,0:T(8,128)(2,1)S(1)}, u32[]{:S(2)}, u32[]{:S(2)}) collective-permute-start(bf16[32,3584]{1,0:T(8,128)(2,1)S(1)} %get-tuple-element.69), channel_id=1, source_target_pairs={{0,24},{1,25},{2,26},{3,27},{4,28},{5,29},{6,30},{7,31},{8,16},{9,... | collective-permute-start | bytes 688136 | tf_op jit(solution)/shard_map/ppermute | solution.py:265
  57.3 8.3 %collective-permute-start.6 = (bf16[48,3584]{1,0:T(8,128)(2,1)}, bf16[48,3584]{1,0:T(8,128)(2,1)S(1)}, u32[]{:S(2)}, u32[]{:S(2)}) collective-permute-start(bf16[48,3584]{1,0:T(8,128)(2,1)} %get-tuple-element.70), channel_id=1, source_target_pairs={{0,2},{1,3},{2,0},{3,1},{4,6},{5,7},{6,4},{7,5},{8,10},{9,11},{10,... | collective-permute-start | bytes 1032200 | tf_op jit(solution)/shard_map/ppermute | solution.py:265
  57.8 7.8 %collective-permute-start.7 = (bf16[48,3584]{1,0:T(8,128)(2,1)S(1)}, bf16[48,3584]{1,0:T(8,128)(2,1)S(1)}, u32[]{:S(2)}, u32[]{:S(2)}) collective-permute-start(bf16[48,3584]{1,0:T(8,128)(2,1)S(1)} %get-tuple-element.71), channel_id=1, source_target_pairs={{0,4},{1,5},{2,6},{3,7},{4,0},{5,1},{6,2},{7,3},{8,12},{9,13},{10,... | collective-permute-start | bytes 1032200 | tf_op jit(solution)/shard_map/ppermute | solution.py:265
  58.7 6.2 %collective-permute-start.11 = (bf16[32,3584]{1,0:T(8,128)(2,1)}, bf16[32,3584]{1,0:T(8,128)(2,1)S(1)}, u32[]{:S(2)}, u32[]{:S(2)}) collective-permute-start(bf16[32,3584]{1,0:T(8,128)(2,1)} %get-tuple-element.77), channel_id=1, source_target_pairs={{0,8},{1,9},{2,10},{3,11},{4,12},{5,13},{6,14},{7,15},{8,0},{9,1},... | collective-permute-start | bytes 688136 | tf_op jit(solution)/shard_map/ppermute | solution.py:265
  65.7 13.4 %collective-permute-start.12 = (bf16[48,3584]{1,0:T(8,128)(2,1)S(1)}, bf16[48,3584]{1,0:T(8,128)(2,1)S(1)}, u32[]{:S(2)}, u32[]{:S(2)}) collective-permute-start(bf16[48,3584]{1,0:T(8,128)(2,1)S(1)} %get-tuple-element.78), channel_id=1, source_target_pairs={{0,2},{1,3},{2,0},{3,1},{4,6},{5,7},{6,4},{7,5},{8,10},{9,11},{10,... | collective-permute-start | bytes 1032200 | tf_op jit(solution)/shard_map/ppermute | solution.py:265
  67.3 11.9 %collective-permute-start.13 = (bf16[48,3584]{1,0:T(8,128)(2,1)S(1)}, bf16[48,3584]{1,0:T(8,128)(2,1)S(1)}, u32[]{:S(2)}, u32[]{:S(2)}) collective-permute-start(bf16[48,3584]{1,0:T(8,128)(2,1)S(1)} %get-tuple-element.79), channel_id=1, source_target_pairs={{0,4},{1,5},{2,6},{3,7},{4,0},{5,1},{6,2},{7,3},{8,12},{9,13},{10,... | collective-permute-start | bytes 1032200 | tf_op jit(solution)/shard_map/ppermute | solution.py:265
  68.4 13.3 %copy-start.2 = (bf16[1,512,3584]{2,1,0:T(8,128)(2,1)S(1)}, bf16[1,512,3584]{2,1,0:T(8,128)(2,1)}, u32[]{:S(2)}) copy-start(bf16[1,512,3584]{2,1,0:T(8,128)(2,1)} %param.25) | copy-start | bytes 11010052
  80.2 11.7 %collective-permute-start.14 = (bf16[16,3584]{1,0:T(8,128)(2,1)S(1)}, bf16[16,3584]{1,0:T(8,128)(2,1)S(1)}, u32[]{:S(2)}, u32[]{:S(2)}) collective-permute-start(bf16[16,3584]{1,0:T(8,128)(2,1)S(1)} %get-tuple-element.80), channel_id=1, source_target_pairs={{0,2},{1,3},{2,0},{3,1},{4,6},{5,7},{6,4},{7,5},{8,10},{9,11},{10,... | collective-permute-start | bytes 344072 | tf_op jit(solution)/shard_map/ppermute | solution.py:265
  80.8 11.0 %collective-permute-start.15 = (bf16[16,3584]{1,0:T(8,128)(2,1)S(1)}, bf16[16,3584]{1,0:T(8,128)(2,1)S(1)}, u32[]{:S(2)}, u32[]{:S(2)}) collective-permute-start(bf16[16,3584]{1,0:T(8,128)(2,1)S(1)} %get-tuple-element.81), channel_id=1, source_target_pairs={{0,4},{1,5},{2,6},{3,7},{4,0},{5,1},{6,2},{7,3},{8,12},{9,13},{10,... | collective-permute-start | bytes 344072 | tf_op jit(solution)/shard_map/ppermute | solution.py:265
  89.2 20.7 %collective-permute-start.10 = (f32[16,3584]{1,0:T(8,128)S(1)}, f32[16,3584]{1,0:T(8,128)S(1)}, u32[]{:S(2)}, u32[]{:S(2)}) collective-permute-start(f32[16,3584]{1,0:T(8,128)S(1)} %get-tuple-element.74), channel_id=1, source_target_pairs={{0,4},{1,5},{2,6},{3,7},{4,0},{5,1},{6,2},{7,3},{8,12},{9,13},{10,... | collective-permute-start | bytes 688136 | tf_op jit(solution)/shard_map/ppermute | solution.py:265
  90.4 19.5 %collective-permute-start.9 = (f32[16,3584]{1,0:T(8,128)S(1)}, f32[16,3584]{1,0:T(8,128)S(1)}, u32[]{:S(2)}, u32[]{:S(2)}) collective-permute-start(f32[16,3584]{1,0:T(8,128)S(1)} %get-tuple-element.73), channel_id=1, source_target_pairs={{0,2},{1,3},{2,0},{3,1},{4,6},{5,7},{6,4},{7,5},{8,10},{9,11},{10,... | collective-permute-start | bytes 688136 | tf_op jit(solution)/shard_map/ppermute | solution.py:265
  110.0 15.0 %collective-permute-start.16 = (f32[48,3584]{1,0:T(8,128)S(1)}, f32[48,3584]{1,0:T(8,128)S(1)}, u32[]{:S(2)}, u32[]{:S(2)}) collective-permute-start(f32[48,3584]{1,0:T(8,128)S(1)} %get-tuple-element.83), channel_id=1, source_target_pairs={{0,2},{1,3},{2,0},{3,1},{4,6},{5,7},{6,4},{7,5},{8,10},{9,11},{10,... | collective-permute-start | bytes 2064392 | tf_op jit(solution)/shard_map/ppermute | solution.py:265
  110.7 14.6 %collective-permute-start.17 = (f32[48,3584]{1,0:T(8,128)S(1)}, f32[48,3584]{1,0:T(8,128)S(1)}, u32[]{:S(2)}, u32[]{:S(2)}) collective-permute-start(f32[48,3584]{1,0:T(8,128)S(1)} %get-tuple-element.84), channel_id=1, source_target_pairs={{0,4},{1,5},{2,6},{3,7},{4,0},{5,1},{6,2},{7,3},{8,12},{9,13},{10,... | collective-permute-start | bytes 2064392 | tf_op jit(solution)/shard_map/ppermute | solution.py:265
  125.4 29.3 %collective-permute-start.18 = (f32[48,3584]{1,0:T(8,128)S(1)}, f32[48,3584]{1,0:T(8,128)S(1)}, u32[]{:S(2)}, u32[]{:S(2)}) collective-permute-start(f32[48,3584]{1,0:T(8,128)S(1)} %get-tuple-element.89), channel_id=1, source_target_pairs={{0,2},{1,3},{2,0},{3,1},{4,6},{5,7},{6,4},{7,5},{8,10},{9,11},{10,... | collective-permute-start | bytes 2064392 | tf_op jit(solution)/shard_map/ppermute | solution.py:265
  127.0 27.7 %collective-permute-start.19 = (f32[48,3584]{1,0:T(8,128)S(1)}, f32[48,3584]{1,0:T(8,128)S(1)}, u32[]{:S(2)}, u32[]{:S(2)}) collective-permute-start(f32[48,3584]{1,0:T(8,128)S(1)} %get-tuple-element.90), channel_id=1, source_target_pairs={{0,4},{1,5},{2,6},{3,7},{4,0},{5,1},{6,2},{7,3},{8,12},{9,13},{10,... | collective-permute-start | bytes 2064392 | tf_op jit(solution)/shard_map/ppermute | solution.py:265
  127.9 26.8 %collective-permute-start.20 = (f32[32,3584]{1,0:T(8,128)S(1)}, f32[32,3584]{1,0:T(8,128)S(1)}, u32[]{:S(2)}, u32[]{:S(2)}) collective-permute-start(f32[32,3584]{1,0:T(8,128)S(1)} %get-tuple-element.96), channel_id=1, source_target_pairs={{0,16},{1,17},{2,18},{3,19},{4,20},{5,21},{6,22},{7,23},{8,24},{9,... | collective-permute-start | bytes 1376264 | tf_op jit(solution)/shard_map/ppermute | solution.py:265
  156.1 14.4 %collective-permute-start.21 = (f32[48,3584]{1,0:T(8,128)}, f32[48,3584]{1,0:T(8,128)S(1)}, u32[]{:S(2)}, u32[]{:S(2)}) collective-permute-start(f32[48,3584]{1,0:T(8,128)} %get-tuple-element.97), channel_id=1, source_target_pairs={{0,2},{1,3},{2,0},{3,1},{4,6},{5,7},{6,4},{7,5},{8,10},{9,11},{10,... | collective-permute-start | bytes 2064392 | tf_op jit(solution)/shard_map/ppermute | solution.py:265
  156.1 14.4 %collective-permute-start.22 = (f32[48,3584]{1,0:T(8,128)}, f32[48,3584]{1,0:T(8,128)S(1)}, u32[]{:S(2)}, u32[]{:S(2)}) collective-permute-start(f32[48,3584]{1,0:T(8,128)} %get-tuple-element.98), channel_id=1, source_target_pairs={{0,4},{1,5},{2,6},{3,7},{4,0},{5,1},{6,2},{7,3},{8,12},{9,13},{10,... | collective-permute-start | bytes 2064392 | tf_op jit(solution)/shard_map/ppermute | solution.py:265
  156.8 13.8 %collective-permute-start.23 = (f32[32,3584]{1,0:T(8,128)}, f32[32,3584]{1,0:T(8,128)}, u32[]{:S(2)}, u32[]{:S(2)}) collective-permute-start(f32[32,3584]{1,0:T(8,128)} %get-tuple-element.103), channel_id=1, source_target_pairs={{0,24},{1,25},{2,26},{3,27},{4,28},{5,29},{6,30},{7,31},{8,16},{9,... | collective-permute-start | bytes 1376264 | tf_op jit(solution)/shard_map/ppermute | solution.py:265
  163.2 12.0 %copy-start.16 = (bf16[1,1024,576]{1,2,0:T(8,128)(2,1)S(1)}, bf16[1,1024,576]{1,2,0:T(8,128)(2,1)}, u32[]{:S(2)}) copy-start(bf16[1,1024,576]{1,2,0:T(8,128)(2,1)} %param.16) | copy-start | bytes 3538948
  171.7 8.5 %collective-permute-start.24 = (f32[32,3584]{1,0:T(8,128)S(1)}, f32[32,3584]{1,0:T(8,128)S(1)}, u32[]{:S(2)}, u32[]{:S(2)}) collective-permute-start(f32[32,3584]{1,0:T(8,128)S(1)} %get-tuple-element.104), channel_id=1, source_target_pairs={{0,2},{1,3},{2,0},{3,1},{4,6},{5,7},{6,4},{7,5},{8,10},{9,11},{10,... | collective-permute-start | bytes 1376264 | tf_op jit(solution)/shard_map/ppermute | solution.py:265
  173.4 8.5 %collective-permute-start.25 = (f32[32,3584]{1,0:T(8,128)S(1)}, f32[32,3584]{1,0:T(8,128)S(1)}, u32[]{:S(2)}, u32[]{:S(2)}) collective-permute-start(f32[32,3584]{1,0:T(8,128)S(1)} %get-tuple-element.105), channel_id=1, source_target_pairs={{0,4},{1,5},{2,6},{3,7},{4,0},{5,1},{6,2},{7,3},{8,12},{9,13},{10,... | collective-permute-start | bytes 1376264 | tf_op jit(solution)/shard_map/ppermute | solution.py:265
  175.2 8.5 %collective-permute-start.26 = (f32[32,3584]{1,0:T(8,128)S(1)}, f32[32,3584]{1,0:T(8,128)S(1)}, u32[]{:S(2)}, u32[]{:S(2)}) collective-permute-start(f32[32,3584]{1,0:T(8,128)S(1)} %get-tuple-element.107), channel_id=1, source_target_pairs={{0,8},{1,9},{2,10},{3,11},{4,12},{5,13},{6,14},{7,15},{8,0},{9,1},... | collective-permute-start | bytes 1376264 | tf_op jit(solution)/shard_map/ppermute | solution.py:265
  (14 other events, 71.3 us)

commit v5 on v1

--- a/solution.py
+++ b/solution.py
@@ -1,6 +1,10 @@
+import functools
+
 import jax
 import jax.numpy as jnp
 from jax import lax
+from jax.experimental import pallas as pl
+from jax.experimental.pallas import tpu as pltpu
 from jax.sharding import PartitionSpec as P
 
 VAL = 512
@@ -46,6 +50,245 @@
         first[1] * left + second[1] * right,
         first[2] * left[:, None] + second[2] * right[:, None],
     )
+
+
+def ring_experts(tokens, share, gate_weight, up_weight, down_weight):
+    rows = lax.all_gather(tokens, "ep", axis=0, tiled=True)
+    gate = jnp.dot(rows, gate_weight[0], preferred_element_type=jnp.float32)
+    upper = jnp.dot(rows, up_weight[0], preferred_element_type=jnp.float32)
+    hidden = (jax.nn.silu(gate) * upper).astype(jnp.bfloat16)
+    if lax.axis_size("tp") > 1:
+        hidden = lax.all_gather(hidden, "tp", axis=1, tiled=True)
+    partial_out = jnp.dot(hidden, down_weight[0], preferred_element_type=jnp.float32)
+    scaled = partial_out * share.reshape(-1)[:, None]
+    return lax.psum_scatter(scaled, "ep", scatter_dimension=0, tiled=True).astype(jnp.bfloat16)
+
+
+MIB = 1024 * 1024
+
+LINKS = (1, 2, 4, 12)
+
+
+def across(value, link):
+    peers = lax.axis_size("ep")
+    return lax.ppermute(value, "ep", [(i, i ^ (2 * LINKS[link])) for i in range(peers)])
+
+
+def swap_cores(value):
+    return lax.ppermute(value, "ep", [(i, i ^ 1) for i in range(lax.axis_size("ep"))])
+
+
+def slot_of(bits, quarter, top_first):
+    count = len(LINKS)
+    slot = 0
+    for i in range(count):
+        at = count - 1 - i if top_first else i
+        slot |= ((bits >> at) & 1) << ((quarter + i) % count)
+    return slot
+
+
+def whole_call(kernel, operands, out_shape, name, after=()):
+    given = len(operands)
+
+    def body(*refs):
+        kernel(*refs[:given], *refs[given + len(after) :])
+
+    return pl.pallas_call(
+        body,
+        in_specs=[pl.BlockSpec(memory_space=pltpu.VMEM)] * given
+        + [pl.BlockSpec(memory_space=pl.ANY)] * len(after),
+        out_specs=[pl.BlockSpec(memory_space=pltpu.VMEM)] * len(out_shape),
+        out_shape=out_shape,
+        compiler_params=pltpu.CompilerParams(vmem_limit_bytes=12 * MIB),
+        cost_estimate=pl.CostEstimate(
+            flops=0,
+            bytes_accessed=sum(x.size * x.dtype.itemsize for x in list(operands) + list(out_shape)),
+            transcendentals=0,
+        ),
+        name=name,
+    )(*operands, *after)
+
+
+def joined(held, got, after):
+    count = len(held)
+    out_shape = [jax.ShapeDtypeStruct((2 * x.shape[0], x.shape[1]), x.dtype) for x in held]
+
+    def kernel(*refs):
+        for first, second, out in zip(refs[:count], refs[count : 2 * count], refs[2 * count :]):
+            rows = first.shape[0]
+            out[:rows] = first[...]
+            out[rows:] = second[...]
+
+    return whole_call(kernel, [*held, *got], out_shape, "joined", after)
+
+
+def hold_back(array, after):
+    def kernel(in_ref, out_ref):
+        out_ref[...] = in_ref[...]
+
+    shape = jax.ShapeDtypeStruct(array.shape, array.dtype)
+    return whole_call(kernel, [array], [shape], "hold_back", (after,))[0]
+
+
+def gather_cube(tokens, others):
+    count = len(LINKS)
+    width = tokens.shape[1] // count
+    held = [tokens[:, q * width : (q + 1) * width] for q in range(count)]
+    for phase in range(count):
+        got = [across(held[q], (q + phase) % count) for q in range(count)]
+        if phase < count - 1:
+            held = joined(held, got, others if phase == 1 else ())
+    return held, got
+
+
+def hidden_kernel(unit, *refs):
+    count = len(LINKS)
+    held, got = refs[:count], refs[count : 2 * count]
+    gate_ref, up_ref, gate_other_ref, up_other_ref, hidden_ref, rows_ref = refs[2 * count :]
+    step = pl.program_id(0)
+    own_steps = pl.num_programs(0) // 2
+
+    @pl.when(step == 0)
+    def _():
+        for quarter in range(count):
+            half, width = held[quarter].shape
+            columns = slice(quarter * width, (quarter + 1) * width)
+            for place in range(2 * half // unit):
+                source = held[quarter] if place * unit < half else got[quarter]
+                at = place * unit % half
+                slot = slot_of(place, quarter, False)
+                rows_ref[slot * unit : (slot + 1) * unit, columns] = source[at : at + unit]
+
+    def units(gate_tile, up_tile):
+        rows = rows_ref[...]
+        gate = jnp.dot(rows, gate_tile[...], preferred_element_type=jnp.float32)
+        upper = jnp.dot(rows, up_tile[...], preferred_element_type=jnp.float32)
+        hidden_ref[...] = (gate / (1.0 + jnp.exp(-gate)) * upper).astype(jnp.bfloat16)
+
+    @pl.when(step < own_steps)
+    def _():
+        units(gate_ref, up_ref)
+
+    @pl.when(step >= own_steps)
+    def _():
+        units(gate_other_ref, up_other_ref)
+
+
+def expert_hidden(unit, held, got, gate, up, gate_other, up_other):
+    width, units = gate.shape
+    count = 2 * held[0].shape[0]
+    tile = 256
+    steps = units // tile
+    own = pl.BlockSpec((width, tile), lambda i: (0, jnp.minimum(i, steps - 1)))
+    other = pl.BlockSpec((width, tile), lambda i: (0, jnp.maximum(i - steps, 0)))
+    return pl.pallas_call(
+        functools.partial(hidden_kernel, unit),
+        grid=(2 * steps,),
+        in_specs=[pl.BlockSpec(array.shape, lambda i: (0, 0)) for array in (*held, *got)]
+        + [own, own, other, other],
+        out_specs=pl.BlockSpec((count, tile), lambda i: (0, i)),
+        out_shape=jax.ShapeDtypeStruct((count, 2 * units), jnp.bfloat16),
+        scratch_shapes=[pltpu.VMEM((count, width), jnp.bfloat16)],
+        compiler_params=pltpu.CompilerParams(vmem_limit_bytes=48 * MIB),
+        cost_estimate=pl.CostEstimate(
+            flops=8 * count * width * units,
+            bytes_accessed=2 * (count * width + 4 * width * units + 2 * count * units),
+            transcendentals=2 * count * units,
+        ),
+        name="expert_hidden",
+    )(*held, *got, gate, up, gate_other, up_other)
+
+
+def output_kernel(unit, quarter, scale_ref, hidden_ref, down_ref, down_other_ref, keep_ref, send_ref):
+    units = down_ref.shape[0]
+    places = hidden_ref.shape[0] // unit
+    for out_ref, first in ((send_ref, places // 2), (keep_ref, 0)):
+        slots = [slot_of(first + at, quarter, True) for at in range(places // 2)]
+        rows = [slice(slot * unit, (slot + 1) * unit) for slot in slots]
+        hidden = jnp.concatenate([hidden_ref[row] for row in rows], axis=0)
+        scale = jnp.concatenate([scale_ref[row] for row in rows], axis=0)
+        out = jnp.dot(hidden[:, :units], down_ref[...], preferred_element_type=jnp.float32)
+        out += jnp.dot(hidden[:, units:], down_other_ref[...], preferred_element_type=jnp.float32)
+        out_ref[...] = out * scale
+
+
+def expert_output(unit, quarter, scale, hidden, down, down_other):
+    units, width = down.shape
+    tile = width // len(LINKS)
+    count = hidden.shape[0]
+    half = jax.ShapeDtypeStruct((count // 2, tile), jnp.float32)
+    return pl.pallas_call(
+        functools.partial(output_kernel, unit, quarter),
+        grid=(1,),
+        in_specs=[
+            pl.BlockSpec((count, 1), lambda i: (0, 0)),
+            pl.BlockSpec((count, 2 * units), lambda i: (0, 0)),
+            pl.BlockSpec((units, tile), lambda i: (0, quarter)),
+            pl.BlockSpec((units, tile), lambda i: (0, quarter)),
+        ],
+        out_specs=[pl.BlockSpec((count // 2, tile), lambda i: (0, 0))] * 2,
+        out_shape=[half] * 2,
+        compiler_params=pltpu.CompilerParams(vmem_limit_bytes=32 * MIB),
+        cost_estimate=pl.CostEstimate(
+            flops=4 * count * tile * units,
+            bytes_accessed=4 * tile * units + 4 * count * (tile + units),
+            transcendentals=0,
+        ),
+        name="expert_output",
+    )(scale, hidden, down, down_other)
+
+
+def halved(keep, got):
+    rows, width = keep.shape
+    half = jax.ShapeDtypeStruct((rows // 2, width), keep.dtype)
+
+    def kernel(keep_ref, got_ref, first_ref, second_ref):
+        second_ref[...] = keep_ref[rows // 2 :] + got_ref[rows // 2 :]
+        first_ref[...] = keep_ref[: rows // 2] + got_ref[: rows // 2]
+
+    return whole_call(kernel, [keep, got], [half, half], "halved")
+
+
+def finished(keep, got):
+    count = len(keep)
+    rows, width = keep[0].shape
+
+    def kernel(*refs):
+        for q in range(count):
+            total = refs[q][...] + refs[count + q][...]
+            refs[2 * count][:, q * width : (q + 1) * width] = total.astype(jnp.bfloat16)
+
+    shape = jax.ShapeDtypeStruct((rows, count * width), jnp.bfloat16)
+    return whole_call(kernel, [*keep, *got], [shape], "finished")[0]
+
+
+def cube_experts(unit, gathered, share, weights, others):
+    count = len(LINKS)
+    peers = lax.axis_size("ep")
+    gate, up, down = weights
+    gate_other, up_other, down_other = others
+    steps = []
+    for slot in range(peers // 2):
+        step = 0
+        for link in range(count):
+            step ^= LINKS[link] * ((slot >> link) & 1)
+        steps.append(2 * step)
+    source = jnp.bitwise_xor(lax.axis_index("ep"), jnp.array(steps, jnp.int32))
+    picks = source[:, None] == jnp.arange(peers, dtype=jnp.int32)[None, :]
+    scale = jnp.sum(jnp.where(picks[:, :, None], share[None, :, :], 0.0), axis=1)
+    scale = scale.reshape(peers // 2 * unit, 1)
+
+    hidden = expert_hidden(unit, *gathered, gate, up, gate_other, up_other)
+    keep, got = [], []
+    for q in range(count):
+        mine, send = expert_output(unit, q, scale, hidden, down, down_other)
+        keep.append(mine)
+        got.append(across(send, q))
+    for phase in range(1, count):
+        for q in range(count):
+            keep[q], send = halved(keep[q], got[q])
+            got[q] = across(send, (q + phase) % count)
+    return finished(keep, got)
 
 
 def per_device(
@@ -67,40 +310,42 @@
     latent = prefill_latent.shape[3]
     tok_rows, top_k = expert_ids.shape
 
-    rows = lax.all_gather(tokens, "ep", axis=0, tiled=True)
-
     owner = block_owner.reshape(blocks)
     same = owner[:, None] == owner[None, :]
     earlier = jnp.arange(blocks)[None, :] < jnp.arange(blocks)[:, None]
     order_in = jnp.sum(jnp.logical_and(same, earlier).astype(jnp.int32), axis=1)
     target = owner * 2 + order_in
     chosen = jnp.arange(2 * peers, dtype=jnp.int32)[:, None] == target[None, :]
-    filled = jnp.sum(chosen.astype(jnp.float32), axis=1)
-    expert_of = jnp.arange(peers, dtype=jnp.int32) // 2
-    named = expert_ids[None, :, :] == expert_of[:, None, None]
-    share = jnp.sum(jnp.where(named, route_weight[None, :, :], 0.0), axis=2)
-    small = lax.all_to_all(
-        jnp.concatenate([share, filled.reshape(peers, 2)], axis=1),
-        "ep",
-        split_axis=0,
-        concat_axis=0,
-        tiled=True,
-    )
-    scale_rows = small[:, :tok_rows].reshape(peers * tok_rows)
-    present = small[:, tok_rows:].reshape(peers * 2)
-
     packed = jnp.dot(
         chosen.astype(jnp.bfloat16),
         prefill_latent.reshape(blocks, block_len * latent),
         preferred_element_type=jnp.float32,
     ).astype(jnp.bfloat16)
-    arrived = lax.all_to_all(
-        packed.reshape(peers, 2 * block_len, latent),
-        "ep",
-        split_axis=0,
-        concat_axis=0,
-        tiled=True,
-    )
+
+    expert_of = jnp.arange(peers, dtype=jnp.int32) // 2
+    named = expert_ids[None, :, :] == expert_of[:, None, None]
+    share = jnp.sum(jnp.where(named, route_weight[None, :, :], 0.0), axis=2)
+    high = lax.reduce_precision(share, 8, 7)
+    middle = lax.reduce_precision(share - high, 8, 7)
+    low = share - high - middle
+    filled = jnp.sum(chosen.astype(jnp.float32), axis=1).reshape(peers, 1, 2)
+    side = jnp.zeros((peers, 2 * block_len, max(tok_rows, 2)), jnp.float32)
+    side = side.at[:, :3, :tok_rows].set(jnp.stack([high, middle, low], axis=1))
+    side = side.at[:, 3:4, :2].set(filled)
+    leaving = jnp.concatenate(
+        [packed.reshape(peers, 2 * block_len, latent), side.astype(jnp.bfloat16)], axis=2
+    )
+    cube = peers == 2 << len(LINKS) and lax.axis_size("tp") == 1
+    weights = (gate_weight[0], up_weight[0], down_weight[0])
+    if cube:
+        others = [swap_cores(weight) for weight in weights]
+        gathered = gather_cube(tokens, others)
+        leaving = hold_back(leaving, gathered[0][0])
+    arrived = lax.all_to_all(leaving, "ep", split_axis=0, concat_axis=0, tiled=True)
+    side_in = arrived[:, :, latent:].astype(jnp.float32)
+    share_in = side_in[:, 0, :tok_rows] + side_in[:, 1, :tok_rows] + side_in[:, 2, :tok_rows]
+    present = side_in[:, 3, :2].reshape(peers * 2)
+    arrived = arrived[:, :, :latent]
     shard_len = latent_cache.shape[1]
     positions = lax.axis_index("tp") * shard_len + jnp.arange(shard_len, dtype=jnp.int32)
     keys = jnp.concatenate(
@@ -111,16 +356,10 @@
     peak, total, mixed = combined_all((peak, total, mixed), "tp", join_parts)
     attn_out = (mixed / total[:, None]).astype(jnp.bfloat16)[None]
 
-    gate = jnp.dot(rows, gate_weight[0], preferred_element_type=jnp.float32)
-    upper = jnp.dot(rows, up_weight[0], preferred_element_type=jnp.float32)
-    hidden = (jax.nn.silu(gate) * upper).astype(jnp.bfloat16)
-    if lax.axis_size("tp") > 1:
-        hidden = lax.all_gather(hidden, "tp", axis=1, tiled=True)
-    partial_out = (
-        jnp.dot(hidden, down_weight[0], preferred_element_type=jnp.float32) * scale_rows[:, None]
-    )
-    combined = lax.psum_scatter(partial_out, "ep", scatter_dimension=0, tiled=True)
-    moe_out = combined.astype(jnp.bfloat16)
+    if cube:
+        moe_out = cube_experts(tok_rows, gathered, share_in, weights, others)
+    else:
+        moe_out = ring_experts(tokens, share_in, gate_weight, up_weight, down_weight)
     return (attn_out, moe_out)
 
 

time: 284 us -> 170 us (0.60)
  waiting for transfers between devices: 218 us -> 60.4 us
  starting transfers between devices: 3.23 us -> 57 us
  Pallas kernels: 0 us -> 30.1 us
  matrix products: 25.4 us -> 2.63 us
  blocking collectives: 14.2 us -> 0 us
  between operations: 14.8 us -> 1.7 us
  local copies, waits for them, and re-layouts: 2.83 us -> 12.5 us
    reduce_scatter x1 -> x0, waiting for transfers between devices: 138 us -> none  [per_device(): lax.psum_scatter(partial_out, 'ep', scatter_dimension=0, tiled=True)]
    all_gather x1 -> x0, waiting for transfers between devices: 62.1 us -> none  [per_device(): rows = lax.all_gather(tokens, 'ep', axis=0, tiled=True)]
    ppermute x0 -> x35, waiting for transfers between devices: none -> 60.4 us  [the longest x32 60.3 us: across(): lax.ppermute(value, 'ep', [(i, i ^ 2 * LINKS[link]) for i in range(peers)])]
    ppermute x0 -> x35, starting transfers between devices: none -> 53.5 us  [the longest x32 52.5 us: across(): lax.ppermute(value, 'ep', [(i, i ^ 2 * LINKS[link]) for i in range(peers)])]
    pallas_call x0 -> x22, Pallas kernels: none -> 30.1 us  [the longest x1 12.8 us: expert_hidden(): pl.pallas_call(functools.partial(hidden_kernel, unit), grid=(2 * steps,),...]
    dot_general x2 -> x0, matrix products: 22.8 us -> none  [the longest x1 15.5 us: per_device(): jnp.dot(hidden, down_weight[0], preferred_element_type=jnp.float32)]
    all_to_all x1, waiting for transfers between devices: 17 us -> 0.01 us  [per_device(): lax.all_to_all(leaving, 'ep', split_axis=0, concat_axis=0, tiled=True)]
    all_to_all x1 -> x0, blocking collectives: 14.2 us -> none  [per_device(): lax.all_to_all(jnp.concatenate([share, filled.reshape(peers, 2)], axis=1)...]
  transfers between devices with their start and end apart: 3 -> 36, of which waited for: 3 -> 15; matrix products, arithmetic and copies ran while one was open for 3% -> 9% of each run, Pallas kernels for 0% -> 15%
where the time goes in v5:
time: 170 us
  waiting for transfers between devices  60.4 us (36%)
  starting transfers between devices  57 us (34%)
  Pallas kernels  30.1 us (18%)
  local copies, waits for them, and re-layouts  12.5 us (7%)
  other arithmetic  5.39 us (3%)
  matrix products  2.63 us (2%)
  between operations  1.7 us (1%)
    ppermute x32, waiting for transfers between devices, across(): lax.ppermute(value, 'ep', [(i, i ^ 2 * LINKS[link]) for i in range(peers)])  60.3 us
    ppermute x32, starting transfers between devices, across(): lax.ppermute(value, 'ep', [(i, i ^ 2 * LINKS[link]) for i in range(peers)])  52.5 us
    pallas_call x1, Pallas kernels, expert_hidden(): pl.pallas_call(functools.partial(hidden_kernel, unit), grid=(2 * steps,),...  12.8 us
    pallas_call x4, Pallas kernels, expert_output(): pl.pallas_call(functools.partial(output_kernel, unit, quarter), grid=(1,)...  10 us
    pallas_call x17, Pallas kernels, whole_call(): pl.pallas_call(body, in_specs=[pl.BlockSpec(memory_space=pltpu.VMEM)] * g...  7.29 us
    unnamed x20, local copies, waits for them, and re-layouts  4.48 us
    reshape x2, local copies, waits for them, and re-layouts, per_device(): arrived.reshape(peers * 2 * block_len, latent)  3.6 us
    all_to_all x1, starting transfers between devices, per_device(): lax.all_to_all(leaving, 'ep', split_axis=0, concat_axis=0, tiled=True)  3.48 us
  transfers between devices with their start and end apart: 36, of which 15 were waited for; matrix products, arithmetic and copies ran while one was open for 9% of the time, Pallas kernels for 15%

profile of v5, /device:TPU:0, one launch (start us, length us, event | category | flops | bytes accessed | tf_op | source)
XLA Modules:
  0.0 169.7 jit_solution(8349120519316305255)
XLA Ops:
  2.6 2.6 %collective-permute-start = (bf16[32,896]{1,0:T(8,128)(2,1)S(1)}, bf16[32,896]{1,0:T(8,128)(2,1)S(1)}, u32[]{:S(2)}, u32[]{:S(2)}) collective-permute-start(bf16[32,896]{1,0:T(8,128)(2,1)S(1)} %get-tuple-element.116.refs_0_), channel_id=1, source_target_pairs={{0,2},{1,3},{2,0},{3,1},{4,6},{5,7},{6,4},{7,5},{8,10},{9,11},{10,... | collective-permute-start | bytes 172040 | tf_op jit(solution)/shard_map/ppermute | solution.py:74
  9.5 1.6 collective-permute-start.2
  11.1 2.5 %collective-permute-start.3 = (bf16[32,896]{1,0:T(8,128)(2,1)S(1)}, bf16[32,896]{1,0:T(8,128)(2,1)S(1)}, u32[]{:S(2)}, u32[]{:S(2)}) collective-permute-start(bf16[32,896]{1,0:T(8,128)(2,1)S(1)} %get-tuple-element.114.refs_3_), channel_id=1, source_target_pairs={{0,24},{1,25},{2,26},{3,27},{4,28},{5,29},{6,30},{7,31},{8,16},{9,... | collective-permute-start | bytes 172040 | tf_op jit(solution)/shard_map/ppermute | solution.py:74
  13.9 3.1 %collective-permute-done.3.refs_7_ = bf16[32,896]{1,0:T(8,128)(2,1)S(1)} collective-permute-done((bf16[32,896]{1,0:T(8,128)(2,1)S(1)}, bf16[32,896]{1,0:T(8,128)(2,1)S(1)}, u32[]{:S(2)}, u32[]{:S(2)}) %collective-permute-start.3) | collective-permute-done | bytes 57376 | tf_op jit(solution)/shard_map/ppermute | solution.py:74
  19.0 3.0 %collective-permute-done.4.refs_4_ = bf16[64,896]{1,0:T(8,128)(2,1)S(1)} collective-permute-done((bf16[64,896]{1,0:T(8,128)(2,1)S(1)}, bf16[64,896]{1,0:T(8,128)(2,1)S(1)}, u32[]{:S(2)}, u32[]{:S(2)}) %collective-permute-start.4) | collective-permute-done | bytes 114720 | tf_op jit(solution)/shard_map/ppermute | solution.py:74
  22.0 2.5 %collective-permute-start.6 = (bf16[64,896]{1,0:T(8,128)(2,1)S(1)}, bf16[64,896]{1,0:T(8,128)(2,1)S(1)}, u32[]{:S(2)}, u32[]{:S(2)}) collective-permute-start(bf16[64,896]{1,0:T(8,128)(2,1)S(1)} %get-tuple-element.72.refs_2_), channel_id=1, source_target_pairs={{0,24},{1,25},{2,26},{3,27},{4,28},{5,29},{6,30},{7,31},{8,16},{9,... | collective-permute-start | bytes 344072 | tf_op jit(solution)/shard_map/ppermute | solution.py:74
  25.1 3.8 %collective-permute-done.6.refs_6_ = bf16[64,896]{1,0:T(8,128)(2,1)S(1)} collective-permute-done((bf16[64,896]{1,0:T(8,128)(2,1)S(1)}, bf16[64,896]{1,0:T(8,128)(2,1)S(1)}, u32[]{:S(2)}, u32[]{:S(2)}) %collective-permute-start.6) | collective-permute-done | bytes 114720 | tf_op jit(solution)/shard_map/ppermute | solution.py:74
  29.4 2.8 %collective-permute-start.12 = (bf16[128,896]{1,0:T(8,128)(2,1)S(1)}, bf16[128,896]{1,0:T(8,128)(2,1)S(1)}, u32[]{:S(2)}, u32[]{:S(2)}) collective-permute-start(bf16[128,896]{1,0:T(8,128)(2,1)S(1)} %get-tuple-element.75.refs_1_), channel_id=1, source_target_pairs={{0,24},{1,25},{2,26},{3,27},{4,28},{5,29},{6,30},{7,31},{8,16},{9,... | collective-permute-start | bytes 688136 | tf_op jit(solution)/shard_map/ppermute | solution.py:74
  36.0 2.6 %collective-permute-done.12.refs_5_ = bf16[128,896]{1,0:T(8,128)(2,1)S(1)} collective-permute-done((bf16[128,896]{1,0:T(8,128)(2,1)S(1)}, bf16[128,896]{1,0:T(8,128)(2,1)S(1)}, u32[]{:S(2)}, u32[]{:S(2)}) %collective-permute-start.12) | collective-permute-done | bytes 229408 | tf_op jit(solution)/shard_map/ppermute | solution.py:74
  39.7 2.6 %collective-permute-start.15 = (bf16[256,896]{1,0:T(8,128)(2,1)S(1)}, bf16[256,896]{1,0:T(8,128)(2,1)S(1)}, u32[]{:S(2)}, u32[]{:S(2)}) collective-permute-start(bf16[256,896]{1,0:T(8,128)(2,1)S(1)} %get-tuple-element.78.refs_1_.refs_0_), channel_id=1, source_target_pairs={{0,24},{1,25},{2,26},{3,27},{4,28},{5,29},{6,30},{7,31},{8,16},{9,... | collective-permute-start | bytes 1376264 | tf_op jit(solution)/shard_map/ppermute | solution.py:74
  43.9 7.8 %collective-permute-start.18 = (bf16[256,896]{1,0:T(8,128)(2,1)}, bf16[256,896]{1,0:T(8,128)(2,1)}, u32[]{:S(2)}, u32[]{:S(2)}) collective-permute-start(bf16[256,896]{1,0:T(8,128)(2,1)} %get-tuple-element.81.refs_3_), channel_id=1, source_target_pairs={{0,8},{1,9},{2,10},{3,11},{4,12},{5,13},{6,14},{7,15},{8,0},{9,1},... | collective-permute-start | bytes 1376264 | tf_op jit(solution)/shard_map/ppermute | solution.py:74
  53.6 3.5 %all-to-all-start = ((bf16[32,8,608]{2,1,0:T(8,128)(2,1)}), bf16[32,8,608]{2,1,0:T(8,128)(2,1)}, u32[]{:S(2)}, u32[]{:S(2)}) async-start(bf16[32,8,608]{2,1,0:T(8,128)(2,1)} %hold_back.1), calls=%async_computation | async-start | bytes 655360 | tf_op jit(solution)/shard_map/all_to_all | solution.py:344
  59.7 12.8 %expert_hidden.1.hidden_ref = bf16[512,1024]{1,0:T(8,128)(2,1)S(1)} custom-call(bf16[256,896]{1,0:T(8,128)(2,1)S(1)} %get-tuple-element.78.refs_1_.refs_0_, bf16[256,896]{1,0:T(8,128)(2,1)S(1)} %get-tuple-element.79.refs_1_, bf16[256,896]{1,0:T(8,128)(2,1)S(1)} %get-tuple-element.80.refs_2_, bf16[256,896]{1,0:T(8,128)(2,1)} %get-tuple-element.81.refs_3_, ...), custom_call_target="tpu_custom_call" | custom-call | flops 7516192768 | bytes 19398656 | tf_op jit(solution)/shard_map/expert_hidden/pallas_call | solution.py:184
  74.5 2.0 %copy-done.1 = bf16[1,512,3584]{2,1,0:T(8,128)(2,1)S(1)} copy-done((bf16[1,512,3584]{2,1,0:T(8,128)(2,1)S(1)}, bf16[1,512,3584]{2,1,0:T(8,128)(2,1)}, u32[]{:S(2)}) %copy-start.1) | copy-done | bytes 3670040
  76.5 2.5 %expert_output.7 = (f32[256,896]{1,0:T(8,128)S(1)}, f32[256,896]{1,0:T(8,128)S(1)}) custom-call(f32[512,1]{1,0:T(8,128)S(1)} %reshape.191.scale_ref, bf16[512,1024]{1,0:T(8,128)(2,1)S(1)} %expert_hidden.1.hidden_ref, bf16[512,3584]{1,0:T(8,128)(2,1)S(1)} %bitcast.22, bf16[512,3584]{1,0:T(8,128)(2,1)} %collective-permute-done.10.refs_10_.down_other_ref), custom_call_target="tpu_custom_call" | custom-call | flops 939524096 | bytes 4718592 | tf_op jit(solution)/shard_map/expert_output/pallas_call | solution.py:220
  79.0 2.9 %collective-permute-start.28 = (f32[256,896]{1,0:T(8,128)S(1)}, f32[256,896]{1,0:T(8,128)S(1)}, u32[]{:S(2)}, u32[]{:S(2)}) collective-permute-start(f32[256,896]{1,0:T(8,128)S(1)} %get-tuple-element.104), channel_id=1, source_target_pairs={{0,24},{1,25},{2,26},{3,27},{4,28},{5,29},{6,30},{7,31},{8,16},{9,... | collective-permute-start | bytes 2752520 | tf_op jit(solution)/shard_map/ppermute | solution.py:74
  81.9 2.5 %expert_output.6 = (f32[256,896]{1,0:T(8,128)S(1)}, f32[256,896]{1,0:T(8,128)S(1)}) custom-call(f32[512,1]{1,0:T(8,128)S(1)} %reshape.191.scale_ref, bf16[512,1024]{1,0:T(8,128)(2,1)S(1)} %expert_hidden.1.hidden_ref, bf16[512,3584]{1,0:T(8,128)(2,1)S(1)} %bitcast.23, bf16[512,3584]{1,0:T(8,128)(2,1)} %collective-permute-done.10.refs_10_.down_other_ref), custom_call_target="tpu_custom_call" | custom-call | flops 939524096 | bytes 4718592 | tf_op jit(solution)/shard_map/expert_output/pallas_call | solution.py:220
  85.2 2.5 %expert_output.5 = (f32[256,896]{1,0:T(8,128)S(1)}, f32[256,896]{1,0:T(8,128)S(1)}) custom-call(f32[512,1]{1,0:T(8,128)S(1)} %reshape.191.scale_ref, bf16[512,1024]{1,0:T(8,128)(2,1)S(1)} %expert_hidden.1.hidden_ref, bf16[512,3584]{1,0:T(8,128)(2,1)S(1)} %bitcast.24, bf16[512,3584]{1,0:T(8,128)(2,1)} %collective-permute-done.10.refs_10_.down_other_ref), custom_call_target="tpu_custom_call" | custom-call | flops 939524096 | bytes 4718592 | tf_op jit(solution)/shard_map/expert_output/pallas_call | solution.py:220
  89.1 2.5 %expert_output.4 = (f32[256,896]{1,0:T(8,128)S(1)}, f32[256,896]{1,0:T(8,128)S(1)}) custom-call(f32[512,1]{1,0:T(8,128)S(1)} %reshape.191.scale_ref, bf16[512,1024]{1,0:T(8,128)(2,1)S(1)} %expert_hidden.1.hidden_ref, bf16[512,3584]{1,0:T(8,128)(2,1)S(1)} %bitcast.25, bf16[512,3584]{1,0:T(8,128)(2,1)} %collective-permute-done.10.refs_10_.down_other_ref), custom_call_target="tpu_custom_call" | custom-call | flops 939524096 | bytes 4718592 | tf_op jit(solution)/shard_map/expert_output/pallas_call | solution.py:220
  93.1 11.1 %collective-permute-done.28.refs_1_ = f32[256,896]{1,0:T(8,128)S(1)} collective-permute-done((f32[256,896]{1,0:T(8,128)S(1)}, f32[256,896]{1,0:T(8,128)S(1)}, u32[]{:S(2)}, u32[]{:S(2)}) %collective-permute-start.28) | collective-permute-done | bytes 917536 | tf_op jit(solution)/shard_map/ppermute | solution.py:74
  106.4 15.8 %collective-permute-done.25.refs_1_ = f32[256,896]{1,0:T(8,128)S(1)} collective-permute-done((f32[256,896]{1,0:T(8,128)S(1)}, f32[256,896]{1,0:T(8,128)S(1)}, u32[]{:S(2)}, u32[]{:S(2)}) %collective-permute-start.25) | collective-permute-done | bytes 917536 | tf_op jit(solution)/shard_map/ppermute | solution.py:74
  123.0 3.5 %collective-permute-start.26 = (f32[128,896]{1,0:T(8,128)}, f32[128,896]{1,0:T(8,128)S(1)}, u32[]{:S(2)}, u32[]{:S(2)}) collective-permute-start(f32[128,896]{1,0:T(8,128)} %get-tuple-element.99), channel_id=1, source_target_pairs={{0,24},{1,25},{2,26},{3,27},{4,28},{5,29},{6,30},{7,31},{8,16},{9,... | collective-permute-start | bytes 1376264 | tf_op jit(solution)/shard_map/ppermute | solution.py:74
  129.8 1.8 %slice_bitcast_fusion = bf16[256,576]{1,0:T(8,128)(2,1)} fusion(bf16[32,8,608]{2,1,0:T(8,128)(2,1)} %all-to-all-done), kind=kLoop, calls=%fused_computation.16 | loop fusion | bytes 589824 | tf_op jit(solution)/shard_map/reshape | solution.py:352
  131.6 1.9 %copy.33 = bf16[256,576]{0,1:T(8,128)(2,1)} copy(bf16[256,576]{1,0:T(8,128)(2,1)} %slice_bitcast_fusion) | data formatting | bytes 589824 | tf_op jit(solution)/shard_map/reshape | solution.py:352
  135.4 3.1 %collective-permute-done.26.refs_1_ = f32[128,896]{1,0:T(8,128)S(1)} collective-permute-done((f32[128,896]{1,0:T(8,128)}, f32[128,896]{1,0:T(8,128)S(1)}, u32[]{:S(2)}, u32[]{:S(2)}) %collective-permute-start.26) | collective-permute-done | bytes 458784 | tf_op jit(solution)/shard_map/ppermute | solution.py:74
  140.2 7.2 %collective-permute-done.23.refs_1_ = f32[128,896]{1,0:T(8,128)S(1)} collective-permute-done((f32[128,896]{1,0:T(8,128)}, f32[128,896]{1,0:T(8,128)S(1)}, u32[]{:S(2)}, u32[]{:S(2)}) %collective-permute-start.23) | collective-permute-done | bytes 458784 | tf_op jit(solution)/shard_map/ppermute | solution.py:74
  147.4 2.6 %collective-permute-start.24 = (f32[64,896]{1,0:T(8,128)S(1)}, f32[64,896]{1,0:T(8,128)S(1)}, u32[]{:S(2)}, u32[]{:S(2)}) collective-permute-start(f32[64,896]{1,0:T(8,128)S(1)} %get-tuple-element.94), channel_id=1, source_target_pairs={{0,24},{1,25},{2,26},{3,27},{4,28},{5,29},{6,30},{7,31},{8,16},{9,... | collective-permute-start | bytes 688136 | tf_op jit(solution)/shard_map/ppermute | solution.py:74
  152.2 2.1 %collective-permute-start.34 = (f32[32,896]{1,0:T(8,128)S(1)}, f32[32,896]{1,0:T(8,128)S(1)}, u32[]{:S(2)}, u32[]{:S(2)}) collective-permute-start(f32[32,896]{1,0:T(8,128)S(1)} %get-tuple-element.113), channel_id=1, source_target_pairs={{0,8},{1,9},{2,10},{3,11},{4,12},{5,13},{6,14},{7,15},{8,0},{9,1},... | collective-permute-start | bytes 344072 | tf_op jit(solution)/shard_map/ppermute | solution.py:74
  154.3 1.6 collective-permute-start.33
  156.0 1.9 %collective-permute-done.24.refs_1_ = f32[64,896]{1,0:T(8,128)S(1)} collective-permute-done((f32[64,896]{1,0:T(8,128)S(1)}, f32[64,896]{1,0:T(8,128)S(1)}, u32[]{:S(2)}, u32[]{:S(2)}) %collective-permute-start.24) | collective-permute-done | bytes 229408 | tf_op jit(solution)/shard_map/ppermute | solution.py:74
  159.5 2.4 %collective-permute-done.21.refs_1_ = f32[64,896]{1,0:T(8,128)S(1)} collective-permute-done((f32[64,896]{1,0:T(8,128)S(1)}, f32[64,896]{1,0:T(8,128)S(1)}, u32[]{:S(2)}, u32[]{:S(2)}) %collective-permute-start.21) | collective-permute-done | bytes 229408 | tf_op jit(solution)/shard_map/ppermute | solution.py:74
  165.1 3.8 %collective-permute-done.31.refs_4_ = f32[32,896]{1,0:T(8,128)S(1)} collective-permute-done((f32[32,896]{1,0:T(8,128)S(1)}, f32[32,896]{1,0:T(8,128)S(1)}, u32[]{:S(2)}, u32[]{:S(2)}) %collective-permute-start.31) | collective-permute-done | bytes 114720 | tf_op jit(solution)/shard_map/ppermute | solution.py:74
  (113 shorter events, 43.2 us)
Async XLA Ops:
  0.7 28.6 %collective-permute-start.10 = (bf16[512,3584]{1,0:T(8,128)(2,1)}, bf16[512,3584]{1,0:T(8,128)(2,1)}, u32[]{:S(2)}, u32[]{:S(2)}) collective-permute-start(bf16[512,3584]{1,0:T(8,128)(2,1)} %bitcast.21), channel_id=1, source_target_pairs={{0,1},{1,0},{2,3},{3,2},{4,5},{5,4},{6,7},{7,6},{8,9},{9,8},{10,11... | collective-permute-start | bytes 11010056 | tf_op jit(solution)/shard_map/ppermute | solution.py:78
  1.2 28.1 %collective-permute-start.8 = (bf16[3584,512]{1,0:T(8,128)(2,1)}, bf16[3584,512]{1,0:T(8,128)(2,1)}, u32[]{:S(2)}, u32[]{:S(2)}) collective-permute-start(bf16[3584,512]{1,0:T(8,128)(2,1)} %bitcast.29), channel_id=1, source_target_pairs={{0,1},{1,0},{2,3},{3,2},{4,5},{5,4},{6,7},{7,6},{8,9},{9,8},{10,11... | collective-permute-start | bytes 11010056 | tf_op jit(solution)/shard_map/ppermute | solution.py:78
  1.3 28.0 %collective-permute-start.9 = (bf16[3584,512]{1,0:T(8,128)(2,1)}, bf16[3584,512]{1,0:T(8,128)(2,1)}, u32[]{:S(2)}, u32[]{:S(2)}) collective-permute-start(bf16[3584,512]{1,0:T(8,128)(2,1)} %bitcast.31), channel_id=1, source_target_pairs={{0,1},{1,0},{2,3},{3,2},{4,5},{5,4},{6,7},{7,6},{8,9},{9,8},{10,11... | collective-permute-start | bytes 11010056 | tf_op jit(solution)/shard_map/ppermute | solution.py:78
  2.6 6.8 %collective-permute-start = (bf16[32,896]{1,0:T(8,128)(2,1)S(1)}, bf16[32,896]{1,0:T(8,128)(2,1)S(1)}, u32[]{:S(2)}, u32[]{:S(2)}) collective-permute-start(bf16[32,896]{1,0:T(8,128)(2,1)S(1)} %get-tuple-element.116.refs_0_), channel_id=1, source_target_pairs={{0,2},{1,3},{2,0},{3,1},{4,6},{5,7},{6,4},{7,5},{8,10},{9,11},{10,... | collective-permute-start | bytes 172040 | tf_op jit(solution)/shard_map/ppermute | solution.py:74
  11.1 6.0 %collective-permute-start.3 = (bf16[32,896]{1,0:T(8,128)(2,1)S(1)}, bf16[32,896]{1,0:T(8,128)(2,1)S(1)}, u32[]{:S(2)}, u32[]{:S(2)}) collective-permute-start(bf16[32,896]{1,0:T(8,128)(2,1)S(1)} %get-tuple-element.114.refs_3_), channel_id=1, source_target_pairs={{0,24},{1,25},{2,26},{3,27},{4,28},{5,29},{6,30},{7,31},{8,16},{9,... | collective-permute-start | bytes 172040 | tf_op jit(solution)/shard_map/ppermute | solution.py:74
  17.7 6.8 %collective-permute-start.5 = (bf16[64,896]{1,0:T(8,128)(2,1)S(1)}, bf16[64,896]{1,0:T(8,128)(2,1)S(1)}, u32[]{:S(2)}, u32[]{:S(2)}) collective-permute-start(bf16[64,896]{1,0:T(8,128)(2,1)S(1)} %get-tuple-element.71.refs_1_), channel_id=1, source_target_pairs={{0,8},{1,9},{2,10},{3,11},{4,12},{5,13},{6,14},{7,15},{8,0},{9,1},... | collective-permute-start | bytes 344072 | tf_op jit(solution)/shard_map/ppermute | solution.py:74
  22.0 6.9 %collective-permute-start.6 = (bf16[64,896]{1,0:T(8,128)(2,1)S(1)}, bf16[64,896]{1,0:T(8,128)(2,1)S(1)}, u32[]{:S(2)}, u32[]{:S(2)}) collective-permute-start(bf16[64,896]{1,0:T(8,128)(2,1)S(1)} %get-tuple-element.72.refs_2_), channel_id=1, source_target_pairs={{0,24},{1,25},{2,26},{3,27},{4,28},{5,29},{6,30},{7,31},{8,16},{9,... | collective-permute-start | bytes 344072 | tf_op jit(solution)/shard_map/ppermute | solution.py:74
  29.4 6.7 %collective-permute-start.11 = (bf16[128,896]{1,0:T(8,128)(2,1)S(1)}, bf16[128,896]{1,0:T(8,128)(2,1)S(1)}, u32[]{:S(2)}, u32[]{:S(2)}) collective-permute-start(bf16[128,896]{1,0:T(8,128)(2,1)S(1)} %get-tuple-element.74.refs_0_), channel_id=1, source_target_pairs={{0,8},{1,9},{2,10},{3,11},{4,12},{5,13},{6,14},{7,15},{8,0},{9,1},... | collective-permute-start | bytes 688136 | tf_op jit(solution)/shard_map/ppermute | solution.py:74
  29.4 9.2 %collective-permute-start.12 = (bf16[128,896]{1,0:T(8,128)(2,1)S(1)}, bf16[128,896]{1,0:T(8,128)(2,1)S(1)}, u32[]{:S(2)}, u32[]{:S(2)}) collective-permute-start(bf16[128,896]{1,0:T(8,128)(2,1)S(1)} %get-tuple-element.75.refs_1_), channel_id=1, source_target_pairs={{0,24},{1,25},{2,26},{3,27},{4,28},{5,29},{6,30},{7,31},{8,16},{9,... | collective-permute-start | bytes 688136 | tf_op jit(solution)/shard_map/ppermute | solution.py:74
  32.2 6.5 %collective-permute-start.13 = (bf16[128,896]{1,0:T(8,128)(2,1)S(1)}, bf16[128,896]{1,0:T(8,128)(2,1)S(1)}, u32[]{:S(2)}, u32[]{:S(2)}) collective-permute-start(bf16[128,896]{1,0:T(8,128)(2,1)S(1)} %get-tuple-element.76.refs_2_), channel_id=1, source_target_pairs={{0,2},{1,3},{2,0},{3,1},{4,6},{5,7},{6,4},{7,5},{8,10},{9,11},{10,... | collective-permute-start | bytes 688136 | tf_op jit(solution)/shard_map/ppermute | solution.py:74
  32.7 6.0 %collective-permute-start.14 = (bf16[128,896]{1,0:T(8,128)(2,1)S(1)}, bf16[128,896]{1,0:T(8,128)(2,1)S(1)}, u32[]{:S(2)}, u32[]{:S(2)}) collective-permute-start(bf16[128,896]{1,0:T(8,128)(2,1)S(1)} %get-tuple-element.77.refs_3_), channel_id=1, source_target_pairs={{0,4},{1,5},{2,6},{3,7},{4,0},{5,1},{6,2},{7,3},{8,12},{9,13},{10,... | collective-permute-start | bytes 688136 | tf_op jit(solution)/shard_map/ppermute | solution.py:74
  39.7 17.4 %collective-permute-start.15 = (bf16[256,896]{1,0:T(8,128)(2,1)S(1)}, bf16[256,896]{1,0:T(8,128)(2,1)S(1)}, u32[]{:S(2)}, u32[]{:S(2)}) collective-permute-start(bf16[256,896]{1,0:T(8,128)(2,1)S(1)} %get-tuple-element.78.refs_1_.refs_0_), channel_id=1, source_target_pairs={{0,24},{1,25},{2,26},{3,27},{4,28},{5,29},{6,30},{7,31},{8,16},{9,... | collective-permute-start | bytes 1376264 | tf_op jit(solution)/shard_map/ppermute | solution.py:74
  42.3 14.8 %collective-permute-start.16 = (bf16[256,896]{1,0:T(8,128)(2,1)S(1)}, bf16[256,896]{1,0:T(8,128)(2,1)S(1)}, u32[]{:S(2)}, u32[]{:S(2)}) collective-permute-start(bf16[256,896]{1,0:T(8,128)(2,1)S(1)} %get-tuple-element.79.refs_1_), channel_id=1, source_target_pairs={{0,2},{1,3},{2,0},{3,1},{4,6},{5,7},{6,4},{7,5},{8,10},{9,11},{10,... | collective-permute-start | bytes 1376264 | tf_op jit(solution)/shard_map/ppermute | solution.py:74
  42.8 14.3 %collective-permute-start.17 = (bf16[256,896]{1,0:T(8,128)(2,1)S(1)}, bf16[256,896]{1,0:T(8,128)(2,1)S(1)}, u32[]{:S(2)}, u32[]{:S(2)}) collective-permute-start(bf16[256,896]{1,0:T(8,128)(2,1)S(1)} %get-tuple-element.80.refs_2_), channel_id=1, source_target_pairs={{0,4},{1,5},{2,6},{3,7},{4,0},{5,1},{6,2},{7,3},{8,12},{9,13},{10,... | collective-permute-start | bytes 1376264 | tf_op jit(solution)/shard_map/ppermute | solution.py:74
  43.9 14.8 %collective-permute-start.18 = (bf16[256,896]{1,0:T(8,128)(2,1)}, bf16[256,896]{1,0:T(8,128)(2,1)}, u32[]{:S(2)}, u32[]{:S(2)}) collective-permute-start(bf16[256,896]{1,0:T(8,128)(2,1)} %get-tuple-element.81.refs_3_), channel_id=1, source_target_pairs={{0,8},{1,9},{2,10},{3,11},{4,12},{5,13},{6,14},{7,15},{8,0},{9,1},... | collective-permute-start | bytes 1376264 | tf_op jit(solution)/shard_map/ppermute | solution.py:74
  53.6 18.9 %all-to-all-start = ((bf16[32,8,608]{2,1,0:T(8,128)(2,1)}), bf16[32,8,608]{2,1,0:T(8,128)(2,1)}, u32[]{:S(2)}, u32[]{:S(2)}) async-start(bf16[32,8,608]{2,1,0:T(8,128)(2,1)} %hold_back.1), calls=%async_computation | async-start | bytes 655360 | tf_op jit(solution)/shard_map/all_to_all | solution.py:344
  79.0 25.2 %collective-permute-start.28 = (f32[256,896]{1,0:T(8,128)S(1)}, f32[256,896]{1,0:T(8,128)S(1)}, u32[]{:S(2)}, u32[]{:S(2)}) collective-permute-start(f32[256,896]{1,0:T(8,128)S(1)} %get-tuple-element.104), channel_id=1, source_target_pairs={{0,24},{1,25},{2,26},{3,27},{4,28},{5,29},{6,30},{7,31},{8,16},{9,... | collective-permute-start | bytes 2752520 | tf_op jit(solution)/shard_map/ppermute | solution.py:74
  84.4 37.7 %collective-permute-start.25 = (f32[256,896]{1,0:T(8,128)S(1)}, f32[256,896]{1,0:T(8,128)S(1)}, u32[]{:S(2)}, u32[]{:S(2)}) collective-permute-start(f32[256,896]{1,0:T(8,128)S(1)} %get-tuple-element.97), channel_id=1, source_target_pairs={{0,8},{1,9},{2,10},{3,11},{4,12},{5,13},{6,14},{7,15},{8,0},{9,1},... | collective-permute-start | bytes 2752520 | tf_op jit(solution)/shard_map/ppermute | solution.py:74
  87.7 38.8 %collective-permute-start.22 = (f32[256,896]{1,0:T(8,128)S(1)}, f32[256,896]{1,0:T(8,128)S(1)}, u32[]{:S(2)}, u32[]{:S(2)}) collective-permute-start(f32[256,896]{1,0:T(8,128)S(1)} %get-tuple-element.90), channel_id=1, source_target_pairs={{0,4},{1,5},{2,6},{3,7},{4,0},{5,1},{6,2},{7,3},{8,12},{9,13},{10,... | collective-permute-start | bytes 2752520 | tf_op jit(solution)/shard_map/ppermute | solution.py:74
  91.6 35.9 %collective-permute-start.19 = (f32[256,896]{1,0:T(8,128)S(1)}, f32[256,896]{1,0:T(8,128)S(1)}, u32[]{:S(2)}, u32[]{:S(2)}) collective-permute-start(f32[256,896]{1,0:T(8,128)S(1)} %get-tuple-element.83), channel_id=1, source_target_pairs={{0,2},{1,3},{2,0},{3,1},{4,6},{5,7},{6,4},{7,5},{8,10},{9,11},{10,... | collective-permute-start | bytes 2752520 | tf_op jit(solution)/shard_map/ppermute | solution.py:74
  105.1 29.7 %collective-permute-start.29 = (f32[128,896]{1,0:T(8,128)}, f32[128,896]{1,0:T(8,128)S(1)}, u32[]{:S(2)}, u32[]{:S(2)}) collective-permute-start(f32[128,896]{1,0:T(8,128)} %get-tuple-element.106), channel_id=1, source_target_pairs={{0,2},{1,3},{2,0},{3,1},{4,6},{5,7},{6,4},{7,5},{8,10},{9,11},{10,... | collective-permute-start | bytes 1376264 | tf_op jit(solution)/shard_map/ppermute | solution.py:74
  123.0 15.5 %collective-permute-start.26 = (f32[128,896]{1,0:T(8,128)}, f32[128,896]{1,0:T(8,128)S(1)}, u32[]{:S(2)}, u32[]{:S(2)}) collective-permute-start(f32[128,896]{1,0:T(8,128)} %get-tuple-element.99), channel_id=1, source_target_pairs={{0,24},{1,25},{2,26},{3,27},{4,28},{5,29},{6,30},{7,31},{8,16},{9,... | collective-permute-start | bytes 1376264 | tf_op jit(solution)/shard_map/ppermute | solution.py:74
  127.4 20.0 %collective-permute-start.23 = (f32[128,896]{1,0:T(8,128)}, f32[128,896]{1,0:T(8,128)S(1)}, u32[]{:S(2)}, u32[]{:S(2)}) collective-permute-start(f32[128,896]{1,0:T(8,128)} %get-tuple-element.92), channel_id=1, source_target_pairs={{0,8},{1,9},{2,10},{3,11},{4,12},{5,13},{6,14},{7,15},{8,0},{9,1},... | collective-permute-start | bytes 1376264 | tf_op jit(solution)/shard_map/ppermute | solution.py:74
  128.3 21.7 %collective-permute-start.20 = (f32[128,896]{1,0:T(8,128)}, f32[128,896]{1,0:T(8,128)}, u32[]{:S(2)}, u32[]{:S(2)}) collective-permute-start(f32[128,896]{1,0:T(8,128)} %get-tuple-element.85), channel_id=1, source_target_pairs={{0,4},{1,5},{2,6},{3,7},{4,0},{5,1},{6,2},{7,3},{8,12},{9,13},{10,... | collective-permute-start | bytes 1376264 | tf_op jit(solution)/shard_map/ppermute | solution.py:74
  134.8 17.4 %collective-permute-start.30 = (f32[64,896]{1,0:T(8,128)S(1)}, f32[64,896]{1,0:T(8,128)S(1)}, u32[]{:S(2)}, u32[]{:S(2)}) collective-permute-start(f32[64,896]{1,0:T(8,128)S(1)} %get-tuple-element.108), channel_id=1, source_target_pairs={{0,4},{1,5},{2,6},{3,7},{4,0},{5,1},{6,2},{7,3},{8,12},{9,13},{10,... | collective-permute-start | bytes 688136 | tf_op jit(solution)/shard_map/ppermute | solution.py:74
  138.5 15.8 %collective-permute-start.27 = (f32[64,896]{1,0:T(8,128)S(1)}, f32[64,896]{1,0:T(8,128)S(1)}, u32[]{:S(2)}, u32[]{:S(2)}) collective-permute-start(f32[64,896]{1,0:T(8,128)S(1)} %get-tuple-element.101), channel_id=1, source_target_pairs={{0,2},{1,3},{2,0},{3,1},{4,6},{5,7},{6,4},{7,5},{8,10},{9,11},{10,... | collective-permute-start | bytes 688136 | tf_op jit(solution)/shard_map/ppermute | solution.py:74
  147.4 10.4 %collective-permute-start.24 = (f32[64,896]{1,0:T(8,128)S(1)}, f32[64,896]{1,0:T(8,128)S(1)}, u32[]{:S(2)}, u32[]{:S(2)}) collective-permute-start(f32[64,896]{1,0:T(8,128)S(1)} %get-tuple-element.94), channel_id=1, source_target_pairs={{0,24},{1,25},{2,26},{3,27},{4,28},{5,29},{6,30},{7,31},{8,16},{9,... | collective-permute-start | bytes 688136 | tf_op jit(solution)/shard_map/ppermute | solution.py:74
  151.1 10.9 %collective-permute-start.21 = (f32[64,896]{1,0:T(8,128)S(1)}, f32[64,896]{1,0:T(8,128)S(1)}, u32[]{:S(2)}, u32[]{:S(2)}) collective-permute-start(f32[64,896]{1,0:T(8,128)S(1)} %get-tuple-element.87), channel_id=1, source_target_pairs={{0,8},{1,9},{2,10},{3,11},{4,12},{5,13},{6,14},{7,15},{8,0},{9,1},... | collective-permute-start | bytes 688136 | tf_op jit(solution)/shard_map/ppermute | solution.py:74
  152.2 12.8 %collective-permute-start.34 = (f32[32,896]{1,0:T(8,128)S(1)}, f32[32,896]{1,0:T(8,128)S(1)}, u32[]{:S(2)}, u32[]{:S(2)}) collective-permute-start(f32[32,896]{1,0:T(8,128)S(1)} %get-tuple-element.113), channel_id=1, source_target_pairs={{0,8},{1,9},{2,10},{3,11},{4,12},{5,13},{6,14},{7,15},{8,0},{9,1},... | collective-permute-start | bytes 344072 | tf_op jit(solution)/shard_map/ppermute | solution.py:74
  154.3 10.8 %collective-permute-start.33 = (f32[32,896]{1,0:T(8,128)S(1)}, f32[32,896]{1,0:T(8,128)S(1)}, u32[]{:S(2)}, u32[]{:S(2)}) collective-permute-start(f32[32,896]{1,0:T(8,128)S(1)} %get-tuple-element.112), channel_id=1, source_target_pairs={{0,4},{1,5},{2,6},{3,7},{4,0},{5,1},{6,2},{7,3},{8,12},{9,13},{10,... | collective-permute-start | bytes 344072 | tf_op jit(solution)/shard_map/ppermute | solution.py:74
  157.9 7.2 %collective-permute-start.32 = (f32[32,896]{1,0:T(8,128)S(1)}, f32[32,896]{1,0:T(8,128)S(1)}, u32[]{:S(2)}, u32[]{:S(2)}) collective-permute-start(f32[32,896]{1,0:T(8,128)S(1)} %get-tuple-element.111), channel_id=1, source_target_pairs={{0,2},{1,3},{2,0},{3,1},{4,6},{5,7},{6,4},{7,5},{8,10},{9,11},{10,... | collective-permute-start | bytes 344072 | tf_op jit(solution)/shard_map/ppermute | solution.py:74
  162.0 6.9 %collective-permute-start.31 = (f32[32,896]{1,0:T(8,128)S(1)}, f32[32,896]{1,0:T(8,128)S(1)}, u32[]{:S(2)}, u32[]{:S(2)}) collective-permute-start(f32[32,896]{1,0:T(8,128)S(1)} %get-tuple-element.110), channel_id=1, source_target_pairs={{0,24},{1,25},{2,26},{3,27},{4,28},{5,29},{6,30},{7,31},{8,16},{9,... | collective-permute-start | bytes 344072 | tf_op jit(solution)/shard_map/ppermute | solution.py:74
  (14 other events, 279.8 us)

commit v6 on v5

--- a/solution.py
+++ b/solution.py
@@ -67,6 +67,8 @@
 MIB = 1024 * 1024
 
 LINKS = (1, 2, 4, 12)
+SHARES = (10, 10, 8)
+ORDERS = ((1, 0, 3, 2), (0, 2, 1, 3), (2, 1, 0, 3))
 
 
 def across(value, link):
@@ -78,13 +80,18 @@
     return lax.ppermute(value, "ep", [(i, i ^ 1) for i in range(lax.axis_size("ep"))])
 
 
-def slot_of(bits, quarter, top_first):
-    count = len(LINKS)
+def slot_of(place, order):
     slot = 0
-    for i in range(count):
-        at = count - 1 - i if top_first else i
-        slot |= ((bits >> at) & 1) << ((quarter + i) % count)
+    for i, step in enumerate(order):
+        slot |= ((place >> (len(order) - 1 - i)) & 1) << step
     return slot
+
+
+def piece_columns(width):
+    share = width // sum(SHARES)
+    ends = [share * sum(SHARES[: at + 1]) for at in range(len(SHARES))]
+    ends[-1] = width
+    return list(zip([0] + ends[:-1], ends))
 
 
 def whole_call(kernel, operands, out_shape, name, after=()):
@@ -131,18 +138,17 @@
 
 
 def gather_cube(tokens, others):
-    count = len(LINKS)
-    width = tokens.shape[1] // count
-    held = [tokens[:, q * width : (q + 1) * width] for q in range(count)]
-    for phase in range(count):
-        got = [across(held[q], (q + phase) % count) for q in range(count)]
-        if phase < count - 1:
+    steps = len(LINKS)
+    held = [tokens[:, start:stop] for start, stop in piece_columns(tokens.shape[1])]
+    for phase in range(steps):
+        got = [across(piece, order[steps - 1 - phase]) for piece, order in zip(held, ORDERS)]
+        if phase < steps - 1:
             held = joined(held, got, others if phase == 1 else ())
     return held, got
 
 
 def hidden_kernel(unit, *refs):
-    count = len(LINKS)
+    count = len(ORDERS)
     held, got = refs[:count], refs[count : 2 * count]
     gate_ref, up_ref, gate_other_ref, up_other_ref, hidden_ref, rows_ref = refs[2 * count :]
     step = pl.program_id(0)
@@ -150,14 +156,13 @@
 
     @pl.when(step == 0)
     def _():
-        for quarter in range(count):
-            half, width = held[quarter].shape
-            columns = slice(quarter * width, (quarter + 1) * width)
+        for piece, (start, stop) in enumerate(piece_columns(rows_ref.shape[1])):
+            half = held[piece].shape[0]
             for place in range(2 * half // unit):
-                source = held[quarter] if place * unit < half else got[quarter]
+                source = held[piece] if place * unit < half else got[piece]
                 at = place * unit % half
-                slot = slot_of(place, quarter, False)
-                rows_ref[slot * unit : (slot + 1) * unit, columns] = source[at : at + unit]
+                slot = slot_of(place, ORDERS[piece])
+                rows_ref[slot * unit : (slot + 1) * unit, start:stop] = source[at : at + unit]
 
     def units(gate_tile, up_tile):
         rows = rows_ref[...]
@@ -199,39 +204,53 @@
     )(*held, *got, gate, up, gate_other, up_other)
 
 
-def output_kernel(unit, quarter, scale_ref, hidden_ref, down_ref, down_other_ref, keep_ref, send_ref):
+def output_kernel(
+    unit, order, scale_ref, hidden_ref, down_ref, down_other_ref, keep_ref, send_ref, rows_ref, factor_ref
+):
     units = down_ref.shape[0]
-    places = hidden_ref.shape[0] // unit
-    for out_ref, first in ((send_ref, places // 2), (keep_ref, 0)):
-        slots = [slot_of(first + at, quarter, True) for at in range(places // 2)]
-        rows = [slice(slot * unit, (slot + 1) * unit) for slot in slots]
-        hidden = jnp.concatenate([hidden_ref[row] for row in rows], axis=0)
-        scale = jnp.concatenate([scale_ref[row] for row in rows], axis=0)
-        out = jnp.dot(hidden[:, :units], down_ref[...], preferred_element_type=jnp.float32)
-        out += jnp.dot(hidden[:, units:], down_other_ref[...], preferred_element_type=jnp.float32)
-        out_ref[...] = out * scale
-
-
-def expert_output(unit, quarter, scale, hidden, down, down_other):
-    units, width = down.shape
-    tile = width // len(LINKS)
+    half = keep_ref.shape[0]
+
+    @pl.when(pl.program_id(0) == 0)
+    def _():
+        for place in range(2 * half // unit):
+            slot = slot_of(place, order)
+            to, source = pl.ds(place * unit, unit), pl.ds(slot * unit, unit)
+            rows_ref[to, :] = hidden_ref[source, :]
+            factor_ref[to, :] = scale_ref[source, :]
+
+    for out_ref, part in ((send_ref, pl.ds(half, half)), (keep_ref, pl.ds(0, half))):
+        out = jnp.dot(rows_ref[part, :units], down_ref[...], preferred_element_type=jnp.float32)
+        out += jnp.dot(
+            rows_ref[part, units:], down_other_ref[...], preferred_element_type=jnp.float32
+        )
+        out_ref[...] = out * factor_ref[part, :]
+
+
+def expert_output(unit, order, columns, scale, hidden, down, down_other):
+    units = down.shape[0]
+    start, stop = columns
     count = hidden.shape[0]
-    half = jax.ShapeDtypeStruct((count // 2, tile), jnp.float32)
+    tile = 256
+    half = jax.ShapeDtypeStruct((count // 2, stop - start), jnp.float32)
     return pl.pallas_call(
-        functools.partial(output_kernel, unit, quarter),
-        grid=(1,),
+        functools.partial(output_kernel, unit, order),
+        grid=((stop - start) // tile,),
         in_specs=[
             pl.BlockSpec((count, 1), lambda i: (0, 0)),
             pl.BlockSpec((count, 2 * units), lambda i: (0, 0)),
-            pl.BlockSpec((units, tile), lambda i: (0, quarter)),
-            pl.BlockSpec((units, tile), lambda i: (0, quarter)),
+            pl.BlockSpec((units, tile), lambda i: (0, start // tile + i)),
+            pl.BlockSpec((units, tile), lambda i: (0, start // tile + i)),
         ],
-        out_specs=[pl.BlockSpec((count // 2, tile), lambda i: (0, 0))] * 2,
+        out_specs=[pl.BlockSpec((count // 2, tile), lambda i: (0, i))] * 2,
         out_shape=[half] * 2,
-        compiler_params=pltpu.CompilerParams(vmem_limit_bytes=32 * MIB),
+        scratch_shapes=[
+            pltpu.VMEM((count, 2 * units), jnp.bfloat16),
+            pltpu.VMEM((count, 1), jnp.float32),
+        ],
+        compiler_params=pltpu.CompilerParams(vmem_limit_bytes=40 * MIB),
         cost_estimate=pl.CostEstimate(
-            flops=4 * count * tile * units,
-            bytes_accessed=4 * tile * units + 4 * count * (tile + units),
+            flops=4 * count * (stop - start) * units,
+            bytes_accessed=4 * (stop - start) * units + 4 * count * (stop - start + units),
             transcendentals=0,
         ),
         name="expert_output",
@@ -251,14 +270,14 @@
 
 def finished(keep, got):
     count = len(keep)
-    rows, width = keep[0].shape
+    width = sum(piece.shape[1] for piece in keep)
 
     def kernel(*refs):
-        for q in range(count):
-            total = refs[q][...] + refs[count + q][...]
-            refs[2 * count][:, q * width : (q + 1) * width] = total.astype(jnp.bfloat16)
-
-    shape = jax.ShapeDtypeStruct((rows, count * width), jnp.bfloat16)
+        for at, (start, stop) in enumerate(piece_columns(width)):
+            total = refs[at][...] + refs[count + at][...]
+            refs[2 * count][:, start:stop] = total.astype(jnp.bfloat16)
+
+    shape = jax.ShapeDtypeStruct((keep[0].shape[0], width), jnp.bfloat16)
     return whole_call(kernel, [*keep, *got], [shape], "finished")[0]
 
 
@@ -280,14 +299,14 @@
 
     hidden = expert_hidden(unit, *gathered, gate, up, gate_other, up_other)
     keep, got = [], []
-    for q in range(count):
-        mine, send = expert_output(unit, q, scale, hidden, down, down_other)
+    for order, columns in zip(ORDERS, piece_columns(down.shape[1])):
+        mine, send = expert_output(unit, order, columns, scale, hidden, down, down_other)
         keep.append(mine)
-        got.append(across(send, q))
+        got.append(across(send, order[0]))
     for phase in range(1, count):
-        for q in range(count):
-            keep[q], send = halved(keep[q], got[q])
-            got[q] = across(send, (q + phase) % count)
+        for at, order in enumerate(ORDERS):
+            keep[at], send = halved(keep[at], got[at])
+            got[at] = across(send, order[phase])
     return finished(keep, got)
 
 

time: 170 us -> 166 us (0.976)
  waiting for transfers between devices: 60.4 us -> 57.5 us
  local copies, waits for them, and re-layouts: 12.5 us -> 10.2 us
    ppermute x32 -> x24, waiting for transfers between devices: 60.3 us -> 50.5 us  [across(): lax.ppermute(value, 'ep', [(i, i ^ 2 * LINKS[link]) for i in range(peers)])]
    all_to_all x1, waiting for transfers between devices: 0.01 us -> 6.95 us  [per_device(): lax.all_to_all(leaving, 'ep', split_axis=0, concat_axis=0, tiled=True)]
    unnamed x20, local copies, waits for them, and re-layouts: 4.48 us -> 1.43 us
    pallas_call x4 -> x3, Pallas kernels: 10 us -> 12.4 us  [expert_output(): pl.pallas_call(functools.partial(output_kernel, unit, order), grid=((stop...]
    ppermute x32 -> x24, starting transfers between devices: 52.5 us -> 50.7 us  [across(): lax.ppermute(value, 'ep', [(i, i ^ 2 * LINKS[link]) for i in range(peers)])]
    pallas_call x17 -> x14, Pallas kernels: 7.29 us -> 5.94 us  [whole_call(): pl.pallas_call(body, in_specs=[pl.BlockSpec(memory_space=pltpu.VMEM)] * g...]
  transfers between devices with their start and end apart: 36 -> 28, of which waited for: 15 -> 15; matrix products, arithmetic and copies ran while one was open for 9% -> 10% of each run, Pallas kernels for 15% -> 7%
where the time goes in v6:
time: 166 us; the launch traced here: 165 us
  waiting for transfers between devices  57.5 us (35%)
  starting transfers between devices  56.4 us (34%)
  Pallas kernels  31.7 us (19%)
  local copies, waits for them, and re-layouts  10.2 us (6%)
  other arithmetic  5.02 us (3%)
  matrix products  2.63 us (2%)
    ppermute x24, starting transfers between devices, across(): lax.ppermute(value, 'ep', [(i, i ^ 2 * LINKS[link]) for i in range(peers)])  50.7 us
    ppermute x24, waiting for transfers between devices, across(): lax.ppermute(value, 'ep', [(i, i ^ 2 * LINKS[link]) for i in range(peers)])  50.5 us
    pallas_call x1, Pallas kernels, expert_hidden(): pl.pallas_call(functools.partial(hidden_kernel, unit), grid=(2 * steps,),...  13.3 us
    pallas_call x3, Pallas kernels, expert_output(): pl.pallas_call(functools.partial(output_kernel, unit, order), grid=((stop...  12.4 us
    all_to_all x1, waiting for transfers between devices, per_device(): lax.all_to_all(leaving, 'ep', split_axis=0, concat_axis=0, tiled=True)  6.95 us
    pallas_call x14, Pallas kernels, whole_call(): pl.pallas_call(body, in_specs=[pl.BlockSpec(memory_space=pltpu.VMEM)] * g...  5.94 us
    all_to_all x1, starting transfers between devices, per_device(): lax.all_to_all(leaving, 'ep', split_axis=0, concat_axis=0, tiled=True)  4.72 us
    reshape x2, local copies, waits for them, and re-layouts, per_device(): arrived.reshape(peers * 2 * block_len, latent)  3.57 us
  transfers between devices with their start and end apart: 28, of which 15 were waited for; matrix products, arithmetic and copies ran while one was open for 10% of the time, Pallas kernels for 7%

profile of v6, /device:TPU:0, one launch (start us, length us, event | category | flops | bytes accessed | tf_op | source)
XLA Modules:
  0.0 165.0 jit_solution(1590059419503344884)
XLA Ops:
  2.6 2.7 %collective-permute-start = (bf16[32,1280]{1,0:T(8,128)(2,1)S(1)}, bf16[32,1280]{1,0:T(8,128)(2,1)S(1)}, u32[]{:S(2)}, u32[]{:S(2)}) collective-permute-start(bf16[32,1280]{1,0:T(8,128)(2,1)S(1)} %get-tuple-element.93.refs_0_), channel_id=1, source_target_pairs={{0,8},{1,9},{2,10},{3,11},{4,12},{5,13},{6,14},{7,15},{8,0},{9,1},... | collective-permute-start | bytes 245768 | tf_op jit(solution)/shard_map/ppermute | solution.py:76
  6.2 2.5 %collective-permute-start.2 = (bf16[32,1024]{1,0:T(8,128)(2,1)S(1)}, bf16[32,1024]{1,0:T(8,128)(2,1)S(1)}, u32[]{:S(2)}, u32[]{:S(2)}) collective-permute-start(bf16[32,1024]{1,0:T(8,128)(2,1)S(1)} %slice.81.refs_2_), channel_id=1, source_target_pairs={{0,24},{1,25},{2,26},{3,27},{4,28},{5,29},{6,30},{7,31},{8,16},{9,... | collective-permute-start | bytes 196616 | tf_op jit(solution)/shard_map/ppermute | solution.py:76
  12.3 2.5 %collective-permute-start.1 = (bf16[32,1280]{1,0:T(8,128)(2,1)S(1)}, bf16[32,1280]{1,0:T(8,128)(2,1)S(1)}, u32[]{:S(2)}, u32[]{:S(2)}) collective-permute-start(bf16[32,1280]{1,0:T(8,128)(2,1)S(1)} %get-tuple-element.92.refs_1_), channel_id=1, source_target_pairs={{0,24},{1,25},{2,26},{3,27},{4,28},{5,29},{6,30},{7,31},{8,16},{9,... | collective-permute-start | bytes 245768 | tf_op jit(solution)/shard_map/ppermute | solution.py:76
  15.2 3.4 %collective-permute-done.1.refs_4_ = bf16[32,1280]{1,0:T(8,128)(2,1)S(1)} collective-permute-done((bf16[32,1280]{1,0:T(8,128)(2,1)S(1)}, bf16[32,1280]{1,0:T(8,128)(2,1)S(1)}, u32[]{:S(2)}, u32[]{:S(2)}) %collective-permute-start.1) | collective-permute-done | bytes 81952 | tf_op jit(solution)/shard_map/ppermute | solution.py:76
  18.6 1.6 collective-permute-start.5
  20.4 2.6 %collective-permute-start.3 = (bf16[64,1280]{1,0:T(8,128)(2,1)S(1)}, bf16[64,1280]{1,0:T(8,128)(2,1)S(1)}, u32[]{:S(2)}, u32[]{:S(2)}) collective-permute-start(bf16[64,1280]{1,0:T(8,128)(2,1)S(1)} %get-tuple-element.59.refs_0_), channel_id=1, source_target_pairs={{0,24},{1,25},{2,26},{3,27},{4,28},{5,29},{6,30},{7,31},{8,16},{9,... | collective-permute-start | bytes 491528 | tf_op jit(solution)/shard_map/ppermute | solution.py:76
  23.6 1.5 collective-permute-start.4
  25.2 2.5 %collective-permute-done.3.refs_3_ = bf16[64,1280]{1,0:T(8,128)(2,1)S(1)} collective-permute-done((bf16[64,1280]{1,0:T(8,128)(2,1)S(1)}, bf16[64,1280]{1,0:T(8,128)(2,1)S(1)}, u32[]{:S(2)}, u32[]{:S(2)}) %collective-permute-start.3) | collective-permute-done | bytes 163872 | tf_op jit(solution)/shard_map/ppermute | solution.py:76
  29.1 2.9 %collective-permute-start.9 = (bf16[128,1280]{1,0:T(8,128)(2,1)S(1)}, bf16[128,1280]{1,0:T(8,128)(2,1)S(1)}, u32[]{:S(2)}, u32[]{:S(2)}) collective-permute-start(bf16[128,1280]{1,0:T(8,128)(2,1)S(1)} %get-tuple-element.62.refs_0_), channel_id=1, source_target_pairs={{0,2},{1,3},{2,0},{3,1},{4,6},{5,7},{6,4},{7,5},{8,10},{9,11},{10,... | collective-permute-start | bytes 983048 | tf_op jit(solution)/shard_map/ppermute | solution.py:76
  32.0 1.5 collective-permute-start.11
  34.9 3.5 %collective-permute-done.11.refs_5_ = bf16[128,1024]{1,0:T(8,128)(2,1)S(1)} collective-permute-done((bf16[128,1024]{1,0:T(8,128)(2,1)S(1)}, bf16[128,1024]{1,0:T(8,128)(2,1)S(1)}, u32[]{:S(2)}, u32[]{:S(2)}) %collective-permute-start.11) | collective-permute-done | bytes 262176 | tf_op jit(solution)/shard_map/ppermute | solution.py:76
  40.0 4.7 %all-to-all-start = ((bf16[32,8,608]{2,1,0:T(8,128)(2,1)}), bf16[32,8,608]{2,1,0:T(8,128)(2,1)}, u32[]{:S(2)}, u32[]{:S(2)}) async-start(bf16[32,8,608]{2,1,0:T(8,128)(2,1)} %hold_back.1), calls=%async_computation | async-start | bytes 655360 | tf_op jit(solution)/shard_map/all_to_all | solution.py:363
  44.8 1.8 %collective-permute-start.12 = (bf16[256,1280]{1,0:T(8,128)(2,1)S(1)}, bf16[256,1280]{1,0:T(8,128)(2,1)S(1)}, u32[]{:S(2)}, u32[]{:S(2)}) collective-permute-start(bf16[256,1280]{1,0:T(8,128)(2,1)S(1)} %get-tuple-element.65.refs_1_.refs_0_), channel_id=1, source_target_pairs={{0,4},{1,5},{2,6},{3,7},{4,0},{5,1},{6,2},{7,3},{8,12},{9,13},{10,... | collective-permute-start | bytes 1966088 | tf_op jit(solution)/shard_map/ppermute | solution.py:76
  48.1 1.5 collective-permute-start.14
  49.6 7.0 %all-to-all-done = bf16[32,8,608]{2,1,0:T(8,128)(2,1)} async-done(((bf16[32,8,608]{2,1,0:T(8,128)(2,1)}), bf16[32,8,608]{2,1,0:T(8,128)(2,1)}, u32[]{:S(2)}, u32[]{:S(2)}) %all-to-all-start) | async-done | bytes 311328 | tf_op jit(solution)/shard_map/all_to_all | solution.py:363
  59.8 4.4 %collective-permute-done.14.refs_5_ = bf16[256,1024]{1,0:T(8,128)(2,1)} collective-permute-done((bf16[256,1024]{1,0:T(8,128)(2,1)S(1)}, bf16[256,1024]{1,0:T(8,128)(2,1)}, u32[]{:S(2)}, u32[]{:S(2)}) %collective-permute-start.14) | collective-permute-done | bytes 524320 | tf_op jit(solution)/shard_map/ppermute | solution.py:76
  65.5 13.3 %expert_hidden.1.hidden_ref = bf16[512,1024]{1,0:T(8,128)(2,1)S(1)} custom-call(bf16[256,1280]{1,0:T(8,128)(2,1)S(1)} %get-tuple-element.65.refs_1_.refs_0_, bf16[256,1280]{1,0:T(8,128)(2,1)S(1)} %get-tuple-element.66.refs_1_, bf16[256,1024]{1,0:T(8,128)(2,1)S(1)} %copy-done.3, bf16[256,1280]{1,0:T(8,128)(2,1)S(1)} %collective-permute-done.12.refs_3_, ...), custom_call_target="tpu_custom_call" | custom-call | flops 7516192768 | bytes 19398656 | tf_op jit(solution)/shard_map/expert_hidden/pallas_call | solution.py:189
  78.8 4.5 %expert_output.4 = (f32[256,1280]{1,0:T(8,128)S(1)}, f32[256,1280]{1,0:T(8,128)S(1)}) custom-call(f32[512,1]{1,0:T(8,128)S(1)} %reshape.191.scale_ref, bf16[512,1024]{1,0:T(8,128)(2,1)S(1)} %expert_hidden.1.hidden_ref, bf16[512,3584]{1,0:T(8,128)(2,1)S(1)} %bitcast.22, bf16[512,3584]{1,0:T(8,128)(2,1)} %collective-permute-done.8.refs_8_.down_other_ref), custom_call_target="tpu_custom_call" | custom-call | flops 1342177280 | bytes 6291456 | tf_op jit(solution)/shard_map/expert_output/pallas_call | solution.py:235
  84.4 4.4 %expert_output.3 = (f32[256,1280]{1,0:T(8,128)S(1)}, f32[256,1280]{1,0:T(8,128)S(1)}) custom-call(f32[512,1]{1,0:T(8,128)S(1)} %reshape.191.scale_ref, bf16[512,1024]{1,0:T(8,128)(2,1)S(1)} %expert_hidden.1.hidden_ref, bf16[512,3584]{1,0:T(8,128)(2,1)S(1)} %bitcast.23, bf16[512,3584]{1,0:T(8,128)(2,1)} %collective-permute-done.8.refs_8_.down_other_ref), custom_call_target="tpu_custom_call" | custom-call | flops 1342177280 | bytes 6291456 | tf_op jit(solution)/shard_map/expert_output/pallas_call | solution.py:235
  89.9 3.5 %expert_output.5 = (f32[256,1024]{1,0:T(8,128)S(1)}, f32[256,1024]{1,0:T(8,128)S(1)}) custom-call(f32[512,1]{1,0:T(8,128)S(1)} %reshape.191.scale_ref, bf16[512,1024]{1,0:T(8,128)(2,1)S(1)} %expert_hidden.1.hidden_ref, bf16[512,3584]{1,0:T(8,128)(2,1)S(1)} %bitcast.24, bf16[512,3584]{1,0:T(8,128)(2,1)} %collective-permute-done.8.refs_8_.down_other_ref), custom_call_target="tpu_custom_call" | custom-call | flops 1073741824 | bytes 5242880 | tf_op jit(solution)/shard_map/expert_output/pallas_call | solution.py:235
  94.6 19.0 %collective-permute-done.18.refs_1_ = f32[256,1280]{1,0:T(8,128)S(1)} collective-permute-done((f32[256,1280]{1,0:T(8,128)S(1)}, f32[256,1280]{1,0:T(8,128)S(1)}, u32[]{:S(2)}, u32[]{:S(2)}) %collective-permute-start.18) | collective-permute-done | bytes 1310752 | tf_op jit(solution)/shard_map/ppermute | solution.py:76
  115.8 3.3 %collective-permute-done.15.refs_1_ = f32[256,1280]{1,0:T(8,128)S(1)} collective-permute-done((f32[256,1280]{1,0:T(8,128)S(1)}, f32[256,1280]{1,0:T(8,128)S(1)}, u32[]{:S(2)}, u32[]{:S(2)}) %collective-permute-start.15) | collective-permute-done | bytes 1310752 | tf_op jit(solution)/shard_map/ppermute | solution.py:76
  123.5 1.7 %slice_bitcast_fusion = bf16[256,576]{1,0:T(8,128)(2,1)} fusion(bf16[32,8,608]{2,1,0:T(8,128)(2,1)} %all-to-all-done), kind=kLoop, calls=%fused_computation.16 | loop fusion | bytes 589824 | tf_op jit(solution)/shard_map/reshape | solution.py:371
  125.3 1.8 %copy.31 = bf16[256,576]{0,1:T(8,128)(2,1)} copy(bf16[256,576]{1,0:T(8,128)(2,1)} %slice_bitcast_fusion) | data formatting | bytes 589824 | tf_op jit(solution)/shard_map/reshape | solution.py:371
  128.4 6.4 %collective-permute-done.22.refs_1_ = f32[128,1024]{1,0:T(8,128)} collective-permute-done((f32[128,1024]{1,0:T(8,128)}, f32[128,1024]{1,0:T(8,128)}, u32[]{:S(2)}, u32[]{:S(2)}) %collective-permute-start.22) | collective-permute-done | bytes 524320 | tf_op jit(solution)/shard_map/ppermute | solution.py:76
  138.3 3.4 %collective-permute-start.17 = (f32[64,1280]{1,0:T(8,128)S(1)}, f32[64,1280]{1,0:T(8,128)S(1)}, u32[]{:S(2)}, u32[]{:S(2)}) collective-permute-start(f32[64,1280]{1,0:T(8,128)S(1)} %get-tuple-element.73), channel_id=1, source_target_pairs={{0,24},{1,25},{2,26},{3,27},{4,28},{5,29},{6,30},{7,31},{8,16},{9,... | collective-permute-start | bytes 983048 | tf_op jit(solution)/shard_map/ppermute | solution.py:76
  142.7 3.1 %collective-permute-start.26 = (f32[32,1024]{1,0:T(8,128)S(1)}, f32[32,1024]{1,0:T(8,128)S(1)}, u32[]{:S(2)}, u32[]{:S(2)}) collective-permute-start(f32[32,1024]{1,0:T(8,128)S(1)} %get-tuple-element.91), channel_id=1, source_target_pairs={{0,24},{1,25},{2,26},{3,27},{4,28},{5,29},{6,30},{7,31},{8,16},{9,... | collective-permute-start | bytes 393224 | tf_op jit(solution)/shard_map/ppermute | solution.py:76
  145.9 2.5 %collective-permute-start.25 = (f32[32,1280]{1,0:T(8,128)S(1)}, f32[32,1280]{1,0:T(8,128)S(1)}, u32[]{:S(2)}, u32[]{:S(2)}) collective-permute-start(f32[32,1280]{1,0:T(8,128)S(1)} %get-tuple-element.90), channel_id=1, source_target_pairs={{0,24},{1,25},{2,26},{3,27},{4,28},{5,29},{6,30},{7,31},{8,16},{9,... | collective-permute-start | bytes 491528 | tf_op jit(solution)/shard_map/ppermute | solution.py:76
  148.4 2.1 %collective-permute-done.17.refs_1_ = f32[64,1280]{1,0:T(8,128)S(1)} collective-permute-done((f32[64,1280]{1,0:T(8,128)S(1)}, f32[64,1280]{1,0:T(8,128)S(1)}, u32[]{:S(2)}, u32[]{:S(2)}) %collective-permute-start.17) | collective-permute-done | bytes 327712 | tf_op jit(solution)/shard_map/ppermute | solution.py:76
  150.5 10.4 %collective-permute-start.24 = (f32[32,1280]{1,0:T(8,128)S(1)}, f32[32,1280]{1,0:T(8,128)S(1)}, u32[]{:S(2)}, u32[]{:S(2)}) collective-permute-start(f32[32,1280]{1,0:T(8,128)S(1)} %get-tuple-element.89), channel_id=1, source_target_pairs={{0,8},{1,9},{2,10},{3,11},{4,12},{5,13},{6,14},{7,15},{8,0},{9,1},... | collective-permute-start | bytes 491528 | tf_op jit(solution)/shard_map/ppermute | solution.py:76
  161.0 1.5 fusion.14
  162.5 1.8 %collective-permute-done.24.refs_3_ = f32[32,1280]{1,0:T(8,128)S(1)} collective-permute-done((f32[32,1280]{1,0:T(8,128)S(1)}, f32[32,1280]{1,0:T(8,128)S(1)}, u32[]{:S(2)}, u32[]{:S(2)}) %collective-permute-start.24) | collective-permute-done | bytes 163872 | tf_op jit(solution)/shard_map/ppermute | solution.py:76
  (94 shorter events, 34.0 us)
Async XLA Ops:
  0.6 141.0 %copy-start = (bf16[1,128,576]{1,2,0:T(8,128)(2,1)S(1)}, bf16[1,128,576]{1,2,0:T(8,128)(2,1)}, u32[]{:S(2)}) copy-start(bf16[1,128,576]{1,2,0:T(8,128)(2,1)} %param.16) | copy-start | bytes 442372
  0.6 19.6 %copy-start.7 = (s32[32,8]{0,1:T(8,128)S(1)}, s32[32,8]{0,1:T(8,128)}, u32[]{:S(2)}) copy-start(s32[32,8]{0,1:T(8,128)} %param.22) | copy-start | bytes 3076
  0.7 19.6 %copy-start.6 = (f32[32,8]{0,1:T(8,128)S(1)}, f32[32,8]{0,1:T(8,128)}, u32[]{:S(2)}) copy-start(f32[32,8]{0,1:T(8,128)} %param.23) | copy-start | bytes 3076
  0.7 28.3 %collective-permute-start.8 = (bf16[512,3584]{1,0:T(8,128)(2,1)}, bf16[512,3584]{1,0:T(8,128)(2,1)}, u32[]{:S(2)}, u32[]{:S(2)}) collective-permute-start(bf16[512,3584]{1,0:T(8,128)(2,1)} %bitcast.21), channel_id=1, source_target_pairs={{0,1},{1,0},{2,3},{3,2},{4,5},{5,4},{6,7},{7,6},{8,9},{9,8},{10,11... | collective-permute-start | bytes 11010056 | tf_op jit(solution)/shard_map/ppermute | solution.py:80
  1.2 27.8 %collective-permute-start.6 = (bf16[3584,512]{1,0:T(8,128)(2,1)}, bf16[3584,512]{1,0:T(8,128)(2,1)}, u32[]{:S(2)}, u32[]{:S(2)}) collective-permute-start(bf16[3584,512]{1,0:T(8,128)(2,1)} %bitcast.28), channel_id=1, source_target_pairs={{0,1},{1,0},{2,3},{3,2},{4,5},{5,4},{6,7},{7,6},{8,9},{9,8},{10,11... | collective-permute-start | bytes 11010056 | tf_op jit(solution)/shard_map/ppermute | solution.py:80
  1.3 27.7 %collective-permute-start.7 = (bf16[3584,512]{1,0:T(8,128)(2,1)}, bf16[3584,512]{1,0:T(8,128)(2,1)}, u32[]{:S(2)}, u32[]{:S(2)}) collective-permute-start(bf16[3584,512]{1,0:T(8,128)(2,1)} %bitcast.30), channel_id=1, source_target_pairs={{0,1},{1,0},{2,3},{3,2},{4,5},{5,4},{6,7},{7,6},{8,9},{9,8},{10,11... | collective-permute-start | bytes 11010056 | tf_op jit(solution)/shard_map/ppermute | solution.py:80
  2.6 12.5 %collective-permute-start = (bf16[32,1280]{1,0:T(8,128)(2,1)S(1)}, bf16[32,1280]{1,0:T(8,128)(2,1)S(1)}, u32[]{:S(2)}, u32[]{:S(2)}) collective-permute-start(bf16[32,1280]{1,0:T(8,128)(2,1)S(1)} %get-tuple-element.93.refs_0_), channel_id=1, source_target_pairs={{0,8},{1,9},{2,10},{3,11},{4,12},{5,13},{6,14},{7,15},{8,0},{9,1},... | collective-permute-start | bytes 245768 | tf_op jit(solution)/shard_map/ppermute | solution.py:76
  6.2 6.1 %collective-permute-start.2 = (bf16[32,1024]{1,0:T(8,128)(2,1)S(1)}, bf16[32,1024]{1,0:T(8,128)(2,1)S(1)}, u32[]{:S(2)}, u32[]{:S(2)}) collective-permute-start(bf16[32,1024]{1,0:T(8,128)(2,1)S(1)} %slice.81.refs_2_), channel_id=1, source_target_pairs={{0,24},{1,25},{2,26},{3,27},{4,28},{5,29},{6,30},{7,31},{8,16},{9,... | collective-permute-start | bytes 196616 | tf_op jit(solution)/shard_map/ppermute | solution.py:76
  12.3 6.2 %collective-permute-start.1 = (bf16[32,1280]{1,0:T(8,128)(2,1)S(1)}, bf16[32,1280]{1,0:T(8,128)(2,1)S(1)}, u32[]{:S(2)}, u32[]{:S(2)}) collective-permute-start(bf16[32,1280]{1,0:T(8,128)(2,1)S(1)} %get-tuple-element.92.refs_1_), channel_id=1, source_target_pairs={{0,24},{1,25},{2,26},{3,27},{4,28},{5,29},{6,30},{7,31},{8,16},{9,... | collective-permute-start | bytes 245768 | tf_op jit(solution)/shard_map/ppermute | solution.py:76
  18.6 5.0 %collective-permute-start.5 = (bf16[64,1024]{1,0:T(8,128)(2,1)S(1)}, bf16[64,1024]{1,0:T(8,128)(2,1)S(1)}, u32[]{:S(2)}, u32[]{:S(2)}) collective-permute-start(bf16[64,1024]{1,0:T(8,128)(2,1)S(1)} %get-tuple-element.61.refs_2_), channel_id=1, source_target_pairs={{0,2},{1,3},{2,0},{3,1},{4,6},{5,7},{6,4},{7,5},{8,10},{9,11},{10,... | collective-permute-start | bytes 393224 | tf_op jit(solution)/shard_map/ppermute | solution.py:76
  20.4 7.3 %collective-permute-start.3 = (bf16[64,1280]{1,0:T(8,128)(2,1)S(1)}, bf16[64,1280]{1,0:T(8,128)(2,1)S(1)}, u32[]{:S(2)}, u32[]{:S(2)}) collective-permute-start(bf16[64,1280]{1,0:T(8,128)(2,1)S(1)} %get-tuple-element.59.refs_0_), channel_id=1, source_target_pairs={{0,24},{1,25},{2,26},{3,27},{4,28},{5,29},{6,30},{7,31},{8,16},{9,... | collective-permute-start | bytes 491528 | tf_op jit(solution)/shard_map/ppermute | solution.py:76
  23.6 5.3 %collective-permute-start.4 = (bf16[64,1280]{1,0:T(8,128)(2,1)S(1)}, bf16[64,1280]{1,0:T(8,128)(2,1)S(1)}, u32[]{:S(2)}, u32[]{:S(2)}) collective-permute-start(bf16[64,1280]{1,0:T(8,128)(2,1)S(1)} %get-tuple-element.60.refs_1_), channel_id=1, source_target_pairs={{0,4},{1,5},{2,6},{3,7},{4,0},{5,1},{6,2},{7,3},{8,12},{9,13},{10,... | collective-permute-start | bytes 491528 | tf_op jit(solution)/shard_map/ppermute | solution.py:76
  29.0 9.4 %collective-permute-start.10 = (bf16[128,1280]{1,0:T(8,128)(2,1)S(1)}, bf16[128,1280]{1,0:T(8,128)(2,1)S(1)}, u32[]{:S(2)}, u32[]{:S(2)}) collective-permute-start(bf16[128,1280]{1,0:T(8,128)(2,1)S(1)} %get-tuple-element.63.refs_1_), channel_id=1, source_target_pairs={{0,8},{1,9},{2,10},{3,11},{4,12},{5,13},{6,14},{7,15},{8,0},{9,1},... | collective-permute-start | bytes 983048 | tf_op jit(solution)/shard_map/ppermute | solution.py:76
  29.1 9.3 %collective-permute-start.9 = (bf16[128,1280]{1,0:T(8,128)(2,1)S(1)}, bf16[128,1280]{1,0:T(8,128)(2,1)S(1)}, u32[]{:S(2)}, u32[]{:S(2)}) collective-permute-start(bf16[128,1280]{1,0:T(8,128)(2,1)S(1)} %get-tuple-element.62.refs_0_), channel_id=1, source_target_pairs={{0,2},{1,3},{2,0},{3,1},{4,6},{5,7},{6,4},{7,5},{8,10},{9,11},{10,... | collective-permute-start | bytes 983048 | tf_op jit(solution)/shard_map/ppermute | solution.py:76
  32.0 6.4 %collective-permute-start.11 = (bf16[128,1024]{1,0:T(8,128)(2,1)S(1)}, bf16[128,1024]{1,0:T(8,128)(2,1)S(1)}, u32[]{:S(2)}, u32[]{:S(2)}) collective-permute-start(bf16[128,1024]{1,0:T(8,128)(2,1)S(1)} %get-tuple-element.64.refs_2_), channel_id=1, source_target_pairs={{0,4},{1,5},{2,6},{3,7},{4,0},{5,1},{6,2},{7,3},{8,12},{9,13},{10,... | collective-permute-start | bytes 786440 | tf_op jit(solution)/shard_map/ppermute | solution.py:76
  40.0 16.5 %all-to-all-start = ((bf16[32,8,608]{2,1,0:T(8,128)(2,1)}), bf16[32,8,608]{2,1,0:T(8,128)(2,1)}, u32[]{:S(2)}, u32[]{:S(2)}) async-start(bf16[32,8,608]{2,1,0:T(8,128)(2,1)} %hold_back.1), calls=%async_computation | async-start | bytes 655360 | tf_op jit(solution)/shard_map/all_to_all | solution.py:363
  44.8 20.3 %collective-permute-start.12 = (bf16[256,1280]{1,0:T(8,128)(2,1)S(1)}, bf16[256,1280]{1,0:T(8,128)(2,1)S(1)}, u32[]{:S(2)}, u32[]{:S(2)}) collective-permute-start(bf16[256,1280]{1,0:T(8,128)(2,1)S(1)} %get-tuple-element.65.refs_1_.refs_0_), channel_id=1, source_target_pairs={{0,4},{1,5},{2,6},{3,7},{4,0},{5,1},{6,2},{7,3},{8,12},{9,13},{10,... | collective-permute-start | bytes 1966088 | tf_op jit(solution)/shard_map/ppermute | solution.py:76
  46.6 18.9 %collective-permute-start.13 = (bf16[256,1280]{1,0:T(8,128)(2,1)S(1)}, bf16[256,1280]{1,0:T(8,128)(2,1)S(1)}, u32[]{:S(2)}, u32[]{:S(2)}) collective-permute-start(bf16[256,1280]{1,0:T(8,128)(2,1)S(1)} %get-tuple-element.66.refs_1_), channel_id=1, source_target_pairs={{0,2},{1,3},{2,0},{3,1},{4,6},{5,7},{6,4},{7,5},{8,10},{9,11},{10,... | collective-permute-start | bytes 1966088 | tf_op jit(solution)/shard_map/ppermute | solution.py:76
  48.1 16.2 %collective-permute-start.14 = (bf16[256,1024]{1,0:T(8,128)(2,1)S(1)}, bf16[256,1024]{1,0:T(8,128)(2,1)}, u32[]{:S(2)}, u32[]{:S(2)}) collective-permute-start(bf16[256,1024]{1,0:T(8,128)(2,1)S(1)} %copy-done.3), channel_id=1, source_target_pairs={{0,8},{1,9},{2,10},{3,11},{4,12},{5,13},{6,14},{7,15},{8,0},{9,1},... | collective-permute-start | bytes 1572872 | tf_op jit(solution)/shard_map/ppermute | solution.py:76
  65.5 13.3 %copy-start.1 = (bf16[1,512,3584]{2,1,0:T(8,128)(2,1)S(1)}, bf16[1,512,3584]{2,1,0:T(8,128)(2,1)}, u32[]{:S(2)}) copy-start(bf16[1,512,3584]{2,1,0:T(8,128)(2,1)} %param.26) | copy-start | bytes 11010052
  83.3 30.4 %collective-permute-start.18 = (f32[256,1280]{1,0:T(8,128)S(1)}, f32[256,1280]{1,0:T(8,128)S(1)}, u32[]{:S(2)}, u32[]{:S(2)}) collective-permute-start(f32[256,1280]{1,0:T(8,128)S(1)} %get-tuple-element.76), channel_id=1, source_target_pairs={{0,2},{1,3},{2,0},{3,1},{4,6},{5,7},{6,4},{7,5},{8,10},{9,11},{10,... | collective-permute-start | bytes 3932168 | tf_op jit(solution)/shard_map/ppermute | solution.py:76
  88.8 30.3 %collective-permute-start.15 = (f32[256,1280]{1,0:T(8,128)S(1)}, f32[256,1280]{1,0:T(8,128)S(1)}, u32[]{:S(2)}, u32[]{:S(2)}) collective-permute-start(f32[256,1280]{1,0:T(8,128)S(1)} %get-tuple-element.69), channel_id=1, source_target_pairs={{0,4},{1,5},{2,6},{3,7},{4,0},{5,1},{6,2},{7,3},{8,12},{9,13},{10,... | collective-permute-start | bytes 3932168 | tf_op jit(solution)/shard_map/ppermute | solution.py:76
  93.4 28.1 %collective-permute-start.21 = (f32[256,1024]{1,0:T(8,128)S(1)}, f32[256,1024]{1,0:T(8,128)S(1)}, u32[]{:S(2)}, u32[]{:S(2)}) collective-permute-start(f32[256,1024]{1,0:T(8,128)S(1)} %get-tuple-element.83), channel_id=1, source_target_pairs={{0,8},{1,9},{2,10},{3,11},{4,12},{5,13},{6,14},{7,15},{8,0},{9,1},... | collective-permute-start | bytes 3145736 | tf_op jit(solution)/shard_map/ppermute | solution.py:76
  114.7 22.7 %collective-permute-start.19 = (f32[128,1280]{1,0:T(8,128)}, f32[128,1280]{1,0:T(8,128)S(1)}, u32[]{:S(2)}, u32[]{:S(2)}) collective-permute-start(f32[128,1280]{1,0:T(8,128)} %get-tuple-element.78), channel_id=1, source_target_pairs={{0,8},{1,9},{2,10},{3,11},{4,12},{5,13},{6,14},{7,15},{8,0},{9,1},... | collective-permute-start | bytes 1966088 | tf_op jit(solution)/shard_map/ppermute | solution.py:76
  120.1 18.1 %collective-permute-start.16 = (f32[128,1280]{1,0:T(8,128)}, f32[128,1280]{1,0:T(8,128)S(1)}, u32[]{:S(2)}, u32[]{:S(2)}) collective-permute-start(f32[128,1280]{1,0:T(8,128)} %get-tuple-element.71), channel_id=1, source_target_pairs={{0,2},{1,3},{2,0},{3,1},{4,6},{5,7},{6,4},{7,5},{8,10},{9,11},{10,... | collective-permute-start | bytes 1966088 | tf_op jit(solution)/shard_map/ppermute | solution.py:76
  122.5 12.3 %collective-permute-start.22 = (f32[128,1024]{1,0:T(8,128)}, f32[128,1024]{1,0:T(8,128)}, u32[]{:S(2)}, u32[]{:S(2)}) collective-permute-start(f32[128,1024]{1,0:T(8,128)} %get-tuple-element.85), channel_id=1, source_target_pairs={{0,4},{1,5},{2,6},{3,7},{4,0},{5,1},{6,2},{7,3},{8,12},{9,13},{10,... | collective-permute-start | bytes 1572872 | tf_op jit(solution)/shard_map/ppermute | solution.py:76
  135.9 6.8 %collective-permute-start.23 = (f32[64,1024]{1,0:T(8,128)S(1)}, f32[64,1024]{1,0:T(8,128)S(1)}, u32[]{:S(2)}, u32[]{:S(2)}) collective-permute-start(f32[64,1024]{1,0:T(8,128)S(1)} %get-tuple-element.87), channel_id=1, source_target_pairs={{0,2},{1,3},{2,0},{3,1},{4,6},{5,7},{6,4},{7,5},{8,10},{9,11},{10,... | collective-permute-start | bytes 786440 | tf_op jit(solution)/shard_map/ppermute | solution.py:76
  137.4 8.4 %collective-permute-start.20 = (f32[64,1280]{1,0:T(8,128)S(1)}, f32[64,1280]{1,0:T(8,128)S(1)}, u32[]{:S(2)}, u32[]{:S(2)}) collective-permute-start(f32[64,1280]{1,0:T(8,128)S(1)} %get-tuple-element.80), channel_id=1, source_target_pairs={{0,4},{1,5},{2,6},{3,7},{4,0},{5,1},{6,2},{7,3},{8,12},{9,13},{10,... | collective-permute-start | bytes 983048 | tf_op jit(solution)/shard_map/ppermute | solution.py:76
  138.3 12.2 %collective-permute-start.17 = (f32[64,1280]{1,0:T(8,128)S(1)}, f32[64,1280]{1,0:T(8,128)S(1)}, u32[]{:S(2)}, u32[]{:S(2)}) collective-permute-start(f32[64,1280]{1,0:T(8,128)S(1)} %get-tuple-element.73), channel_id=1, source_target_pairs={{0,24},{1,25},{2,26},{3,27},{4,28},{5,29},{6,30},{7,31},{8,16},{9,... | collective-permute-start | bytes 983048 | tf_op jit(solution)/shard_map/ppermute | solution.py:76
  142.7 19.8 %collective-permute-start.26 = (f32[32,1024]{1,0:T(8,128)S(1)}, f32[32,1024]{1,0:T(8,128)S(1)}, u32[]{:S(2)}, u32[]{:S(2)}) collective-permute-start(f32[32,1024]{1,0:T(8,128)S(1)} %get-tuple-element.91), channel_id=1, source_target_pairs={{0,24},{1,25},{2,26},{3,27},{4,28},{5,29},{6,30},{7,31},{8,16},{9,... | collective-permute-start | bytes 393224 | tf_op jit(solution)/shard_map/ppermute | solution.py:76
  145.9 16.6 %collective-permute-start.25 = (f32[32,1280]{1,0:T(8,128)S(1)}, f32[32,1280]{1,0:T(8,128)S(1)}, u32[]{:S(2)}, u32[]{:S(2)}) collective-permute-start(f32[32,1280]{1,0:T(8,128)S(1)} %get-tuple-element.90), channel_id=1, source_target_pairs={{0,24},{1,25},{2,26},{3,27},{4,28},{5,29},{6,30},{7,31},{8,16},{9,... | collective-permute-start | bytes 491528 | tf_op jit(solution)/shard_map/ppermute | solution.py:76
  150.5 13.7 %collective-permute-start.24 = (f32[32,1280]{1,0:T(8,128)S(1)}, f32[32,1280]{1,0:T(8,128)S(1)}, u32[]{:S(2)}, u32[]{:S(2)}) collective-permute-start(f32[32,1280]{1,0:T(8,128)S(1)} %get-tuple-element.89), channel_id=1, source_target_pairs={{0,8},{1,9},{2,10},{3,11},{4,12},{5,13},{6,14},{7,15},{8,0},{9,1},... | collective-permute-start | bytes 491528 | tf_op jit(solution)/shard_map/ppermute | solution.py:76
  (6 other events, 31.7 us)

commit v7 on v6

--- a/solution.py
+++ b/solution.py
@@ -137,20 +137,25 @@
     return whole_call(kernel, [array], [shape], "hold_back", (after,))[0]
 
 
-def gather_cube(tokens, others):
+def gather_cube(tokens, side, gate, up, down):
     steps = len(LINKS)
+    others = [swap_cores(gate), swap_cores(up)]
     held = [tokens[:, start:stop] for start, stop in piece_columns(tokens.shape[1])]
+    held[-1] = jnp.concatenate([held[-1], side], axis=1)
     for phase in range(steps):
         got = [across(piece, order[steps - 1 - phase]) for piece, order in zip(held, ORDERS)]
         if phase < steps - 1:
             held = joined(held, got, others if phase == 1 else ())
-    return held, got
-
-
-def hidden_kernel(unit, *refs):
+        if phase == 1:
+            others.append(swap_cores(hold_back(down, held[0])))
+    return held, got, others
+
+
+def hidden_kernel(unit, chip_ref, *refs):
     count = len(ORDERS)
     held, got = refs[:count], refs[count : 2 * count]
-    gate_ref, up_ref, gate_other_ref, up_other_ref, hidden_ref, rows_ref = refs[2 * count :]
+    gate_ref, up_ref, gate_other_ref, up_other_ref = refs[2 * count : 2 * count + 4]
+    hidden_ref, scale_ref, rows_ref, side_ref = refs[2 * count + 4 :]
     step = pl.program_id(0)
     own_steps = pl.num_programs(0) // 2
 
@@ -162,7 +167,15 @@
                 source = held[piece] if place * unit < half else got[piece]
                 at = place * unit % half
                 slot = slot_of(place, ORDERS[piece])
-                rows_ref[slot * unit : (slot + 1) * unit, start:stop] = source[at : at + unit]
+                to = slice(slot * unit, (slot + 1) * unit)
+                rows_ref[to, start:stop] = source[at : at + unit, : stop - start]
+                if piece == count - 1:
+                    side_ref[to, :] = source[at : at + unit, stop - start :]
+        column = lax.broadcasted_iota(jnp.int32, side_ref.shape, 1)
+        experts = 1 << len(LINKS)
+        mine = jnp.logical_and(column % experts == chip_ref[0], column < 3 * experts)
+        parts = jnp.where(mine, side_ref[...].astype(jnp.float32), 0.0)
+        scale_ref[...] = jnp.sum(parts, axis=1, keepdims=True)
 
     def units(gate_tile, up_tile):
         rows = rows_ref[...]
@@ -179,7 +192,7 @@
         units(gate_other_ref, up_other_ref)
 
 
-def expert_hidden(unit, held, got, gate, up, gate_other, up_other):
+def expert_hidden(unit, chip, held, got, gate, up, gate_other, up_other):
     width, units = gate.shape
     count = 2 * held[0].shape[0]
     tile = 256
@@ -189,19 +202,29 @@
     return pl.pallas_call(
         functools.partial(hidden_kernel, unit),
         grid=(2 * steps,),
-        in_specs=[pl.BlockSpec(array.shape, lambda i: (0, 0)) for array in (*held, *got)]
+        in_specs=[pl.BlockSpec(memory_space=pltpu.SMEM)]
+        + [pl.BlockSpec(array.shape, lambda i: (0, 0)) for array in (*held, *got)]
         + [own, own, other, other],
-        out_specs=pl.BlockSpec((count, tile), lambda i: (0, i)),
-        out_shape=jax.ShapeDtypeStruct((count, 2 * units), jnp.bfloat16),
-        scratch_shapes=[pltpu.VMEM((count, width), jnp.bfloat16)],
-        compiler_params=pltpu.CompilerParams(vmem_limit_bytes=48 * MIB),
+        out_specs=[
+            pl.BlockSpec((count, tile), lambda i: (0, i)),
+            pl.BlockSpec((count, 1), lambda i: (0, 0)),
+        ],
+        out_shape=[
+            jax.ShapeDtypeStruct((count, 2 * units), jnp.bfloat16),
+            jax.ShapeDtypeStruct((count, 1), jnp.float32),
+        ],
+        scratch_shapes=[
+            pltpu.VMEM((count, width), jnp.bfloat16),
+            pltpu.VMEM((count, sum(piece.shape[1] for piece in held) - width), jnp.bfloat16),
+        ],
+        compiler_params=pltpu.CompilerParams(vmem_limit_bytes=38 * MIB),
         cost_estimate=pl.CostEstimate(
             flops=8 * count * width * units,
             bytes_accessed=2 * (count * width + 4 * width * units + 2 * count * units),
             transcendentals=2 * count * units,
         ),
         name="expert_hidden",
-    )(*held, *got, gate, up, gate_other, up_other)
+    )(chip, *held, *got, gate, up, gate_other, up_other)
 
 
 def output_kernel(
@@ -218,12 +241,11 @@
             rows_ref[to, :] = hidden_ref[source, :]
             factor_ref[to, :] = scale_ref[source, :]
 
-    for out_ref, part in ((send_ref, pl.ds(half, half)), (keep_ref, pl.ds(0, half))):
-        out = jnp.dot(rows_ref[part, :units], down_ref[...], preferred_element_type=jnp.float32)
-        out += jnp.dot(
-            rows_ref[part, units:], down_other_ref[...], preferred_element_type=jnp.float32
-        )
-        out_ref[...] = out * factor_ref[part, :]
+    out = jnp.dot(rows_ref[:, :units], down_ref[...], preferred_element_type=jnp.float32)
+    out += jnp.dot(rows_ref[:, units:], down_other_ref[...], preferred_element_type=jnp.float32)
+    out = out * factor_ref[...]
+    keep_ref[...] = out[:half]
+    send_ref[...] = out[half:]
 
 
 def expert_output(unit, order, columns, scale, hidden, down, down_other):
@@ -281,33 +303,32 @@
     return whole_call(kernel, [*keep, *got], [shape], "finished")[0]
 
 
-def cube_experts(unit, gathered, share, weights, others):
-    count = len(LINKS)
-    peers = lax.axis_size("ep")
+def cube_outputs(unit, held, got, weights, others):
     gate, up, down = weights
     gate_other, up_other, down_other = others
-    steps = []
-    for slot in range(peers // 2):
-        step = 0
-        for link in range(count):
-            step ^= LINKS[link] * ((slot >> link) & 1)
-        steps.append(2 * step)
-    source = jnp.bitwise_xor(lax.axis_index("ep"), jnp.array(steps, jnp.int32))
-    picks = source[:, None] == jnp.arange(peers, dtype=jnp.int32)[None, :]
-    scale = jnp.sum(jnp.where(picks[:, :, None], share[None, :, :], 0.0), axis=1)
-    scale = scale.reshape(peers // 2 * unit, 1)
-
-    hidden = expert_hidden(unit, *gathered, gate, up, gate_other, up_other)
-    keep, got = [], []
+    chip = (lax.axis_index("ep") // 2).astype(jnp.int32).reshape(1)
+    hidden, scale = expert_hidden(unit, chip, held, got, gate, up, gate_other, up_other)
+    keep, coming = [], []
     for order, columns in zip(ORDERS, piece_columns(down.shape[1])):
         mine, send = expert_output(unit, order, columns, scale, hidden, down, down_other)
         keep.append(mine)
-        got.append(across(send, order[0]))
-    for phase in range(1, count):
+        coming.append(across(send, order[0]))
+    return keep, coming
+
+
+def cube_sums(keep, got):
+    keep, got = list(keep), list(got)
+    for phase in range(1, len(LINKS)):
         for at, order in enumerate(ORDERS):
             keep[at], send = halved(keep[at], got[at])
             got[at] = across(send, order[phase])
     return finished(keep, got)
+
+
+def three_parts(value):
+    high = lax.reduce_precision(value, 8, 7)
+    middle = lax.reduce_precision(value - high, 8, 7)
+    return high, middle, value - high - middle
 
 
 def per_device(
@@ -341,28 +362,30 @@
         preferred_element_type=jnp.float32,
     ).astype(jnp.bfloat16)
 
-    expert_of = jnp.arange(peers, dtype=jnp.int32) // 2
-    named = expert_ids[None, :, :] == expert_of[:, None, None]
-    share = jnp.sum(jnp.where(named, route_weight[None, :, :], 0.0), axis=2)
-    high = lax.reduce_precision(share, 8, 7)
-    middle = lax.reduce_precision(share - high, 8, 7)
-    low = share - high - middle
+    cube = peers == 2 << len(LINKS) and lax.axis_size("tp") == 1
+    weights = (gate_weight[0], up_weight[0], down_weight[0])
     filled = jnp.sum(chosen.astype(jnp.float32), axis=1).reshape(peers, 1, 2)
     side = jnp.zeros((peers, 2 * block_len, max(tok_rows, 2)), jnp.float32)
-    side = side.at[:, :3, :tok_rows].set(jnp.stack([high, middle, low], axis=1))
     side = side.at[:, 3:4, :2].set(filled)
+    if not cube:
+        expert_of = jnp.arange(peers, dtype=jnp.int32) // 2
+        named = expert_ids[None, :, :] == expert_of[:, None, None]
+        share = jnp.sum(jnp.where(named, route_weight[None, :, :], 0.0), axis=2)
+        side = side.at[:, :3, :tok_rows].set(jnp.stack(three_parts(share), axis=1))
     leaving = jnp.concatenate(
         [packed.reshape(peers, 2 * block_len, latent), side.astype(jnp.bfloat16)], axis=2
     )
-    cube = peers == 2 << len(LINKS) and lax.axis_size("tp") == 1
-    weights = (gate_weight[0], up_weight[0], down_weight[0])
     if cube:
-        others = [swap_cores(weight) for weight in weights]
-        gathered = gather_cube(tokens, others)
-        leaving = hold_back(leaving, gathered[0][0])
+        experts = jnp.arange(peers // 2, dtype=jnp.int32)
+        named = expert_ids[:, :, None] == experts[None, None, :]
+        share = jnp.sum(jnp.where(named, route_weight[:, :, None], 0.0), axis=1)
+        parts = jnp.concatenate(three_parts(share), axis=1).astype(jnp.bfloat16)
+        parts = jnp.pad(parts, ((0, 0), (0, 128 - parts.shape[1])))
+        *gathered, others = gather_cube(tokens, parts, *weights)
+        keep, coming = cube_outputs(tok_rows, *gathered, weights, others)
+        leaving = hold_back(leaving, keep[-1])
     arrived = lax.all_to_all(leaving, "ep", split_axis=0, concat_axis=0, tiled=True)
     side_in = arrived[:, :, latent:].astype(jnp.float32)
-    share_in = side_in[:, 0, :tok_rows] + side_in[:, 1, :tok_rows] + side_in[:, 2, :tok_rows]
     present = side_in[:, 3, :2].reshape(peers * 2)
     arrived = arrived[:, :, :latent]
     shard_len = latent_cache.shape[1]
@@ -376,8 +399,9 @@
     attn_out = (mixed / total[:, None]).astype(jnp.bfloat16)[None]
 
     if cube:
-        moe_out = cube_experts(tok_rows, gathered, share_in, weights, others)
+        moe_out = cube_sums(keep, coming)
     else:
+        share_in = jnp.sum(side_in[:, :3, :tok_rows], axis=1)
         moe_out = ring_experts(tokens, share_in, gate_weight, up_weight, down_weight)
     return (attn_out, moe_out)
 

time: 166 us -> 161 us (0.970)
  starting transfers between devices: 56.4 us -> 42.9 us
  local copies, waits for them, and re-layouts: 10.2 us -> 19.8 us
  waiting for transfers between devices: 57.5 us -> 50.2 us
  Pallas kernels: 31.7 us -> 37.1 us
    ppermute x24, starting transfers between devices: 50.7 us -> 38 us  [across(): lax.ppermute(value, 'ep', [(i, i ^ 2 * LINKS[link]) for i in range(peers)])]
    unnamed x20 -> x34, local copies, waits for them, and re-layouts: 1.43 us -> 10.5 us
    all_to_all x1, waiting for transfers between devices: 6.95 us -> 0.01 us  [per_device(): lax.all_to_all(leaving, 'ep', split_axis=0, concat_axis=0, tiled=True)]
    pallas_call x14 -> x15, Pallas kernels: 5.94 us -> 10.7 us  [whole_call(): pl.pallas_call(body, in_specs=[pl.BlockSpec(memory_space=pltpu.VMEM)] * g...]
    pallas_call x3, Pallas kernels: 12.4 us -> 15 us  [expert_output(): pl.pallas_call(functools.partial(output_kernel, unit, order), grid=((stop...]
    pallas_call x1, Pallas kernels: 13.3 us -> 11.4 us  [expert_hidden(): pl.pallas_call(functools.partial(hidden_kernel, unit), grid=(2 * steps,),...]
    reshape x2, local copies, waits for them, and re-layouts: 3.57 us -> 1.89 us  [per_device(): arrived.reshape(peers * 2 * block_len, latent)]
    reshape x1, local copies, waits for them, and re-layouts: 0.39 us -> 2.06 us  [per_device(): packed.reshape(peers, 2 * block_len, latent)]
  transfers between devices with their start and end apart: 28 -> 28, of which waited for: 15 -> 14; matrix products, arithmetic and copies ran while one was open for 10% -> 11% of each run, Pallas kernels for 7% -> 18%
where the time goes in v7:
time: 161 us; the launch traced here: 160 us
  waiting for transfers between devices  50.2 us (31%)
  starting transfers between devices  42.9 us (27%)
  Pallas kernels  37.1 us (23%)
  local copies, waits for them, and re-layouts  19.8 us (12%)
  matrix products  4.25 us (3%)
  other arithmetic  3.95 us (2%)
    ppermute x24, waiting for transfers between devices, across(): lax.ppermute(value, 'ep', [(i, i ^ 2 * LINKS[link]) for i in range(peers)])  50.2 us
    ppermute x24, starting transfers between devices, across(): lax.ppermute(value, 'ep', [(i, i ^ 2 * LINKS[link]) for i in range(peers)])  38 us
    pallas_call x3, Pallas kernels, expert_output(): pl.pallas_call(functools.partial(output_kernel, unit, order), grid=((stop...  15 us
    pallas_call x1, Pallas kernels, expert_hidden(): pl.pallas_call(functools.partial(hidden_kernel, unit), grid=(2 * steps,),...  11.4 us
    pallas_call x15, Pallas kernels, whole_call(): pl.pallas_call(body, in_specs=[pl.BlockSpec(memory_space=pltpu.VMEM)] * g...  10.7 us
    unnamed x34, local copies, waits for them, and re-layouts  10.5 us
    all_to_all x1, starting transfers between devices, per_device(): lax.all_to_all(leaving, 'ep', split_axis=0, concat_axis=0, tiled=True)  4.3 us
  transfers between devices with their start and end apart: 28, of which 14 were waited for; matrix products, arithmetic and copies ran while one was open for 11% of the time, Pallas kernels for 18%

profile of v7, /device:TPU:0, one launch (start us, length us, event | category | flops | bytes accessed | tf_op | source)
XLA Modules:
  0.0 159.6 jit_solution(2341010806741749792)
XLA Ops:
  2.2 3.1 %collective-permute-start = (bf16[32,1280]{1,0:T(8,128)(2,1)S(1)}, bf16[32,1280]{1,0:T(8,128)(2,1)S(1)}, u32[]{:S(2)}, u32[]{:S(2)}) collective-permute-start(bf16[32,1280]{1,0:T(8,128)(2,1)S(1)} %get-tuple-element.85.refs_0_), channel_id=1, source_target_pairs={{0,8},{1,9},{2,10},{3,11},{4,12},{5,13},{6,14},{7,15},{8,0},{9,1},... | collective-permute-start | bytes 245768 | tf_op jit(solution)/shard_map/ppermute | solution.py:76
  5.3 2.5 %collective-permute-start.1 = (bf16[32,1280]{1,0:T(8,128)(2,1)S(1)}, bf16[32,1280]{1,0:T(8,128)(2,1)S(1)}, u32[]{:S(2)}, u32[]{:S(2)}) collective-permute-start(bf16[32,1280]{1,0:T(8,128)(2,1)S(1)} %get-tuple-element.84.refs_1_), channel_id=1, source_target_pairs={{0,24},{1,25},{2,26},{3,27},{4,28},{5,29},{6,30},{7,31},{8,16},{9,... | collective-permute-start | bytes 245768 | tf_op jit(solution)/shard_map/ppermute | solution.py:76
  11.0 4.8 %collective-permute-done.2.refs_5_ = bf16[32,1152]{1,0:T(8,128)(2,1)S(1)} collective-permute-done((bf16[32,1152]{1,0:T(8,128)(2,1)S(1)}, bf16[32,1152]{1,0:T(8,128)(2,1)S(1)}, u32[]{:S(2)}, u32[]{:S(2)}) %collective-permute-start.2) | collective-permute-done | bytes 73760 | tf_op jit(solution)/shard_map/ppermute | solution.py:76
  15.8 1.5 collective-permute-start.3
  17.3 1.5 collective-permute-start.4
  20.3 3.7 %collective-permute-done.5.refs_5_ = bf16[64,1152]{1,0:T(8,128)(2,1)S(1)} collective-permute-done((bf16[64,1152]{1,0:T(8,128)(2,1)S(1)}, bf16[64,1152]{1,0:T(8,128)(2,1)S(1)}, u32[]{:S(2)}, u32[]{:S(2)}) %collective-permute-start.5) | collective-permute-done | bytes 147488 | tf_op jit(solution)/shard_map/ppermute | solution.py:76
  24.1 2.0 %copy-done.1 = bf16[1,512,3584]{2,1,0:T(8,128)(2,1)S(1)} copy-done((bf16[1,512,3584]{2,1,0:T(8,128)(2,1)S(1)}, bf16[1,512,3584]{2,1,0:T(8,128)(2,1)}, u32[]{:S(2)}) %copy-start.1) | copy-done | bytes 3670040
  26.1 2.0 %hold_back.2 = bf16[512,3584]{1,0:T(8,128)(2,1)} custom-call(bf16[512,3584]{1,0:T(8,128)(2,1)S(1)} %bitcast.19, bf16[128,1280]{1,0:T(8,128)(2,1)S(1)} %get-tuple-element.52.refs_0_.refs_1_), custom_call_target="tpu_custom_call" | custom-call | bytes 7340032 | tf_op jit(solution)/shard_map/hold_back/pallas_call | solution.py:103
  31.5 7.3 %collective-permute-done.10.refs_5_ = bf16[128,1152]{1,0:T(8,128)(2,1)S(1)} collective-permute-done((bf16[128,1152]{1,0:T(8,128)(2,1)S(1)}, bf16[128,1152]{1,0:T(8,128)(2,1)S(1)}, u32[]{:S(2)}, u32[]{:S(2)}) %collective-permute-start.10) | collective-permute-done | bytes 294944 | tf_op jit(solution)/shard_map/ppermute | solution.py:76
  42.1 13.0 %collective-permute-done.13.refs_5_ = bf16[256,1152]{1,0:T(8,128)(2,1)} collective-permute-done((bf16[256,1152]{1,0:T(8,128)(2,1)S(1)}, bf16[256,1152]{1,0:T(8,128)(2,1)}, u32[]{:S(2)}, u32[]{:S(2)}) %collective-permute-start.13) | collective-permute-done | bytes 589856 | tf_op jit(solution)/shard_map/ppermute | solution.py:76
  56.0 2.0 %copy-done.11 = bf16[1,3584,512]{2,1,0:T(8,128)(2,1)S(1)} copy-done((bf16[1,3584,512]{2,1,0:T(8,128)(2,1)S(1)}, bf16[1,3584,512]{2,1,0:T(8,128)(2,1)}, u32[]{:S(2)}) %copy-start.11) | copy-done | bytes 3670040
  58.0 2.0 %copy-done.12 = bf16[1,3584,512]{2,1,0:T(8,128)(2,1)S(1)} copy-done((bf16[1,3584,512]{2,1,0:T(8,128)(2,1)S(1)}, bf16[1,3584,512]{2,1,0:T(8,128)(2,1)}, u32[]{:S(2)}) %copy-start.12) | copy-done | bytes 3670040
  60.1 11.4 %expert_hidden.1 = (bf16[512,1024]{1,0:T(8,128)(2,1)S(1)}, f32[512,1]{1,0:T(8,128)S(1)}) custom-call(s32[1]{0:T(128)} %bitcast.2.chip_ref, bf16[256,1280]{1,0:T(8,128)(2,1)S(1)} %get-tuple-element.55.refs_0_, bf16[256,1280]{1,0:T(8,128)(2,1)S(1)} %get-tuple-element.56.refs_1_, bf16[256,1152]{1,0:T(8,128)(2,1)S(1)} %get-tuple-element.57.refs_2_, ...), custom_call_target="tpu_custom_call" | custom-call | flops 7516192768 | bytes 19398656 | tf_op jit(solution)/shard_map/expert_hidden/pallas_call | solution.py:202
  71.6 5.3 %expert_output.4 = (f32[256,1280]{1,0:T(8,128)S(1)}, f32[256,1280]{1,0:T(8,128)}) custom-call(f32[512,1]{1,0:T(8,128)S(1)} %get-tuple-element.58.scale_ref, bf16[512,1024]{1,0:T(8,128)(2,1)S(1)} %get-tuple-element.59.hidden_ref, bf16[512,3584]{1,0:T(8,128)(2,1)S(1)} %bitcast.20, bf16[512,3584]{1,0:T(8,128)(2,1)} %collective-permute-done.14.down_other_ref), custom_call_target="tpu_custom_call" | custom-call | flops 1342177280 | bytes 6291456 | tf_op jit(solution)/shard_map/expert_output/pallas_call | solution.py:257
  78.2 5.3 %expert_output.5 = (f32[256,1280]{1,0:T(8,128)S(1)}, f32[256,1280]{1,0:T(8,128)}) custom-call(f32[512,1]{1,0:T(8,128)S(1)} %get-tuple-element.58.scale_ref, bf16[512,1024]{1,0:T(8,128)(2,1)S(1)} %get-tuple-element.59.hidden_ref, bf16[512,3584]{1,0:T(8,128)(2,1)S(1)} %bitcast.21, bf16[512,3584]{1,0:T(8,128)(2,1)} %collective-permute-done.14.down_other_ref), custom_call_target="tpu_custom_call" | custom-call | flops 1342177280 | bytes 6291456 | tf_op jit(solution)/shard_map/expert_output/pallas_call | solution.py:257
  84.3 4.4 %expert_output.3 = (f32[256,1024]{1,0:T(8,128)S(1)}, f32[256,1024]{1,0:T(8,128)}) custom-call(f32[512,1]{1,0:T(8,128)S(1)} %get-tuple-element.58.scale_ref, bf16[512,1024]{1,0:T(8,128)(2,1)S(1)} %get-tuple-element.59.hidden_ref, bf16[512,3584]{1,0:T(8,128)(2,1)S(1)} %bitcast.22, bf16[512,3584]{1,0:T(8,128)(2,1)} %collective-permute-done.14.down_other_ref), custom_call_target="tpu_custom_call" | custom-call | flops 1073741824 | bytes 5242880 | tf_op jit(solution)/shard_map/expert_output/pallas_call | solution.py:257
  91.9 1.8 %reshape.85 = bf16[32,2304]{1,0:T(8,128)(2,1)} reshape(bf16[1,32,4,576]{3,2,1,0:T(4,128)(2,1)} %param.16) | data formatting | bytes 294912 | tf_op jit(solution)/shard_map/reshape | solution.py:361
  93.7 2.0 %convolution_convert_fusion = bf16[64,2304]{1,0:T(8,128)(2,1)} fusion(bf16[32,2304]{1,0:T(8,128)(2,1)} %reshape.85, s32[32]{0:T(128)} %copy-done.14), kind=kOutput, calls=%fused_computation | convolution fusion | flops 9586688 | bytes 442496 | tf_op jit(solution)/shard_map/dot_general | solution.py:359
  95.7 2.1 %reshape.86 = bf16[32,8,576]{2,1,0:T(8,128)(2,1)} reshape(bf16[64,2304]{1,0:T(8,128)(2,1)} %convolution_convert_fusion) | data formatting | bytes 589824 | tf_op jit(solution)/shard_map/reshape | solution.py:376
  99.6 4.3 %all-to-all-start = ((bf16[32,8,608]{2,1,0:T(8,128)(2,1)}), bf16[32,8,608]{2,1,0:T(8,128)(2,1)}, u32[]{:S(2)}, u32[]{:S(2)}) async-start(bf16[32,8,608]{2,1,0:T(8,128)(2,1)} %hold_back.3), calls=%async_computation | async-start | bytes 655360 | tf_op jit(solution)/shard_map/all_to_all | solution.py:387
  103.9 2.2 %collective-permute-done.15.refs_1_ = f32[256,1280]{1,0:T(8,128)} collective-permute-done((f32[256,1280]{1,0:T(8,128)}, f32[256,1280]{1,0:T(8,128)}, u32[]{:S(2)}, u32[]{:S(2)}) %collective-permute-start.15) | collective-permute-done | bytes 1310752 | tf_op jit(solution)/shard_map/ppermute | solution.py:76
  107.4 2.3 %halved.9 = (f32[128,1280]{1,0:T(8,128)S(1)}, f32[128,1280]{1,0:T(8,128)}) custom-call(f32[256,1280]{1,0:T(8,128)S(1)} %copy-done.4, f32[256,1280]{1,0:T(8,128)} %collective-permute-done.15.refs_1_), custom_call_target="tpu_custom_call" | custom-call | bytes 3932160 | tf_op jit(solution)/shard_map/halved/pallas_call | solution.py:103
  111.3 6.4 %collective-permute-done.18.refs_1_ = f32[256,1280]{1,0:T(8,128)} collective-permute-done((f32[256,1280]{1,0:T(8,128)}, f32[256,1280]{1,0:T(8,128)}, u32[]{:S(2)}, u32[]{:S(2)}) %collective-permute-start.18) | collective-permute-done | bytes 1310752 | tf_op jit(solution)/shard_map/ppermute | solution.py:76
  117.6 2.3 %halved.12 = (f32[128,1280]{1,0:T(8,128)S(1)}, f32[128,1280]{1,0:T(8,128)}) custom-call(f32[256,1280]{1,0:T(8,128)S(1)} %get-tuple-element.68.refs_0_, f32[256,1280]{1,0:T(8,128)} %collective-permute-done.18.refs_1_), custom_call_target="tpu_custom_call" | custom-call | bytes 3932160 | tf_op jit(solution)/shard_map/halved/pallas_call | solution.py:103
  127.6 5.0 %collective-permute-done.22.refs_1_ = f32[128,1024]{1,0:T(8,128)S(1)} collective-permute-done((f32[128,1024]{1,0:T(8,128)}, f32[128,1024]{1,0:T(8,128)S(1)}, u32[]{:S(2)}, u32[]{:S(2)}) %collective-permute-start.22) | collective-permute-done | bytes 524320 | tf_op jit(solution)/shard_map/ppermute | solution.py:76
  134.0 2.1 %collective-permute-start.17 = (f32[64,1280]{1,0:T(8,128)S(1)}, f32[64,1280]{1,0:T(8,128)S(1)}, u32[]{:S(2)}, u32[]{:S(2)}) collective-permute-start(f32[64,1280]{1,0:T(8,128)S(1)} %get-tuple-element.66), channel_id=1, source_target_pairs={{0,24},{1,25},{2,26},{3,27},{4,28},{5,29},{6,30},{7,31},{8,16},{9,... | collective-permute-start | bytes 983048 | tf_op jit(solution)/shard_map/ppermute | solution.py:76
  139.1 2.1 %collective-permute-start.26 = (f32[32,1024]{1,0:T(8,128)S(1)}, f32[32,1024]{1,0:T(8,128)S(1)}, u32[]{:S(2)}, u32[]{:S(2)}) collective-permute-start(f32[32,1024]{1,0:T(8,128)S(1)} %get-tuple-element.83), channel_id=1, source_target_pairs={{0,24},{1,25},{2,26},{3,27},{4,28},{5,29},{6,30},{7,31},{8,16},{9,... | collective-permute-start | bytes 393224 | tf_op jit(solution)/shard_map/ppermute | solution.py:76
  141.2 1.9 %collective-permute-done.17.refs_1_ = f32[64,1280]{1,0:T(8,128)S(1)} collective-permute-done((f32[64,1280]{1,0:T(8,128)S(1)}, f32[64,1280]{1,0:T(8,128)S(1)}, u32[]{:S(2)}, u32[]{:S(2)}) %collective-permute-start.17) | collective-permute-done | bytes 327712 | tf_op jit(solution)/shard_map/ppermute | solution.py:76
  143.2 8.5 %collective-permute-start.24 = (f32[32,1280]{1,0:T(8,128)S(1)}, f32[32,1280]{1,0:T(8,128)S(1)}, u32[]{:S(2)}, u32[]{:S(2)}) collective-permute-start(f32[32,1280]{1,0:T(8,128)S(1)} %get-tuple-element.81), channel_id=1, source_target_pairs={{0,8},{1,9},{2,10},{3,11},{4,12},{5,13},{6,14},{7,15},{8,0},{9,1},... | collective-permute-start | bytes 491528 | tf_op jit(solution)/shard_map/ppermute | solution.py:76
  151.7 2.0 %collective-permute-start.25 = (f32[32,1280]{1,0:T(8,128)S(1)}, f32[32,1280]{1,0:T(8,128)S(1)}, u32[]{:S(2)}, u32[]{:S(2)}) collective-permute-start(f32[32,1280]{1,0:T(8,128)S(1)} %get-tuple-element.82), channel_id=1, source_target_pairs={{0,24},{1,25},{2,26},{3,27},{4,28},{5,29},{6,30},{7,31},{8,16},{9,... | collective-permute-start | bytes 491528 | tf_op jit(solution)/shard_map/ppermute | solution.py:76
  153.7 1.5 fusion.14
  155.9 3.0 %collective-permute-done.25.refs_4_ = f32[32,1280]{1,0:T(8,128)S(1)} collective-permute-done((f32[32,1280]{1,0:T(8,128)S(1)}, f32[32,1280]{1,0:T(8,128)S(1)}, u32[]{:S(2)}, u32[]{:S(2)}) %collective-permute-start.25) | collective-permute-done | bytes 163872 | tf_op jit(solution)/shard_map/ppermute | solution.py:76
  (105 shorter events, 36.9 us)
Async XLA Ops:
  0.6 136.8 %copy-start = (bf16[1,128,576]{1,2,0:T(8,128)(2,1)S(1)}, bf16[1,128,576]{1,2,0:T(8,128)(2,1)}, u32[]{:S(2)}) copy-start(bf16[1,128,576]{1,2,0:T(8,128)(2,1)} %param.13) | copy-start | bytes 442372
  0.6 23.4 %collective-permute-start.6 = (bf16[3584,512]{1,0:T(8,128)(2,1)}, bf16[3584,512]{1,0:T(8,128)(2,1)}, u32[]{:S(2)}, u32[]{:S(2)}) collective-permute-start(bf16[3584,512]{1,0:T(8,128)(2,1)} %bitcast.23), channel_id=1, source_target_pairs={{0,1},{1,0},{2,3},{3,2},{4,5},{5,4},{6,7},{7,6},{8,9},{9,8},{10,11... | collective-permute-start | bytes 11010056 | tf_op jit(solution)/shard_map/ppermute | solution.py:80
  1.2 22.9 %collective-permute-start.7 = (bf16[3584,512]{1,0:T(8,128)(2,1)}, bf16[3584,512]{1,0:T(8,128)(2,1)}, u32[]{:S(2)}, u32[]{:S(2)}) collective-permute-start(bf16[3584,512]{1,0:T(8,128)(2,1)} %bitcast.25), channel_id=1, source_target_pairs={{0,1},{1,0},{2,3},{3,2},{4,5},{5,4},{6,7},{7,6},{8,9},{9,8},{10,11... | collective-permute-start | bytes 11010056 | tf_op jit(solution)/shard_map/ppermute | solution.py:80
  2.2 13.6 %collective-permute-start = (bf16[32,1280]{1,0:T(8,128)(2,1)S(1)}, bf16[32,1280]{1,0:T(8,128)(2,1)S(1)}, u32[]{:S(2)}, u32[]{:S(2)}) collective-permute-start(bf16[32,1280]{1,0:T(8,128)(2,1)S(1)} %get-tuple-element.85.refs_0_), channel_id=1, source_target_pairs={{0,8},{1,9},{2,10},{3,11},{4,12},{5,13},{6,14},{7,15},{8,0},{9,1},... | collective-permute-start | bytes 245768 | tf_op jit(solution)/shard_map/ppermute | solution.py:76
  5.3 10.5 %collective-permute-start.1 = (bf16[32,1280]{1,0:T(8,128)(2,1)S(1)}, bf16[32,1280]{1,0:T(8,128)(2,1)S(1)}, u32[]{:S(2)}, u32[]{:S(2)}) collective-permute-start(bf16[32,1280]{1,0:T(8,128)(2,1)S(1)} %get-tuple-element.84.refs_1_), channel_id=1, source_target_pairs={{0,24},{1,25},{2,26},{3,27},{4,28},{5,29},{6,30},{7,31},{8,16},{9,... | collective-permute-start | bytes 245768 | tf_op jit(solution)/shard_map/ppermute | solution.py:76
  9.6 6.2 %collective-permute-start.2 = (bf16[32,1152]{1,0:T(8,128)(2,1)S(1)}, bf16[32,1152]{1,0:T(8,128)(2,1)S(1)}, u32[]{:S(2)}, u32[]{:S(2)}) collective-permute-start(bf16[32,1152]{1,0:T(8,128)(2,1)S(1)} %pad_maximum_fusion.refs_2_), channel_id=1, source_target_pairs={{0,24},{1,25},{2,26},{3,27},{4,28},{5,29},{6,30},{7,31},{8,16},{9,... | collective-permute-start | bytes 221192 | tf_op jit(solution)/shard_map/ppermute | solution.py:76
  15.8 8.2 %collective-permute-start.3 = (bf16[64,1280]{1,0:T(8,128)(2,1)S(1)}, bf16[64,1280]{1,0:T(8,128)(2,1)S(1)}, u32[]{:S(2)}, u32[]{:S(2)}) collective-permute-start(bf16[64,1280]{1,0:T(8,128)(2,1)S(1)} %get-tuple-element.49.refs_0_), channel_id=1, source_target_pairs={{0,24},{1,25},{2,26},{3,27},{4,28},{5,29},{6,30},{7,31},{8,16},{9,... | collective-permute-start | bytes 491528 | tf_op jit(solution)/shard_map/ppermute | solution.py:76
  17.3 6.7 %collective-permute-start.4 = (bf16[64,1280]{1,0:T(8,128)(2,1)S(1)}, bf16[64,1280]{1,0:T(8,128)(2,1)S(1)}, u32[]{:S(2)}, u32[]{:S(2)}) collective-permute-start(bf16[64,1280]{1,0:T(8,128)(2,1)S(1)} %get-tuple-element.50.refs_1_), channel_id=1, source_target_pairs={{0,4},{1,5},{2,6},{3,7},{4,0},{5,1},{6,2},{7,3},{8,12},{9,13},{10,... | collective-permute-start | bytes 491528 | tf_op jit(solution)/shard_map/ppermute | solution.py:76
  18.9 5.1 %collective-permute-start.5 = (bf16[64,1152]{1,0:T(8,128)(2,1)S(1)}, bf16[64,1152]{1,0:T(8,128)(2,1)S(1)}, u32[]{:S(2)}, u32[]{:S(2)}) collective-permute-start(bf16[64,1152]{1,0:T(8,128)(2,1)S(1)} %get-tuple-element.51.refs_2_), channel_id=1, source_target_pairs={{0,2},{1,3},{2,0},{3,1},{4,6},{5,7},{6,4},{7,5},{8,10},{9,11},{10,... | collective-permute-start | bytes 442376 | tf_op jit(solution)/shard_map/ppermute | solution.py:76
  28.1 43.4 %collective-permute-start.14 = (bf16[512,3584]{1,0:T(8,128)(2,1)}, bf16[512,3584]{1,0:T(8,128)(2,1)}, u32[]{:S(2)}, u32[]{:S(2)}) collective-permute-start(bf16[512,3584]{1,0:T(8,128)(2,1)} %hold_back.2), channel_id=1, source_target_pairs={{0,1},{1,0},{2,3},{3,2},{4,5},{5,4},{6,7},{7,6},{8,9},{9,8},{10,11... | collective-permute-start | bytes 11010056 | tf_op jit(solution)/shard_map/ppermute | solution.py:80
  28.1 10.7 %collective-permute-start.8 = (bf16[128,1280]{1,0:T(8,128)(2,1)S(1)}, bf16[128,1280]{1,0:T(8,128)(2,1)S(1)}, u32[]{:S(2)}, u32[]{:S(2)}) collective-permute-start(bf16[128,1280]{1,0:T(8,128)(2,1)S(1)} %get-tuple-element.52.refs_0_.refs_1_), channel_id=1, source_target_pairs={{0,2},{1,3},{2,0},{3,1},{4,6},{5,7},{6,4},{7,5},{8,10},{9,11},{10,... | collective-permute-start | bytes 983048 | tf_op jit(solution)/shard_map/ppermute | solution.py:76
  29.6 9.8 %collective-permute-start.9 = (bf16[128,1280]{1,0:T(8,128)(2,1)S(1)}, bf16[128,1280]{1,0:T(8,128)(2,1)S(1)}, u32[]{:S(2)}, u32[]{:S(2)}) collective-permute-start(bf16[128,1280]{1,0:T(8,128)(2,1)S(1)} %get-tuple-element.53.refs_1_), channel_id=1, source_target_pairs={{0,8},{1,9},{2,10},{3,11},{4,12},{5,13},{6,14},{7,15},{8,0},{9,1},... | collective-permute-start | bytes 983048 | tf_op jit(solution)/shard_map/ppermute | solution.py:76
  30.0 8.9 %collective-permute-start.10 = (bf16[128,1152]{1,0:T(8,128)(2,1)S(1)}, bf16[128,1152]{1,0:T(8,128)(2,1)S(1)}, u32[]{:S(2)}, u32[]{:S(2)}) collective-permute-start(bf16[128,1152]{1,0:T(8,128)(2,1)S(1)} %get-tuple-element.54.refs_2_), channel_id=1, source_target_pairs={{0,4},{1,5},{2,6},{3,7},{4,0},{5,1},{6,2},{7,3},{8,12},{9,13},{10,... | collective-permute-start | bytes 884744 | tf_op jit(solution)/shard_map/ppermute | solution.py:76
  39.6 16.1 %collective-permute-start.11 = (bf16[256,1280]{1,0:T(8,128)(2,1)S(1)}, bf16[256,1280]{1,0:T(8,128)(2,1)S(1)}, u32[]{:S(2)}, u32[]{:S(2)}) collective-permute-start(bf16[256,1280]{1,0:T(8,128)(2,1)S(1)} %get-tuple-element.55.refs_0_), channel_id=1, source_target_pairs={{0,4},{1,5},{2,6},{3,7},{4,0},{5,1},{6,2},{7,3},{8,12},{9,13},{10,... | collective-permute-start | bytes 1966088 | tf_op jit(solution)/shard_map/ppermute | solution.py:76
  40.5 15.5 %collective-permute-start.12 = (bf16[256,1280]{1,0:T(8,128)(2,1)S(1)}, bf16[256,1280]{1,0:T(8,128)(2,1)S(1)}, u32[]{:S(2)}, u32[]{:S(2)}) collective-permute-start(bf16[256,1280]{1,0:T(8,128)(2,1)S(1)} %get-tuple-element.56.refs_1_), channel_id=1, source_target_pairs={{0,2},{1,3},{2,0},{3,1},{4,6},{5,7},{6,4},{7,5},{8,10},{9,11},{10,... | collective-permute-start | bytes 1966088 | tf_op jit(solution)/shard_map/ppermute | solution.py:76
  41.1 13.9 %collective-permute-start.13 = (bf16[256,1152]{1,0:T(8,128)(2,1)S(1)}, bf16[256,1152]{1,0:T(8,128)(2,1)}, u32[]{:S(2)}, u32[]{:S(2)}) collective-permute-start(bf16[256,1152]{1,0:T(8,128)(2,1)S(1)} %get-tuple-element.57.refs_2_), channel_id=1, source_target_pairs={{0,8},{1,9},{2,10},{3,11},{4,12},{5,13},{6,14},{7,15},{8,0},{9,1},... | collective-permute-start | bytes 1769480 | tf_op jit(solution)/shard_map/ppermute | solution.py:76
  60.1 11.5 %copy-start.2 = (bf16[1,512,3584]{2,1,0:T(8,128)(2,1)S(1)}, bf16[1,512,3584]{2,1,0:T(8,128)(2,1)}, u32[]{:S(2)}) copy-start(bf16[1,512,3584]{2,1,0:T(8,128)(2,1)} %param.23) | copy-start | bytes 11010052
  76.8 29.3 %collective-permute-start.15 = (f32[256,1280]{1,0:T(8,128)}, f32[256,1280]{1,0:T(8,128)}, u32[]{:S(2)}, u32[]{:S(2)}) collective-permute-start(f32[256,1280]{1,0:T(8,128)} %get-tuple-element.62), channel_id=1, source_target_pairs={{0,4},{1,5},{2,6},{3,7},{4,0},{5,1},{6,2},{7,3},{8,12},{9,13},{10,... | collective-permute-start | bytes 3932168 | tf_op jit(solution)/shard_map/ppermute | solution.py:76
  83.5 34.1 %collective-permute-start.18 = (f32[256,1280]{1,0:T(8,128)}, f32[256,1280]{1,0:T(8,128)}, u32[]{:S(2)}, u32[]{:S(2)}) collective-permute-start(f32[256,1280]{1,0:T(8,128)} %get-tuple-element.69), channel_id=1, source_target_pairs={{0,2},{1,3},{2,0},{3,1},{4,6},{5,7},{6,4},{7,5},{8,10},{9,11},{10,... | collective-permute-start | bytes 3932168 | tf_op jit(solution)/shard_map/ppermute | solution.py:76
  88.7 32.7 %collective-permute-start.21 = (f32[256,1024]{1,0:T(8,128)}, f32[256,1024]{1,0:T(8,128)S(1)}, u32[]{:S(2)}, u32[]{:S(2)}) collective-permute-start(f32[256,1024]{1,0:T(8,128)} %get-tuple-element.75), channel_id=1, source_target_pairs={{0,8},{1,9},{2,10},{3,11},{4,12},{5,13},{6,14},{7,15},{8,0},{9,1},... | collective-permute-start | bytes 3145736 | tf_op jit(solution)/shard_map/ppermute | solution.py:76
  99.6 24.8 %all-to-all-start = ((bf16[32,8,608]{2,1,0:T(8,128)(2,1)}), bf16[32,8,608]{2,1,0:T(8,128)(2,1)}, u32[]{:S(2)}, u32[]{:S(2)}) async-start(bf16[32,8,608]{2,1,0:T(8,128)(2,1)} %hold_back.3), calls=%async_computation | async-start | bytes 655360 | tf_op jit(solution)/shard_map/all_to_all | solution.py:387
  110.6 22.2 %collective-permute-start.16 = (f32[128,1280]{1,0:T(8,128)}, f32[128,1280]{1,0:T(8,128)}, u32[]{:S(2)}, u32[]{:S(2)}) collective-permute-start(f32[128,1280]{1,0:T(8,128)} %get-tuple-element.64), channel_id=1, source_target_pairs={{0,2},{1,3},{2,0},{3,1},{4,6},{5,7},{6,4},{7,5},{8,10},{9,11},{10,... | collective-permute-start | bytes 1966088 | tf_op jit(solution)/shard_map/ppermute | solution.py:76
  120.8 15.3 %collective-permute-start.19 = (f32[128,1280]{1,0:T(8,128)}, f32[128,1280]{1,0:T(8,128)S(1)}, u32[]{:S(2)}, u32[]{:S(2)}) collective-permute-start(f32[128,1280]{1,0:T(8,128)} %get-tuple-element.71), channel_id=1, source_target_pairs={{0,8},{1,9},{2,10},{3,11},{4,12},{5,13},{6,14},{7,15},{8,0},{9,1},... | collective-permute-start | bytes 1966088 | tf_op jit(solution)/shard_map/ppermute | solution.py:76
  123.2 9.6 %copy-start.6 = (f32[128,1280]{1,0:T(8,128)S(1)}, f32[128,1280]{1,0:T(8,128)}, u32[]{:S(2)}) copy-start(f32[128,1280]{1,0:T(8,128)} %copy-done.5) | copy-start | bytes 1966084
  123.2 9.4 %collective-permute-start.22 = (f32[128,1024]{1,0:T(8,128)}, f32[128,1024]{1,0:T(8,128)S(1)}, u32[]{:S(2)}, u32[]{:S(2)}) collective-permute-start(f32[128,1024]{1,0:T(8,128)} %get-tuple-element.77), channel_id=1, source_target_pairs={{0,4},{1,5},{2,6},{3,7},{4,0},{5,1},{6,2},{7,3},{8,12},{9,13},{10,... | collective-permute-start | bytes 1572872 | tf_op jit(solution)/shard_map/ppermute | solution.py:76
  125.4 10.7 %copy-start.8 = (f32[128,1280]{1,0:T(8,128)S(1)}, f32[128,1280]{1,0:T(8,128)}, u32[]{:S(2)}) copy-start(f32[128,1280]{1,0:T(8,128)} %copy-done.7) | copy-start | bytes 1966084
  132.7 6.4 %collective-permute-start.23 = (f32[64,1024]{1,0:T(8,128)S(1)}, f32[64,1024]{1,0:T(8,128)S(1)}, u32[]{:S(2)}, u32[]{:S(2)}) collective-permute-start(f32[64,1024]{1,0:T(8,128)S(1)} %get-tuple-element.79), channel_id=1, source_target_pairs={{0,2},{1,3},{2,0},{3,1},{4,6},{5,7},{6,4},{7,5},{8,10},{9,11},{10,... | collective-permute-start | bytes 786440 | tf_op jit(solution)/shard_map/ppermute | solution.py:76
  134.0 9.1 %collective-permute-start.17 = (f32[64,1280]{1,0:T(8,128)S(1)}, f32[64,1280]{1,0:T(8,128)S(1)}, u32[]{:S(2)}, u32[]{:S(2)}) collective-permute-start(f32[64,1280]{1,0:T(8,128)S(1)} %get-tuple-element.66), channel_id=1, source_target_pairs={{0,24},{1,25},{2,26},{3,27},{4,28},{5,29},{6,30},{7,31},{8,16},{9,... | collective-permute-start | bytes 983048 | tf_op jit(solution)/shard_map/ppermute | solution.py:76
  136.2 15.5 %collective-permute-start.20 = (f32[64,1280]{1,0:T(8,128)S(1)}, f32[64,1280]{1,0:T(8,128)S(1)}, u32[]{:S(2)}, u32[]{:S(2)}) collective-permute-start(f32[64,1280]{1,0:T(8,128)S(1)} %get-tuple-element.73), channel_id=1, source_target_pairs={{0,4},{1,5},{2,6},{3,7},{4,0},{5,1},{6,2},{7,3},{8,12},{9,13},{10,... | collective-permute-start | bytes 983048 | tf_op jit(solution)/shard_map/ppermute | solution.py:76
  139.1 16.1 %collective-permute-start.26 = (f32[32,1024]{1,0:T(8,128)S(1)}, f32[32,1024]{1,0:T(8,128)S(1)}, u32[]{:S(2)}, u32[]{:S(2)}) collective-permute-start(f32[32,1024]{1,0:T(8,128)S(1)} %get-tuple-element.83), channel_id=1, source_target_pairs={{0,24},{1,25},{2,26},{3,27},{4,28},{5,29},{6,30},{7,31},{8,16},{9,... | collective-permute-start | bytes 393224 | tf_op jit(solution)/shard_map/ppermute | solution.py:76
  143.2 12.7 %collective-permute-start.24 = (f32[32,1280]{1,0:T(8,128)S(1)}, f32[32,1280]{1,0:T(8,128)S(1)}, u32[]{:S(2)}, u32[]{:S(2)}) collective-permute-start(f32[32,1280]{1,0:T(8,128)S(1)} %get-tuple-element.81), channel_id=1, source_target_pairs={{0,8},{1,9},{2,10},{3,11},{4,12},{5,13},{6,14},{7,15},{8,0},{9,1},... | collective-permute-start | bytes 491528 | tf_op jit(solution)/shard_map/ppermute | solution.py:76
  151.7 7.2 %collective-permute-start.25 = (f32[32,1280]{1,0:T(8,128)S(1)}, f32[32,1280]{1,0:T(8,128)S(1)}, u32[]{:S(2)}, u32[]{:S(2)}) collective-permute-start(f32[32,1280]{1,0:T(8,128)S(1)} %get-tuple-element.82), channel_id=1, source_target_pairs={{0,24},{1,25},{2,26},{3,27},{4,28},{5,29},{6,30},{7,31},{8,16},{9,... | collective-permute-start | bytes 491528 | tf_op jit(solution)/shard_map/ppermute | solution.py:76
  (13 other events, 43.5 us)

commit v8 on v7

--- a/solution.py
+++ b/solution.py
@@ -67,8 +67,8 @@
 MIB = 1024 * 1024
 
 LINKS = (1, 2, 4, 12)
-SHARES = (10, 10, 8)
-ORDERS = ((1, 0, 3, 2), (0, 2, 1, 3), (2, 1, 0, 3))
+OUT = ((5, (1, 0, 3, 2)), (5, (0, 2, 1, 3)), (4, (2, 1, 0, 3)))
+BACK = ((5, (1, 0, 2, 3)), (5, (0, 1, 3, 2)), (2, (3, 2, 1, 0)), (2, (2, 3, 0, 1)))
 
 
 def across(value, link):
@@ -87,9 +87,14 @@
     return slot
 
 
-def piece_columns(width):
-    share = width // sum(SHARES)
-    ends = [share * sum(SHARES[: at + 1]) for at in range(len(SHARES))]
+def orders_of(pieces):
+    return [order for _, order in pieces]
+
+
+def piece_columns(width, pieces):
+    shares = [share for share, _ in pieces]
+    one = width // sum(shares)
+    ends = [one * sum(shares[: at + 1]) for at in range(len(shares))]
     ends[-1] = width
     return list(zip([0] + ends[:-1], ends))
 
@@ -137,22 +142,41 @@
     return whole_call(kernel, [array], [shape], "hold_back", (after,))[0]
 
 
+def hold_back_tiles(array, after):
+    tile = array.shape[1] // 4
+
+    def kernel(in_ref, after_ref, out_ref):
+        out_ref[...] = in_ref[...]
+
+    spec = pl.BlockSpec((array.shape[0], tile), lambda i: (0, i))
+    return pl.pallas_call(
+        kernel,
+        grid=(4,),
+        in_specs=[spec, pl.BlockSpec(memory_space=pl.ANY)],
+        out_specs=spec,
+        out_shape=jax.ShapeDtypeStruct(array.shape, array.dtype),
+        compiler_params=pltpu.CompilerParams(vmem_limit_bytes=32 * MIB),
+        cost_estimate=pl.CostEstimate(flops=0, bytes_accessed=4 * array.size, transcendentals=0),
+        name="hold_back_tiles",
+    )(array, after)
+
+
 def gather_cube(tokens, side, gate, up, down):
     steps = len(LINKS)
     others = [swap_cores(gate), swap_cores(up)]
-    held = [tokens[:, start:stop] for start, stop in piece_columns(tokens.shape[1])]
+    held = [tokens[:, start:stop] for start, stop in piece_columns(tokens.shape[1], OUT)]
     held[-1] = jnp.concatenate([held[-1], side], axis=1)
     for phase in range(steps):
-        got = [across(piece, order[steps - 1 - phase]) for piece, order in zip(held, ORDERS)]
+        got = [across(piece, order[steps - 1 - phase]) for piece, order in zip(held, orders_of(OUT))]
         if phase < steps - 1:
             held = joined(held, got, others if phase == 1 else ())
         if phase == 1:
-            others.append(swap_cores(hold_back(down, held[0])))
+            others.append(swap_cores(hold_back_tiles(down, held[0])))
     return held, got, others
 
 
 def hidden_kernel(unit, chip_ref, *refs):
-    count = len(ORDERS)
+    count = len(OUT)
     held, got = refs[:count], refs[count : 2 * count]
     gate_ref, up_ref, gate_other_ref, up_other_ref = refs[2 * count : 2 * count + 4]
     hidden_ref, scale_ref, rows_ref, side_ref = refs[2 * count + 4 :]
@@ -161,12 +185,12 @@
 
     @pl.when(step == 0)
     def _():
-        for piece, (start, stop) in enumerate(piece_columns(rows_ref.shape[1])):
+        for piece, (start, stop) in enumerate(piece_columns(rows_ref.shape[1], OUT)):
             half = held[piece].shape[0]
             for place in range(2 * half // unit):
                 source = held[piece] if place * unit < half else got[piece]
                 at = place * unit % half
-                slot = slot_of(place, ORDERS[piece])
+                slot = slot_of(place, OUT[piece][1])
                 to = slice(slot * unit, (slot + 1) * unit)
                 rows_ref[to, start:stop] = source[at : at + unit, : stop - start]
                 if piece == count - 1:
@@ -217,7 +241,7 @@
             pltpu.VMEM((count, width), jnp.bfloat16),
             pltpu.VMEM((count, sum(piece.shape[1] for piece in held) - width), jnp.bfloat16),
         ],
-        compiler_params=pltpu.CompilerParams(vmem_limit_bytes=38 * MIB),
+        compiler_params=pltpu.CompilerParams(vmem_limit_bytes=48 * MIB),
         cost_estimate=pl.CostEstimate(
             flops=8 * count * width * units,
             bytes_accessed=2 * (count * width + 4 * width * units + 2 * count * units),
@@ -227,25 +251,20 @@
     )(chip, *held, *got, gate, up, gate_other, up_other)
 
 
-def output_kernel(
-    unit, order, scale_ref, hidden_ref, down_ref, down_other_ref, keep_ref, send_ref, rows_ref, factor_ref
-):
-    units = down_ref.shape[0]
-    half = keep_ref.shape[0]
-
-    @pl.when(pl.program_id(0) == 0)
-    def _():
-        for place in range(2 * half // unit):
-            slot = slot_of(place, order)
-            to, source = pl.ds(place * unit, unit), pl.ds(slot * unit, unit)
-            rows_ref[to, :] = hidden_ref[source, :]
-            factor_ref[to, :] = scale_ref[source, :]
-
-    out = jnp.dot(rows_ref[:, :units], down_ref[...], preferred_element_type=jnp.float32)
-    out += jnp.dot(rows_ref[:, units:], down_other_ref[...], preferred_element_type=jnp.float32)
-    out = out * factor_ref[...]
-    keep_ref[...] = out[:half]
-    send_ref[...] = out[half:]
+def output_kernel(unit, order, tiles, scale_ref, hidden_ref, *refs):
+    down, down_other = refs[:tiles], refs[tiles : 2 * tiles]
+    keep_ref, send_ref = refs[2 * tiles :]
+    units, tile = down[0].shape
+    places = hidden_ref.shape[0] // unit
+    for out_ref, first in ((send_ref, places // 2), (keep_ref, 0)):
+        slots = [slot_of(first + at, order) for at in range(places // 2)]
+        rows = [slice(slot * unit, (slot + 1) * unit) for slot in slots]
+        hidden = jnp.concatenate([hidden_ref[row] for row in rows], axis=0)
+        scale = jnp.concatenate([scale_ref[row] for row in rows], axis=0)
+        for at in range(tiles):
+            out = jnp.dot(hidden[:, :units], down[at][...], preferred_element_type=jnp.float32)
+            out += jnp.dot(hidden[:, units:], down_other[at][...], preferred_element_type=jnp.float32)
+            out_ref[:, at * tile : (at + 1) * tile] = out * scale
 
 
 def expert_output(unit, order, columns, scale, hidden, down, down_other):
@@ -253,30 +272,30 @@
     start, stop = columns
     count = hidden.shape[0]
     tile = 256
+    tiles = (stop - start) // tile
     half = jax.ShapeDtypeStruct((count // 2, stop - start), jnp.float32)
+
+    def tile_at(at):
+        return pl.BlockSpec((units, tile), lambda i: (0, start // tile + at))
+
     return pl.pallas_call(
-        functools.partial(output_kernel, unit, order),
-        grid=((stop - start) // tile,),
+        functools.partial(output_kernel, unit, order, tiles),
+        grid=(1,),
         in_specs=[
             pl.BlockSpec((count, 1), lambda i: (0, 0)),
             pl.BlockSpec((count, 2 * units), lambda i: (0, 0)),
-            pl.BlockSpec((units, tile), lambda i: (0, start // tile + i)),
-            pl.BlockSpec((units, tile), lambda i: (0, start // tile + i)),
-        ],
-        out_specs=[pl.BlockSpec((count // 2, tile), lambda i: (0, i))] * 2,
+        ]
+        + [tile_at(at) for at in range(tiles)] * 2,
+        out_specs=[pl.BlockSpec((count // 2, stop - start), lambda i: (0, 0))] * 2,
         out_shape=[half] * 2,
-        scratch_shapes=[
-            pltpu.VMEM((count, 2 * units), jnp.bfloat16),
-            pltpu.VMEM((count, 1), jnp.float32),
-        ],
-        compiler_params=pltpu.CompilerParams(vmem_limit_bytes=40 * MIB),
+        compiler_params=pltpu.CompilerParams(vmem_limit_bytes=24 * MIB),
         cost_estimate=pl.CostEstimate(
             flops=4 * count * (stop - start) * units,
             bytes_accessed=4 * (stop - start) * units + 4 * count * (stop - start + units),
             transcendentals=0,
         ),
         name="expert_output",
-    )(scale, hidden, down, down_other)
+    )(scale, hidden, *[down] * tiles, *[down_other] * tiles)
 
 
 def halved(keep, got):
@@ -295,7 +314,7 @@
     width = sum(piece.shape[1] for piece in keep)
 
     def kernel(*refs):
-        for at, (start, stop) in enumerate(piece_columns(width)):
+        for at, (start, stop) in enumerate(piece_columns(width, BACK)):
             total = refs[at][...] + refs[count + at][...]
             refs[2 * count][:, start:stop] = total.astype(jnp.bfloat16)
 
@@ -309,7 +328,7 @@
     chip = (lax.axis_index("ep") // 2).astype(jnp.int32).reshape(1)
     hidden, scale = expert_hidden(unit, chip, held, got, gate, up, gate_other, up_other)
     keep, coming = [], []
-    for order, columns in zip(ORDERS, piece_columns(down.shape[1])):
+    for order, columns in zip(orders_of(BACK), piece_columns(down.shape[1], BACK)):
         mine, send = expert_output(unit, order, columns, scale, hidden, down, down_other)
         keep.append(mine)
         coming.append(across(send, order[0]))
@@ -319,7 +338,7 @@
 def cube_sums(keep, got):
     keep, got = list(keep), list(got)
     for phase in range(1, len(LINKS)):
-        for at, order in enumerate(ORDERS):
+        for at, order in enumerate(orders_of(BACK)):
             keep[at], send = halved(keep[at], got[at])
             got[at] = across(send, order[phase])
     return finished(keep, got)

time: 161 us -> 166 us (1.031)
  starting transfers between devices: 42.9 us -> 53.3 us
  local copies, waits for them, and re-layouts: 19.8 us -> 16.5 us
    ppermute x24 -> x28, starting transfers between devices: 38 us -> 48.8 us  [across(): lax.ppermute(value, 'ep', [(i, i ^ 2 * LINKS[link]) for i in range(peers)])]
    pallas_call x1, Pallas kernels: 11.4 us -> 13.3 us  [expert_hidden(): pl.pallas_call(functools.partial(hidden_kernel, unit), grid=(2 * steps,),...]
    pallas_call x3 -> x5, Pallas kernels: 15 us -> 13.1 us  [the longest x4 10.5 us: expert_output(): pl.pallas_call(functools.partial(output_kernel, unit, order, tiles), grid...]
    ppermute x24 -> x28, waiting for transfers between devices: 50.2 us -> 51.2 us  [across(): lax.ppermute(value, 'ep', [(i, i ^ 2 * LINKS[link]) for i in range(peers)])]
    pallas_call x15 -> x17, Pallas kernels: 10.7 us -> 10.3 us  [whole_call(): pl.pallas_call(body, in_specs=[pl.BlockSpec(memory_space=pltpu.VMEM)] * g...]
  transfers between devices with their start and end apart: 28 -> 32, of which waited for: 14 -> 14; matrix products, arithmetic and copies ran while one was open for 11% -> 7% of each run, Pallas kernels for 18% -> 18%
where the time goes in v8:
time: 166 us; the launch traced here: 165 us
  starting transfers between devices  53.3 us (32%)
  waiting for transfers between devices  51.2 us (31%)
  Pallas kernels  36.7 us (22%)
  local copies, waits for them, and re-layouts  16.5 us (10%)
  matrix products  3.36 us (2%)
  other arithmetic  2.45 us (1%)
    ppermute x28, waiting for transfers between devices, across(): lax.ppermute(value, 'ep', [(i, i ^ 2 * LINKS[link]) for i in range(peers)])  51.2 us
    ppermute x28, starting transfers between devices, across(): lax.ppermute(value, 'ep', [(i, i ^ 2 * LINKS[link]) for i in range(peers)])  48.8 us
    pallas_call x1, Pallas kernels, expert_hidden(): pl.pallas_call(functools.partial(hidden_kernel, unit), grid=(2 * steps,),...  13.3 us
    unnamed x34, local copies, waits for them, and re-layouts  10.7 us
    pallas_call x4, Pallas kernels, expert_output(): pl.pallas_call(functools.partial(output_kernel, unit, order, tiles), grid...  10.5 us
    pallas_call x17, Pallas kernels, whole_call(): pl.pallas_call(body, in_specs=[pl.BlockSpec(memory_space=pltpu.VMEM)] * g...  10.3 us
    all_to_all x1, starting transfers between devices, per_device(): lax.all_to_all(leaving, 'ep', split_axis=0, concat_axis=0, tiled=True)  3.89 us
  transfers between devices with their start and end apart: 32, of which 14 were waited for; matrix products, arithmetic and copies ran while one was open for 7% of the time, Pallas kernels for 18%

profile of v8, /device:TPU:0, one launch (start us, length us, event | category | flops | bytes accessed | tf_op | source)
XLA Modules:
  0.0 165.0 jit_solution(12646488837787706929)
XLA Ops:
  2.2 3.1 %collective-permute-start = (bf16[32,1280]{1,0:T(8,128)(2,1)S(1)}, bf16[32,1280]{1,0:T(8,128)(2,1)S(1)}, u32[]{:S(2)}, u32[]{:S(2)}) collective-permute-start(bf16[32,1280]{1,0:T(8,128)(2,1)S(1)} %get-tuple-element.101.refs_0_), channel_id=1, source_target_pairs={{0,8},{1,9},{2,10},{3,11},{4,12},{5,13},{6,14},{7,15},{8,0},{9,1},... | collective-permute-start | bytes 245768 | tf_op jit(solution)/shard_map/ppermute | solution.py:76
  5.3 2.5 %collective-permute-start.1 = (bf16[32,1280]{1,0:T(8,128)(2,1)S(1)}, bf16[32,1280]{1,0:T(8,128)(2,1)S(1)}, u32[]{:S(2)}, u32[]{:S(2)}) collective-permute-start(bf16[32,1280]{1,0:T(8,128)(2,1)S(1)} %get-tuple-element.100.refs_1_), channel_id=1, source_target_pairs={{0,24},{1,25},{2,26},{3,27},{4,28},{5,29},{6,30},{7,31},{8,16},{9,... | collective-permute-start | bytes 245768 | tf_op jit(solution)/shard_map/ppermute | solution.py:76
  11.0 4.8 %collective-permute-done.2.refs_5_ = bf16[32,1152]{1,0:T(8,128)(2,1)S(1)} collective-permute-done((bf16[32,1152]{1,0:T(8,128)(2,1)S(1)}, bf16[32,1152]{1,0:T(8,128)(2,1)S(1)}, u32[]{:S(2)}, u32[]{:S(2)}) %collective-permute-start.2) | collective-permute-done | bytes 73760 | tf_op jit(solution)/shard_map/ppermute | solution.py:76
  20.3 3.7 %collective-permute-done.5.refs_5_ = bf16[64,1152]{1,0:T(8,128)(2,1)S(1)} collective-permute-done((bf16[64,1152]{1,0:T(8,128)(2,1)S(1)}, bf16[64,1152]{1,0:T(8,128)(2,1)S(1)}, u32[]{:S(2)}, u32[]{:S(2)}) %collective-permute-start.5) | collective-permute-done | bytes 147488 | tf_op jit(solution)/shard_map/ppermute | solution.py:76
  24.1 2.0 %copy-done.1 = bf16[1,512,3584]{2,1,0:T(8,128)(2,1)S(1)} copy-done((bf16[1,512,3584]{2,1,0:T(8,128)(2,1)S(1)}, bf16[1,512,3584]{2,1,0:T(8,128)(2,1)}, u32[]{:S(2)}) %copy-start.1) | copy-done | bytes 3670040
  26.1 2.6 %hold_back_tiles.1 = bf16[512,3584]{1,0:T(8,128)(2,1)} custom-call(bf16[512,3584]{1,0:T(8,128)(2,1)S(1)} %bitcast.19, bf16[128,1280]{1,0:T(8,128)(2,1)S(1)} %get-tuple-element.60.refs_0_.after_ref), custom_call_target="tpu_custom_call" | custom-call | bytes 7340032 | tf_op jit(solution)/shard_map/hold_back_tiles/pallas_call | solution.py:152
  32.1 7.3 %collective-permute-done.10.refs_5_ = bf16[128,1152]{1,0:T(8,128)(2,1)S(1)} collective-permute-done((bf16[128,1152]{1,0:T(8,128)(2,1)S(1)}, bf16[128,1152]{1,0:T(8,128)(2,1)S(1)}, u32[]{:S(2)}, u32[]{:S(2)}) %collective-permute-start.10) | collective-permute-done | bytes 294944 | tf_op jit(solution)/shard_map/ppermute | solution.py:76
  43.5 12.1 %collective-permute-done.13.refs_5_ = bf16[256,1152]{1,0:T(8,128)(2,1)} collective-permute-done((bf16[256,1152]{1,0:T(8,128)(2,1)S(1)}, bf16[256,1152]{1,0:T(8,128)(2,1)}, u32[]{:S(2)}, u32[]{:S(2)}) %collective-permute-start.13) | collective-permute-done | bytes 589856 | tf_op jit(solution)/shard_map/ppermute | solution.py:76
  59.6 13.3 %expert_hidden.1 = (bf16[512,1024]{1,0:T(8,128)(2,1)S(1)}, f32[512,1]{1,0:T(8,128)S(1)}) custom-call(s32[1]{0:T(128)} %bitcast.2.chip_ref, bf16[256,1280]{1,0:T(8,128)(2,1)S(1)} %get-tuple-element.63.refs_0_, bf16[256,1280]{1,0:T(8,128)(2,1)S(1)} %get-tuple-element.64.refs_1_, bf16[256,1152]{1,0:T(8,128)(2,1)S(1)} %copy-done.10, ...), custom_call_target="tpu_custom_call" | custom-call | flops 7516192768 | bytes 19398656 | tf_op jit(solution)/shard_map/expert_hidden/pallas_call | solution.py:226
  73.0 3.4 %expert_output.5 = (f32[256,1280]{1,0:T(8,128)S(1)}, f32[256,1280]{1,0:T(8,128)}) custom-call(f32[512,1]{1,0:T(8,128)S(1)} %get-tuple-element.66.scale_ref, bf16[512,1024]{1,0:T(8,128)(2,1)S(1)} %get-tuple-element.67.hidden_ref, bf16[512,3584]{1,0:T(8,128)(2,1)S(1)} %bitcast.20, bf16[512,3584]{1,0:T(8,128)(2,1)S(1)} %bitcast.21, ...), custom_call_target="tpu_custom_call" | custom-call | flops 1342177280 | bytes 6291456 | tf_op jit(solution)/shard_map/expert_output/pallas_call | solution.py:281
  77.9 3.4 %expert_output.6 = (f32[256,1280]{1,0:T(8,128)S(1)}, f32[256,1280]{1,0:T(8,128)}) custom-call(f32[512,1]{1,0:T(8,128)S(1)} %get-tuple-element.66.scale_ref, bf16[512,1024]{1,0:T(8,128)(2,1)S(1)} %get-tuple-element.67.hidden_ref, bf16[512,3584]{1,0:T(8,128)(2,1)S(1)} %bitcast.25, bf16[512,3584]{1,0:T(8,128)(2,1)S(1)} %bitcast.26, ...), custom_call_target="tpu_custom_call" | custom-call | flops 1342177280 | bytes 6291456 | tf_op jit(solution)/shard_map/expert_output/pallas_call | solution.py:281
  85.0 2.0 %copy-done.3 = bf16[1,512,3584]{2,1,0:T(8,128)(2,1)S(1)} copy-done((bf16[1,512,3584]{2,1,0:T(8,128)(2,1)S(1)}, bf16[1,512,3584]{2,1,0:T(8,128)(2,1)}, u32[]{:S(2)}) %copy-start.3) | copy-done | bytes 3670040
  87.0 1.8 %expert_output.4 = (f32[256,512]{1,0:T(8,128)S(1)}, f32[256,512]{1,0:T(8,128)S(1)}) custom-call(f32[512,1]{1,0:T(8,128)S(1)} %get-tuple-element.66.scale_ref, bf16[512,1024]{1,0:T(8,128)(2,1)S(1)} %get-tuple-element.67.hidden_ref, bf16[512,3584]{1,0:T(8,128)(2,1)S(1)} %bitcast.30, bf16[512,3584]{1,0:T(8,128)(2,1)S(1)} %bitcast.31, ...), custom_call_target="tpu_custom_call" | custom-call | flops 536870912 | bytes 3145728 | tf_op jit(solution)/shard_map/expert_output/pallas_call | solution.py:281
  90.3 3.9 %all-to-all-start = ((bf16[32,8,608]{2,1,0:T(8,128)(2,1)}), bf16[32,8,608]{2,1,0:T(8,128)(2,1)}, u32[]{:S(2)}, u32[]{:S(2)}) async-start(bf16[32,8,608]{2,1,0:T(8,128)(2,1)} %hold_back.1), calls=%async_computation | async-start | bytes 655360 | tf_op jit(solution)/shard_map/all_to_all | solution.py:406
  94.2 2.0 %copy-done.4 = bf16[1,512,3584]{2,1,0:T(8,128)(2,1)S(1)} copy-done((bf16[1,512,3584]{2,1,0:T(8,128)(2,1)S(1)}, bf16[1,512,3584]{2,1,0:T(8,128)(2,1)}, u32[]{:S(2)}) %copy-start.4) | copy-done | bytes 3670040
  96.3 1.9 %expert_output.7 = (f32[256,512]{1,0:T(8,128)S(1)}, f32[256,512]{1,0:T(8,128)S(1)}) custom-call(f32[512,1]{1,0:T(8,128)S(1)} %get-tuple-element.66.scale_ref, bf16[512,1024]{1,0:T(8,128)(2,1)S(1)} %get-tuple-element.67.hidden_ref, bf16[512,3584]{1,0:T(8,128)(2,1)S(1)} %bitcast.32, bf16[512,3584]{1,0:T(8,128)(2,1)S(1)} %bitcast.33, ...), custom_call_target="tpu_custom_call" | custom-call | flops 536870912 | bytes 3145728 | tf_op jit(solution)/shard_map/expert_output/pallas_call | solution.py:281
  98.2 3.5 %collective-permute-start.21 = (f32[256,512]{1,0:T(8,128)S(1)}, f32[256,512]{1,0:T(8,128)S(1)}, u32[]{:S(2)}, u32[]{:S(2)}) collective-permute-start(f32[256,512]{1,0:T(8,128)S(1)} %get-tuple-element.84), channel_id=1, source_target_pairs={{0,24},{1,25},{2,26},{3,27},{4,28},{5,29},{6,30},{7,31},{8,16},{9,... | collective-permute-start | bytes 1572872 | tf_op jit(solution)/shard_map/ppermute | solution.py:76
  101.6 6.7 %collective-permute-done.15.refs_1_ = f32[256,1280]{1,0:T(8,128)} collective-permute-done((f32[256,1280]{1,0:T(8,128)}, f32[256,1280]{1,0:T(8,128)}, u32[]{:S(2)}, u32[]{:S(2)}) %collective-permute-start.15) | collective-permute-done | bytes 1310752 | tf_op jit(solution)/shard_map/ppermute | solution.py:76
  108.4 2.3 %halved.12 = (f32[128,1280]{1,0:T(8,128)S(1)}, f32[128,1280]{1,0:T(8,128)}) custom-call(f32[256,1280]{1,0:T(8,128)S(1)} %copy-done.6, f32[256,1280]{1,0:T(8,128)} %collective-permute-done.15.refs_1_), custom_call_target="tpu_custom_call" | custom-call | bytes 3932160 | tf_op jit(solution)/shard_map/halved/pallas_call | solution.py:108
  111.5 4.4 %collective-permute-done.18.refs_1_ = f32[256,1280]{1,0:T(8,128)} collective-permute-done((f32[256,1280]{1,0:T(8,128)}, f32[256,1280]{1,0:T(8,128)}, u32[]{:S(2)}, u32[]{:S(2)}) %collective-permute-start.18) | collective-permute-done | bytes 1310752 | tf_op jit(solution)/shard_map/ppermute | solution.py:76
  115.8 2.3 %halved.15 = (f32[128,1280]{1,0:T(8,128)S(1)}, f32[128,1280]{1,0:T(8,128)}) custom-call(f32[256,1280]{1,0:T(8,128)S(1)} %get-tuple-element.76.refs_0_, f32[256,1280]{1,0:T(8,128)} %collective-permute-done.18.refs_1_), custom_call_target="tpu_custom_call" | custom-call | bytes 3932160 | tf_op jit(solution)/shard_map/halved/pallas_call | solution.py:108
  119.5 9.0 %collective-permute-start.22 = (f32[128,512]{1,0:T(8,128)}, f32[128,512]{1,0:T(8,128)}, u32[]{:S(2)}, u32[]{:S(2)}) collective-permute-start(f32[128,512]{1,0:T(8,128)} %get-tuple-element.86), channel_id=1, source_target_pairs={{0,8},{1,9},{2,10},{3,11},{4,12},{5,13},{6,14},{7,15},{8,0},{9,1},... | collective-permute-start | bytes 786440 | tf_op jit(solution)/shard_map/ppermute | solution.py:76
  135.3 2.5 %collective-permute-start.20 = (f32[64,1280]{1,0:T(8,128)S(1)}, f32[64,1280]{1,0:T(8,128)S(1)}, u32[]{:S(2)}, u32[]{:S(2)}) collective-permute-start(f32[64,1280]{1,0:T(8,128)S(1)} %get-tuple-element.81), channel_id=1, source_target_pairs={{0,24},{1,25},{2,26},{3,27},{4,28},{5,29},{6,30},{7,31},{8,16},{9,... | collective-permute-start | bytes 983048 | tf_op jit(solution)/shard_map/ppermute | solution.py:76
  139.6 1.5 collective-permute-start.23
  141.1 1.8 %collective-permute-done.25.refs_1_ = f32[128,512]{1,0:T(8,128)S(1)} collective-permute-done((f32[128,512]{1,0:T(8,128)}, f32[128,512]{1,0:T(8,128)S(1)}, u32[]{:S(2)}, u32[]{:S(2)}) %collective-permute-start.25) | collective-permute-done | bytes 262176 | tf_op jit(solution)/shard_map/ppermute | solution.py:76
  143.0 1.6 collective-permute-start.26
  146.1 1.9 %collective-permute-done.26.refs_1_ = f32[64,512]{1,0:T(8,128)S(1)} collective-permute-done((f32[64,512]{1,0:T(8,128)S(1)}, f32[64,512]{1,0:T(8,128)S(1)}, u32[]{:S(2)}, u32[]{:S(2)}) %collective-permute-start.26) | collective-permute-done | bytes 131104 | tf_op jit(solution)/shard_map/ppermute | solution.py:76
  148.0 1.6 collective-permute-start.30
  149.8 2.3 %collective-permute-start.27 = (f32[32,1280]{1,0:T(8,128)S(1)}, f32[32,1280]{1,0:T(8,128)S(1)}, u32[]{:S(2)}, u32[]{:S(2)}) collective-permute-start(f32[32,1280]{1,0:T(8,128)S(1)} %get-tuple-element.96), channel_id=1, source_target_pairs={{0,24},{1,25},{2,26},{3,27},{4,28},{5,29},{6,30},{7,31},{8,16},{9,... | collective-permute-start | bytes 491528 | tf_op jit(solution)/shard_map/ppermute | solution.py:76
  152.1 4.9 %collective-permute-done.20.refs_1_ = f32[64,1280]{1,0:T(8,128)S(1)} collective-permute-done((f32[64,1280]{1,0:T(8,128)S(1)}, f32[64,1280]{1,0:T(8,128)S(1)}, u32[]{:S(2)}, u32[]{:S(2)}) %collective-permute-start.20) | collective-permute-done | bytes 327712 | tf_op jit(solution)/shard_map/ppermute | solution.py:76
  157.1 3.8 %collective-permute-start.28 = (f32[32,1280]{1,0:T(8,128)S(1)}, f32[32,1280]{1,0:T(8,128)S(1)}, u32[]{:S(2)}, u32[]{:S(2)}) collective-permute-start(f32[32,1280]{1,0:T(8,128)S(1)} %get-tuple-element.97), channel_id=1, source_target_pairs={{0,8},{1,9},{2,10},{3,11},{4,12},{5,13},{6,14},{7,15},{8,0},{9,1},... | collective-permute-start | bytes 491528 | tf_op jit(solution)/shard_map/ppermute | solution.py:76
  162.5 1.8 %collective-permute-done.28.refs_5_ = f32[32,1280]{1,0:T(8,128)S(1)} collective-permute-done((f32[32,1280]{1,0:T(8,128)S(1)}, f32[32,1280]{1,0:T(8,128)S(1)}, u32[]{:S(2)}, u32[]{:S(2)}) %collective-permute-start.28) | collective-permute-done | bytes 163872 | tf_op jit(solution)/shard_map/ppermute | solution.py:76
  (117 shorter events, 41.7 us)
Async XLA Ops:
  0.6 23.4 %collective-permute-start.6 = (bf16[3584,512]{1,0:T(8,128)(2,1)}, bf16[3584,512]{1,0:T(8,128)(2,1)}, u32[]{:S(2)}, u32[]{:S(2)}) collective-permute-start(bf16[3584,512]{1,0:T(8,128)(2,1)} %bitcast.34), channel_id=1, source_target_pairs={{0,1},{1,0},{2,3},{3,2},{4,5},{5,4},{6,7},{7,6},{8,9},{9,8},{10,11... | collective-permute-start | bytes 11010056 | tf_op jit(solution)/shard_map/ppermute | solution.py:80
  1.2 22.9 %collective-permute-start.7 = (bf16[3584,512]{1,0:T(8,128)(2,1)}, bf16[3584,512]{1,0:T(8,128)(2,1)}, u32[]{:S(2)}, u32[]{:S(2)}) collective-permute-start(bf16[3584,512]{1,0:T(8,128)(2,1)} %bitcast.36), channel_id=1, source_target_pairs={{0,1},{1,0},{2,3},{3,2},{4,5},{5,4},{6,7},{7,6},{8,9},{9,8},{10,11... | collective-permute-start | bytes 11010056 | tf_op jit(solution)/shard_map/ppermute | solution.py:80
  2.2 13.6 %collective-permute-start = (bf16[32,1280]{1,0:T(8,128)(2,1)S(1)}, bf16[32,1280]{1,0:T(8,128)(2,1)S(1)}, u32[]{:S(2)}, u32[]{:S(2)}) collective-permute-start(bf16[32,1280]{1,0:T(8,128)(2,1)S(1)} %get-tuple-element.101.refs_0_), channel_id=1, source_target_pairs={{0,8},{1,9},{2,10},{3,11},{4,12},{5,13},{6,14},{7,15},{8,0},{9,1},... | collective-permute-start | bytes 245768 | tf_op jit(solution)/shard_map/ppermute | solution.py:76
  5.3 10.5 %collective-permute-start.1 = (bf16[32,1280]{1,0:T(8,128)(2,1)S(1)}, bf16[32,1280]{1,0:T(8,128)(2,1)S(1)}, u32[]{:S(2)}, u32[]{:S(2)}) collective-permute-start(bf16[32,1280]{1,0:T(8,128)(2,1)S(1)} %get-tuple-element.100.refs_1_), channel_id=1, source_target_pairs={{0,24},{1,25},{2,26},{3,27},{4,28},{5,29},{6,30},{7,31},{8,16},{9,... | collective-permute-start | bytes 245768 | tf_op jit(solution)/shard_map/ppermute | solution.py:76
  9.6 6.2 %collective-permute-start.2 = (bf16[32,1152]{1,0:T(8,128)(2,1)S(1)}, bf16[32,1152]{1,0:T(8,128)(2,1)S(1)}, u32[]{:S(2)}, u32[]{:S(2)}) collective-permute-start(bf16[32,1152]{1,0:T(8,128)(2,1)S(1)} %pad_maximum_fusion.refs_2_), channel_id=1, source_target_pairs={{0,24},{1,25},{2,26},{3,27},{4,28},{5,29},{6,30},{7,31},{8,16},{9,... | collective-permute-start | bytes 221192 | tf_op jit(solution)/shard_map/ppermute | solution.py:76
  15.8 8.2 %collective-permute-start.3 = (bf16[64,1280]{1,0:T(8,128)(2,1)S(1)}, bf16[64,1280]{1,0:T(8,128)(2,1)S(1)}, u32[]{:S(2)}, u32[]{:S(2)}) collective-permute-start(bf16[64,1280]{1,0:T(8,128)(2,1)S(1)} %get-tuple-element.57.refs_0_), channel_id=1, source_target_pairs={{0,24},{1,25},{2,26},{3,27},{4,28},{5,29},{6,30},{7,31},{8,16},{9,... | collective-permute-start | bytes 491528 | tf_op jit(solution)/shard_map/ppermute | solution.py:76
  17.3 6.7 %collective-permute-start.4 = (bf16[64,1280]{1,0:T(8,128)(2,1)S(1)}, bf16[64,1280]{1,0:T(8,128)(2,1)S(1)}, u32[]{:S(2)}, u32[]{:S(2)}) collective-permute-start(bf16[64,1280]{1,0:T(8,128)(2,1)S(1)} %get-tuple-element.58.refs_1_), channel_id=1, source_target_pairs={{0,4},{1,5},{2,6},{3,7},{4,0},{5,1},{6,2},{7,3},{8,12},{9,13},{10,... | collective-permute-start | bytes 491528 | tf_op jit(solution)/shard_map/ppermute | solution.py:76
  18.9 5.1 %collective-permute-start.5 = (bf16[64,1152]{1,0:T(8,128)(2,1)S(1)}, bf16[64,1152]{1,0:T(8,128)(2,1)S(1)}, u32[]{:S(2)}, u32[]{:S(2)}) collective-permute-start(bf16[64,1152]{1,0:T(8,128)(2,1)S(1)} %get-tuple-element.59.refs_2_), channel_id=1, source_target_pairs={{0,2},{1,3},{2,0},{3,1},{4,6},{5,7},{6,4},{7,5},{8,10},{9,11},{10,... | collective-permute-start | bytes 442376 | tf_op jit(solution)/shard_map/ppermute | solution.py:76
  28.7 44.3 %collective-permute-start.14 = (bf16[512,3584]{1,0:T(8,128)(2,1)}, bf16[512,3584]{1,0:T(8,128)(2,1)}, u32[]{:S(2)}, u32[]{:S(2)}) collective-permute-start(bf16[512,3584]{1,0:T(8,128)(2,1)} %hold_back_tiles.1), channel_id=1, source_target_pairs={{0,1},{1,0},{2,3},{3,2},{4,5},{5,4},{6,7},{7,6},{8,9},{9,8},{10,11... | collective-permute-start | bytes 11010056 | tf_op jit(solution)/shard_map/ppermute | solution.py:80
  28.7 10.7 %collective-permute-start.8 = (bf16[128,1280]{1,0:T(8,128)(2,1)S(1)}, bf16[128,1280]{1,0:T(8,128)(2,1)S(1)}, u32[]{:S(2)}, u32[]{:S(2)}) collective-permute-start(bf16[128,1280]{1,0:T(8,128)(2,1)S(1)} %get-tuple-element.60.refs_0_.after_ref), channel_id=1, source_target_pairs={{0,2},{1,3},{2,0},{3,1},{4,6},{5,7},{6,4},{7,5},{8,10},{9,11},{10,... | collective-permute-start | bytes 983048 | tf_op jit(solution)/shard_map/ppermute | solution.py:76
  30.2 9.8 %collective-permute-start.9 = (bf16[128,1280]{1,0:T(8,128)(2,1)S(1)}, bf16[128,1280]{1,0:T(8,128)(2,1)S(1)}, u32[]{:S(2)}, u32[]{:S(2)}) collective-permute-start(bf16[128,1280]{1,0:T(8,128)(2,1)S(1)} %get-tuple-element.61.refs_1_), channel_id=1, source_target_pairs={{0,8},{1,9},{2,10},{3,11},{4,12},{5,13},{6,14},{7,15},{8,0},{9,1},... | collective-permute-start | bytes 983048 | tf_op jit(solution)/shard_map/ppermute | solution.py:76
  30.6 8.9 %collective-permute-start.10 = (bf16[128,1152]{1,0:T(8,128)(2,1)S(1)}, bf16[128,1152]{1,0:T(8,128)(2,1)S(1)}, u32[]{:S(2)}, u32[]{:S(2)}) collective-permute-start(bf16[128,1152]{1,0:T(8,128)(2,1)S(1)} %get-tuple-element.62.refs_2_), channel_id=1, source_target_pairs={{0,4},{1,5},{2,6},{3,7},{4,0},{5,1},{6,2},{7,3},{8,12},{9,13},{10,... | collective-permute-start | bytes 884744 | tf_op jit(solution)/shard_map/ppermute | solution.py:76
  40.1 16.1 %collective-permute-start.11 = (bf16[256,1280]{1,0:T(8,128)(2,1)S(1)}, bf16[256,1280]{1,0:T(8,128)(2,1)S(1)}, u32[]{:S(2)}, u32[]{:S(2)}) collective-permute-start(bf16[256,1280]{1,0:T(8,128)(2,1)S(1)} %get-tuple-element.63.refs_0_), channel_id=1, source_target_pairs={{0,4},{1,5},{2,6},{3,7},{4,0},{5,1},{6,2},{7,3},{8,12},{9,13},{10,... | collective-permute-start | bytes 1966088 | tf_op jit(solution)/shard_map/ppermute | solution.py:76
  41.1 15.5 %collective-permute-start.12 = (bf16[256,1280]{1,0:T(8,128)(2,1)S(1)}, bf16[256,1280]{1,0:T(8,128)(2,1)S(1)}, u32[]{:S(2)}, u32[]{:S(2)}) collective-permute-start(bf16[256,1280]{1,0:T(8,128)(2,1)S(1)} %get-tuple-element.64.refs_1_), channel_id=1, source_target_pairs={{0,2},{1,3},{2,0},{3,1},{4,6},{5,7},{6,4},{7,5},{8,10},{9,11},{10,... | collective-permute-start | bytes 1966088 | tf_op jit(solution)/shard_map/ppermute | solution.py:76
  41.7 13.9 %collective-permute-start.13 = (bf16[256,1152]{1,0:T(8,128)(2,1)S(1)}, bf16[256,1152]{1,0:T(8,128)(2,1)}, u32[]{:S(2)}, u32[]{:S(2)}) collective-permute-start(bf16[256,1152]{1,0:T(8,128)(2,1)S(1)} %get-tuple-element.65.refs_2_), channel_id=1, source_target_pairs={{0,8},{1,9},{2,10},{3,11},{4,12},{5,13},{6,14},{7,15},{8,0},{9,1},... | collective-permute-start | bytes 1769480 | tf_op jit(solution)/shard_map/ppermute | solution.py:76
  76.4 32.0 %collective-permute-start.15 = (f32[256,1280]{1,0:T(8,128)}, f32[256,1280]{1,0:T(8,128)}, u32[]{:S(2)}, u32[]{:S(2)}) collective-permute-start(f32[256,1280]{1,0:T(8,128)} %get-tuple-element.70), channel_id=1, source_target_pairs={{0,4},{1,5},{2,6},{3,7},{4,0},{5,1},{6,2},{7,3},{8,12},{9,13},{10,... | collective-permute-start | bytes 3932168 | tf_op jit(solution)/shard_map/ppermute | solution.py:76
  81.3 34.6 %collective-permute-start.18 = (f32[256,1280]{1,0:T(8,128)}, f32[256,1280]{1,0:T(8,128)}, u32[]{:S(2)}, u32[]{:S(2)}) collective-permute-start(f32[256,1280]{1,0:T(8,128)} %get-tuple-element.77), channel_id=1, source_target_pairs={{0,2},{1,3},{2,0},{3,1},{4,6},{5,7},{6,4},{7,5},{8,10},{9,11},{10,... | collective-permute-start | bytes 3932168 | tf_op jit(solution)/shard_map/ppermute | solution.py:76
  90.3 40.3 %all-to-all-start = ((bf16[32,8,608]{2,1,0:T(8,128)(2,1)}), bf16[32,8,608]{2,1,0:T(8,128)(2,1)}, u32[]{:S(2)}, u32[]{:S(2)}) async-start(bf16[32,8,608]{2,1,0:T(8,128)(2,1)} %hold_back.1), calls=%async_computation | async-start | bytes 655360 | tf_op jit(solution)/shard_map/all_to_all | solution.py:406
  98.2 20.6 %collective-permute-start.21 = (f32[256,512]{1,0:T(8,128)S(1)}, f32[256,512]{1,0:T(8,128)S(1)}, u32[]{:S(2)}, u32[]{:S(2)}) collective-permute-start(f32[256,512]{1,0:T(8,128)S(1)} %get-tuple-element.84), channel_id=1, source_target_pairs={{0,24},{1,25},{2,26},{3,27},{4,28},{5,29},{6,30},{7,31},{8,16},{9,... | collective-permute-start | bytes 1572872 | tf_op jit(solution)/shard_map/ppermute | solution.py:76
  101.6 26.9 %collective-permute-start.24 = (f32[256,512]{1,0:T(8,128)S(1)}, f32[256,512]{1,0:T(8,128)S(1)}, u32[]{:S(2)}, u32[]{:S(2)}) collective-permute-start(f32[256,512]{1,0:T(8,128)S(1)} %copy-done.12), channel_id=1, source_target_pairs={{0,8},{1,9},{2,10},{3,11},{4,12},{5,13},{6,14},{7,15},{8,0},{9,1},... | collective-permute-start | bytes 1572872 | tf_op jit(solution)/shard_map/ppermute | solution.py:76
  110.7 23.1 %collective-permute-start.16 = (f32[128,1280]{1,0:T(8,128)}, f32[128,1280]{1,0:T(8,128)}, u32[]{:S(2)}, u32[]{:S(2)}) collective-permute-start(f32[128,1280]{1,0:T(8,128)} %get-tuple-element.72), channel_id=1, source_target_pairs={{0,2},{1,3},{2,0},{3,1},{4,6},{5,7},{6,4},{7,5},{8,10},{9,11},{10,... | collective-permute-start | bytes 1966088 | tf_op jit(solution)/shard_map/ppermute | solution.py:76
  118.1 17.1 %collective-permute-start.19 = (f32[128,1280]{1,0:T(8,128)}, f32[128,1280]{1,0:T(8,128)S(1)}, u32[]{:S(2)}, u32[]{:S(2)}) collective-permute-start(f32[128,1280]{1,0:T(8,128)} %get-tuple-element.79), channel_id=1, source_target_pairs={{0,4},{1,5},{2,6},{3,7},{4,0},{5,1},{6,2},{7,3},{8,12},{9,13},{10,... | collective-permute-start | bytes 1966088 | tf_op jit(solution)/shard_map/ppermute | solution.py:76
  119.5 19.0 %collective-permute-start.22 = (f32[128,512]{1,0:T(8,128)}, f32[128,512]{1,0:T(8,128)}, u32[]{:S(2)}, u32[]{:S(2)}) collective-permute-start(f32[128,512]{1,0:T(8,128)} %get-tuple-element.86), channel_id=1, source_target_pairs={{0,8},{1,9},{2,10},{3,11},{4,12},{5,13},{6,14},{7,15},{8,0},{9,1},... | collective-permute-start | bytes 786440 | tf_op jit(solution)/shard_map/ppermute | solution.py:76
  129.3 13.7 %collective-permute-start.25 = (f32[128,512]{1,0:T(8,128)}, f32[128,512]{1,0:T(8,128)S(1)}, u32[]{:S(2)}, u32[]{:S(2)}) collective-permute-start(f32[128,512]{1,0:T(8,128)} %get-tuple-element.92), channel_id=1, source_target_pairs={{0,24},{1,25},{2,26},{3,27},{4,28},{5,29},{6,30},{7,31},{8,16},{9,... | collective-permute-start | bytes 786440 | tf_op jit(solution)/shard_map/ppermute | solution.py:76
  135.1 14.7 %collective-permute-start.17 = (f32[64,1280]{1,0:T(8,128)S(1)}, f32[64,1280]{1,0:T(8,128)S(1)}, u32[]{:S(2)}, u32[]{:S(2)}) collective-permute-start(f32[64,1280]{1,0:T(8,128)S(1)} %get-tuple-element.74), channel_id=1, source_target_pairs={{0,8},{1,9},{2,10},{3,11},{4,12},{5,13},{6,14},{7,15},{8,0},{9,1},... | collective-permute-start | bytes 983048 | tf_op jit(solution)/shard_map/ppermute | solution.py:76
  135.3 21.8 %collective-permute-start.20 = (f32[64,1280]{1,0:T(8,128)S(1)}, f32[64,1280]{1,0:T(8,128)S(1)}, u32[]{:S(2)}, u32[]{:S(2)}) collective-permute-start(f32[64,1280]{1,0:T(8,128)S(1)} %get-tuple-element.81), channel_id=1, source_target_pairs={{0,24},{1,25},{2,26},{3,27},{4,28},{5,29},{6,30},{7,31},{8,16},{9,... | collective-permute-start | bytes 983048 | tf_op jit(solution)/shard_map/ppermute | solution.py:76
  139.6 5.2 %collective-permute-start.23 = (f32[64,512]{1,0:T(8,128)S(1)}, f32[64,512]{1,0:T(8,128)S(1)}, u32[]{:S(2)}, u32[]{:S(2)}) collective-permute-start(f32[64,512]{1,0:T(8,128)S(1)} %get-tuple-element.88), channel_id=1, source_target_pairs={{0,4},{1,5},{2,6},{3,7},{4,0},{5,1},{6,2},{7,3},{8,12},{9,13},{10,... | collective-permute-start | bytes 393224 | tf_op jit(solution)/shard_map/ppermute | solution.py:76
  143.0 5.0 %collective-permute-start.26 = (f32[64,512]{1,0:T(8,128)S(1)}, f32[64,512]{1,0:T(8,128)S(1)}, u32[]{:S(2)}, u32[]{:S(2)}) collective-permute-start(f32[64,512]{1,0:T(8,128)S(1)} %get-tuple-element.94), channel_id=1, source_target_pairs={{0,2},{1,3},{2,0},{3,1},{4,6},{5,7},{6,4},{7,5},{8,10},{9,11},{10,... | collective-permute-start | bytes 393224 | tf_op jit(solution)/shard_map/ppermute | solution.py:76
  144.8 17.6 %collective-permute-start.29 = (f32[32,512]{1,0:T(8,128)S(1)}, f32[32,512]{1,0:T(8,128)S(1)}, u32[]{:S(2)}, u32[]{:S(2)}) collective-permute-start(f32[32,512]{1,0:T(8,128)S(1)} %get-tuple-element.98), channel_id=1, source_target_pairs={{0,2},{1,3},{2,0},{3,1},{4,6},{5,7},{6,4},{7,5},{8,10},{9,11},{10,... | collective-permute-start | bytes 196616 | tf_op jit(solution)/shard_map/ppermute | solution.py:76
  148.0 14.4 %collective-permute-start.30 = (f32[32,512]{1,0:T(8,128)S(1)}, f32[32,512]{1,0:T(8,128)S(1)}, u32[]{:S(2)}, u32[]{:S(2)}) collective-permute-start(f32[32,512]{1,0:T(8,128)S(1)} %get-tuple-element.99), channel_id=1, source_target_pairs={{0,4},{1,5},{2,6},{3,7},{4,0},{5,1},{6,2},{7,3},{8,12},{9,13},{10,... | collective-permute-start | bytes 196616 | tf_op jit(solution)/shard_map/ppermute | solution.py:76
  149.8 12.6 %collective-permute-start.27 = (f32[32,1280]{1,0:T(8,128)S(1)}, f32[32,1280]{1,0:T(8,128)S(1)}, u32[]{:S(2)}, u32[]{:S(2)}) collective-permute-start(f32[32,1280]{1,0:T(8,128)S(1)} %get-tuple-element.96), channel_id=1, source_target_pairs={{0,24},{1,25},{2,26},{3,27},{4,28},{5,29},{6,30},{7,31},{8,16},{9,... | collective-permute-start | bytes 491528 | tf_op jit(solution)/shard_map/ppermute | solution.py:76
  157.1 7.1 %collective-permute-start.28 = (f32[32,1280]{1,0:T(8,128)S(1)}, f32[32,1280]{1,0:T(8,128)S(1)}, u32[]{:S(2)}, u32[]{:S(2)}) collective-permute-start(f32[32,1280]{1,0:T(8,128)S(1)} %get-tuple-element.97), channel_id=1, source_target_pairs={{0,8},{1,9},{2,10},{3,11},{4,12},{5,13},{6,14},{7,15},{8,0},{9,1},... | collective-permute-start | bytes 491528 | tf_op jit(solution)/shard_map/ppermute | solution.py:76
  (17 other events, 202.9 us)

commit v9 on v8

--- a/solution.py
+++ b/solution.py
@@ -67,8 +67,8 @@
 MIB = 1024 * 1024
 
 LINKS = (1, 2, 4, 12)
-OUT = ((5, (1, 0, 3, 2)), (5, (0, 2, 1, 3)), (4, (2, 1, 0, 3)))
-BACK = ((5, (1, 0, 2, 3)), (5, (0, 1, 3, 2)), (2, (3, 2, 1, 0)), (2, (2, 3, 0, 1)))
+PIECES = ((5, (1, 0, 3, 2)), (5, (0, 2, 1, 3)), (4, (2, 1, 0, 3)))
+TURNS = (0, 2, 1)
 
 
 def across(value, link):
@@ -87,12 +87,11 @@
     return slot
 
 
-def orders_of(pieces):
-    return [order for _, order in pieces]
-
-
-def piece_columns(width, pieces):
-    shares = [share for share, _ in pieces]
+ORDERS = [order for _, order in PIECES]
+
+
+def piece_columns(width):
+    shares = [share for share, _ in PIECES]
     one = width // sum(shares)
     ends = [one * sum(shares[: at + 1]) for at in range(len(shares))]
     ends[-1] = width
@@ -142,41 +141,20 @@
     return whole_call(kernel, [array], [shape], "hold_back", (after,))[0]
 
 
-def hold_back_tiles(array, after):
-    tile = array.shape[1] // 4
-
-    def kernel(in_ref, after_ref, out_ref):
-        out_ref[...] = in_ref[...]
-
-    spec = pl.BlockSpec((array.shape[0], tile), lambda i: (0, i))
-    return pl.pallas_call(
-        kernel,
-        grid=(4,),
-        in_specs=[spec, pl.BlockSpec(memory_space=pl.ANY)],
-        out_specs=spec,
-        out_shape=jax.ShapeDtypeStruct(array.shape, array.dtype),
-        compiler_params=pltpu.CompilerParams(vmem_limit_bytes=32 * MIB),
-        cost_estimate=pl.CostEstimate(flops=0, bytes_accessed=4 * array.size, transcendentals=0),
-        name="hold_back_tiles",
-    )(array, after)
-
-
 def gather_cube(tokens, side, gate, up, down):
     steps = len(LINKS)
-    others = [swap_cores(gate), swap_cores(up)]
-    held = [tokens[:, start:stop] for start, stop in piece_columns(tokens.shape[1], OUT)]
+    others = [swap_cores(weight) for weight in (gate, up, down)]
+    held = [tokens[:, start:stop] for start, stop in piece_columns(tokens.shape[1])]
     held[-1] = jnp.concatenate([held[-1], side], axis=1)
     for phase in range(steps):
-        got = [across(piece, order[steps - 1 - phase]) for piece, order in zip(held, orders_of(OUT))]
+        got = [across(piece, order[steps - 1 - phase]) for piece, order in zip(held, ORDERS)]
         if phase < steps - 1:
-            held = joined(held, got, others if phase == 1 else ())
-        if phase == 1:
-            others.append(swap_cores(hold_back_tiles(down, held[0])))
+            held = joined(held, got, (others[2:], others[:2], ())[phase])
     return held, got, others
 
 
 def hidden_kernel(unit, chip_ref, *refs):
-    count = len(OUT)
+    count = len(ORDERS)
     held, got = refs[:count], refs[count : 2 * count]
     gate_ref, up_ref, gate_other_ref, up_other_ref = refs[2 * count : 2 * count + 4]
     hidden_ref, scale_ref, rows_ref, side_ref = refs[2 * count + 4 :]
@@ -185,12 +163,12 @@
 
     @pl.when(step == 0)
     def _():
-        for piece, (start, stop) in enumerate(piece_columns(rows_ref.shape[1], OUT)):
+        for piece, (start, stop) in enumerate(piece_columns(rows_ref.shape[1])):
             half = held[piece].shape[0]
             for place in range(2 * half // unit):
                 source = held[piece] if place * unit < half else got[piece]
                 at = place * unit % half
-                slot = slot_of(place, OUT[piece][1])
+                slot = slot_of(place, ORDERS[piece])
                 to = slice(slot * unit, (slot + 1) * unit)
                 rows_ref[to, start:stop] = source[at : at + unit, : stop - start]
                 if piece == count - 1:
@@ -253,7 +231,7 @@
 
 def output_kernel(unit, order, tiles, scale_ref, hidden_ref, *refs):
     down, down_other = refs[:tiles], refs[tiles : 2 * tiles]
-    keep_ref, send_ref = refs[2 * tiles :]
+    keep_ref, send_ref = refs[-2:]
     units, tile = down[0].shape
     places = hidden_ref.shape[0] // unit
     for out_ref, first in ((send_ref, places // 2), (keep_ref, 0)):
@@ -267,7 +245,7 @@
             out_ref[:, at * tile : (at + 1) * tile] = out * scale
 
 
-def expert_output(unit, order, columns, scale, hidden, down, down_other):
+def expert_output(unit, order, columns, scale, hidden, down, down_other, after):
     units = down.shape[0]
     start, stop = columns
     count = hidden.shape[0]
@@ -285,7 +263,8 @@
             pl.BlockSpec((count, 1), lambda i: (0, 0)),
             pl.BlockSpec((count, 2 * units), lambda i: (0, 0)),
         ]
-        + [tile_at(at) for at in range(tiles)] * 2,
+        + [tile_at(at) for at in range(tiles)] * 2
+        + [pl.BlockSpec(memory_space=pl.ANY)] * len(after),
         out_specs=[pl.BlockSpec((count // 2, stop - start), lambda i: (0, 0))] * 2,
         out_shape=[half] * 2,
         compiler_params=pltpu.CompilerParams(vmem_limit_bytes=24 * MIB),
@@ -295,10 +274,10 @@
             transcendentals=0,
         ),
         name="expert_output",
-    )(scale, hidden, *[down] * tiles, *[down_other] * tiles)
-
-
-def halved(keep, got):
+    )(scale, hidden, *[down] * tiles, *[down_other] * tiles, *after)
+
+
+def halved(keep, got, after):
     rows, width = keep.shape
     half = jax.ShapeDtypeStruct((rows // 2, width), keep.dtype)
 
@@ -306,7 +285,7 @@
         second_ref[...] = keep_ref[rows // 2 :] + got_ref[rows // 2 :]
         first_ref[...] = keep_ref[: rows // 2] + got_ref[: rows // 2]
 
-    return whole_call(kernel, [keep, got], [half, half], "halved")
+    return whole_call(kernel, [keep, got], [half, half], "halved", after)
 
 
 def finished(keep, got):
@@ -314,7 +293,7 @@
     width = sum(piece.shape[1] for piece in keep)
 
     def kernel(*refs):
-        for at, (start, stop) in enumerate(piece_columns(width, BACK)):
+        for at, (start, stop) in enumerate(piece_columns(width)):
             total = refs[at][...] + refs[count + at][...]
             refs[2 * count][:, start:stop] = total.astype(jnp.bfloat16)
 
@@ -328,19 +307,21 @@
     chip = (lax.axis_index("ep") // 2).astype(jnp.int32).reshape(1)
     hidden, scale = expert_hidden(unit, chip, held, got, gate, up, gate_other, up_other)
     keep, coming = [], []
-    for order, columns in zip(orders_of(BACK), piece_columns(down.shape[1], BACK)):
-        mine, send = expert_output(unit, order, columns, scale, hidden, down, down_other)
+    for order, columns in zip(ORDERS, piece_columns(down.shape[1])):
+        after = keep[-1:]
+        mine, send = expert_output(unit, order, columns, scale, hidden, down, down_other, after)
         keep.append(mine)
         coming.append(across(send, order[0]))
     return keep, coming
 
 
 def cube_sums(keep, got):
-    keep, got = list(keep), list(got)
+    keep, got, after = list(keep), list(got), ()
     for phase in range(1, len(LINKS)):
-        for at, order in enumerate(orders_of(BACK)):
-            keep[at], send = halved(keep[at], got[at])
-            got[at] = across(send, order[phase])
+        for at in TURNS:
+            keep[at], send = halved(keep[at], got[at], after)
+            got[at] = across(send, ORDERS[at][phase])
+            after = (keep[at],)
     return finished(keep, got)
 
 
@@ -369,6 +350,18 @@
     latent = prefill_latent.shape[3]
     tok_rows, top_k = expert_ids.shape
 
+    cube = peers == 2 << len(LINKS) and lax.axis_size("tp") == 1
+    weights = (gate_weight[0], up_weight[0], down_weight[0])
+    if cube:
+        experts = jnp.arange(peers // 2, dtype=jnp.int32)
+        named = expert_ids[:, :, None] == experts[None, None, :]
+        share = jnp.sum(jnp.where(named, route_weight[:, :, None], 0.0), axis=1)
+        parts = jnp.concatenate(three_parts(share), axis=1).astype(jnp.bfloat16)
+        parts = jnp.pad(parts, ((0, 0), (0, 128 - parts.shape[1])))
+        *gathered, others = gather_cube(tokens, parts, *weights)
+        keep, coming = cube_outputs(tok_rows, *gathered, weights, others)
+        prefill_latent = hold_back(prefill_latent, keep[-1])
+
     owner = block_owner.reshape(blocks)
     same = owner[:, None] == owner[None, :]
     earlier = jnp.arange(blocks)[None, :] < jnp.arange(blocks)[:, None]
@@ -381,8 +374,6 @@
         preferred_element_type=jnp.float32,
     ).astype(jnp.bfloat16)
 
-    cube = peers == 2 << len(LINKS) and lax.axis_size("tp") == 1
-    weights = (gate_weight[0], up_weight[0], down_weight[0])
     filled = jnp.sum(chosen.astype(jnp.float32), axis=1).reshape(peers, 1, 2)
     side = jnp.zeros((peers, 2 * block_len, max(tok_rows, 2)), jnp.float32)
     side = side.at[:, 3:4, :2].set(filled)
@@ -394,15 +385,6 @@
     leaving = jnp.concatenate(
         [packed.reshape(peers, 2 * block_len, latent), side.astype(jnp.bfloat16)], axis=2
     )
-    if cube:
-        experts = jnp.arange(peers // 2, dtype=jnp.int32)
-        named = expert_ids[:, :, None] == experts[None, None, :]
-        share = jnp.sum(jnp.where(named, route_weight[:, :, None], 0.0), axis=1)
-        parts = jnp.concatenate(three_parts(share), axis=1).astype(jnp.bfloat16)
-        parts = jnp.pad(parts, ((0, 0), (0, 128 - parts.shape[1])))
-        *gathered, others = gather_cube(tokens, parts, *weights)
-        keep, coming = cube_outputs(tok_rows, *gathered, weights, others)
-        leaving = hold_back(leaving, keep[-1])
     arrived = lax.all_to_all(leaving, "ep", split_axis=0, concat_axis=0, tiled=True)
     side_in = arrived[:, :, latent:].astype(jnp.float32)
     present = side_in[:, 3, :2].reshape(peers * 2)

time: 166 us -> 145 us (0.87)
  local copies, waits for them, and re-layouts: 16.5 us -> 8.8 us
  starting transfers between devices: 53.3 us -> 46.6 us
  Pallas kernels: 36.7 us -> 33.5 us
  waiting for transfers between devices: 51.2 us -> 48.1 us
    ppermute x28 -> x24, starting transfers between devices: 48.8 us -> 42.1 us  [across(): lax.ppermute(value, 'ep', [(i, i ^ 2 * LINKS[link]) for i in range(peers)])]
    unnamed x34 -> x22, local copies, waits for them, and re-layouts: 10.7 us -> 4.04 us
    ppermute x28 -> x24, waiting for transfers between devices: 51.2 us -> 48.1 us  [across(): lax.ppermute(value, 'ep', [(i, i ^ 2 * LINKS[link]) for i in range(peers)])]
    pallas_call x1 -> x0, Pallas kernels: 2.61 us -> none  [hold_back_tiles(): pl.pallas_call(kernel, grid=(4,), in_specs=[spec, pl.BlockSpec(memory_spa...]
    pallas_call x4 -> x3, Pallas kernels: 10.5 us -> 9.81 us  [expert_output(): pl.pallas_call(functools.partial(output_kernel, unit, order, tiles), grid...]
    pallas_call x17 -> x14, Pallas kernels: 10.3 us -> 10.3 us  [whole_call(): pl.pallas_call(body, in_specs=[pl.BlockSpec(memory_space=pltpu.VMEM)] * g...]
  transfers between devices with their start and end apart: 32 -> 28, of which waited for: 14 -> 13; matrix products, arithmetic and copies ran while one was open for 7% -> 7% of each run, Pallas kernels for 18% -> 11%
where the time goes in v9:
time: 145 us; the launch traced here: 144 us
  waiting for transfers between devices  48.1 us (33%)
  starting transfers between devices  46.6 us (32%)
  Pallas kernels  33.5 us (23%)
  local copies, waits for them, and re-layouts  8.8 us (6%)
  other arithmetic  3.19 us (2%)
  matrix products  2.63 us (2%)
  between operations  1.54 us (1%)
    ppermute x24, waiting for transfers between devices, across(): lax.ppermute(value, 'ep', [(i, i ^ 2 * LINKS[link]) for i in range(peers)])  48.1 us
    ppermute x24, starting transfers between devices, across(): lax.ppermute(value, 'ep', [(i, i ^ 2 * LINKS[link]) for i in range(peers)])  42.1 us
    pallas_call x1, Pallas kernels, expert_hidden(): pl.pallas_call(functools.partial(hidden_kernel, unit), grid=(2 * steps,),...  13.4 us
    pallas_call x14, Pallas kernels, whole_call(): pl.pallas_call(body, in_specs=[pl.BlockSpec(memory_space=pltpu.VMEM)] * g...  10.3 us
    pallas_call x3, Pallas kernels, expert_output(): pl.pallas_call(functools.partial(output_kernel, unit, order, tiles), grid...  9.81 us
    unnamed x22, local copies, waits for them, and re-layouts  4.04 us
    all_to_all x1, starting transfers between devices, per_device(): lax.all_to_all(leaving, 'ep', split_axis=0, concat_axis=0, tiled=True)  3.48 us
  transfers between devices with their start and end apart: 28, of which 13 were waited for; matrix products, arithmetic and copies ran while one was open for 7% of the time, Pallas kernels for 11%

profile of v9, /device:TPU:0, one launch (start us, length us, event | category | flops | bytes accessed | tf_op | source)
XLA Modules:
  0.0 144.3 jit_solution(3537352425148703911)
XLA Ops:
  3.5 4.7 %collective-permute-start.2 = (bf16[32,1152]{1,0:T(8,128)(2,1)S(1)}, bf16[32,1152]{1,0:T(8,128)(2,1)S(1)}, u32[]{:S(2)}, u32[]{:S(2)}) collective-permute-start(bf16[32,1152]{1,0:T(8,128)(2,1)S(1)} %pad_maximum_fusion.refs_2_), channel_id=1, source_target_pairs={{0,24},{1,25},{2,26},{3,27},{4,28},{5,29},{6,30},{7,31},{8,16},{9,... | collective-permute-start | bytes 221192 | tf_op jit(solution)/shard_map/ppermute | solution.py:76
  9.3 2.1 %collective-permute-done.2.refs_5_ = bf16[32,1152]{1,0:T(8,128)(2,1)S(1)} collective-permute-done((bf16[32,1152]{1,0:T(8,128)(2,1)S(1)}, bf16[32,1152]{1,0:T(8,128)(2,1)S(1)}, u32[]{:S(2)}, u32[]{:S(2)}) %collective-permute-start.2) | collective-permute-done | bytes 73760 | tf_op jit(solution)/shard_map/ppermute | solution.py:76
  11.4 3.7 %collective-permute-start.1 = (bf16[32,1280]{1,0:T(8,128)(2,1)S(1)}, bf16[32,1280]{1,0:T(8,128)(2,1)S(1)}, u32[]{:S(2)}, u32[]{:S(2)}) collective-permute-start(bf16[32,1280]{1,0:T(8,128)(2,1)S(1)} %get-tuple-element.84.refs_1_), channel_id=1, source_target_pairs={{0,24},{1,25},{2,26},{3,27},{4,28},{5,29},{6,30},{7,31},{8,16},{9,... | collective-permute-start | bytes 245768 | tf_op jit(solution)/shard_map/ppermute | solution.py:76
  15.1 2.6 %collective-permute-done.1.refs_4_ = bf16[32,1280]{1,0:T(8,128)(2,1)S(1)} collective-permute-done((bf16[32,1280]{1,0:T(8,128)(2,1)S(1)}, bf16[32,1280]{1,0:T(8,128)(2,1)S(1)}, u32[]{:S(2)}, u32[]{:S(2)}) %collective-permute-start.1) | collective-permute-done | bytes 81952 | tf_op jit(solution)/shard_map/ppermute | solution.py:76
  17.8 3.8 %collective-permute-start.4 = (bf16[64,1280]{1,0:T(8,128)(2,1)S(1)}, bf16[64,1280]{1,0:T(8,128)(2,1)S(1)}, u32[]{:S(2)}, u32[]{:S(2)}) collective-permute-start(bf16[64,1280]{1,0:T(8,128)(2,1)S(1)} %get-tuple-element.49.refs_0_), channel_id=1, source_target_pairs={{0,24},{1,25},{2,26},{3,27},{4,28},{5,29},{6,30},{7,31},{8,16},{9,... | collective-permute-start | bytes 491528 | tf_op jit(solution)/shard_map/ppermute | solution.py:76
  21.6 1.5 %collective-permute-start.5 = (bf16[64,1280]{1,0:T(8,128)(2,1)S(1)}, bf16[64,1280]{1,0:T(8,128)(2,1)S(1)}, u32[]{:S(2)}, u32[]{:S(2)}) collective-permute-start(bf16[64,1280]{1,0:T(8,128)(2,1)S(1)} %get-tuple-element.50.refs_1_), channel_id=1, source_target_pairs={{0,4},{1,5},{2,6},{3,7},{4,0},{5,1},{6,2},{7,3},{8,12},{9,13},{10,... | collective-permute-start | bytes 491528 | tf_op jit(solution)/shard_map/ppermute | solution.py:76
  24.6 4.2 %collective-permute-done.6.refs_5_ = bf16[64,1152]{1,0:T(8,128)(2,1)S(1)} collective-permute-done((bf16[64,1152]{1,0:T(8,128)(2,1)S(1)}, bf16[64,1152]{1,0:T(8,128)(2,1)S(1)}, u32[]{:S(2)}, u32[]{:S(2)}) %collective-permute-start.6) | collective-permute-done | bytes 147488 | tf_op jit(solution)/shard_map/ppermute | solution.py:76
  29.0 1.6 %collective-permute-start.9 = (bf16[128,1280]{1,0:T(8,128)(2,1)S(1)}, bf16[128,1280]{1,0:T(8,128)(2,1)S(1)}, u32[]{:S(2)}, u32[]{:S(2)}) collective-permute-start(bf16[128,1280]{1,0:T(8,128)(2,1)S(1)} %get-tuple-element.52.refs_0_), channel_id=1, source_target_pairs={{0,2},{1,3},{2,0},{3,1},{4,6},{5,7},{6,4},{7,5},{8,10},{9,11},{10,... | collective-permute-start | bytes 983048 | tf_op jit(solution)/shard_map/ppermute | solution.py:76
  31.0 8.8 %collective-permute-done.11.refs_5_ = bf16[128,1152]{1,0:T(8,128)(2,1)S(1)} collective-permute-done((bf16[128,1152]{1,0:T(8,128)(2,1)S(1)}, bf16[128,1152]{1,0:T(8,128)(2,1)S(1)}, u32[]{:S(2)}, u32[]{:S(2)}) %collective-permute-start.11) | collective-permute-done | bytes 294944 | tf_op jit(solution)/shard_map/ppermute | solution.py:76
  40.6 2.4 %collective-permute-start.14 = (bf16[256,1152]{1,0:T(8,128)(2,1)S(1)}, bf16[256,1152]{1,0:T(8,128)(2,1)}, u32[]{:S(2)}, u32[]{:S(2)}) collective-permute-start(bf16[256,1152]{1,0:T(8,128)(2,1)S(1)} %get-tuple-element.57.refs_2_), channel_id=1, source_target_pairs={{0,8},{1,9},{2,10},{3,11},{4,12},{5,13},{6,14},{7,15},{8,0},{9,1},... | collective-permute-start | bytes 1769480 | tf_op jit(solution)/shard_map/ppermute | solution.py:76
  43.0 8.0 %collective-permute-done.14.refs_5_ = bf16[256,1152]{1,0:T(8,128)(2,1)} collective-permute-done((bf16[256,1152]{1,0:T(8,128)(2,1)S(1)}, bf16[256,1152]{1,0:T(8,128)(2,1)}, u32[]{:S(2)}, u32[]{:S(2)}) %collective-permute-start.14) | collective-permute-done | bytes 589856 | tf_op jit(solution)/shard_map/ppermute | solution.py:76
  51.3 13.4 %expert_hidden.1 = (bf16[512,1024]{1,0:T(8,128)(2,1)S(1)}, f32[512,1]{1,0:T(8,128)S(1)}) custom-call(s32[1]{0:T(128)} %bitcast.2.chip_ref, bf16[256,1280]{1,0:T(8,128)(2,1)S(1)} %get-tuple-element.55.refs_0_, bf16[256,1280]{1,0:T(8,128)(2,1)S(1)} %get-tuple-element.56.refs_1_, bf16[256,1152]{1,0:T(8,128)(2,1)S(1)} %get-tuple-element.57.refs_2_, ...), custom_call_target="tpu_custom_call" | custom-call | flops 7516192768 | bytes 19398656 | tf_op jit(solution)/shard_map/expert_hidden/pallas_call | solution.py:204
  64.7 3.5 %expert_output.3 = (f32[256,1280]{1,0:T(8,128)S(1)}, f32[256,1280]{1,0:T(8,128)}) custom-call(f32[512,1]{1,0:T(8,128)S(1)} %get-tuple-element.58.scale_ref, bf16[512,1024]{1,0:T(8,128)(2,1)S(1)} %get-tuple-element.59.hidden_ref, bf16[512,3584]{1,0:T(8,128)(2,1)S(1)} %bitcast.20, bf16[512,3584]{1,0:T(8,128)(2,1)S(1)} %bitcast.21, ...), custom_call_target="tpu_custom_call" | custom-call | flops 1342177280 | bytes 6291456 | tf_op jit(solution)/shard_map/expert_output/pallas_call | solution.py:259
  69.5 3.4 %expert_output.4 = (f32[256,1280]{1,0:T(8,128)S(1)}, f32[256,1280]{1,0:T(8,128)}) custom-call(f32[512,1]{1,0:T(8,128)S(1)} %get-tuple-element.58.scale_ref, bf16[512,1024]{1,0:T(8,128)(2,1)S(1)} %get-tuple-element.59.hidden_ref, bf16[512,3584]{1,0:T(8,128)(2,1)S(1)} %bitcast.25, bf16[512,3584]{1,0:T(8,128)(2,1)S(1)} %bitcast.26, ...), custom_call_target="tpu_custom_call" | custom-call | flops 1342177280 | bytes 6291456 | tf_op jit(solution)/shard_map/expert_output/pallas_call | solution.py:259
  74.6 2.9 %expert_output.5 = (f32[256,1024]{1,0:T(8,128)S(1)}, f32[256,1024]{1,0:T(8,128)}) custom-call(f32[512,1]{1,0:T(8,128)S(1)} %get-tuple-element.58.scale_ref, bf16[512,1024]{1,0:T(8,128)(2,1)S(1)} %get-tuple-element.59.hidden_ref, bf16[512,3584]{1,0:T(8,128)(2,1)S(1)} %bitcast.30, bf16[512,3584]{1,0:T(8,128)(2,1)S(1)} %bitcast.31, ...), custom_call_target="tpu_custom_call" | custom-call | flops 1073741824 | bytes 5242880 | tf_op jit(solution)/shard_map/expert_output/pallas_call | solution.py:259
  78.5 1.9 %collective-permute-start.18 = (f32[256,1024]{1,0:T(8,128)}, f32[256,1024]{1,0:T(8,128)}, u32[]{:S(2)}, u32[]{:S(2)}) collective-permute-start(f32[256,1024]{1,0:T(8,128)} %get-tuple-element.67), channel_id=1, source_target_pairs={{0,8},{1,9},{2,10},{3,11},{4,12},{5,13},{6,14},{7,15},{8,0},{9,1},... | collective-permute-start | bytes 3145736 | tf_op jit(solution)/shard_map/ppermute | solution.py:76
  83.6 3.5 %all-to-all-start = ((bf16[32,8,608]{2,1,0:T(8,128)(2,1)}), bf16[32,8,608]{2,1,0:T(8,128)(2,1)}, u32[]{:S(2)}, u32[]{:S(2)}) async-start(bf16[32,8,608]{2,1,0:T(8,128)(2,1)} %fusion.21), calls=%async_computation | async-start | bytes 655360 | tf_op jit(solution)/shard_map/all_to_all | solution.py:388
  87.1 7.3 %collective-permute-done.15.refs_1_ = f32[256,1280]{1,0:T(8,128)} collective-permute-done((f32[256,1280]{1,0:T(8,128)}, f32[256,1280]{1,0:T(8,128)}, u32[]{:S(2)}, u32[]{:S(2)}) %collective-permute-start.15) | collective-permute-done | bytes 1310752 | tf_op jit(solution)/shard_map/ppermute | solution.py:76
  94.4 2.4 %halved.9 = (f32[128,1280]{1,0:T(8,128)S(1)}, f32[128,1280]{1,0:T(8,128)}) custom-call(f32[256,1280]{1,0:T(8,128)S(1)} %get-tuple-element.60.refs_10_.refs_0_, f32[256,1280]{1,0:T(8,128)} %collective-permute-done.15.refs_1_), custom_call_target="tpu_custom_call" | custom-call | bytes 3932160 | tf_op jit(solution)/shard_map/halved/pallas_call | solution.py:107
  97.9 2.8 %collective-permute-done.18.refs_1_ = f32[256,1024]{1,0:T(8,128)} collective-permute-done((f32[256,1024]{1,0:T(8,128)}, f32[256,1024]{1,0:T(8,128)}, u32[]{:S(2)}, u32[]{:S(2)}) %collective-permute-start.18) | collective-permute-done | bytes 1048608 | tf_op jit(solution)/shard_map/ppermute | solution.py:76
  100.8 2.1 %halved.10 = (f32[128,1024]{1,0:T(8,128)S(1)}, f32[128,1024]{1,0:T(8,128)}) custom-call(f32[256,1024]{1,0:T(8,128)S(1)} %copy-done.4, f32[256,1024]{1,0:T(8,128)} %collective-permute-done.18.refs_1_, f32[128,1280]{1,0:T(8,128)S(1)} %get-tuple-element.64.refs_2_.refs_0_), custom_call_target="tpu_custom_call" | custom-call | bytes 3145728 | tf_op jit(solution)/shard_map/halved/pallas_call | solution.py:107
  104.2 2.3 %halved.11 = (f32[128,1280]{1,0:T(8,128)S(1)}, f32[128,1280]{1,0:T(8,128)}) custom-call(f32[256,1280]{1,0:T(8,128)S(1)} %get-tuple-element.61.refs_8_.refs_0_, f32[256,1280]{1,0:T(8,128)} %collective-permute-done.17.refs_1_, f32[128,1024]{1,0:T(8,128)S(1)} %get-tuple-element.68.refs_2_.refs_0_), custom_call_target="tpu_custom_call" | custom-call | bytes 3932160 | tf_op jit(solution)/shard_map/halved/pallas_call | solution.py:107
  106.5 2.5 %collective-permute-start.20 = (f32[128,1280]{1,0:T(8,128)}, f32[128,1280]{1,0:T(8,128)}, u32[]{:S(2)}, u32[]{:S(2)}) collective-permute-start(f32[128,1280]{1,0:T(8,128)} %get-tuple-element.72), channel_id=1, source_target_pairs={{0,8},{1,9},{2,10},{3,11},{4,12},{5,13},{6,14},{7,15},{8,0},{9,1},... | collective-permute-start | bytes 1966088 | tf_op jit(solution)/shard_map/ppermute | solution.py:76
  109.6 1.9 %collective-permute-start.21 = (f32[128,1024]{1,0:T(8,128)}, f32[128,1024]{1,0:T(8,128)S(1)}, u32[]{:S(2)}, u32[]{:S(2)}) collective-permute-start(f32[128,1024]{1,0:T(8,128)} %get-tuple-element.73), channel_id=1, source_target_pairs={{0,4},{1,5},{2,6},{3,7},{4,0},{5,1},{6,2},{7,3},{8,12},{9,13},{10,... | collective-permute-start | bytes 1572872 | tf_op jit(solution)/shard_map/ppermute | solution.py:76
  115.9 1.6 %collective-permute-start.19 = (f32[64,1280]{1,0:T(8,128)S(1)}, f32[64,1280]{1,0:T(8,128)S(1)}, u32[]{:S(2)}, u32[]{:S(2)}) collective-permute-start(f32[64,1280]{1,0:T(8,128)S(1)} %get-tuple-element.71), channel_id=1, source_target_pairs={{0,24},{1,25},{2,26},{3,27},{4,28},{5,29},{6,30},{7,31},{8,16},{9,... | collective-permute-start | bytes 983048 | tf_op jit(solution)/shard_map/ppermute | solution.py:76
  117.6 1.5 %collective-permute-done.21.refs_1_ = f32[128,1024]{1,0:T(8,128)S(1)} collective-permute-done((f32[128,1024]{1,0:T(8,128)}, f32[128,1024]{1,0:T(8,128)S(1)}, u32[]{:S(2)}, u32[]{:S(2)}) %collective-permute-start.21) | collective-permute-done | bytes 524320 | tf_op jit(solution)/shard_map/ppermute | solution.py:76
  122.5 5.5 %collective-permute-start.22 = (f32[64,1280]{1,0:T(8,128)S(1)}, f32[64,1280]{1,0:T(8,128)S(1)}, u32[]{:S(2)}, u32[]{:S(2)}) collective-permute-start(f32[64,1280]{1,0:T(8,128)S(1)} %get-tuple-element.77), channel_id=1, source_target_pairs={{0,4},{1,5},{2,6},{3,7},{4,0},{5,1},{6,2},{7,3},{8,12},{9,13},{10,... | collective-permute-start | bytes 983048 | tf_op jit(solution)/shard_map/ppermute | solution.py:76
  129.1 3.9 %collective-permute-done.22.refs_1_ = f32[64,1280]{1,0:T(8,128)S(1)} collective-permute-done((f32[64,1280]{1,0:T(8,128)S(1)}, f32[64,1280]{1,0:T(8,128)S(1)}, u32[]{:S(2)}, u32[]{:S(2)}) %collective-permute-start.22) | collective-permute-done | bytes 327712 | tf_op jit(solution)/shard_map/ppermute | solution.py:76
  133.1 3.8 %collective-permute-start.26 = (f32[32,1024]{1,0:T(8,128)S(1)}, f32[32,1024]{1,0:T(8,128)S(1)}, u32[]{:S(2)}, u32[]{:S(2)}) collective-permute-start(f32[32,1024]{1,0:T(8,128)S(1)} %get-tuple-element.83), channel_id=1, source_target_pairs={{0,24},{1,25},{2,26},{3,27},{4,28},{5,29},{6,30},{7,31},{8,16},{9,... | collective-permute-start | bytes 393224 | tf_op jit(solution)/shard_map/ppermute | solution.py:76
  137.0 1.5 %fusion.14 = bf16[1,128,512]{2,1,0:T(8,128)(2,1)} fusion(bf16[256,576]{0,1:T(8,128)(2,1)S(1)} %copy-done.8, bf16[1024,576]{0,1:T(8,128)(2,1)S(1)} %bitcast.39, f32[1280,128]{1,0:T(8,128)S(1)} %get-tuple-element.90, f32[128]{0:T(128)S(1)} %get-tuple-element.89, pred[1280]{0:T(1024)(128)(4,1)S(1)} %pad_add_fusion, f32[128]{0:T(128)S(1)} %fusion.18), kind=kOutput, calls=%fused_computation.12 | convolution fusion | flops 171016192 | bytes 2263296 | tf_op jit(solution)/shard_map/dot_general | solution.py:38
  138.5 3.4 %collective-permute-done.26.refs_5_ = f32[32,1024]{1,0:T(8,128)S(1)} collective-permute-done((f32[32,1024]{1,0:T(8,128)S(1)}, f32[32,1024]{1,0:T(8,128)S(1)}, u32[]{:S(2)}, u32[]{:S(2)}) %collective-permute-start.26) | collective-permute-done | bytes 131104 | tf_op jit(solution)/shard_map/ppermute | solution.py:76
  141.9 1.6 %collective-permute-done.24.refs_3_ = f32[32,1280]{1,0:T(8,128)S(1)} collective-permute-done((f32[32,1280]{1,0:T(8,128)S(1)}, f32[32,1280]{1,0:T(8,128)S(1)}, u32[]{:S(2)}, u32[]{:S(2)}) %collective-permute-start.24) | collective-permute-done | bytes 163872 | tf_op jit(solution)/shard_map/ppermute | solution.py:76
  (92 shorter events, 26.5 us)
Async XLA Ops:
  0.6 127.3 %copy-start = (bf16[1,128,576]{1,2,0:T(8,128)(2,1)S(1)}, bf16[1,128,576]{1,2,0:T(8,128)(2,1)}, u32[]{:S(2)}) copy-start(bf16[1,128,576]{1,2,0:T(8,128)(2,1)} %param.13) | copy-start | bytes 442372
  0.6 17.1 %collective-permute-start.3 = (bf16[512,3584]{1,0:T(8,128)(2,1)}, bf16[512,3584]{1,0:T(8,128)(2,1)}, u32[]{:S(2)}, u32[]{:S(2)}) collective-permute-start(bf16[512,3584]{1,0:T(8,128)(2,1)} %bitcast.19), channel_id=1, source_target_pairs={{0,1},{1,0},{2,3},{3,2},{4,5},{5,4},{6,7},{7,6},{8,9},{9,8},{10,11... | collective-permute-start | bytes 11010056 | tf_op jit(solution)/shard_map/ppermute | solution.py:80
  1.2 23.4 %collective-permute-start.7 = (bf16[3584,512]{1,0:T(8,128)(2,1)}, bf16[3584,512]{1,0:T(8,128)(2,1)}, u32[]{:S(2)}, u32[]{:S(2)}) collective-permute-start(bf16[3584,512]{1,0:T(8,128)(2,1)} %bitcast.34), channel_id=1, source_target_pairs={{0,1},{1,0},{2,3},{3,2},{4,5},{5,4},{6,7},{7,6},{8,9},{9,8},{10,11... | collective-permute-start | bytes 11010056 | tf_op jit(solution)/shard_map/ppermute | solution.py:80
  1.2 23.4 %collective-permute-start.8 = (bf16[3584,512]{1,0:T(8,128)(2,1)}, bf16[3584,512]{1,0:T(8,128)(2,1)}, u32[]{:S(2)}, u32[]{:S(2)}) collective-permute-start(bf16[3584,512]{1,0:T(8,128)(2,1)} %bitcast.36), channel_id=1, source_target_pairs={{0,1},{1,0},{2,3},{3,2},{4,5},{5,4},{6,7},{7,6},{8,9},{9,8},{10,11... | collective-permute-start | bytes 11010056 | tf_op jit(solution)/shard_map/ppermute | solution.py:80
  3.5 7.9 %collective-permute-start.2 = (bf16[32,1152]{1,0:T(8,128)(2,1)S(1)}, bf16[32,1152]{1,0:T(8,128)(2,1)S(1)}, u32[]{:S(2)}, u32[]{:S(2)}) collective-permute-start(bf16[32,1152]{1,0:T(8,128)(2,1)S(1)} %pad_maximum_fusion.refs_2_), channel_id=1, source_target_pairs={{0,24},{1,25},{2,26},{3,27},{4,28},{5,29},{6,30},{7,31},{8,16},{9,... | collective-permute-start | bytes 221192 | tf_op jit(solution)/shard_map/ppermute | solution.py:76
  9.2 5.9 %collective-permute-start = (bf16[32,1280]{1,0:T(8,128)(2,1)S(1)}, bf16[32,1280]{1,0:T(8,128)(2,1)S(1)}, u32[]{:S(2)}, u32[]{:S(2)}) collective-permute-start(bf16[32,1280]{1,0:T(8,128)(2,1)S(1)} %get-tuple-element.85.refs_0_), channel_id=1, source_target_pairs={{0,8},{1,9},{2,10},{3,11},{4,12},{5,13},{6,14},{7,15},{8,0},{9,1},... | collective-permute-start | bytes 245768 | tf_op jit(solution)/shard_map/ppermute | solution.py:76
  11.4 6.3 %collective-permute-start.1 = (bf16[32,1280]{1,0:T(8,128)(2,1)S(1)}, bf16[32,1280]{1,0:T(8,128)(2,1)S(1)}, u32[]{:S(2)}, u32[]{:S(2)}) collective-permute-start(bf16[32,1280]{1,0:T(8,128)(2,1)S(1)} %get-tuple-element.84.refs_1_), channel_id=1, source_target_pairs={{0,24},{1,25},{2,26},{3,27},{4,28},{5,29},{6,30},{7,31},{8,16},{9,... | collective-permute-start | bytes 245768 | tf_op jit(solution)/shard_map/ppermute | solution.py:76
  17.8 11.1 %collective-permute-start.4 = (bf16[64,1280]{1,0:T(8,128)(2,1)S(1)}, bf16[64,1280]{1,0:T(8,128)(2,1)S(1)}, u32[]{:S(2)}, u32[]{:S(2)}) collective-permute-start(bf16[64,1280]{1,0:T(8,128)(2,1)S(1)} %get-tuple-element.49.refs_0_), channel_id=1, source_target_pairs={{0,24},{1,25},{2,26},{3,27},{4,28},{5,29},{6,30},{7,31},{8,16},{9,... | collective-permute-start | bytes 491528 | tf_op jit(solution)/shard_map/ppermute | solution.py:76
  21.6 7.2 %collective-permute-start.5 = (bf16[64,1280]{1,0:T(8,128)(2,1)S(1)}, bf16[64,1280]{1,0:T(8,128)(2,1)S(1)}, u32[]{:S(2)}, u32[]{:S(2)}) collective-permute-start(bf16[64,1280]{1,0:T(8,128)(2,1)S(1)} %get-tuple-element.50.refs_1_), channel_id=1, source_target_pairs={{0,4},{1,5},{2,6},{3,7},{4,0},{5,1},{6,2},{7,3},{8,12},{9,13},{10,... | collective-permute-start | bytes 491528 | tf_op jit(solution)/shard_map/ppermute | solution.py:76
  23.1 5.7 %collective-permute-start.6 = (bf16[64,1152]{1,0:T(8,128)(2,1)S(1)}, bf16[64,1152]{1,0:T(8,128)(2,1)S(1)}, u32[]{:S(2)}, u32[]{:S(2)}) collective-permute-start(bf16[64,1152]{1,0:T(8,128)(2,1)S(1)} %get-tuple-element.51.refs_2_), channel_id=1, source_target_pairs={{0,2},{1,3},{2,0},{3,1},{4,6},{5,7},{6,4},{7,5},{8,10},{9,11},{10,... | collective-permute-start | bytes 442376 | tf_op jit(solution)/shard_map/ppermute | solution.py:76
  28.9 11.0 %collective-permute-start.10 = (bf16[128,1280]{1,0:T(8,128)(2,1)S(1)}, bf16[128,1280]{1,0:T(8,128)(2,1)S(1)}, u32[]{:S(2)}, u32[]{:S(2)}) collective-permute-start(bf16[128,1280]{1,0:T(8,128)(2,1)S(1)} %get-tuple-element.53.refs_1_), channel_id=1, source_target_pairs={{0,8},{1,9},{2,10},{3,11},{4,12},{5,13},{6,14},{7,15},{8,0},{9,1},... | collective-permute-start | bytes 983048 | tf_op jit(solution)/shard_map/ppermute | solution.py:76
  29.0 10.9 %collective-permute-start.9 = (bf16[128,1280]{1,0:T(8,128)(2,1)S(1)}, bf16[128,1280]{1,0:T(8,128)(2,1)S(1)}, u32[]{:S(2)}, u32[]{:S(2)}) collective-permute-start(bf16[128,1280]{1,0:T(8,128)(2,1)S(1)} %get-tuple-element.52.refs_0_), channel_id=1, source_target_pairs={{0,2},{1,3},{2,0},{3,1},{4,6},{5,7},{6,4},{7,5},{8,10},{9,11},{10,... | collective-permute-start | bytes 983048 | tf_op jit(solution)/shard_map/ppermute | solution.py:76
  30.5 9.4 %collective-permute-start.11 = (bf16[128,1152]{1,0:T(8,128)(2,1)S(1)}, bf16[128,1152]{1,0:T(8,128)(2,1)S(1)}, u32[]{:S(2)}, u32[]{:S(2)}) collective-permute-start(bf16[128,1152]{1,0:T(8,128)(2,1)S(1)} %get-tuple-element.54.refs_2_), channel_id=1, source_target_pairs={{0,4},{1,5},{2,6},{3,7},{4,0},{5,1},{6,2},{7,3},{8,12},{9,13},{10,... | collective-permute-start | bytes 884744 | tf_op jit(solution)/shard_map/ppermute | solution.py:76
  40.0 11.3 %collective-permute-start.12 = (bf16[256,1280]{1,0:T(8,128)(2,1)S(1)}, bf16[256,1280]{1,0:T(8,128)(2,1)S(1)}, u32[]{:S(2)}, u32[]{:S(2)}) collective-permute-start(bf16[256,1280]{1,0:T(8,128)(2,1)S(1)} %get-tuple-element.55.refs_0_), channel_id=1, source_target_pairs={{0,4},{1,5},{2,6},{3,7},{4,0},{5,1},{6,2},{7,3},{8,12},{9,13},{10,... | collective-permute-start | bytes 1966088 | tf_op jit(solution)/shard_map/ppermute | solution.py:76
  40.6 10.7 %collective-permute-start.13 = (bf16[256,1280]{1,0:T(8,128)(2,1)S(1)}, bf16[256,1280]{1,0:T(8,128)(2,1)S(1)}, u32[]{:S(2)}, u32[]{:S(2)}) collective-permute-start(bf16[256,1280]{1,0:T(8,128)(2,1)S(1)} %get-tuple-element.56.refs_1_), channel_id=1, source_target_pairs={{0,2},{1,3},{2,0},{3,1},{4,6},{5,7},{6,4},{7,5},{8,10},{9,11},{10,... | collective-permute-start | bytes 1966088 | tf_op jit(solution)/shard_map/ppermute | solution.py:76
  40.6 10.3 %collective-permute-start.14 = (bf16[256,1152]{1,0:T(8,128)(2,1)S(1)}, bf16[256,1152]{1,0:T(8,128)(2,1)}, u32[]{:S(2)}, u32[]{:S(2)}) collective-permute-start(bf16[256,1152]{1,0:T(8,128)(2,1)S(1)} %get-tuple-element.57.refs_2_), channel_id=1, source_target_pairs={{0,8},{1,9},{2,10},{3,11},{4,12},{5,13},{6,14},{7,15},{8,0},{9,1},... | collective-permute-start | bytes 1769480 | tf_op jit(solution)/shard_map/ppermute | solution.py:76
  51.3 13.4 %copy-start.1 = (bf16[1,512,3584]{2,1,0:T(8,128)(2,1)S(1)}, bf16[1,512,3584]{2,1,0:T(8,128)(2,1)}, u32[]{:S(2)}) copy-start(bf16[1,512,3584]{2,1,0:T(8,128)(2,1)} %param.23) | copy-start | bytes 11010052
  68.1 26.3 %collective-permute-start.15 = (f32[256,1280]{1,0:T(8,128)}, f32[256,1280]{1,0:T(8,128)}, u32[]{:S(2)}, u32[]{:S(2)}) collective-permute-start(f32[256,1280]{1,0:T(8,128)} %get-tuple-element.63), channel_id=1, source_target_pairs={{0,4},{1,5},{2,6},{3,7},{4,0},{5,1},{6,2},{7,3},{8,12},{9,13},{10,... | collective-permute-start | bytes 3932168 | tf_op jit(solution)/shard_map/ppermute | solution.py:76
  72.9 31.3 %collective-permute-start.17 = (f32[256,1280]{1,0:T(8,128)}, f32[256,1280]{1,0:T(8,128)}, u32[]{:S(2)}, u32[]{:S(2)}) collective-permute-start(f32[256,1280]{1,0:T(8,128)} %get-tuple-element.66), channel_id=1, source_target_pairs={{0,2},{1,3},{2,0},{3,1},{4,6},{5,7},{6,4},{7,5},{8,10},{9,11},{10,... | collective-permute-start | bytes 3932168 | tf_op jit(solution)/shard_map/ppermute | solution.py:76
  78.5 22.3 %collective-permute-start.18 = (f32[256,1024]{1,0:T(8,128)}, f32[256,1024]{1,0:T(8,128)}, u32[]{:S(2)}, u32[]{:S(2)}) collective-permute-start(f32[256,1024]{1,0:T(8,128)} %get-tuple-element.67), channel_id=1, source_target_pairs={{0,8},{1,9},{2,10},{3,11},{4,12},{5,13},{6,14},{7,15},{8,0},{9,1},... | collective-permute-start | bytes 3145736 | tf_op jit(solution)/shard_map/ppermute | solution.py:76
  83.6 27.9 %all-to-all-start = ((bf16[32,8,608]{2,1,0:T(8,128)(2,1)}), bf16[32,8,608]{2,1,0:T(8,128)(2,1)}, u32[]{:S(2)}, u32[]{:S(2)}) async-start(bf16[32,8,608]{2,1,0:T(8,128)(2,1)} %fusion.21), calls=%async_computation | async-start | bytes 655360 | tf_op jit(solution)/shard_map/all_to_all | solution.py:388
  87.1 13.6 %copy-start.4 = (f32[256,1024]{1,0:T(8,128)S(1)}, f32[256,1024]{1,0:T(8,128)}, u32[]{:S(2)}) copy-start(f32[256,1024]{1,0:T(8,128)} %copy-done.2) | copy-start | bytes 3145732
  96.8 18.0 %collective-permute-start.16 = (f32[128,1280]{1,0:T(8,128)}, f32[128,1280]{1,0:T(8,128)}, u32[]{:S(2)}, u32[]{:S(2)}) collective-permute-start(f32[128,1280]{1,0:T(8,128)} %get-tuple-element.65), channel_id=1, source_target_pairs={{0,2},{1,3},{2,0},{3,1},{4,6},{5,7},{6,4},{7,5},{8,10},{9,11},{10,... | collective-permute-start | bytes 1966088 | tf_op jit(solution)/shard_map/ppermute | solution.py:76
  106.5 14.8 %collective-permute-start.20 = (f32[128,1280]{1,0:T(8,128)}, f32[128,1280]{1,0:T(8,128)}, u32[]{:S(2)}, u32[]{:S(2)}) collective-permute-start(f32[128,1280]{1,0:T(8,128)} %get-tuple-element.72), channel_id=1, source_target_pairs={{0,8},{1,9},{2,10},{3,11},{4,12},{5,13},{6,14},{7,15},{8,0},{9,1},... | collective-permute-start | bytes 1966088 | tf_op jit(solution)/shard_map/ppermute | solution.py:76
  109.6 9.5 %collective-permute-start.21 = (f32[128,1024]{1,0:T(8,128)}, f32[128,1024]{1,0:T(8,128)S(1)}, u32[]{:S(2)}, u32[]{:S(2)}) collective-permute-start(f32[128,1024]{1,0:T(8,128)} %get-tuple-element.73), channel_id=1, source_target_pairs={{0,4},{1,5},{2,6},{3,7},{4,0},{5,1},{6,2},{7,3},{8,12},{9,13},{10,... | collective-permute-start | bytes 1572872 | tf_op jit(solution)/shard_map/ppermute | solution.py:76
  115.9 13.1 %collective-permute-start.19 = (f32[64,1280]{1,0:T(8,128)S(1)}, f32[64,1280]{1,0:T(8,128)S(1)}, u32[]{:S(2)}, u32[]{:S(2)}) collective-permute-start(f32[64,1280]{1,0:T(8,128)S(1)} %get-tuple-element.71), channel_id=1, source_target_pairs={{0,24},{1,25},{2,26},{3,27},{4,28},{5,29},{6,30},{7,31},{8,16},{9,... | collective-permute-start | bytes 983048 | tf_op jit(solution)/shard_map/ppermute | solution.py:76
  120.9 7.1 %copy-start.9 = (bf16[1,1024,576]{1,2,0:T(8,128)(2,1)S(1)}, bf16[1,1024,576]{1,2,0:T(8,128)(2,1)}, u32[]{:S(2)}) copy-start(bf16[1,1024,576]{1,2,0:T(8,128)(2,1)} %param.14) | copy-start | bytes 3538948
  121.0 8.1 %collective-permute-start.23 = (f32[64,1024]{1,0:T(8,128)S(1)}, f32[64,1024]{1,0:T(8,128)S(1)}, u32[]{:S(2)}, u32[]{:S(2)}) collective-permute-start(f32[64,1024]{1,0:T(8,128)S(1)} %get-tuple-element.78), channel_id=1, source_target_pairs={{0,2},{1,3},{2,0},{3,1},{4,6},{5,7},{6,4},{7,5},{8,10},{9,11},{10,... | collective-permute-start | bytes 786440 | tf_op jit(solution)/shard_map/ppermute | solution.py:76
  122.5 10.5 %collective-permute-start.22 = (f32[64,1280]{1,0:T(8,128)S(1)}, f32[64,1280]{1,0:T(8,128)S(1)}, u32[]{:S(2)}, u32[]{:S(2)}) collective-permute-start(f32[64,1280]{1,0:T(8,128)S(1)} %get-tuple-element.77), channel_id=1, source_target_pairs={{0,4},{1,5},{2,6},{3,7},{4,0},{5,1},{6,2},{7,3},{8,12},{9,13},{10,... | collective-permute-start | bytes 983048 | tf_op jit(solution)/shard_map/ppermute | solution.py:76
  133.1 8.8 %collective-permute-start.25 = (f32[32,1280]{1,0:T(8,128)S(1)}, f32[32,1280]{1,0:T(8,128)S(1)}, u32[]{:S(2)}, u32[]{:S(2)}) collective-permute-start(f32[32,1280]{1,0:T(8,128)S(1)} %get-tuple-element.82), channel_id=1, source_target_pairs={{0,24},{1,25},{2,26},{3,27},{4,28},{5,29},{6,30},{7,31},{8,16},{9,... | collective-permute-start | bytes 491528 | tf_op jit(solution)/shard_map/ppermute | solution.py:76
  133.1 8.7 %collective-permute-start.26 = (f32[32,1024]{1,0:T(8,128)S(1)}, f32[32,1024]{1,0:T(8,128)S(1)}, u32[]{:S(2)}, u32[]{:S(2)}) collective-permute-start(f32[32,1024]{1,0:T(8,128)S(1)} %get-tuple-element.83), channel_id=1, source_target_pairs={{0,24},{1,25},{2,26},{3,27},{4,28},{5,29},{6,30},{7,31},{8,16},{9,... | collective-permute-start | bytes 393224 | tf_op jit(solution)/shard_map/ppermute | solution.py:76
  137.0 6.6 %collective-permute-start.24 = (f32[32,1280]{1,0:T(8,128)S(1)}, f32[32,1280]{1,0:T(8,128)S(1)}, u32[]{:S(2)}, u32[]{:S(2)}) collective-permute-start(f32[32,1280]{1,0:T(8,128)S(1)} %get-tuple-element.81), channel_id=1, source_target_pairs={{0,8},{1,9},{2,10},{3,11},{4,12},{5,13},{6,14},{7,15},{8,0},{9,1},... | collective-permute-start | bytes 491528 | tf_op jit(solution)/shard_map/ppermute | solution.py:76
  (7 other events, 22.0 us)

commit v10 on v9

--- a/solution.py
+++ b/solution.py
@@ -141,15 +141,36 @@
     return whole_call(kernel, [array], [shape], "hold_back", (after,))[0]
 
 
+def first_joined(held, got, widths, after):
+    rows = held[0].shape[0]
+    out_shape = [jax.ShapeDtypeStruct((2 * rows, width), held[0].dtype) for width in widths]
+
+    def kernel(first, rest, got_first, got_rest, *outs):
+        outs[0][:rows] = first[...]
+        outs[0][rows:] = got_first[...]
+        start = 0
+        for out, width in zip(outs[1:], widths[1:]):
+            out[:rows] = rest[:, start : start + width]
+            out[rows:] = got_rest[:, start : start + width]
+            start += width
+
+    return whole_call(kernel, [*held, *got], out_shape, "first_joined", after)
+
+
 def gather_cube(tokens, side, gate, up, down):
     steps = len(LINKS)
     others = [swap_cores(weight) for weight in (gate, up, down)]
-    held = [tokens[:, start:stop] for start, stop in piece_columns(tokens.shape[1])]
-    held[-1] = jnp.concatenate([held[-1], side], axis=1)
-    for phase in range(steps):
+    columns = piece_columns(tokens.shape[1])
+    widths = [stop - start for start, stop in columns]
+    widths[-1] += side.shape[1]
+    cut = columns[0][1]
+    held = [tokens[:, :cut], jnp.concatenate([tokens[:, cut:], side], axis=1)]
+    got = [across(piece, order[-1]) for piece, order in zip(held, ORDERS)]
+    held = first_joined(held, got, widths, others[2:])
+    for phase in range(1, steps):
         got = [across(piece, order[steps - 1 - phase]) for piece, order in zip(held, ORDERS)]
         if phase < steps - 1:
-            held = joined(held, got, (others[2:], others[:2], ())[phase])
+            held = joined(held, got, others[:2] if phase == 1 else ())
     return held, got, others
 
 
@@ -277,28 +298,69 @@
     )(scale, hidden, *[down] * tiles, *[down_other] * tiles, *after)
 
 
-def halved(keep, got, after):
-    rows, width = keep.shape
-    half = jax.ShapeDtypeStruct((rows // 2, width), keep.dtype)
-
-    def kernel(keep_ref, got_ref, first_ref, second_ref):
-        second_ref[...] = keep_ref[rows // 2 :] + got_ref[rows // 2 :]
-        first_ref[...] = keep_ref[: rows // 2] + got_ref[: rows // 2]
-
-    return whole_call(kernel, [keep, got], [half, half], "halved", after)
-
-
-def finished(keep, got):
-    count = len(keep)
-    width = sum(piece.shape[1] for piece in keep)
+def summed(pieces, after):
+    rows = pieces[0][-1].shape[0] // 2
+    widths = [arrays[0].shape[1] for arrays in pieces]
+    operands = [array for arrays in pieces for array in arrays]
 
     def kernel(*refs):
-        for at, (start, stop) in enumerate(piece_columns(width)):
-            total = refs[at][...] + refs[count + at][...]
-            refs[2 * count][:, start:stop] = total.astype(jnp.bfloat16)
-
-    shape = jax.ShapeDtypeStruct((keep[0].shape[0], width), jnp.bfloat16)
-    return whole_call(kernel, [*keep, *got], [shape], "finished")[0]
+        out_ref = refs[-1]
+        refs, start = list(refs), 0
+        for arrays, width in zip(pieces, widths):
+            total = refs.pop(0)[...]
+            for _ in arrays[1:]:
+                total = total + refs.pop(0)[...]
+            out_ref[:, start : start + width] = total
+            start += width
+
+    return pl.pallas_call(
+        kernel,
+        grid=(1,),
+        in_specs=[pl.BlockSpec((rows, array.shape[1]), lambda i: (1, 0)) for array in operands]
+        + [pl.BlockSpec(memory_space=pl.ANY)] * len(after),
+        out_specs=pl.BlockSpec((rows, sum(widths)), lambda i: (0, 0)),
+        out_shape=jax.ShapeDtypeStruct((rows, sum(widths)), jnp.float32),
+        compiler_params=pltpu.CompilerParams(vmem_limit_bytes=14 * MIB),
+        cost_estimate=pl.CostEstimate(
+            flops=len(operands) * rows * widths[0],
+            bytes_accessed=4 * rows * (sum(array.shape[1] for array in operands) + sum(widths)),
+            transcendentals=0,
+        ),
+        name="summed",
+    )(*operands, *after)
+
+
+def finished(pieces, last):
+    rows = last[0].shape[0]
+    columns = piece_columns(sum(arrays[0].shape[1] for arrays in pieces))
+    operands = [array for arrays in pieces for array in arrays]
+
+    def kernel(*refs):
+        first, rest, out_ref = refs[-3:]
+        refs, cut = list(refs), columns[0][1]
+        for at, (start, stop) in enumerate(columns):
+            total = refs.pop(0)[...]
+            for _ in pieces[at][1:]:
+                total = total + refs.pop(0)[...]
+            total = total + (first[...] if at == 0 else rest[:, start - cut : stop - cut])
+            out_ref[:, start:stop] = total.astype(jnp.bfloat16)
+
+    def top(array):
+        return pl.BlockSpec((rows, array.shape[1]), lambda i: (0, 0))
+
+    width = columns[-1][1]
+    return pl.pallas_call(
+        kernel,
+        grid=(1,),
+        in_specs=[top(array) for array in (*operands, *last)],
+        out_specs=pl.BlockSpec((rows, width), lambda i: (0, 0)),
+        out_shape=jax.ShapeDtypeStruct((rows, width), jnp.bfloat16),
+        compiler_params=pltpu.CompilerParams(vmem_limit_bytes=14 * MIB),
+        cost_estimate=pl.CostEstimate(
+            flops=5 * rows * width, bytes_accessed=22 * rows * width, transcendentals=0
+        ),
+        name="finished",
+    )(*operands, *last)
 
 
 def cube_outputs(unit, held, got, weights, others):
@@ -316,13 +378,15 @@
 
 
 def cube_sums(keep, got):
-    keep, got, after = list(keep), list(got), ()
-    for phase in range(1, len(LINKS)):
+    pieces, after = [list(pair) for pair in zip(keep, got)], ()
+    for phase in range(1, len(LINKS) - 1):
         for at in TURNS:
-            keep[at], send = halved(keep[at], got[at], after)
-            got[at] = across(send, ORDERS[at][phase])
-            after = (keep[at],)
-    return finished(keep, got)
+            send = summed([pieces[at]], after)
+            pieces[at].append(across(send, ORDERS[at][phase]))
+            after = (send,)
+    first = summed(pieces[:1], after)
+    rest = summed(pieces[1:], (first,))
+    return finished(pieces, [across(first, ORDERS[0][-1]), across(rest, ORDERS[1][-1])])
 
 
 def three_parts(value):

time: 145 us -> 150 us (1.034)
  Pallas kernels: 33.5 us -> 39.3 us
  starting transfers between devices: 46.6 us -> 43.5 us
    pallas_call x0 -> x9, Pallas kernels: none -> 16 us  [the longest x8 13.8 us: summed(): pl.pallas_call(kernel, grid=(1,), in_specs=[pl.BlockSpec((rows, array.sha...]
    pallas_call x14 -> x4, Pallas kernels: 10.3 us -> 0.24 us  [whole_call(): pl.pallas_call(body, in_specs=[pl.BlockSpec(memory_space=pltpu.VMEM)] * g...]
    ppermute x24 -> x22, starting transfers between devices: 42.1 us -> 36.7 us  [across(): lax.ppermute(value, 'ep', [(i, i ^ 2 * LINKS[link]) for i in range(peers)])]
    all_to_all x1, starting transfers between devices: 3.48 us -> 5.77 us  [per_device(): lax.all_to_all(leaving, 'ep', split_axis=0, concat_axis=0, tiled=True)]
    unnamed x22, local copies, waits for them, and re-layouts: 4.04 us -> 2.22 us
    reshape x2, local copies, waits for them, and re-layouts: 1.86 us -> 3.6 us  [per_device(): arrived.reshape(peers * 2 * block_len, latent)]
    ppermute x24 -> x22, waiting for transfers between devices: 48.1 us -> 48.1 us  [across(): lax.ppermute(value, 'ep', [(i, i ^ 2 * LINKS[link]) for i in range(peers)])]
  transfers between devices with their start and end apart: 28 -> 26, of which waited for: 13 -> 11; matrix products, arithmetic and copies ran while one was open for 7% -> 9% of each run, Pallas kernels for 11% -> 13%
where the time goes in v10:
time: 150 us; the launch traced here: 148 us
  waiting for transfers between devices  48.2 us (32%)
  starting transfers between devices  43.5 us (29%)
  Pallas kernels  39.3 us (26%)
  local copies, waits for them, and re-layouts  8.76 us (6%)
  matrix products  3.99 us (3%)
  other arithmetic  3.19 us (2%)
  between operations  1.52 us (1%)
    ppermute x22, waiting for transfers between devices, across(): lax.ppermute(value, 'ep', [(i, i ^ 2 * LINKS[link]) for i in range(peers)])  48.1 us
    ppermute x22, starting transfers between devices, across(): lax.ppermute(value, 'ep', [(i, i ^ 2 * LINKS[link]) for i in range(peers)])  36.7 us
    pallas_call x8, Pallas kernels, summed(): pl.pallas_call(kernel, grid=(1,), in_specs=[pl.BlockSpec((rows, array.sha...  13.8 us
    pallas_call x1, Pallas kernels, expert_hidden(): pl.pallas_call(functools.partial(hidden_kernel, unit), grid=(2 * steps,),...  13.3 us
    pallas_call x3, Pallas kernels, expert_output(): pl.pallas_call(functools.partial(output_kernel, unit, order, tiles), grid...  9.75 us
    all_to_all x1, starting transfers between devices, per_device(): lax.all_to_all(leaving, 'ep', split_axis=0, concat_axis=0, tiled=True)  5.77 us
    reshape x2, local copies, waits for them, and re-layouts, per_device(): arrived.reshape(peers * 2 * block_len, latent)  3.6 us
  transfers between devices with their start and end apart: 26, of which 11 were waited for; matrix products, arithmetic and copies ran while one was open for 9% of the time, Pallas kernels for 13%

profile of v10, /device:TPU:0, one launch (start us, length us, event | category | flops | bytes accessed | tf_op | source)
XLA Modules:
  0.0 148.4 jit_solution(5806440091789421390)
XLA Ops:
  3.6 4.7 %collective-permute-start.1 = (bf16[32,2432]{1,0:T(8,128)(2,1)S(1)}, bf16[32,2432]{1,0:T(8,128)(2,1)S(1)}, u32[]{:S(2)}, u32[]{:S(2)}) collective-permute-start(bf16[32,2432]{1,0:T(8,128)(2,1)S(1)} %pad_maximum_fusion.refs_1_), channel_id=1, source_target_pairs={{0,24},{1,25},{2,26},{3,27},{4,28},{5,29},{6,30},{7,31},{8,16},{9,... | collective-permute-start | bytes 466952 | tf_op jit(solution)/shard_map/ppermute | solution.py:76
  9.2 5.6 %collective-permute-done.refs_2_ = bf16[32,1280]{1,0:T(8,128)(2,1)S(1)} collective-permute-done((bf16[32,1280]{1,0:T(8,128)(2,1)S(1)}, bf16[32,1280]{1,0:T(8,128)(2,1)S(1)}, u32[]{:S(2)}, u32[]{:S(2)}) %collective-permute-start) | collective-permute-done | bytes 81952 | tf_op jit(solution)/shard_map/ppermute | solution.py:76
  14.9 2.6 %collective-permute-start.3 = (bf16[64,1280]{1,0:T(8,128)(2,1)S(1)}, bf16[64,1280]{1,0:T(8,128)(2,1)S(1)}, u32[]{:S(2)}, u32[]{:S(2)}) collective-permute-start(bf16[64,1280]{1,0:T(8,128)(2,1)S(1)} %get-tuple-element.31.refs_0_), channel_id=1, source_target_pairs={{0,24},{1,25},{2,26},{3,27},{4,28},{5,29},{6,30},{7,31},{8,16},{9,... | collective-permute-start | bytes 491528 | tf_op jit(solution)/shard_map/ppermute | solution.py:76
  20.5 3.6 %collective-permute-done.5.refs_5_ = bf16[64,1152]{1,0:T(8,128)(2,1)S(1)} collective-permute-done((bf16[64,1152]{1,0:T(8,128)(2,1)S(1)}, bf16[64,1152]{1,0:T(8,128)(2,1)S(1)}, u32[]{:S(2)}, u32[]{:S(2)}) %collective-permute-start.5) | collective-permute-done | bytes 147488 | tf_op jit(solution)/shard_map/ppermute | solution.py:76
  24.2 1.6 %collective-permute-start.8 = (bf16[128,1280]{1,0:T(8,128)(2,1)S(1)}, bf16[128,1280]{1,0:T(8,128)(2,1)S(1)}, u32[]{:S(2)}, u32[]{:S(2)}) collective-permute-start(bf16[128,1280]{1,0:T(8,128)(2,1)S(1)} %get-tuple-element.34.refs_0_), channel_id=1, source_target_pairs={{0,2},{1,3},{2,0},{3,1},{4,6},{5,7},{6,4},{7,5},{8,10},{9,11},{10,... | collective-permute-start | bytes 983048 | tf_op jit(solution)/shard_map/ppermute | solution.py:76
  25.8 1.7 %collective-permute-start.9 = (bf16[128,1280]{1,0:T(8,128)(2,1)S(1)}, bf16[128,1280]{1,0:T(8,128)(2,1)S(1)}, u32[]{:S(2)}, u32[]{:S(2)}) collective-permute-start(bf16[128,1280]{1,0:T(8,128)(2,1)S(1)} %get-tuple-element.35.refs_1_), channel_id=1, source_target_pairs={{0,8},{1,9},{2,10},{3,11},{4,12},{5,13},{6,14},{7,15},{8,0},{9,1},... | collective-permute-start | bytes 983048 | tf_op jit(solution)/shard_map/ppermute | solution.py:76
  27.5 1.5 %collective-permute-start.10 = (bf16[128,1152]{1,0:T(8,128)(2,1)S(1)}, bf16[128,1152]{1,0:T(8,128)(2,1)S(1)}, u32[]{:S(2)}, u32[]{:S(2)}) collective-permute-start(bf16[128,1152]{1,0:T(8,128)(2,1)S(1)} %get-tuple-element.36.refs_2_), channel_id=1, source_target_pairs={{0,4},{1,5},{2,6},{3,7},{4,0},{5,1},{6,2},{7,3},{8,12},{9,13},{10,... | collective-permute-start | bytes 884744 | tf_op jit(solution)/shard_map/ppermute | solution.py:76
  29.0 5.7 %collective-permute-done.10.refs_5_ = bf16[128,1152]{1,0:T(8,128)(2,1)S(1)} collective-permute-done((bf16[128,1152]{1,0:T(8,128)(2,1)S(1)}, bf16[128,1152]{1,0:T(8,128)(2,1)S(1)}, u32[]{:S(2)}, u32[]{:S(2)}) %collective-permute-start.10) | collective-permute-done | bytes 294944 | tf_op jit(solution)/shard_map/ppermute | solution.py:76
  34.9 1.6 %collective-permute-start.11 = (bf16[256,1280]{1,0:T(8,128)(2,1)S(1)}, bf16[256,1280]{1,0:T(8,128)(2,1)S(1)}, u32[]{:S(2)}, u32[]{:S(2)}) collective-permute-start(bf16[256,1280]{1,0:T(8,128)(2,1)S(1)} %get-tuple-element.37.refs_0_), channel_id=1, source_target_pairs={{0,4},{1,5},{2,6},{3,7},{4,0},{5,1},{6,2},{7,3},{8,12},{9,13},{10,... | collective-permute-start | bytes 1966088 | tf_op jit(solution)/shard_map/ppermute | solution.py:76
  38.0 11.2 %collective-permute-done.13.refs_5_ = bf16[256,1152]{1,0:T(8,128)(2,1)} collective-permute-done((bf16[256,1152]{1,0:T(8,128)(2,1)S(1)}, bf16[256,1152]{1,0:T(8,128)(2,1)}, u32[]{:S(2)}, u32[]{:S(2)}) %collective-permute-start.13) | collective-permute-done | bytes 589856 | tf_op jit(solution)/shard_map/ppermute | solution.py:76
  50.3 13.3 %expert_hidden.1 = (bf16[512,1024]{1,0:T(8,128)(2,1)S(1)}, f32[512,1]{1,0:T(8,128)S(1)}) custom-call(s32[1]{0:T(128)} %bitcast.2.chip_ref, bf16[256,1280]{1,0:T(8,128)(2,1)S(1)} %get-tuple-element.37.refs_0_, bf16[256,1280]{1,0:T(8,128)(2,1)S(1)} %get-tuple-element.38.refs_1_, bf16[256,1152]{1,0:T(8,128)(2,1)S(1)} %get-tuple-element.39.refs_2_, ...), custom_call_target="tpu_custom_call" | custom-call | flops 7516192768 | bytes 19398656 | tf_op jit(solution)/shard_map/expert_hidden/pallas_call | solution.py:225
  63.7 3.4 %expert_output.3 = (f32[256,1280]{1,0:T(8,128)S(1)}, f32[256,1280]{1,0:T(8,128)}) custom-call(f32[512,1]{1,0:T(8,128)S(1)} %get-tuple-element.40.scale_ref, bf16[512,1024]{1,0:T(8,128)(2,1)S(1)} %get-tuple-element.41.hidden_ref, bf16[512,3584]{1,0:T(8,128)(2,1)S(1)} %bitcast.20, bf16[512,3584]{1,0:T(8,128)(2,1)S(1)} %bitcast.21, ...), custom_call_target="tpu_custom_call" | custom-call | flops 1342177280 | bytes 6291456 | tf_op jit(solution)/shard_map/expert_output/pallas_call | solution.py:280
  67.6 3.4 %expert_output.4 = (f32[256,1280]{1,0:T(8,128)S(1)}, f32[256,1280]{1,0:T(8,128)}) custom-call(f32[512,1]{1,0:T(8,128)S(1)} %get-tuple-element.40.scale_ref, bf16[512,1024]{1,0:T(8,128)(2,1)S(1)} %get-tuple-element.41.hidden_ref, bf16[512,3584]{1,0:T(8,128)(2,1)S(1)} %bitcast.25, bf16[512,3584]{1,0:T(8,128)(2,1)S(1)} %bitcast.26, ...), custom_call_target="tpu_custom_call" | custom-call | flops 1342177280 | bytes 6291456 | tf_op jit(solution)/shard_map/expert_output/pallas_call | solution.py:280
  71.5 3.0 %expert_output.5 = (f32[256,1024]{1,0:T(8,128)S(1)}, f32[256,1024]{1,0:T(8,128)}) custom-call(f32[512,1]{1,0:T(8,128)S(1)} %get-tuple-element.40.scale_ref, bf16[512,1024]{1,0:T(8,128)(2,1)S(1)} %get-tuple-element.41.hidden_ref, bf16[512,3584]{1,0:T(8,128)(2,1)S(1)} %bitcast.30, bf16[512,3584]{1,0:T(8,128)(2,1)S(1)} %bitcast.31, ...), custom_call_target="tpu_custom_call" | custom-call | flops 1073741824 | bytes 5242880 | tf_op jit(solution)/shard_map/expert_output/pallas_call | solution.py:280
  80.1 5.8 %all-to-all-start = ((bf16[32,8,608]{2,1,0:T(8,128)(2,1)}), bf16[32,8,608]{2,1,0:T(8,128)(2,1)}, u32[]{:S(2)}, u32[]{:S(2)}) async-start(bf16[32,8,608]{2,1,0:T(8,128)(2,1)} %fusion.21), calls=%async_computation | async-start | bytes 655360 | tf_op jit(solution)/shard_map/all_to_all | solution.py:452
  85.9 10.2 %collective-permute-done.14.refs_1_ = f32[256,1280]{1,0:T(8,128)} collective-permute-done((f32[256,1280]{1,0:T(8,128)}, f32[256,1280]{1,0:T(8,128)}, u32[]{:S(2)}, u32[]{:S(2)}) %collective-permute-start.14) | collective-permute-done | bytes 1310752 | tf_op jit(solution)/shard_map/ppermute | solution.py:76
  96.1 2.1 %summed.8.refs_2_ = f32[128,1280]{1,0:T(8,128)} custom-call(f32[256,1280]{1,0:T(8,128)S(1)} %get-tuple-element.42.refs_10_.refs_0_, f32[256,1280]{1,0:T(8,128)} %collective-permute-done.14.refs_1_), custom_call_target="tpu_custom_call" | custom-call | flops 327680 | bytes 1966080 | tf_op jit(solution)/shard_map/summed/pallas_call | solution.py:316
  99.9 1.9 %summed.9.refs_2_ = f32[128,1024]{1,0:T(8,128)} custom-call(f32[256,1024]{1,0:T(8,128)S(1)} %copy-done.4, f32[256,1024]{1,0:T(8,128)} %collective-permute-done.17.refs_1_.refs_5_.refs_9_, f32[128,1280]{1,0:T(8,128)} %summed.8.refs_2_), custom_call_target="tpu_custom_call" | custom-call | flops 262144 | bytes 1572864 | tf_op jit(solution)/shard_map/summed/pallas_call | solution.py:316
  101.9 3.7 %collective-permute-done.16.refs_1_.refs_5_ = f32[256,1280]{1,0:T(8,128)} collective-permute-done((f32[256,1280]{1,0:T(8,128)}, f32[256,1280]{1,0:T(8,128)}, u32[]{:S(2)}, u32[]{:S(2)}) %collective-permute-start.16) | collective-permute-done | bytes 1310752 | tf_op jit(solution)/shard_map/ppermute | solution.py:76
  105.6 2.0 %summed.10.refs_3_ = f32[128,1280]{1,0:T(8,128)} custom-call(f32[256,1280]{1,0:T(8,128)S(1)} %get-tuple-element.43.refs_8_.refs_0_.refs_4_, f32[256,1280]{1,0:T(8,128)} %collective-permute-done.16.refs_1_.refs_5_, f32[128,1024]{1,0:T(8,128)} %summed.9.refs_2_), custom_call_target="tpu_custom_call" | custom-call | flops 327680 | bytes 1966080 | tf_op jit(solution)/shard_map/summed/pallas_call | solution.py:316
  112.3 1.7 %slice_bitcast_fusion = bf16[256,576]{1,0:T(8,128)(2,1)} fusion(bf16[32,8,608]{2,1,0:T(8,128)(2,1)} %all-to-all-done), kind=kLoop, calls=%fused_computation.19 | loop fusion | bytes 589824 | tf_op jit(solution)/shard_map/reshape | solution.py:459
  114.0 1.5 %collective-permute-done.15.refs_2_ = f32[128,1280]{1,0:T(8,128)S(1)} collective-permute-done((f32[128,1280]{1,0:T(8,128)}, f32[128,1280]{1,0:T(8,128)S(1)}, u32[]{:S(2)}, u32[]{:S(2)}) %collective-permute-start.15) | collective-permute-done | bytes 655392 | tf_op jit(solution)/shard_map/ppermute | solution.py:76
  115.5 1.7 %summed.11.refs_3_ = f32[64,1280]{1,0:T(8,128)} custom-call(f32[256,1280]{1,0:T(8,128)S(1)} %get-tuple-element.42.refs_10_.refs_0_, f32[256,1280]{1,0:T(8,128)} %collective-permute-done.14.refs_1_, f32[128,1280]{1,0:T(8,128)S(1)} %collective-permute-done.15.refs_2_, f32[128,1280]{1,0:T(8,128)} %summed.10.refs_3_), custom_call_target="tpu_custom_call" | custom-call | flops 245760 | bytes 1310720 | tf_op jit(solution)/shard_map/summed/pallas_call | solution.py:316
  117.3 3.9 %collective-permute-start.18 = (f32[64,1280]{1,0:T(8,128)}, f32[64,1280]{1,0:T(8,128)}, u32[]{:S(2)}, u32[]{:S(2)}) collective-permute-start(f32[64,1280]{1,0:T(8,128)} %summed.11.refs_3_), channel_id=1, source_target_pairs={{0,24},{1,25},{2,26},{3,27},{4,28},{5,29},{6,30},{7,31},{8,16},{9,... | collective-permute-start | bytes 983048 | tf_op jit(solution)/shard_map/ppermute | solution.py:76
  121.2 1.8 %summed.12.refs_3_ = f32[64,1024]{1,0:T(8,128)} custom-call(f32[256,1024]{1,0:T(8,128)S(1)} %copy-done.5, f32[256,1024]{1,0:T(8,128)} %collective-permute-done.17.refs_1_.refs_5_.refs_9_, f32[128,1024]{1,0:T(8,128)} %collective-permute-done.20.refs_2_.refs_6_.refs_10_, f32[64,1280]{1,0:T(8,128)} %summed.11.refs_3_), custom_call_target="tpu_custom_call" | custom-call | flops 196608 | bytes 1048576 | tf_op jit(solution)/shard_map/summed/pallas_call | solution.py:316
  123.5 1.8 %summed.13.refs_4_ = f32[64,1280]{1,0:T(8,128)} custom-call(f32[256,1280]{1,0:T(8,128)S(1)} %get-tuple-element.43.refs_8_.refs_0_.refs_4_, f32[256,1280]{1,0:T(8,128)} %collective-permute-done.16.refs_1_.refs_5_, f32[128,1280]{1,0:T(8,128)} %collective-permute-done.19.refs_2_.refs_6_, f32[64,1024]{1,0:T(8,128)} %summed.12.refs_3_), custom_call_target="tpu_custom_call" | custom-call | flops 245760 | bytes 1310720 | tf_op jit(solution)/shard_map/summed/pallas_call | solution.py:316
  126.8 1.9 %copy.29 = bf16[256,576]{0,1:T(8,128)(2,1)} copy(bf16[256,576]{1,0:T(8,128)(2,1)} %slice_bitcast_fusion) | data formatting | bytes 589824 | tf_op jit(solution)/shard_map/reshape | solution.py:459
  128.7 2.1 %fusion.37 = (f32[128]{0:T(128)S(1)}, f32[1280,128]{1,0:T(8,128)S(1)}) fusion(bf16[1,128,576]{1,2,0:T(8,128)(2,1)S(1)} %copy-done, bf16[256,576]{0,1:T(8,128)(2,1)} %copy.29, bf16[1024,576]{0,1:T(8,128)(2,1)} %bitcast.38, pred[1280]{0:T(1024)(128)(4,1)S(1)} %pad_add_fusion), kind=kOutput, calls=%fused_computation.50 | convolution fusion | flops 192184192 | bytes 2279168 | tf_op jit(solution)/shard_map/dot_general | solution.py:31
  134.9 6.4 %collective-permute-start.23 = (f32[32,1280]{1,0:T(8,128)S(1)}, f32[32,1280]{1,0:T(8,128)S(1)}, u32[]{:S(2)}, u32[]{:S(2)}) collective-permute-start(f32[32,1280]{1,0:T(8,128)S(1)} %summed.14.refs_8_), channel_id=1, source_target_pairs={{0,8},{1,9},{2,10},{3,11},{4,12},{5,13},{6,14},{7,15},{8,0},{9,1},... | collective-permute-start | bytes 491528 | tf_op jit(solution)/shard_map/ppermute | solution.py:76
  141.3 1.5 %fusion.14 = bf16[1,128,512]{2,1,0:T(8,128)(2,1)} fusion(bf16[256,576]{0,1:T(8,128)(2,1)S(1)} %copy-done.8, bf16[1024,576]{0,1:T(8,128)(2,1)S(1)} %bitcast.39, f32[1280,128]{1,0:T(8,128)S(1)} %get-tuple-element.52, f32[128]{0:T(128)S(1)} %get-tuple-element.51, pred[1280]{0:T(1024)(128)(4,1)S(1)} %pad_add_fusion, f32[128]{0:T(128)S(1)} %fusion.18), kind=kOutput, calls=%fused_computation.12 | convolution fusion | flops 171016192 | bytes 2263296 | tf_op jit(solution)/shard_map/dot_general | solution.py:38
  142.9 3.4 %collective-permute-done.23.refs_12_ = f32[32,1280]{1,0:T(8,128)S(1)} collective-permute-done((f32[32,1280]{1,0:T(8,128)S(1)}, f32[32,1280]{1,0:T(8,128)S(1)}, u32[]{:S(2)}, u32[]{:S(2)}) %collective-permute-start.23) | collective-permute-done | bytes 163872 | tf_op jit(solution)/shard_map/ppermute | solution.py:76
  146.2 2.2 %finished.1 = bf16[32,3584]{1,0:T(8,128)(2,1)} custom-call(f32[256,1280]{1,0:T(8,128)S(1)} %get-tuple-element.42.refs_10_.refs_0_, f32[256,1280]{1,0:T(8,128)} %collective-permute-done.14.refs_1_, f32[128,1280]{1,0:T(8,128)S(1)} %collective-permute-done.15.refs_2_, f32[64,1280]{1,0:T(8,128)} %collective-permute-done.18.refs_3_, ...), custom_call_target="tpu_custom_call" | custom-call | flops 573440 | bytes 2523136 | tf_op jit(solution)/shard_map/finished/pallas_call | solution.py:352
  (87 shorter events, 28.1 us)
Async XLA Ops:
  0.6 128.1 %copy-start = (bf16[1,128,576]{1,2,0:T(8,128)(2,1)S(1)}, bf16[1,128,576]{1,2,0:T(8,128)(2,1)}, u32[]{:S(2)}) copy-start(bf16[1,128,576]{1,2,0:T(8,128)(2,1)} %param.13) | copy-start | bytes 442372
  0.6 14.2 %collective-permute-start.2 = (bf16[512,3584]{1,0:T(8,128)(2,1)}, bf16[512,3584]{1,0:T(8,128)(2,1)}, u32[]{:S(2)}, u32[]{:S(2)}) collective-permute-start(bf16[512,3584]{1,0:T(8,128)(2,1)} %bitcast.19), channel_id=1, source_target_pairs={{0,1},{1,0},{2,3},{3,2},{4,5},{5,4},{6,7},{7,6},{8,9},{9,8},{10,11... | collective-permute-start | bytes 11010056 | tf_op jit(solution)/shard_map/ppermute | solution.py:80
  1.2 19.3 %collective-permute-start.6 = (bf16[3584,512]{1,0:T(8,128)(2,1)}, bf16[3584,512]{1,0:T(8,128)(2,1)}, u32[]{:S(2)}, u32[]{:S(2)}) collective-permute-start(bf16[3584,512]{1,0:T(8,128)(2,1)} %bitcast.34), channel_id=1, source_target_pairs={{0,1},{1,0},{2,3},{3,2},{4,5},{5,4},{6,7},{7,6},{8,9},{9,8},{10,11... | collective-permute-start | bytes 11010056 | tf_op jit(solution)/shard_map/ppermute | solution.py:80
  1.2 19.3 %collective-permute-start.7 = (bf16[3584,512]{1,0:T(8,128)(2,1)}, bf16[3584,512]{1,0:T(8,128)(2,1)}, u32[]{:S(2)}, u32[]{:S(2)}) collective-permute-start(bf16[3584,512]{1,0:T(8,128)(2,1)} %bitcast.36), channel_id=1, source_target_pairs={{0,1},{1,0},{2,3},{3,2},{4,5},{5,4},{6,7},{7,6},{8,9},{9,8},{10,11... | collective-permute-start | bytes 11010056 | tf_op jit(solution)/shard_map/ppermute | solution.py:80
  3.6 11.2 %collective-permute-start.1 = (bf16[32,2432]{1,0:T(8,128)(2,1)S(1)}, bf16[32,2432]{1,0:T(8,128)(2,1)S(1)}, u32[]{:S(2)}, u32[]{:S(2)}) collective-permute-start(bf16[32,2432]{1,0:T(8,128)(2,1)S(1)} %pad_maximum_fusion.refs_1_), channel_id=1, source_target_pairs={{0,24},{1,25},{2,26},{3,27},{4,28},{5,29},{6,30},{7,31},{8,16},{9,... | collective-permute-start | bytes 466952 | tf_op jit(solution)/shard_map/ppermute | solution.py:76
  9.2 5.6 %collective-permute-start = (bf16[32,1280]{1,0:T(8,128)(2,1)S(1)}, bf16[32,1280]{1,0:T(8,128)(2,1)S(1)}, u32[]{:S(2)}, u32[]{:S(2)}) collective-permute-start(bf16[32,1280]{1,0:T(8,128)(2,1)S(1)} %slice.47.refs_0_), channel_id=1, source_target_pairs={{0,8},{1,9},{2,10},{3,11},{4,12},{5,13},{6,14},{7,15},{8,0},{9,1},... | collective-permute-start | bytes 245768 | tf_op jit(solution)/shard_map/ppermute | solution.py:76
  14.9 9.3 %collective-permute-start.3 = (bf16[64,1280]{1,0:T(8,128)(2,1)S(1)}, bf16[64,1280]{1,0:T(8,128)(2,1)S(1)}, u32[]{:S(2)}, u32[]{:S(2)}) collective-permute-start(bf16[64,1280]{1,0:T(8,128)(2,1)S(1)} %get-tuple-element.31.refs_0_), channel_id=1, source_target_pairs={{0,24},{1,25},{2,26},{3,27},{4,28},{5,29},{6,30},{7,31},{8,16},{9,... | collective-permute-start | bytes 491528 | tf_op jit(solution)/shard_map/ppermute | solution.py:76
  17.5 6.7 %collective-permute-start.4 = (bf16[64,1280]{1,0:T(8,128)(2,1)S(1)}, bf16[64,1280]{1,0:T(8,128)(2,1)S(1)}, u32[]{:S(2)}, u32[]{:S(2)}) collective-permute-start(bf16[64,1280]{1,0:T(8,128)(2,1)S(1)} %get-tuple-element.32.refs_1_), channel_id=1, source_target_pairs={{0,4},{1,5},{2,6},{3,7},{4,0},{5,1},{6,2},{7,3},{8,12},{9,13},{10,... | collective-permute-start | bytes 491528 | tf_op jit(solution)/shard_map/ppermute | solution.py:76
  19.0 5.1 %collective-permute-start.5 = (bf16[64,1152]{1,0:T(8,128)(2,1)S(1)}, bf16[64,1152]{1,0:T(8,128)(2,1)S(1)}, u32[]{:S(2)}, u32[]{:S(2)}) collective-permute-start(bf16[64,1152]{1,0:T(8,128)(2,1)S(1)} %get-tuple-element.33.refs_2_), channel_id=1, source_target_pairs={{0,2},{1,3},{2,0},{3,1},{4,6},{5,7},{6,4},{7,5},{8,10},{9,11},{10,... | collective-permute-start | bytes 442376 | tf_op jit(solution)/shard_map/ppermute | solution.py:76
  24.2 10.6 %collective-permute-start.8 = (bf16[128,1280]{1,0:T(8,128)(2,1)S(1)}, bf16[128,1280]{1,0:T(8,128)(2,1)S(1)}, u32[]{:S(2)}, u32[]{:S(2)}) collective-permute-start(bf16[128,1280]{1,0:T(8,128)(2,1)S(1)} %get-tuple-element.34.refs_0_), channel_id=1, source_target_pairs={{0,2},{1,3},{2,0},{3,1},{4,6},{5,7},{6,4},{7,5},{8,10},{9,11},{10,... | collective-permute-start | bytes 983048 | tf_op jit(solution)/shard_map/ppermute | solution.py:76
  25.8 9.0 %collective-permute-start.9 = (bf16[128,1280]{1,0:T(8,128)(2,1)S(1)}, bf16[128,1280]{1,0:T(8,128)(2,1)S(1)}, u32[]{:S(2)}, u32[]{:S(2)}) collective-permute-start(bf16[128,1280]{1,0:T(8,128)(2,1)S(1)} %get-tuple-element.35.refs_1_), channel_id=1, source_target_pairs={{0,8},{1,9},{2,10},{3,11},{4,12},{5,13},{6,14},{7,15},{8,0},{9,1},... | collective-permute-start | bytes 983048 | tf_op jit(solution)/shard_map/ppermute | solution.py:76
  27.5 7.3 %collective-permute-start.10 = (bf16[128,1152]{1,0:T(8,128)(2,1)S(1)}, bf16[128,1152]{1,0:T(8,128)(2,1)S(1)}, u32[]{:S(2)}, u32[]{:S(2)}) collective-permute-start(bf16[128,1152]{1,0:T(8,128)(2,1)S(1)} %get-tuple-element.36.refs_2_), channel_id=1, source_target_pairs={{0,4},{1,5},{2,6},{3,7},{4,0},{5,1},{6,2},{7,3},{8,12},{9,13},{10,... | collective-permute-start | bytes 884744 | tf_op jit(solution)/shard_map/ppermute | solution.py:76
  34.9 14.3 %collective-permute-start.11 = (bf16[256,1280]{1,0:T(8,128)(2,1)S(1)}, bf16[256,1280]{1,0:T(8,128)(2,1)S(1)}, u32[]{:S(2)}, u32[]{:S(2)}) collective-permute-start(bf16[256,1280]{1,0:T(8,128)(2,1)S(1)} %get-tuple-element.37.refs_0_), channel_id=1, source_target_pairs={{0,4},{1,5},{2,6},{3,7},{4,0},{5,1},{6,2},{7,3},{8,12},{9,13},{10,... | collective-permute-start | bytes 1966088 | tf_op jit(solution)/shard_map/ppermute | solution.py:76
  36.5 13.8 %collective-permute-start.12 = (bf16[256,1280]{1,0:T(8,128)(2,1)S(1)}, bf16[256,1280]{1,0:T(8,128)(2,1)S(1)}, u32[]{:S(2)}, u32[]{:S(2)}) collective-permute-start(bf16[256,1280]{1,0:T(8,128)(2,1)S(1)} %get-tuple-element.38.refs_1_), channel_id=1, source_target_pairs={{0,2},{1,3},{2,0},{3,1},{4,6},{5,7},{6,4},{7,5},{8,10},{9,11},{10,... | collective-permute-start | bytes 1966088 | tf_op jit(solution)/shard_map/ppermute | solution.py:76
  37.1 12.2 %collective-permute-start.13 = (bf16[256,1152]{1,0:T(8,128)(2,1)S(1)}, bf16[256,1152]{1,0:T(8,128)(2,1)}, u32[]{:S(2)}, u32[]{:S(2)}) collective-permute-start(bf16[256,1152]{1,0:T(8,128)(2,1)S(1)} %get-tuple-element.39.refs_2_), channel_id=1, source_target_pairs={{0,8},{1,9},{2,10},{3,11},{4,12},{5,13},{6,14},{7,15},{8,0},{9,1},... | collective-permute-start | bytes 1769480 | tf_op jit(solution)/shard_map/ppermute | solution.py:76
  50.3 13.4 %copy-start.1 = (bf16[1,512,3584]{2,1,0:T(8,128)(2,1)S(1)}, bf16[1,512,3584]{2,1,0:T(8,128)(2,1)}, u32[]{:S(2)}) copy-start(bf16[1,512,3584]{2,1,0:T(8,128)(2,1)} %param.23) | copy-start | bytes 11010052
  67.1 29.0 %collective-permute-start.14 = (f32[256,1280]{1,0:T(8,128)}, f32[256,1280]{1,0:T(8,128)}, u32[]{:S(2)}, u32[]{:S(2)}) collective-permute-start(f32[256,1280]{1,0:T(8,128)} %get-tuple-element.45), channel_id=1, source_target_pairs={{0,4},{1,5},{2,6},{3,7},{4,0},{5,1},{6,2},{7,3},{8,12},{9,13},{10,... | collective-permute-start | bytes 3932168 | tf_op jit(solution)/shard_map/ppermute | solution.py:76
  71.0 34.7 %collective-permute-start.16 = (f32[256,1280]{1,0:T(8,128)}, f32[256,1280]{1,0:T(8,128)}, u32[]{:S(2)}, u32[]{:S(2)}) collective-permute-start(f32[256,1280]{1,0:T(8,128)} %get-tuple-element.46), channel_id=1, source_target_pairs={{0,2},{1,3},{2,0},{3,1},{4,6},{5,7},{6,4},{7,5},{8,10},{9,11},{10,... | collective-permute-start | bytes 3932168 | tf_op jit(solution)/shard_map/ppermute | solution.py:76
  75.4 24.5 %collective-permute-start.17 = (f32[256,1024]{1,0:T(8,128)}, f32[256,1024]{1,0:T(8,128)}, u32[]{:S(2)}, u32[]{:S(2)}) collective-permute-start(f32[256,1024]{1,0:T(8,128)} %get-tuple-element.47), channel_id=1, source_target_pairs={{0,8},{1,9},{2,10},{3,11},{4,12},{5,13},{6,14},{7,15},{8,0},{9,1},... | collective-permute-start | bytes 3145736 | tf_op jit(solution)/shard_map/ppermute | solution.py:76
  80.1 30.8 %all-to-all-start = ((bf16[32,8,608]{2,1,0:T(8,128)(2,1)}), bf16[32,8,608]{2,1,0:T(8,128)(2,1)}, u32[]{:S(2)}, u32[]{:S(2)}) async-start(bf16[32,8,608]{2,1,0:T(8,128)(2,1)} %fusion.21), calls=%async_computation | async-start | bytes 655360 | tf_op jit(solution)/shard_map/all_to_all | solution.py:452
  85.9 14.0 %copy-start.4 = (f32[256,1024]{1,0:T(8,128)S(1)}, f32[256,1024]{1,0:T(8,128)}, u32[]{:S(2)}) copy-start(f32[256,1024]{1,0:T(8,128)} %copy-done.2) | copy-start | bytes 3145732
  98.2 17.4 %collective-permute-start.15 = (f32[128,1280]{1,0:T(8,128)}, f32[128,1280]{1,0:T(8,128)S(1)}, u32[]{:S(2)}, u32[]{:S(2)}) collective-permute-start(f32[128,1280]{1,0:T(8,128)} %summed.8.refs_2_), channel_id=1, source_target_pairs={{0,2},{1,3},{2,0},{3,1},{4,6},{5,7},{6,4},{7,5},{8,10},{9,11},{10,... | collective-permute-start | bytes 1966088 | tf_op jit(solution)/shard_map/ppermute | solution.py:76
  107.6 15.9 %collective-permute-start.19 = (f32[128,1280]{1,0:T(8,128)}, f32[128,1280]{1,0:T(8,128)}, u32[]{:S(2)}, u32[]{:S(2)}) collective-permute-start(f32[128,1280]{1,0:T(8,128)} %summed.10.refs_3_), channel_id=1, source_target_pairs={{0,8},{1,9},{2,10},{3,11},{4,12},{5,13},{6,14},{7,15},{8,0},{9,1},... | collective-permute-start | bytes 1966088 | tf_op jit(solution)/shard_map/ppermute | solution.py:76
  108.9 12.3 %collective-permute-start.20 = (f32[128,1024]{1,0:T(8,128)}, f32[128,1024]{1,0:T(8,128)}, u32[]{:S(2)}, u32[]{:S(2)}) collective-permute-start(f32[128,1024]{1,0:T(8,128)} %summed.9.refs_2_), channel_id=1, source_target_pairs={{0,4},{1,5},{2,6},{3,7},{4,0},{5,1},{6,2},{7,3},{8,12},{9,13},{10,... | collective-permute-start | bytes 1572872 | tf_op jit(solution)/shard_map/ppermute | solution.py:76
  114.0 7.2 %copy-start.5 = (f32[256,1024]{1,0:T(8,128)S(1)}, f32[256,1024]{1,0:T(8,128)}, u32[]{:S(2)}) copy-start(f32[256,1024]{1,0:T(8,128)} %copy-done.2) | copy-start | bytes 3145732
  117.3 13.6 %collective-permute-start.18 = (f32[64,1280]{1,0:T(8,128)}, f32[64,1280]{1,0:T(8,128)}, u32[]{:S(2)}, u32[]{:S(2)}) collective-permute-start(f32[64,1280]{1,0:T(8,128)} %summed.11.refs_3_), channel_id=1, source_target_pairs={{0,24},{1,25},{2,26},{3,27},{4,28},{5,29},{6,30},{7,31},{8,16},{9,... | collective-permute-start | bytes 983048 | tf_op jit(solution)/shard_map/ppermute | solution.py:76
  123.0 9.0 %collective-permute-start.22 = (f32[64,1024]{1,0:T(8,128)}, f32[64,1024]{1,0:T(8,128)}, u32[]{:S(2)}, u32[]{:S(2)}) collective-permute-start(f32[64,1024]{1,0:T(8,128)} %summed.12.refs_3_), channel_id=1, source_target_pairs={{0,2},{1,3},{2,0},{3,1},{4,6},{5,7},{6,4},{7,5},{8,10},{9,11},{10,... | collective-permute-start | bytes 786440 | tf_op jit(solution)/shard_map/ppermute | solution.py:76
  125.4 7.4 %collective-permute-start.21 = (f32[64,1280]{1,0:T(8,128)}, f32[64,1280]{1,0:T(8,128)}, u32[]{:S(2)}, u32[]{:S(2)}) collective-permute-start(f32[64,1280]{1,0:T(8,128)} %summed.13.refs_4_), channel_id=1, source_target_pairs={{0,4},{1,5},{2,6},{3,7},{4,0},{5,1},{6,2},{7,3},{8,12},{9,13},{10,... | collective-permute-start | bytes 983048 | tf_op jit(solution)/shard_map/ppermute | solution.py:76
  132.0 9.4 %copy-start.8 = (bf16[256,576]{0,1:T(8,128)(2,1)S(1)}, bf16[256,576]{0,1:T(8,128)(2,1)}, u32[]{:S(2)}) copy-start(bf16[256,576]{0,1:T(8,128)(2,1)} %copy.29) | copy-start | bytes 884740
  132.0 9.3 %copy-start.9 = (bf16[1,1024,576]{1,2,0:T(8,128)(2,1)S(1)}, bf16[1,1024,576]{1,2,0:T(8,128)(2,1)}, u32[]{:S(2)}) copy-start(bf16[1,1024,576]{1,2,0:T(8,128)(2,1)} %param.14) | copy-start | bytes 3538948
  134.1 12.2 %collective-permute-start.24 = (f32[32,2304]{1,0:T(8,128)S(1)}, f32[32,2304]{1,0:T(8,128)S(1)}, u32[]{:S(2)}, u32[]{:S(2)}) collective-permute-start(f32[32,2304]{1,0:T(8,128)S(1)} %summed.15), channel_id=1, source_target_pairs={{0,24},{1,25},{2,26},{3,27},{4,28},{5,29},{6,30},{7,31},{8,16},{9,... | collective-permute-start | bytes 884744 | tf_op jit(solution)/shard_map/ppermute | solution.py:76
  134.9 11.3 %collective-permute-start.23 = (f32[32,1280]{1,0:T(8,128)S(1)}, f32[32,1280]{1,0:T(8,128)S(1)}, u32[]{:S(2)}, u32[]{:S(2)}) collective-permute-start(f32[32,1280]{1,0:T(8,128)S(1)} %summed.14.refs_8_), channel_id=1, source_target_pairs={{0,8},{1,9},{2,10},{3,11},{4,12},{5,13},{6,14},{7,15},{8,0},{9,1},... | collective-permute-start | bytes 491528 | tf_op jit(solution)/shard_map/ppermute | solution.py:76
  (5 other events, 14.9 us)

commit v11 on v9

--- a/solution.py
+++ b/solution.py
@@ -141,49 +141,88 @@
     return whole_call(kernel, [array], [shape], "hold_back", (after,))[0]
 
 
-def gather_cube(tokens, side, gate, up, down):
+def first_joined(held, got, widths, after):
+    rows = held[0].shape[0]
+    out_shape = [jax.ShapeDtypeStruct((2 * rows, width), held[0].dtype) for width in widths]
+
+    def kernel(first, rest, got_first, got_rest, *outs):
+        outs[0][:rows] = first[...]
+        outs[0][rows:] = got_first[...]
+        start = 0
+        for out, width in zip(outs[1:], widths[1:]):
+            out[:rows] = rest[:, start : start + width]
+            out[rows:] = got_rest[:, start : start + width]
+            start += width
+
+    return whole_call(kernel, [*held, *got], out_shape, "first_joined", after)
+
+
+def gather_cube(unit, chip, tokens, side, gate, up, down):
     steps = len(LINKS)
     others = [swap_cores(weight) for weight in (gate, up, down)]
-    held = [tokens[:, start:stop] for start, stop in piece_columns(tokens.shape[1])]
-    held[-1] = jnp.concatenate([held[-1], side], axis=1)
-    for phase in range(steps):
+    columns = piece_columns(tokens.shape[1])
+    widths = [stop - start for start, stop in columns]
+    widths[-1] += side.shape[1]
+    cut = columns[0][1]
+    held = [tokens[:, :cut], jnp.concatenate([tokens[:, cut:], side], axis=1)]
+    got = [across(piece, order[-1]) for piece, order in zip(held, ORDERS)]
+    held = first_joined(held, got, widths, others[2:])
+    for phase in range(1, steps):
         got = [across(piece, order[steps - 1 - phase]) for piece, order in zip(held, ORDERS)]
         if phase < steps - 1:
-            held = joined(held, got, (others[2:], others[:2], ())[phase])
-    return held, got, others
-
-
-def hidden_kernel(unit, chip_ref, *refs):
+            held = joined(held, got, others[:2] if phase == 1 else ())
+    weights = (gate, up, *others[:2])
+    so_far = expert_part(unit, chip, held, weights)
+    return expert_part(unit, chip, got, weights, so_far), others
+
+
+def part_kernel(unit, last, chip_ref, *refs):
     count = len(ORDERS)
-    held, got = refs[:count], refs[count : 2 * count]
-    gate_ref, up_ref, gate_other_ref, up_other_ref = refs[2 * count : 2 * count + 4]
-    hidden_ref, scale_ref, rows_ref, side_ref = refs[2 * count + 4 :]
+    pieces = refs[:count]
+    gate_ref, up_ref, gate_other_ref, up_other_ref = refs[count : count + 4]
+    if last:
+        gate_part, up_part, scale_part, hidden_ref, scale_ref, gate_sum, up_sum = refs[count + 4 :]
+    else:
+        gate_sum, up_sum, scale_ref = refs[count + 4 :]
     step = pl.program_id(0)
     own_steps = pl.num_programs(0) // 2
+    columns = piece_columns(gate_ref.shape[0])
+    places = pieces[0].shape[0] // unit
+
+    def slots(order):
+        for at in range(places):
+            slot = slot_of(at + (places if last else 0), order)
+            yield slice(slot * unit, (slot + 1) * unit), slice(at * unit, (at + 1) * unit)
 
     @pl.when(step == 0)
     def _():
-        for piece, (start, stop) in enumerate(piece_columns(rows_ref.shape[1])):
-            half = held[piece].shape[0]
-            for place in range(2 * half // unit):
-                source = held[piece] if place * unit < half else got[piece]
-                at = place * unit % half
-                slot = slot_of(place, ORDERS[piece])
-                to = slice(slot * unit, (slot + 1) * unit)
-                rows_ref[to, start:stop] = source[at : at + unit, : stop - start]
-                if piece == count - 1:
-                    side_ref[to, :] = source[at : at + unit, stop - start :]
-        column = lax.broadcasted_iota(jnp.int32, side_ref.shape, 1)
+        scale_ref[...] = scale_part[...] if last else jnp.zeros_like(scale_ref)
+        start, stop = columns[-1]
+        side = pieces[-1][:, stop - start :].astype(jnp.float32)
+        column = lax.broadcasted_iota(jnp.int32, side.shape, 1)
         experts = 1 << len(LINKS)
         mine = jnp.logical_and(column % experts == chip_ref[0], column < 3 * experts)
-        parts = jnp.where(mine, side_ref[...].astype(jnp.float32), 0.0)
-        scale_ref[...] = jnp.sum(parts, axis=1, keepdims=True)
+        scale = jnp.sum(jnp.where(mine, side, 0.0), axis=1, keepdims=True)
+        for to, source in slots(ORDERS[-1]):
+            scale_ref[to, :] = scale[source]
+
+    def add_up(tile, total, so_far):
+        total[...] = so_far[...] if last else jnp.zeros_like(total)
+        for piece, (start, stop) in enumerate(columns):
+            part = jnp.dot(
+                pieces[piece][:, : stop - start],
+                tile[start:stop, :],
+                preferred_element_type=jnp.float32,
+            )
+            for to, source in slots(ORDERS[piece]):
+                total[to, :] += part[source]
 
     def units(gate_tile, up_tile):
-        rows = rows_ref[...]
-        gate = jnp.dot(rows, gate_tile[...], preferred_element_type=jnp.float32)
-        upper = jnp.dot(rows, up_tile[...], preferred_element_type=jnp.float32)
-        hidden_ref[...] = (gate / (1.0 + jnp.exp(-gate)) * upper).astype(jnp.bfloat16)
+        add_up(gate_tile, gate_sum, gate_part if last else None)
+        add_up(up_tile, up_sum, up_part if last else None)
+        if last:
+            gate = gate_sum[...]
+            hidden_ref[...] = (gate / (1.0 + jnp.exp(-gate)) * up_sum[...]).astype(jnp.bfloat16)
 
     @pl.when(step < own_steps)
     def _():
@@ -194,39 +233,37 @@
         units(gate_other_ref, up_other_ref)
 
 
-def expert_hidden(unit, chip, held, got, gate, up, gate_other, up_other):
-    width, units = gate.shape
-    count = 2 * held[0].shape[0]
+def expert_part(unit, chip, pieces, weights, so_far=()):
+    width, units = weights[0].shape
+    rows = pieces[0].shape[0]
     tile = 256
     steps = units // tile
     own = pl.BlockSpec((width, tile), lambda i: (0, jnp.minimum(i, steps - 1)))
     other = pl.BlockSpec((width, tile), lambda i: (0, jnp.maximum(i - steps, 0)))
+    tiled = pl.BlockSpec((2 * rows, tile), lambda i: (0, i))
+    single = pl.BlockSpec((2 * rows, 1), lambda i: (0, 0))
+    total = jax.ShapeDtypeStruct((2 * rows, 2 * units), jnp.float32)
+    scale = jax.ShapeDtypeStruct((2 * rows, 1), jnp.float32)
+    hidden = jax.ShapeDtypeStruct((2 * rows, 2 * units), jnp.bfloat16)
+    last = len(so_far) > 0
     return pl.pallas_call(
-        functools.partial(hidden_kernel, unit),
+        functools.partial(part_kernel, unit, last),
         grid=(2 * steps,),
         in_specs=[pl.BlockSpec(memory_space=pltpu.SMEM)]
-        + [pl.BlockSpec(array.shape, lambda i: (0, 0)) for array in (*held, *got)]
-        + [own, own, other, other],
-        out_specs=[
-            pl.BlockSpec((count, tile), lambda i: (0, i)),
-            pl.BlockSpec((count, 1), lambda i: (0, 0)),
-        ],
-        out_shape=[
-            jax.ShapeDtypeStruct((count, 2 * units), jnp.bfloat16),
-            jax.ShapeDtypeStruct((count, 1), jnp.float32),
-        ],
-        scratch_shapes=[
-            pltpu.VMEM((count, width), jnp.bfloat16),
-            pltpu.VMEM((count, sum(piece.shape[1] for piece in held) - width), jnp.bfloat16),
-        ],
+        + [pl.BlockSpec(array.shape, lambda i: (0, 0)) for array in pieces]
+        + [own, own, other, other]
+        + ([tiled, tiled, single] if last else []),
+        out_specs=[tiled, single] if last else [tiled, tiled, single],
+        out_shape=[hidden, scale] if last else [total, total, scale],
+        scratch_shapes=[pltpu.VMEM((2 * rows, tile), jnp.float32)] * (2 if last else 0),
         compiler_params=pltpu.CompilerParams(vmem_limit_bytes=48 * MIB),
         cost_estimate=pl.CostEstimate(
-            flops=8 * count * width * units,
-            bytes_accessed=2 * (count * width + 4 * width * units + 2 * count * units),
-            transcendentals=2 * count * units,
+            flops=8 * rows * width * units,
+            bytes_accessed=8 * width * units + 2 * rows * width + 24 * rows * units,
+            transcendentals=4 * rows * units if last else 0,
         ),
-        name="expert_hidden",
-    )(chip, *held, *got, gate, up, gate_other, up_other)
+        name="expert_part",
+    )(chip, *pieces, *weights, *so_far)
 
 
 def output_kernel(unit, order, tiles, scale_ref, hidden_ref, *refs):
@@ -301,11 +338,7 @@
     return whole_call(kernel, [*keep, *got], [shape], "finished")[0]
 
 
-def cube_outputs(unit, held, got, weights, others):
-    gate, up, down = weights
-    gate_other, up_other, down_other = others
-    chip = (lax.axis_index("ep") // 2).astype(jnp.int32).reshape(1)
-    hidden, scale = expert_hidden(unit, chip, held, got, gate, up, gate_other, up_other)
+def cube_outputs(unit, hidden, scale, down, down_other):
     keep, coming = [], []
     for order, columns in zip(ORDERS, piece_columns(down.shape[1])):
         after = keep[-1:]
@@ -358,8 +391,9 @@
         share = jnp.sum(jnp.where(named, route_weight[:, :, None], 0.0), axis=1)
         parts = jnp.concatenate(three_parts(share), axis=1).astype(jnp.bfloat16)
         parts = jnp.pad(parts, ((0, 0), (0, 128 - parts.shape[1])))
-        *gathered, others = gather_cube(tokens, parts, *weights)
-        keep, coming = cube_outputs(tok_rows, *gathered, weights, others)
+        chip = (lax.axis_index("ep") // 2).astype(jnp.int32).reshape(1)
+        (hidden, scale), others = gather_cube(tok_rows, chip, tokens, parts, *weights)
+        keep, coming = cube_outputs(tok_rows, hidden, scale, weights[2], others[2])
         prefill_latent = hold_back(prefill_latent, keep[-1])
 
     owner = block_owner.reshape(blocks)

time: 145 us -> 142 us (0.979)
  waiting for transfers between devices: 48.1 us -> 41.6 us
  Pallas kernels: 33.5 us -> 39.7 us
  starting transfers between devices: 46.6 us -> 43.3 us
    ppermute x24 -> x23, waiting for transfers between devices: 48.1 us -> 41.6 us  [across(): lax.ppermute(value, 'ep', [(i, i ^ 2 * LINKS[link]) for i in range(peers)])]
    pallas_call x1 -> x2, Pallas kernels: 13.4 us -> 19.6 us  [expert_part(): pl.pallas_call(functools.partial(part_kernel, unit, last), grid=(2 * step...]
    ppermute x24 -> x23, starting transfers between devices: 42.1 us -> 36.5 us  [across(): lax.ppermute(value, 'ep', [(i, i ^ 2 * LINKS[link]) for i in range(peers)])]
    all_to_all x1, starting transfers between devices: 3.48 us -> 5.76 us  [per_device(): lax.all_to_all(leaving, 'ep', split_axis=0, concat_axis=0, tiled=True)]
  transfers between devices with their start and end apart: 28 -> 27, of which waited for: 13 -> 14; matrix products, arithmetic and copies ran while one was open for 7% -> 8% of each run, Pallas kernels for 11% -> 18%
where the time goes in v11:
time: 142 us; the launch traced here: 141 us
  starting transfers between devices  43.3 us (30%)
  waiting for transfers between devices  41.6 us (29%)
  Pallas kernels  39.7 us (28%)
  local copies, waits for them, and re-layouts  8.86 us (6%)
  other arithmetic  3.21 us (2%)
  matrix products  2.63 us (2%)
  between operations  1.5 us (1%)
    ppermute x23, waiting for transfers between devices, across(): lax.ppermute(value, 'ep', [(i, i ^ 2 * LINKS[link]) for i in range(peers)])  41.6 us
    ppermute x23, starting transfers between devices, across(): lax.ppermute(value, 'ep', [(i, i ^ 2 * LINKS[link]) for i in range(peers)])  36.5 us
    pallas_call x2, Pallas kernels, expert_part(): pl.pallas_call(functools.partial(part_kernel, unit, last), grid=(2 * step...  19.6 us
    pallas_call x14, Pallas kernels, whole_call(): pl.pallas_call(body, in_specs=[pl.BlockSpec(memory_space=pltpu.VMEM)] * g...  10.2 us
    pallas_call x3, Pallas kernels, expert_output(): pl.pallas_call(functools.partial(output_kernel, unit, order, tiles), grid...  9.83 us
    all_to_all x1, starting transfers between devices, per_device(): lax.all_to_all(leaving, 'ep', split_axis=0, concat_axis=0, tiled=True)  5.76 us
    unnamed x22, local copies, waits for them, and re-layouts  4.07 us
  transfers between devices with their start and end apart: 27, of which 14 were waited for; matrix products, arithmetic and copies ran while one was open for 8% of the time, Pallas kernels for 18%

profile of v11, /device:TPU:0, one launch (start us, length us, event | category | flops | bytes accessed | tf_op | source)
XLA Modules:
  0.0 140.8 jit_solution(14712537869578517241)
XLA Ops:
  3.6 4.7 %collective-permute-start.1 = (bf16[32,2432]{1,0:T(8,128)(2,1)S(1)}, bf16[32,2432]{1,0:T(8,128)(2,1)S(1)}, u32[]{:S(2)}, u32[]{:S(2)}) collective-permute-start(bf16[32,2432]{1,0:T(8,128)(2,1)S(1)} %pad_maximum_fusion.refs_1_), channel_id=1, source_target_pairs={{0,24},{1,25},{2,26},{3,27},{4,28},{5,29},{6,30},{7,31},{8,16},{9,... | collective-permute-start | bytes 466952 | tf_op jit(solution)/shard_map/ppermute | solution.py:76
  9.2 5.6 %collective-permute-done.refs_2_ = bf16[32,1280]{1,0:T(8,128)(2,1)S(1)} collective-permute-done((bf16[32,1280]{1,0:T(8,128)(2,1)S(1)}, bf16[32,1280]{1,0:T(8,128)(2,1)S(1)}, u32[]{:S(2)}, u32[]{:S(2)}) %collective-permute-start) | collective-permute-done | bytes 81952 | tf_op jit(solution)/shard_map/ppermute | solution.py:76
  14.9 2.6 %collective-permute-start.3 = (bf16[64,1280]{1,0:T(8,128)(2,1)S(1)}, bf16[64,1280]{1,0:T(8,128)(2,1)S(1)}, u32[]{:S(2)}, u32[]{:S(2)}) collective-permute-start(bf16[64,1280]{1,0:T(8,128)(2,1)S(1)} %get-tuple-element.52.refs_0_), channel_id=1, source_target_pairs={{0,24},{1,25},{2,26},{3,27},{4,28},{5,29},{6,30},{7,31},{8,16},{9,... | collective-permute-start | bytes 491528 | tf_op jit(solution)/shard_map/ppermute | solution.py:76
  17.5 1.5 %collective-permute-start.4 = (bf16[64,1280]{1,0:T(8,128)(2,1)S(1)}, bf16[64,1280]{1,0:T(8,128)(2,1)S(1)}, u32[]{:S(2)}, u32[]{:S(2)}) collective-permute-start(bf16[64,1280]{1,0:T(8,128)(2,1)S(1)} %get-tuple-element.53.refs_1_), channel_id=1, source_target_pairs={{0,4},{1,5},{2,6},{3,7},{4,0},{5,1},{6,2},{7,3},{8,12},{9,13},{10,... | collective-permute-start | bytes 491528 | tf_op jit(solution)/shard_map/ppermute | solution.py:76
  19.0 1.5 %collective-permute-start.5 = (bf16[64,1152]{1,0:T(8,128)(2,1)S(1)}, bf16[64,1152]{1,0:T(8,128)(2,1)S(1)}, u32[]{:S(2)}, u32[]{:S(2)}) collective-permute-start(bf16[64,1152]{1,0:T(8,128)(2,1)S(1)} %get-tuple-element.54.refs_2_), channel_id=1, source_target_pairs={{0,2},{1,3},{2,0},{3,1},{4,6},{5,7},{6,4},{7,5},{8,10},{9,11},{10,... | collective-permute-start | bytes 442376 | tf_op jit(solution)/shard_map/ppermute | solution.py:76
  20.5 3.6 %collective-permute-done.5.refs_5_ = bf16[64,1152]{1,0:T(8,128)(2,1)S(1)} collective-permute-done((bf16[64,1152]{1,0:T(8,128)(2,1)S(1)}, bf16[64,1152]{1,0:T(8,128)(2,1)S(1)}, u32[]{:S(2)}, u32[]{:S(2)}) %collective-permute-start.5) | collective-permute-done | bytes 147488 | tf_op jit(solution)/shard_map/ppermute | solution.py:76
  24.2 1.6 %collective-permute-start.8 = (bf16[128,1280]{1,0:T(8,128)(2,1)S(1)}, bf16[128,1280]{1,0:T(8,128)(2,1)S(1)}, u32[]{:S(2)}, u32[]{:S(2)}) collective-permute-start(bf16[128,1280]{1,0:T(8,128)(2,1)S(1)} %get-tuple-element.55.refs_0_), channel_id=1, source_target_pairs={{0,2},{1,3},{2,0},{3,1},{4,6},{5,7},{6,4},{7,5},{8,10},{9,11},{10,... | collective-permute-start | bytes 983048 | tf_op jit(solution)/shard_map/ppermute | solution.py:76
  25.8 1.7 %collective-permute-start.9 = (bf16[128,1280]{1,0:T(8,128)(2,1)S(1)}, bf16[128,1280]{1,0:T(8,128)(2,1)S(1)}, u32[]{:S(2)}, u32[]{:S(2)}) collective-permute-start(bf16[128,1280]{1,0:T(8,128)(2,1)S(1)} %get-tuple-element.56.refs_1_), channel_id=1, source_target_pairs={{0,8},{1,9},{2,10},{3,11},{4,12},{5,13},{6,14},{7,15},{8,0},{9,1},... | collective-permute-start | bytes 983048 | tf_op jit(solution)/shard_map/ppermute | solution.py:76
  27.5 1.5 %collective-permute-start.10 = (bf16[128,1152]{1,0:T(8,128)(2,1)S(1)}, bf16[128,1152]{1,0:T(8,128)(2,1)S(1)}, u32[]{:S(2)}, u32[]{:S(2)}) collective-permute-start(bf16[128,1152]{1,0:T(8,128)(2,1)S(1)} %get-tuple-element.57.refs_2_), channel_id=1, source_target_pairs={{0,4},{1,5},{2,6},{3,7},{4,0},{5,1},{6,2},{7,3},{8,12},{9,13},{10,... | collective-permute-start | bytes 884744 | tf_op jit(solution)/shard_map/ppermute | solution.py:76
  29.0 5.7 %collective-permute-done.10.refs_5_ = bf16[128,1152]{1,0:T(8,128)(2,1)S(1)} collective-permute-done((bf16[128,1152]{1,0:T(8,128)(2,1)S(1)}, bf16[128,1152]{1,0:T(8,128)(2,1)S(1)}, u32[]{:S(2)}, u32[]{:S(2)}) %collective-permute-start.10) | collective-permute-done | bytes 294944 | tf_op jit(solution)/shard_map/ppermute | solution.py:76
  34.9 1.6 %collective-permute-start.11 = (bf16[256,1280]{1,0:T(8,128)(2,1)S(1)}, bf16[256,1280]{1,0:T(8,128)(2,1)S(1)}, u32[]{:S(2)}, u32[]{:S(2)}) collective-permute-start(bf16[256,1280]{1,0:T(8,128)(2,1)S(1)} %get-tuple-element.58.refs_0_), channel_id=1, source_target_pairs={{0,4},{1,5},{2,6},{3,7},{4,0},{5,1},{6,2},{7,3},{8,12},{9,13},{10,... | collective-permute-start | bytes 1966088 | tf_op jit(solution)/shard_map/ppermute | solution.py:76
  38.0 10.0 %expert_part.2 = (f32[512,1024]{1,0:T(8,128)S(1)}, f32[512,1024]{1,0:T(8,128)}, f32[512,1]{1,0:T(8,128)S(1)}) custom-call(s32[1]{0:T(128)} %bitcast.2.chip_ref, bf16[256,1280]{1,0:T(8,128)(2,1)S(1)} %get-tuple-element.58.refs_0_, bf16[256,1280]{1,0:T(8,128)(2,1)S(1)} %get-tuple-element.59.refs_1_, bf16[256,1152]{1,0:T(8,128)(2,1)S(1)} %get-tuple-element.60.refs_2_, ...), custom_call_target="tpu_custom_call" | custom-call | flops 3758096384 | bytes 19660800 | tf_op jit(solution)/shard_map/expert_part/pallas_call | solution.py:249
  50.3 9.6 %expert_part.3 = (bf16[512,1024]{1,0:T(8,128)(2,1)S(1)}, f32[512,1]{1,0:T(8,128)S(1)}) custom-call(s32[1]{0:T(128)} %bitcast.2.chip_ref, bf16[256,1280]{1,0:T(8,128)(2,1)S(1)} %collective-permute-done.11.refs_0_, bf16[256,1280]{1,0:T(8,128)(2,1)S(1)} %collective-permute-done.12.refs_1_, bf16[256,1152]{1,0:T(8,128)(2,1)} %collective-permute-done.13.refs_2_, ...), custom_call_target="tpu_custom_call" | custom-call | flops 3758096384 | bytes 19660800 | tf_op jit(solution)/shard_map/expert_part/pallas_call | solution.py:249
  59.9 3.5 %expert_output.3 = (f32[256,1280]{1,0:T(8,128)S(1)}, f32[256,1280]{1,0:T(8,128)}) custom-call(f32[512,1]{1,0:T(8,128)S(1)} %get-tuple-element.64.scale_ref, bf16[512,1024]{1,0:T(8,128)(2,1)S(1)} %get-tuple-element.65.hidden_ref, bf16[512,3584]{1,0:T(8,128)(2,1)S(1)} %bitcast.20, bf16[512,3584]{1,0:T(8,128)(2,1)S(1)} %bitcast.21, ...), custom_call_target="tpu_custom_call" | custom-call | flops 1342177280 | bytes 6291456 | tf_op jit(solution)/shard_map/expert_output/pallas_call | solution.py:296
  63.9 3.4 %expert_output.4 = (f32[256,1280]{1,0:T(8,128)S(1)}, f32[256,1280]{1,0:T(8,128)}) custom-call(f32[512,1]{1,0:T(8,128)S(1)} %get-tuple-element.64.scale_ref, bf16[512,1024]{1,0:T(8,128)(2,1)S(1)} %get-tuple-element.65.hidden_ref, bf16[512,3584]{1,0:T(8,128)(2,1)S(1)} %bitcast.25, bf16[512,3584]{1,0:T(8,128)(2,1)S(1)} %bitcast.26, ...), custom_call_target="tpu_custom_call" | custom-call | flops 1342177280 | bytes 6291456 | tf_op jit(solution)/shard_map/expert_output/pallas_call | solution.py:296
  68.0 2.9 %expert_output.5 = (f32[256,1024]{1,0:T(8,128)S(1)}, f32[256,1024]{1,0:T(8,128)}) custom-call(f32[512,1]{1,0:T(8,128)S(1)} %get-tuple-element.64.scale_ref, bf16[512,1024]{1,0:T(8,128)(2,1)S(1)} %get-tuple-element.65.hidden_ref, bf16[512,3584]{1,0:T(8,128)(2,1)S(1)} %bitcast.30, bf16[512,3584]{1,0:T(8,128)(2,1)S(1)} %bitcast.31, ...), custom_call_target="tpu_custom_call" | custom-call | flops 1073741824 | bytes 5242880 | tf_op jit(solution)/shard_map/expert_output/pallas_call | solution.py:296
  76.5 5.8 %all-to-all-start = ((bf16[32,8,608]{2,1,0:T(8,128)(2,1)}), bf16[32,8,608]{2,1,0:T(8,128)(2,1)}, u32[]{:S(2)}, u32[]{:S(2)}) async-start(bf16[32,8,608]{2,1,0:T(8,128)(2,1)} %fusion.21), calls=%async_computation | async-start | bytes 655360 | tf_op jit(solution)/shard_map/all_to_all | solution.py:422
  82.2 10.1 %collective-permute-done.14.refs_1_ = f32[256,1280]{1,0:T(8,128)} collective-permute-done((f32[256,1280]{1,0:T(8,128)}, f32[256,1280]{1,0:T(8,128)}, u32[]{:S(2)}, u32[]{:S(2)}) %collective-permute-start.14) | collective-permute-done | bytes 1310752 | tf_op jit(solution)/shard_map/ppermute | solution.py:76
  92.3 2.3 %halved.9 = (f32[128,1280]{1,0:T(8,128)S(1)}, f32[128,1280]{1,0:T(8,128)}) custom-call(f32[256,1280]{1,0:T(8,128)S(1)} %get-tuple-element.66.refs_10_.refs_0_, f32[256,1280]{1,0:T(8,128)} %collective-permute-done.14.refs_1_), custom_call_target="tpu_custom_call" | custom-call | bytes 3932160 | tf_op jit(solution)/shard_map/halved/pallas_call | solution.py:107
  96.5 2.1 %halved.10 = (f32[128,1024]{1,0:T(8,128)S(1)}, f32[128,1024]{1,0:T(8,128)}) custom-call(f32[256,1024]{1,0:T(8,128)S(1)} %copy-done.4, f32[256,1024]{1,0:T(8,128)} %collective-permute-done.17.refs_1_, f32[128,1280]{1,0:T(8,128)S(1)} %get-tuple-element.70.refs_2_.refs_0_), custom_call_target="tpu_custom_call" | custom-call | bytes 3145728 | tf_op jit(solution)/shard_map/halved/pallas_call | solution.py:107
  98.6 3.3 %collective-permute-done.16.refs_1_ = f32[256,1280]{1,0:T(8,128)} collective-permute-done((f32[256,1280]{1,0:T(8,128)}, f32[256,1280]{1,0:T(8,128)}, u32[]{:S(2)}, u32[]{:S(2)}) %collective-permute-start.16) | collective-permute-done | bytes 1310752 | tf_op jit(solution)/shard_map/ppermute | solution.py:76
  101.9 2.3 %halved.11 = (f32[128,1280]{1,0:T(8,128)S(1)}, f32[128,1280]{1,0:T(8,128)}) custom-call(f32[256,1280]{1,0:T(8,128)S(1)} %get-tuple-element.67.refs_8_.refs_0_, f32[256,1280]{1,0:T(8,128)} %collective-permute-done.16.refs_1_, f32[128,1024]{1,0:T(8,128)S(1)} %get-tuple-element.74.refs_2_.refs_0_), custom_call_target="tpu_custom_call" | custom-call | bytes 3932160 | tf_op jit(solution)/shard_map/halved/pallas_call | solution.py:107
  104.2 1.4 collective-permute-start.19
  106.2 1.6 %collective-permute-start.20 = (f32[128,1024]{1,0:T(8,128)}, f32[128,1024]{1,0:T(8,128)S(1)}, u32[]{:S(2)}, u32[]{:S(2)}) collective-permute-start(f32[128,1024]{1,0:T(8,128)} %get-tuple-element.79), channel_id=1, source_target_pairs={{0,4},{1,5},{2,6},{3,7},{4,0},{5,1},{6,2},{7,3},{8,12},{9,13},{10,... | collective-permute-start | bytes 1572872 | tf_op jit(solution)/shard_map/ppermute | solution.py:76
  113.2 4.0 %collective-permute-start.18 = (f32[64,1280]{1,0:T(8,128)S(1)}, f32[64,1280]{1,0:T(8,128)S(1)}, u32[]{:S(2)}, u32[]{:S(2)}) collective-permute-start(f32[64,1280]{1,0:T(8,128)S(1)} %get-tuple-element.77), channel_id=1, source_target_pairs={{0,24},{1,25},{2,26},{3,27},{4,28},{5,29},{6,30},{7,31},{8,16},{9,... | collective-permute-start | bytes 983048 | tf_op jit(solution)/shard_map/ppermute | solution.py:76
  120.8 1.5 %collective-permute-start.21 = (f32[64,1280]{1,0:T(8,128)S(1)}, f32[64,1280]{1,0:T(8,128)S(1)}, u32[]{:S(2)}, u32[]{:S(2)}) collective-permute-start(f32[64,1280]{1,0:T(8,128)S(1)} %get-tuple-element.83), channel_id=1, source_target_pairs={{0,4},{1,5},{2,6},{3,7},{4,0},{5,1},{6,2},{7,3},{8,12},{9,13},{10,... | collective-permute-start | bytes 983048 | tf_op jit(solution)/shard_map/ppermute | solution.py:76
  125.5 2.4 %collective-permute-done.21.refs_1_ = f32[64,1280]{1,0:T(8,128)S(1)} collective-permute-done((f32[64,1280]{1,0:T(8,128)S(1)}, f32[64,1280]{1,0:T(8,128)S(1)}, u32[]{:S(2)}, u32[]{:S(2)}) %collective-permute-start.21) | collective-permute-done | bytes 327712 | tf_op jit(solution)/shard_map/ppermute | solution.py:76
  128.0 1.9 %collective-permute-start.24 = (f32[32,1280]{1,0:T(8,128)S(1)}, f32[32,1280]{1,0:T(8,128)S(1)}, u32[]{:S(2)}, u32[]{:S(2)}) collective-permute-start(f32[32,1280]{1,0:T(8,128)S(1)} %get-tuple-element.88), channel_id=1, source_target_pairs={{0,24},{1,25},{2,26},{3,27},{4,28},{5,29},{6,30},{7,31},{8,16},{9,... | collective-permute-start | bytes 491528 | tf_op jit(solution)/shard_map/ppermute | solution.py:76
  129.8 2.0 %collective-permute-start.25 = (f32[32,1024]{1,0:T(8,128)S(1)}, f32[32,1024]{1,0:T(8,128)S(1)}, u32[]{:S(2)}, u32[]{:S(2)}) collective-permute-start(f32[32,1024]{1,0:T(8,128)S(1)} %get-tuple-element.89), channel_id=1, source_target_pairs={{0,24},{1,25},{2,26},{3,27},{4,28},{5,29},{6,30},{7,31},{8,16},{9,... | collective-permute-start | bytes 393224 | tf_op jit(solution)/shard_map/ppermute | solution.py:76
  131.8 2.6 %collective-permute-start.23 = (f32[32,1280]{1,0:T(8,128)S(1)}, f32[32,1280]{1,0:T(8,128)S(1)}, u32[]{:S(2)}, u32[]{:S(2)}) collective-permute-start(f32[32,1280]{1,0:T(8,128)S(1)} %get-tuple-element.87), channel_id=1, source_target_pairs={{0,8},{1,9},{2,10},{3,11},{4,12},{5,13},{6,14},{7,15},{8,0},{9,1},... | collective-permute-start | bytes 491528 | tf_op jit(solution)/shard_map/ppermute | solution.py:76
  134.4 1.5 %fusion.14 = bf16[1,128,512]{2,1,0:T(8,128)(2,1)} fusion(bf16[256,576]{0,1:T(8,128)(2,1)S(1)} %copy-done.8, bf16[1024,576]{0,1:T(8,128)(2,1)S(1)} %bitcast.41, f32[1280,128]{1,0:T(8,128)S(1)} %get-tuple-element.94, f32[128]{0:T(128)S(1)} %get-tuple-element.93, pred[1280]{0:T(1024)(128)(4,1)S(1)} %pad_add_fusion, f32[128]{0:T(128)S(1)} %fusion.18), kind=kOutput, calls=%fused_computation.12 | convolution fusion | flops 171016192 | bytes 2263296 | tf_op jit(solution)/shard_map/dot_general | solution.py:38
  136.8 3.3 %collective-permute-done.23.refs_3_ = f32[32,1280]{1,0:T(8,128)S(1)} collective-permute-done((f32[32,1280]{1,0:T(8,128)S(1)}, f32[32,1280]{1,0:T(8,128)S(1)}, u32[]{:S(2)}, u32[]{:S(2)}) %collective-permute-start.23) | collective-permute-done | bytes 163872 | tf_op jit(solution)/shard_map/ppermute | solution.py:76
  (91 shorter events, 30.1 us)
Async XLA Ops:
  0.6 121.7 %copy-start = (bf16[1,128,576]{1,2,0:T(8,128)(2,1)S(1)}, bf16[1,128,576]{1,2,0:T(8,128)(2,1)}, u32[]{:S(2)}) copy-start(bf16[1,128,576]{1,2,0:T(8,128)(2,1)} %param.13) | copy-start | bytes 442372
  0.6 14.2 %collective-permute-start.2 = (bf16[512,3584]{1,0:T(8,128)(2,1)}, bf16[512,3584]{1,0:T(8,128)(2,1)}, u32[]{:S(2)}, u32[]{:S(2)}) collective-permute-start(bf16[512,3584]{1,0:T(8,128)(2,1)} %bitcast.19), channel_id=1, source_target_pairs={{0,1},{1,0},{2,3},{3,2},{4,5},{5,4},{6,7},{7,6},{8,9},{9,8},{10,11... | collective-permute-start | bytes 11010056 | tf_op jit(solution)/shard_map/ppermute | solution.py:80
  1.2 19.3 %collective-permute-start.6 = (bf16[3584,512]{1,0:T(8,128)(2,1)}, bf16[3584,512]{1,0:T(8,128)(2,1)}, u32[]{:S(2)}, u32[]{:S(2)}) collective-permute-start(bf16[3584,512]{1,0:T(8,128)(2,1)} %bitcast.34), channel_id=1, source_target_pairs={{0,1},{1,0},{2,3},{3,2},{4,5},{5,4},{6,7},{7,6},{8,9},{9,8},{10,11... | collective-permute-start | bytes 11010056 | tf_op jit(solution)/shard_map/ppermute | solution.py:80
  1.2 19.3 %collective-permute-start.7 = (bf16[3584,512]{1,0:T(8,128)(2,1)}, bf16[3584,512]{1,0:T(8,128)(2,1)}, u32[]{:S(2)}, u32[]{:S(2)}) collective-permute-start(bf16[3584,512]{1,0:T(8,128)(2,1)} %bitcast.37), channel_id=1, source_target_pairs={{0,1},{1,0},{2,3},{3,2},{4,5},{5,4},{6,7},{7,6},{8,9},{9,8},{10,11... | collective-permute-start | bytes 11010056 | tf_op jit(solution)/shard_map/ppermute | solution.py:80
  3.6 11.2 %collective-permute-start.1 = (bf16[32,2432]{1,0:T(8,128)(2,1)S(1)}, bf16[32,2432]{1,0:T(8,128)(2,1)S(1)}, u32[]{:S(2)}, u32[]{:S(2)}) collective-permute-start(bf16[32,2432]{1,0:T(8,128)(2,1)S(1)} %pad_maximum_fusion.refs_1_), channel_id=1, source_target_pairs={{0,24},{1,25},{2,26},{3,27},{4,28},{5,29},{6,30},{7,31},{8,16},{9,... | collective-permute-start | bytes 466952 | tf_op jit(solution)/shard_map/ppermute | solution.py:76
  9.2 5.6 %collective-permute-start = (bf16[32,1280]{1,0:T(8,128)(2,1)S(1)}, bf16[32,1280]{1,0:T(8,128)(2,1)S(1)}, u32[]{:S(2)}, u32[]{:S(2)}) collective-permute-start(bf16[32,1280]{1,0:T(8,128)(2,1)S(1)} %slice.47.refs_0_), channel_id=1, source_target_pairs={{0,8},{1,9},{2,10},{3,11},{4,12},{5,13},{6,14},{7,15},{8,0},{9,1},... | collective-permute-start | bytes 245768 | tf_op jit(solution)/shard_map/ppermute | solution.py:76
  14.9 9.3 %collective-permute-start.3 = (bf16[64,1280]{1,0:T(8,128)(2,1)S(1)}, bf16[64,1280]{1,0:T(8,128)(2,1)S(1)}, u32[]{:S(2)}, u32[]{:S(2)}) collective-permute-start(bf16[64,1280]{1,0:T(8,128)(2,1)S(1)} %get-tuple-element.52.refs_0_), channel_id=1, source_target_pairs={{0,24},{1,25},{2,26},{3,27},{4,28},{5,29},{6,30},{7,31},{8,16},{9,... | collective-permute-start | bytes 491528 | tf_op jit(solution)/shard_map/ppermute | solution.py:76
  17.5 6.7 %collective-permute-start.4 = (bf16[64,1280]{1,0:T(8,128)(2,1)S(1)}, bf16[64,1280]{1,0:T(8,128)(2,1)S(1)}, u32[]{:S(2)}, u32[]{:S(2)}) collective-permute-start(bf16[64,1280]{1,0:T(8,128)(2,1)S(1)} %get-tuple-element.53.refs_1_), channel_id=1, source_target_pairs={{0,4},{1,5},{2,6},{3,7},{4,0},{5,1},{6,2},{7,3},{8,12},{9,13},{10,... | collective-permute-start | bytes 491528 | tf_op jit(solution)/shard_map/ppermute | solution.py:76
  19.0 5.1 %collective-permute-start.5 = (bf16[64,1152]{1,0:T(8,128)(2,1)S(1)}, bf16[64,1152]{1,0:T(8,128)(2,1)S(1)}, u32[]{:S(2)}, u32[]{:S(2)}) collective-permute-start(bf16[64,1152]{1,0:T(8,128)(2,1)S(1)} %get-tuple-element.54.refs_2_), channel_id=1, source_target_pairs={{0,2},{1,3},{2,0},{3,1},{4,6},{5,7},{6,4},{7,5},{8,10},{9,11},{10,... | collective-permute-start | bytes 442376 | tf_op jit(solution)/shard_map/ppermute | solution.py:76
  24.2 10.6 %collective-permute-start.8 = (bf16[128,1280]{1,0:T(8,128)(2,1)S(1)}, bf16[128,1280]{1,0:T(8,128)(2,1)S(1)}, u32[]{:S(2)}, u32[]{:S(2)}) collective-permute-start(bf16[128,1280]{1,0:T(8,128)(2,1)S(1)} %get-tuple-element.55.refs_0_), channel_id=1, source_target_pairs={{0,2},{1,3},{2,0},{3,1},{4,6},{5,7},{6,4},{7,5},{8,10},{9,11},{10,... | collective-permute-start | bytes 983048 | tf_op jit(solution)/shard_map/ppermute | solution.py:76
  25.8 9.0 %collective-permute-start.9 = (bf16[128,1280]{1,0:T(8,128)(2,1)S(1)}, bf16[128,1280]{1,0:T(8,128)(2,1)S(1)}, u32[]{:S(2)}, u32[]{:S(2)}) collective-permute-start(bf16[128,1280]{1,0:T(8,128)(2,1)S(1)} %get-tuple-element.56.refs_1_), channel_id=1, source_target_pairs={{0,8},{1,9},{2,10},{3,11},{4,12},{5,13},{6,14},{7,15},{8,0},{9,1},... | collective-permute-start | bytes 983048 | tf_op jit(solution)/shard_map/ppermute | solution.py:76
  27.5 7.3 %collective-permute-start.10 = (bf16[128,1152]{1,0:T(8,128)(2,1)S(1)}, bf16[128,1152]{1,0:T(8,128)(2,1)S(1)}, u32[]{:S(2)}, u32[]{:S(2)}) collective-permute-start(bf16[128,1152]{1,0:T(8,128)(2,1)S(1)} %get-tuple-element.57.refs_2_), channel_id=1, source_target_pairs={{0,4},{1,5},{2,6},{3,7},{4,0},{5,1},{6,2},{7,3},{8,12},{9,13},{10,... | collective-permute-start | bytes 884744 | tf_op jit(solution)/shard_map/ppermute | solution.py:76
  34.9 14.3 %collective-permute-start.11 = (bf16[256,1280]{1,0:T(8,128)(2,1)S(1)}, bf16[256,1280]{1,0:T(8,128)(2,1)S(1)}, u32[]{:S(2)}, u32[]{:S(2)}) collective-permute-start(bf16[256,1280]{1,0:T(8,128)(2,1)S(1)} %get-tuple-element.58.refs_0_), channel_id=1, source_target_pairs={{0,4},{1,5},{2,6},{3,7},{4,0},{5,1},{6,2},{7,3},{8,12},{9,13},{10,... | collective-permute-start | bytes 1966088 | tf_op jit(solution)/shard_map/ppermute | solution.py:76
  36.5 13.8 %collective-permute-start.12 = (bf16[256,1280]{1,0:T(8,128)(2,1)S(1)}, bf16[256,1280]{1,0:T(8,128)(2,1)S(1)}, u32[]{:S(2)}, u32[]{:S(2)}) collective-permute-start(bf16[256,1280]{1,0:T(8,128)(2,1)S(1)} %get-tuple-element.59.refs_1_), channel_id=1, source_target_pairs={{0,2},{1,3},{2,0},{3,1},{4,6},{5,7},{6,4},{7,5},{8,10},{9,11},{10,... | collective-permute-start | bytes 1966088 | tf_op jit(solution)/shard_map/ppermute | solution.py:76
  37.1 12.2 %collective-permute-start.13 = (bf16[256,1152]{1,0:T(8,128)(2,1)S(1)}, bf16[256,1152]{1,0:T(8,128)(2,1)}, u32[]{:S(2)}, u32[]{:S(2)}) collective-permute-start(bf16[256,1152]{1,0:T(8,128)(2,1)S(1)} %get-tuple-element.60.refs_2_), channel_id=1, source_target_pairs={{0,8},{1,9},{2,10},{3,11},{4,12},{5,13},{6,14},{7,15},{8,0},{9,1},... | collective-permute-start | bytes 1769480 | tf_op jit(solution)/shard_map/ppermute | solution.py:76
  50.3 9.6 %copy-start.1 = (bf16[1,512,3584]{2,1,0:T(8,128)(2,1)S(1)}, bf16[1,512,3584]{2,1,0:T(8,128)(2,1)}, u32[]{:S(2)}) copy-start(bf16[1,512,3584]{2,1,0:T(8,128)(2,1)} %param.23) | copy-start | bytes 11010052
  63.4 29.0 %collective-permute-start.14 = (f32[256,1280]{1,0:T(8,128)}, f32[256,1280]{1,0:T(8,128)}, u32[]{:S(2)}, u32[]{:S(2)}) collective-permute-start(f32[256,1280]{1,0:T(8,128)} %get-tuple-element.69), channel_id=1, source_target_pairs={{0,4},{1,5},{2,6},{3,7},{4,0},{5,1},{6,2},{7,3},{8,12},{9,13},{10,... | collective-permute-start | bytes 3932168 | tf_op jit(solution)/shard_map/ppermute | solution.py:76
  63.9 4.0 %copy-start.10 = (s32[1,32,1]{1,2,0:T(1,128)S(1)}, s32[1,32,1]{1,2,0:T(1,128)}, u32[]{:S(2)}) copy-start(s32[1,32,1]{1,2,0:T(1,128)} %param.17) | copy-start | bytes 388
  67.3 34.6 %collective-permute-start.16 = (f32[256,1280]{1,0:T(8,128)}, f32[256,1280]{1,0:T(8,128)}, u32[]{:S(2)}, u32[]{:S(2)}) collective-permute-start(f32[256,1280]{1,0:T(8,128)} %get-tuple-element.72), channel_id=1, source_target_pairs={{0,2},{1,3},{2,0},{3,1},{4,6},{5,7},{6,4},{7,5},{8,10},{9,11},{10,... | collective-permute-start | bytes 3932168 | tf_op jit(solution)/shard_map/ppermute | solution.py:76
  68.0 5.4 %copy-start.7 = (bf16[1,32,4,576]{3,2,1,0:T(4,128)(2,1)S(1)}, bf16[1,32,4,576]{3,2,1,0:T(4,128)(2,1)}, u32[]{:S(2)}) copy-start(bf16[1,32,4,576]{3,2,1,0:T(4,128)(2,1)} %refs_0_.1) | copy-start | bytes 442372
  71.9 24.5 %collective-permute-start.17 = (f32[256,1024]{1,0:T(8,128)}, f32[256,1024]{1,0:T(8,128)}, u32[]{:S(2)}, u32[]{:S(2)}) collective-permute-start(f32[256,1024]{1,0:T(8,128)} %get-tuple-element.73), channel_id=1, source_target_pairs={{0,8},{1,9},{2,10},{3,11},{4,12},{5,13},{6,14},{7,15},{8,0},{9,1},... | collective-permute-start | bytes 3145736 | tf_op jit(solution)/shard_map/ppermute | solution.py:76
  76.5 31.3 %all-to-all-start = ((bf16[32,8,608]{2,1,0:T(8,128)(2,1)}), bf16[32,8,608]{2,1,0:T(8,128)(2,1)}, u32[]{:S(2)}, u32[]{:S(2)}) async-start(bf16[32,8,608]{2,1,0:T(8,128)(2,1)} %fusion.21), calls=%async_computation | async-start | bytes 655360 | tf_op jit(solution)/shard_map/all_to_all | solution.py:422
  82.2 14.2 %copy-start.4 = (f32[256,1024]{1,0:T(8,128)S(1)}, f32[256,1024]{1,0:T(8,128)}, u32[]{:S(2)}) copy-start(f32[256,1024]{1,0:T(8,128)} %copy-done.2) | copy-start | bytes 3145732
  94.7 17.3 %collective-permute-start.15 = (f32[128,1280]{1,0:T(8,128)}, f32[128,1280]{1,0:T(8,128)}, u32[]{:S(2)}, u32[]{:S(2)}) collective-permute-start(f32[128,1280]{1,0:T(8,128)} %get-tuple-element.71), channel_id=1, source_target_pairs={{0,2},{1,3},{2,0},{3,1},{4,6},{5,7},{6,4},{7,5},{8,10},{9,11},{10,... | collective-permute-start | bytes 1966088 | tf_op jit(solution)/shard_map/ppermute | solution.py:76
  104.2 15.5 %collective-permute-start.19 = (f32[128,1280]{1,0:T(8,128)}, f32[128,1280]{1,0:T(8,128)}, u32[]{:S(2)}, u32[]{:S(2)}) collective-permute-start(f32[128,1280]{1,0:T(8,128)} %get-tuple-element.78), channel_id=1, source_target_pairs={{0,8},{1,9},{2,10},{3,11},{4,12},{5,13},{6,14},{7,15},{8,0},{9,1},... | collective-permute-start | bytes 1966088 | tf_op jit(solution)/shard_map/ppermute | solution.py:76
  106.2 10.9 %collective-permute-start.20 = (f32[128,1024]{1,0:T(8,128)}, f32[128,1024]{1,0:T(8,128)S(1)}, u32[]{:S(2)}, u32[]{:S(2)}) collective-permute-start(f32[128,1024]{1,0:T(8,128)} %get-tuple-element.79), channel_id=1, source_target_pairs={{0,4},{1,5},{2,6},{3,7},{4,0},{5,1},{6,2},{7,3},{8,12},{9,13},{10,... | collective-permute-start | bytes 1572872 | tf_op jit(solution)/shard_map/ppermute | solution.py:76
  113.2 11.1 %collective-permute-start.18 = (f32[64,1280]{1,0:T(8,128)S(1)}, f32[64,1280]{1,0:T(8,128)S(1)}, u32[]{:S(2)}, u32[]{:S(2)}) collective-permute-start(f32[64,1280]{1,0:T(8,128)S(1)} %get-tuple-element.77), channel_id=1, source_target_pairs={{0,24},{1,25},{2,26},{3,27},{4,28},{5,29},{6,30},{7,31},{8,16},{9,... | collective-permute-start | bytes 983048 | tf_op jit(solution)/shard_map/ppermute | solution.py:76
  119.0 6.4 %collective-permute-start.22 = (f32[64,1024]{1,0:T(8,128)S(1)}, f32[64,1024]{1,0:T(8,128)S(1)}, u32[]{:S(2)}, u32[]{:S(2)}) collective-permute-start(f32[64,1024]{1,0:T(8,128)S(1)} %get-tuple-element.84), channel_id=1, source_target_pairs={{0,2},{1,3},{2,0},{3,1},{4,6},{5,7},{6,4},{7,5},{8,10},{9,11},{10,... | collective-permute-start | bytes 786440 | tf_op jit(solution)/shard_map/ppermute | solution.py:76
  120.8 7.1 %collective-permute-start.21 = (f32[64,1280]{1,0:T(8,128)S(1)}, f32[64,1280]{1,0:T(8,128)S(1)}, u32[]{:S(2)}, u32[]{:S(2)}) collective-permute-start(f32[64,1280]{1,0:T(8,128)S(1)} %get-tuple-element.83), channel_id=1, source_target_pairs={{0,4},{1,5},{2,6},{3,7},{4,0},{5,1},{6,2},{7,3},{8,12},{9,13},{10,... | collective-permute-start | bytes 983048 | tf_op jit(solution)/shard_map/ppermute | solution.py:76
  128.0 8.9 %collective-permute-start.24 = (f32[32,1280]{1,0:T(8,128)S(1)}, f32[32,1280]{1,0:T(8,128)S(1)}, u32[]{:S(2)}, u32[]{:S(2)}) collective-permute-start(f32[32,1280]{1,0:T(8,128)S(1)} %get-tuple-element.88), channel_id=1, source_target_pairs={{0,24},{1,25},{2,26},{3,27},{4,28},{5,29},{6,30},{7,31},{8,16},{9,... | collective-permute-start | bytes 491528 | tf_op jit(solution)/shard_map/ppermute | solution.py:76
  129.8 7.0 %collective-permute-start.25 = (f32[32,1024]{1,0:T(8,128)S(1)}, f32[32,1024]{1,0:T(8,128)S(1)}, u32[]{:S(2)}, u32[]{:S(2)}) collective-permute-start(f32[32,1024]{1,0:T(8,128)S(1)} %get-tuple-element.89), channel_id=1, source_target_pairs={{0,24},{1,25},{2,26},{3,27},{4,28},{5,29},{6,30},{7,31},{8,16},{9,... | collective-permute-start | bytes 393224 | tf_op jit(solution)/shard_map/ppermute | solution.py:76
  131.8 8.2 %collective-permute-start.23 = (f32[32,1280]{1,0:T(8,128)S(1)}, f32[32,1280]{1,0:T(8,128)S(1)}, u32[]{:S(2)}, u32[]{:S(2)}) collective-permute-start(f32[32,1280]{1,0:T(8,128)S(1)} %get-tuple-element.87), channel_id=1, source_target_pairs={{0,8},{1,9},{2,10},{3,11},{4,12},{5,13},{6,14},{7,15},{8,0},{9,1},... | collective-permute-start | bytes 491528 | tf_op jit(solution)/shard_map/ppermute | solution.py:76
  (6 other events, 10.7 us)

commit v12 on v11

--- a/solution.py
+++ b/solution.py
@@ -266,35 +266,32 @@
     )(chip, *pieces, *weights, *so_far)
 
 
-def output_kernel(unit, order, tiles, scale_ref, hidden_ref, *refs):
-    down, down_other = refs[:tiles], refs[tiles : 2 * tiles]
-    keep_ref, send_ref = refs[-2:]
+def output_kernel(unit, order, first, tiles, scale_ref, hidden_ref, *refs):
+    down, down_other, out_ref = refs[:tiles], refs[tiles : 2 * tiles], refs[-1]
     units, tile = down[0].shape
-    places = hidden_ref.shape[0] // unit
-    for out_ref, first in ((send_ref, places // 2), (keep_ref, 0)):
-        slots = [slot_of(first + at, order) for at in range(places // 2)]
-        rows = [slice(slot * unit, (slot + 1) * unit) for slot in slots]
-        hidden = jnp.concatenate([hidden_ref[row] for row in rows], axis=0)
-        scale = jnp.concatenate([scale_ref[row] for row in rows], axis=0)
-        for at in range(tiles):
-            out = jnp.dot(hidden[:, :units], down[at][...], preferred_element_type=jnp.float32)
-            out += jnp.dot(hidden[:, units:], down_other[at][...], preferred_element_type=jnp.float32)
-            out_ref[:, at * tile : (at + 1) * tile] = out * scale
-
-
-def expert_output(unit, order, columns, scale, hidden, down, down_other, after):
+    slots = [slot_of(first + at, order) for at in range(out_ref.shape[0] // unit)]
+    rows = [slice(slot * unit, (slot + 1) * unit) for slot in slots]
+    hidden = jnp.concatenate([hidden_ref[row] for row in rows], axis=0)
+    scale = jnp.concatenate([scale_ref[row] for row in rows], axis=0)
+    for at in range(tiles):
+        out = jnp.dot(hidden[:, :units], down[at][...], preferred_element_type=jnp.float32)
+        out += jnp.dot(hidden[:, units:], down_other[at][...], preferred_element_type=jnp.float32)
+        out_ref[:, at * tile : (at + 1) * tile] = out * scale
+
+
+def expert_output(unit, order, send, columns, scale, hidden, down, down_other, after):
     units = down.shape[0]
     start, stop = columns
     count = hidden.shape[0]
     tile = 256
     tiles = (stop - start) // tile
-    half = jax.ShapeDtypeStruct((count // 2, stop - start), jnp.float32)
+    first = count // unit // 2 if send else 0
 
     def tile_at(at):
         return pl.BlockSpec((units, tile), lambda i: (0, start // tile + at))
 
     return pl.pallas_call(
-        functools.partial(output_kernel, unit, order, tiles),
+        functools.partial(output_kernel, unit, order, first, tiles),
         grid=(1,),
         in_specs=[
             pl.BlockSpec((count, 1), lambda i: (0, 0)),
@@ -302,11 +299,11 @@
         ]
         + [tile_at(at) for at in range(tiles)] * 2
         + [pl.BlockSpec(memory_space=pl.ANY)] * len(after),
-        out_specs=[pl.BlockSpec((count // 2, stop - start), lambda i: (0, 0))] * 2,
-        out_shape=[half] * 2,
+        out_specs=pl.BlockSpec((count // 2, stop - start), lambda i: (0, 0)),
+        out_shape=jax.ShapeDtypeStruct((count // 2, stop - start), jnp.float32),
         compiler_params=pltpu.CompilerParams(vmem_limit_bytes=24 * MIB),
         cost_estimate=pl.CostEstimate(
-            flops=4 * count * (stop - start) * units,
+            flops=2 * count * (stop - start) * units,
             bytes_accessed=4 * (stop - start) * units + 4 * count * (stop - start + units),
             transcendentals=0,
         ),
@@ -339,12 +336,17 @@
 
 
 def cube_outputs(unit, hidden, scale, down, down_other):
-    keep, coming = [], []
-    for order, columns in zip(ORDERS, piece_columns(down.shape[1])):
-        after = keep[-1:]
-        mine, send = expert_output(unit, order, columns, scale, hidden, down, down_other, after)
-        keep.append(mine)
+    columns = piece_columns(down.shape[1])
+    arrays = (scale, hidden, down, down_other)
+    keep, coming, after = {}, [], ()
+    for order, piece in zip(ORDERS, columns):
+        send = expert_output(unit, order, True, piece, *arrays, after)
         coming.append(across(send, order[0]))
+        after = (send,)
+    for at in TURNS:
+        keep[at] = expert_output(unit, ORDERS[at], False, columns[at], *arrays, after)
+        after = (keep[at],)
+    keep = [keep[at] for at in range(len(ORDERS))]
     return keep, coming
 
 
@@ -394,7 +396,7 @@
         chip = (lax.axis_index("ep") // 2).astype(jnp.int32).reshape(1)
         (hidden, scale), others = gather_cube(tok_rows, chip, tokens, parts, *weights)
         keep, coming = cube_outputs(tok_rows, hidden, scale, weights[2], others[2])
-        prefill_latent = hold_back(prefill_latent, keep[-1])
+        prefill_latent = hold_back(prefill_latent, keep[TURNS[-1]])
 
     owner = block_owner.reshape(blocks)
     same = owner[:, None] == owner[None, :]

time: 142 us -> 145 us (1.021)
  waiting for transfers between devices: 41.6 us -> 32.3 us
  Pallas kernels: 39.7 us -> 48.2 us
  starting transfers between devices: 43.3 us -> 50 us
  local copies, waits for them, and re-layouts: 8.86 us -> 6.98 us
    ppermute x23, waiting for transfers between devices: 41.6 us -> 32.3 us  [across(): lax.ppermute(value, 'ep', [(i, i ^ 2 * LINKS[link]) for i in range(peers)])]
    ppermute x23, starting transfers between devices: 36.5 us -> 43.5 us  [across(): lax.ppermute(value, 'ep', [(i, i ^ 2 * LINKS[link]) for i in range(peers)])]
    pallas_call x3 -> x6, Pallas kernels: 9.83 us -> 16.1 us  [expert_output(): pl.pallas_call(functools.partial(output_kernel, unit, order, first, tiles...]
  transfers between devices with their start and end apart: 27 -> 27, of which waited for: 14 -> 11; matrix products, arithmetic and copies ran while one was open for 8% -> 6% of each run, Pallas kernels for 18% -> 23%
where the time goes in v12:
time: 145 us; the launch traced here: 144 us
  starting transfers between devices  50 us (34%)
  Pallas kernels  48.2 us (33%)
  waiting for transfers between devices  32.3 us (22%)
  local copies, waits for them, and re-layouts  6.98 us (5%)
  matrix products  2.62 us (2%)
  other arithmetic  2.35 us (2%)
  between operations  1.55 us (1%)
    ppermute x23, starting transfers between devices, across(): lax.ppermute(value, 'ep', [(i, i ^ 2 * LINKS[link]) for i in range(peers)])  43.5 us
    ppermute x23, waiting for transfers between devices, across(): lax.ppermute(value, 'ep', [(i, i ^ 2 * LINKS[link]) for i in range(peers)])  32.3 us
    pallas_call x2, Pallas kernels, expert_part(): pl.pallas_call(functools.partial(part_kernel, unit, last), grid=(2 * step...  21 us
    pallas_call x6, Pallas kernels, expert_output(): pl.pallas_call(functools.partial(output_kernel, unit, order, first, tiles...  16.1 us
    pallas_call x14, Pallas kernels, whole_call(): pl.pallas_call(body, in_specs=[pl.BlockSpec(memory_space=pltpu.VMEM)] * g...  11.1 us
    all_to_all x1, starting transfers between devices, per_device(): lax.all_to_all(leaving, 'ep', split_axis=0, concat_axis=0, tiled=True)  5.51 us
    unnamed x22, local copies, waits for them, and re-layouts  3.16 us
  transfers between devices with their start and end apart: 27, of which 11 were waited for; matrix products, arithmetic and copies ran while one was open for 6% of the time, Pallas kernels for 23%

profile of v12, /device:TPU:0, one launch (start us, length us, event | category | flops | bytes accessed | tf_op | source)
XLA Modules:
  0.0 144.0 jit_solution(17201387597253011088)
XLA Ops:
  3.6 4.7 %collective-permute-start.1 = (bf16[32,2432]{1,0:T(8,128)(2,1)S(1)}, bf16[32,2432]{1,0:T(8,128)(2,1)S(1)}, u32[]{:S(2)}, u32[]{:S(2)}) collective-permute-start(bf16[32,2432]{1,0:T(8,128)(2,1)S(1)} %pad_maximum_fusion.refs_1_), channel_id=1, source_target_pairs={{0,24},{1,25},{2,26},{3,27},{4,28},{5,29},{6,30},{7,31},{8,16},{9,... | collective-permute-start | bytes 466952 | tf_op jit(solution)/shard_map/ppermute | solution.py:76
  9.2 5.6 %collective-permute-done.refs_2_ = bf16[32,1280]{1,0:T(8,128)(2,1)S(1)} collective-permute-done((bf16[32,1280]{1,0:T(8,128)(2,1)S(1)}, bf16[32,1280]{1,0:T(8,128)(2,1)S(1)}, u32[]{:S(2)}, u32[]{:S(2)}) %collective-permute-start) | collective-permute-done | bytes 81952 | tf_op jit(solution)/shard_map/ppermute | solution.py:76
  14.9 2.6 %collective-permute-start.3 = (bf16[64,1280]{1,0:T(8,128)(2,1)S(1)}, bf16[64,1280]{1,0:T(8,128)(2,1)S(1)}, u32[]{:S(2)}, u32[]{:S(2)}) collective-permute-start(bf16[64,1280]{1,0:T(8,128)(2,1)S(1)} %get-tuple-element.46.refs_0_), channel_id=1, source_target_pairs={{0,24},{1,25},{2,26},{3,27},{4,28},{5,29},{6,30},{7,31},{8,16},{9,... | collective-permute-start | bytes 491528 | tf_op jit(solution)/shard_map/ppermute | solution.py:76
  20.5 3.6 %collective-permute-done.5.refs_5_ = bf16[64,1152]{1,0:T(8,128)(2,1)S(1)} collective-permute-done((bf16[64,1152]{1,0:T(8,128)(2,1)S(1)}, bf16[64,1152]{1,0:T(8,128)(2,1)S(1)}, u32[]{:S(2)}, u32[]{:S(2)}) %collective-permute-start.5) | collective-permute-done | bytes 147488 | tf_op jit(solution)/shard_map/ppermute | solution.py:76
  24.2 1.6 %collective-permute-start.8 = (bf16[128,1280]{1,0:T(8,128)(2,1)S(1)}, bf16[128,1280]{1,0:T(8,128)(2,1)S(1)}, u32[]{:S(2)}, u32[]{:S(2)}) collective-permute-start(bf16[128,1280]{1,0:T(8,128)(2,1)S(1)} %get-tuple-element.49.refs_0_), channel_id=1, source_target_pairs={{0,2},{1,3},{2,0},{3,1},{4,6},{5,7},{6,4},{7,5},{8,10},{9,11},{10,... | collective-permute-start | bytes 983048 | tf_op jit(solution)/shard_map/ppermute | solution.py:76
  25.8 1.7 %collective-permute-start.9 = (bf16[128,1280]{1,0:T(8,128)(2,1)S(1)}, bf16[128,1280]{1,0:T(8,128)(2,1)S(1)}, u32[]{:S(2)}, u32[]{:S(2)}) collective-permute-start(bf16[128,1280]{1,0:T(8,128)(2,1)S(1)} %get-tuple-element.50.refs_1_), channel_id=1, source_target_pairs={{0,8},{1,9},{2,10},{3,11},{4,12},{5,13},{6,14},{7,15},{8,0},{9,1},... | collective-permute-start | bytes 983048 | tf_op jit(solution)/shard_map/ppermute | solution.py:76
  27.5 1.5 %collective-permute-start.10 = (bf16[128,1152]{1,0:T(8,128)(2,1)S(1)}, bf16[128,1152]{1,0:T(8,128)(2,1)S(1)}, u32[]{:S(2)}, u32[]{:S(2)}) collective-permute-start(bf16[128,1152]{1,0:T(8,128)(2,1)S(1)} %get-tuple-element.51.refs_2_), channel_id=1, source_target_pairs={{0,4},{1,5},{2,6},{3,7},{4,0},{5,1},{6,2},{7,3},{8,12},{9,13},{10,... | collective-permute-start | bytes 884744 | tf_op jit(solution)/shard_map/ppermute | solution.py:76
  29.1 5.7 %collective-permute-done.10.refs_5_ = bf16[128,1152]{1,0:T(8,128)(2,1)S(1)} collective-permute-done((bf16[128,1152]{1,0:T(8,128)(2,1)S(1)}, bf16[128,1152]{1,0:T(8,128)(2,1)S(1)}, u32[]{:S(2)}, u32[]{:S(2)}) %collective-permute-start.10) | collective-permute-done | bytes 294944 | tf_op jit(solution)/shard_map/ppermute | solution.py:76
  35.8 1.5 %collective-permute-start.11 = (bf16[256,1280]{1,0:T(8,128)(2,1)S(1)}, bf16[256,1280]{1,0:T(8,128)(2,1)S(1)}, u32[]{:S(2)}, u32[]{:S(2)}) collective-permute-start(bf16[256,1280]{1,0:T(8,128)(2,1)S(1)} %get-tuple-element.52.refs_0_), channel_id=1, source_target_pairs={{0,4},{1,5},{2,6},{3,7},{4,0},{5,1},{6,2},{7,3},{8,12},{9,13},{10,... | collective-permute-start | bytes 1966088 | tf_op jit(solution)/shard_map/ppermute | solution.py:76
  39.0 11.4 %expert_part.2 = (f32[512,1024]{1,0:T(8,128)S(1)}, f32[512,1024]{1,0:T(8,128)}, f32[512,1]{1,0:T(8,128)S(1)}) custom-call(s32[1]{0:T(128)} %bitcast.2.chip_ref, bf16[256,1280]{1,0:T(8,128)(2,1)S(1)} %get-tuple-element.52.refs_0_, bf16[256,1280]{1,0:T(8,128)(2,1)S(1)} %get-tuple-element.53.refs_1_, bf16[256,1152]{1,0:T(8,128)(2,1)} %get-tuple-element.54.refs_2_, ...), custom_call_target="tpu_custom_call" | custom-call | flops 3758096384 | bytes 19660800 | tf_op jit(solution)/shard_map/expert_part/pallas_call | solution.py:249
  51.1 9.6 %expert_part.3 = (bf16[512,1024]{1,0:T(8,128)(2,1)S(1)}, f32[512,1]{1,0:T(8,128)S(1)}) custom-call(s32[1]{0:T(128)} %bitcast.2.chip_ref, bf16[256,1280]{1,0:T(8,128)(2,1)S(1)} %collective-permute-done.11.refs_0_, bf16[256,1280]{1,0:T(8,128)(2,1)S(1)} %collective-permute-done.12.refs_1_, bf16[256,1152]{1,0:T(8,128)(2,1)} %collective-permute-done.13.refs_2_, ...), custom_call_target="tpu_custom_call" | custom-call | flops 3758096384 | bytes 19660800 | tf_op jit(solution)/shard_map/expert_part/pallas_call | solution.py:249
  60.7 3.3 %expert_output.6.refs_10_ = f32[256,1280]{1,0:T(8,128)} custom-call(f32[512,1]{1,0:T(8,128)S(1)} %get-tuple-element.58.scale_ref, bf16[512,1024]{1,0:T(8,128)(2,1)S(1)} %get-tuple-element.59.hidden_ref, bf16[512,3584]{1,0:T(8,128)(2,1)S(1)} %bitcast.20, bf16[512,3584]{1,0:T(8,128)(2,1)S(1)} %bitcast.21, bf16[512,3584]{1,0:T(8,128)(2,1)S(1)} %bitcast.22, ...), custom_call_target="tpu_custom_call" | custom-call | flops 671088640 | bytes 6291456 | tf_op jit(solution)/shard_map/expert_output/pallas_call | solution.py:293
  64.5 3.3 %expert_output.7.refs_8_ = f32[256,1280]{1,0:T(8,128)} custom-call(f32[512,1]{1,0:T(8,128)S(1)} %get-tuple-element.58.scale_ref, bf16[512,1024]{1,0:T(8,128)(2,1)S(1)} %get-tuple-element.59.hidden_ref, bf16[512,3584]{1,0:T(8,128)(2,1)S(1)} %bitcast.25, bf16[512,3584]{1,0:T(8,128)(2,1)S(1)} %bitcast.26, bf16[512,3584]{1,0:T(8,128)(2,1)S(1)} %bitcast.27, ...), custom_call_target="tpu_custom_call" | custom-call | flops 671088640 | bytes 6291456 | tf_op jit(solution)/shard_map/expert_output/pallas_call | solution.py:293
  68.6 2.9 %expert_output.8.refs_10_ = f32[256,1024]{1,0:T(8,128)} custom-call(f32[512,1]{1,0:T(8,128)S(1)} %get-tuple-element.58.scale_ref, bf16[512,1024]{1,0:T(8,128)(2,1)S(1)} %get-tuple-element.59.hidden_ref, bf16[512,3584]{1,0:T(8,128)(2,1)S(1)} %bitcast.33, bf16[512,3584]{1,0:T(8,128)(2,1)S(1)} %bitcast.31, bf16[512,3584]{1,0:T(8,128)(2,1)S(1)} %bitcast.32, ...), custom_call_target="tpu_custom_call" | custom-call | flops 536870912 | bytes 5242880 | tf_op jit(solution)/shard_map/expert_output/pallas_call | solution.py:293
  72.8 2.0 %copy-done.2 = bf16[1,512,3584]{2,1,0:T(8,128)(2,1)S(1)} copy-done((bf16[1,512,3584]{2,1,0:T(8,128)(2,1)S(1)}, bf16[1,512,3584]{2,1,0:T(8,128)(2,1)}, u32[]{:S(2)}) %copy-start.2) | copy-done | bytes 3670040
  74.8 2.2 %expert_output.9.refs_8_.refs_0_ = f32[256,1280]{1,0:T(8,128)S(1)} custom-call(f32[512,1]{1,0:T(8,128)S(1)} %get-tuple-element.58.scale_ref, bf16[512,1024]{1,0:T(8,128)(2,1)S(1)} %get-tuple-element.59.hidden_ref, bf16[512,3584]{1,0:T(8,128)(2,1)S(1)} %bitcast.34, bf16[512,3584]{1,0:T(8,128)(2,1)S(1)} %bitcast.35, bf16[512,3584]{1,0:T(8,128)(2,1)S(1)} %bitcast.36, ...), custom_call_target="tpu_custom_call" | custom-call | flops 671088640 | bytes 6291456 | tf_op jit(solution)/shard_map/expert_output/pallas_call | solution.py:293
  77.0 1.9 %expert_output.10.refs_10_.refs_0_ = f32[256,1024]{1,0:T(8,128)S(1)} custom-call(f32[512,1]{1,0:T(8,128)S(1)} %get-tuple-element.58.scale_ref, bf16[512,1024]{1,0:T(8,128)(2,1)S(1)} %get-tuple-element.59.hidden_ref, bf16[512,3584]{1,0:T(8,128)(2,1)S(1)} %bitcast.39, bf16[512,3584]{1,0:T(8,128)(2,1)S(1)} %bitcast.40, bf16[512,3584]{1,0:T(8,128)(2,1)S(1)} %bitcast.41, ...), custom_call_target="tpu_custom_call" | custom-call | flops 536870912 | bytes 5242880 | tf_op jit(solution)/shard_map/expert_output/pallas_call | solution.py:293
  79.0 2.5 %expert_output.11.refs_1_.refs_0_ = f32[256,1280]{1,0:T(8,128)S(1)} custom-call(f32[512,1]{1,0:T(8,128)S(1)} %get-tuple-element.58.scale_ref, bf16[512,1024]{1,0:T(8,128)(2,1)S(1)} %get-tuple-element.59.hidden_ref, bf16[512,3584]{1,0:T(8,128)(2,1)S(1)} %bitcast.43, bf16[512,3584]{1,0:T(8,128)(2,1)S(1)} %bitcast.44, bf16[512,3584]{1,0:T(8,128)(2,1)S(1)} %bitcast.45, ...), custom_call_target="tpu_custom_call" | custom-call | flops 671088640 | bytes 6291456 | tf_op jit(solution)/shard_map/expert_output/pallas_call | solution.py:293
  84.4 5.5 %all-to-all-start = ((bf16[32,8,608]{2,1,0:T(8,128)(2,1)}), bf16[32,8,608]{2,1,0:T(8,128)(2,1)S(1)}, u32[]{:S(2)}, u32[]{:S(2)}) async-start(bf16[32,8,608]{2,1,0:T(8,128)(2,1)} %fusion.21), calls=%async_computation | async-start | bytes 655360 | tf_op jit(solution)/shard_map/all_to_all | solution.py:424
  91.3 2.4 %halved.9 = (f32[128,1280]{1,0:T(8,128)S(1)}, f32[128,1280]{1,0:T(8,128)}) custom-call(f32[256,1280]{1,0:T(8,128)S(1)} %expert_output.9.refs_8_.refs_0_, f32[256,1280]{1,0:T(8,128)} %collective-permute-done.14.refs_1_), custom_call_target="tpu_custom_call" | custom-call | bytes 3932160 | tf_op jit(solution)/shard_map/halved/pallas_call | solution.py:107
  95.1 2.1 %halved.10 = (f32[128,1024]{1,0:T(8,128)S(1)}, f32[128,1024]{1,0:T(8,128)}) custom-call(f32[256,1024]{1,0:T(8,128)S(1)} %copy-done.6, f32[256,1024]{1,0:T(8,128)} %collective-permute-done.17.refs_1_, f32[128,1280]{1,0:T(8,128)S(1)} %get-tuple-element.60.refs_2_.refs_0_), custom_call_target="tpu_custom_call" | custom-call | bytes 3145728 | tf_op jit(solution)/shard_map/halved/pallas_call | solution.py:107
  97.9 2.3 %halved.11 = (f32[128,1280]{1,0:T(8,128)S(1)}, f32[128,1280]{1,0:T(8,128)}) custom-call(f32[256,1280]{1,0:T(8,128)S(1)} %copy-done.4, f32[256,1280]{1,0:T(8,128)} %collective-permute-done.16.refs_1_, f32[128,1024]{1,0:T(8,128)S(1)} %get-tuple-element.62.refs_2_.refs_0_), custom_call_target="tpu_custom_call" | custom-call | bytes 3932160 | tf_op jit(solution)/shard_map/halved/pallas_call | solution.py:107
  102.0 1.5 %collective-permute-start.20 = (f32[128,1024]{1,0:T(8,128)}, f32[128,1024]{1,0:T(8,128)}, u32[]{:S(2)}, u32[]{:S(2)}) collective-permute-start(f32[128,1024]{1,0:T(8,128)} %get-tuple-element.67), channel_id=1, source_target_pairs={{0,4},{1,5},{2,6},{3,7},{4,0},{5,1},{6,2},{7,3},{8,12},{9,13},{10,... | collective-permute-start | bytes 1572872 | tf_op jit(solution)/shard_map/ppermute | solution.py:76
  104.9 7.5 %collective-permute-done.15.refs_1_ = f32[128,1280]{1,0:T(8,128)} collective-permute-done((f32[128,1280]{1,0:T(8,128)}, f32[128,1280]{1,0:T(8,128)}, u32[]{:S(2)}, u32[]{:S(2)}) %collective-permute-start.15) | collective-permute-done | bytes 655392 | tf_op jit(solution)/shard_map/ppermute | solution.py:76
  113.6 4.0 %collective-permute-start.18 = (f32[64,1280]{1,0:T(8,128)S(1)}, f32[64,1280]{1,0:T(8,128)S(1)}, u32[]{:S(2)}, u32[]{:S(2)}) collective-permute-start(f32[64,1280]{1,0:T(8,128)S(1)} %get-tuple-element.65), channel_id=1, source_target_pairs={{0,24},{1,25},{2,26},{3,27},{4,28},{5,29},{6,30},{7,31},{8,16},{9,... | collective-permute-start | bytes 983048 | tf_op jit(solution)/shard_map/ppermute | solution.py:76
  119.6 1.6 %collective-permute-start.21 = (f32[64,1280]{1,0:T(8,128)S(1)}, f32[64,1280]{1,0:T(8,128)S(1)}, u32[]{:S(2)}, u32[]{:S(2)}) collective-permute-start(f32[64,1280]{1,0:T(8,128)S(1)} %get-tuple-element.71), channel_id=1, source_target_pairs={{0,4},{1,5},{2,6},{3,7},{4,0},{5,1},{6,2},{7,3},{8,12},{9,13},{10,... | collective-permute-start | bytes 983048 | tf_op jit(solution)/shard_map/ppermute | solution.py:76
  122.2 1.9 %collective-permute-done.18.refs_1_ = f32[64,1280]{1,0:T(8,128)S(1)} collective-permute-done((f32[64,1280]{1,0:T(8,128)S(1)}, f32[64,1280]{1,0:T(8,128)S(1)}, u32[]{:S(2)}, u32[]{:S(2)}) %collective-permute-start.18) | collective-permute-done | bytes 327712 | tf_op jit(solution)/shard_map/ppermute | solution.py:76
  125.2 2.3 %collective-permute-done.21.refs_1_ = f32[64,1280]{1,0:T(8,128)S(1)} collective-permute-done((f32[64,1280]{1,0:T(8,128)S(1)}, f32[64,1280]{1,0:T(8,128)S(1)}, u32[]{:S(2)}, u32[]{:S(2)}) %collective-permute-start.21) | collective-permute-done | bytes 327712 | tf_op jit(solution)/shard_map/ppermute | solution.py:76
  128.4 3.0 %collective-permute-start.25 = (f32[32,1024]{1,0:T(8,128)S(1)}, f32[32,1024]{1,0:T(8,128)S(1)}, u32[]{:S(2)}, u32[]{:S(2)}) collective-permute-start(f32[32,1024]{1,0:T(8,128)S(1)} %get-tuple-element.77), channel_id=1, source_target_pairs={{0,24},{1,25},{2,26},{3,27},{4,28},{5,29},{6,30},{7,31},{8,16},{9,... | collective-permute-start | bytes 393224 | tf_op jit(solution)/shard_map/ppermute | solution.py:76
  131.4 8.5 %collective-permute-start.23 = (f32[32,1280]{1,0:T(8,128)S(1)}, f32[32,1280]{1,0:T(8,128)S(1)}, u32[]{:S(2)}, u32[]{:S(2)}) collective-permute-start(f32[32,1280]{1,0:T(8,128)S(1)} %get-tuple-element.75), channel_id=1, source_target_pairs={{0,8},{1,9},{2,10},{3,11},{4,12},{5,13},{6,14},{7,15},{8,0},{9,1},... | collective-permute-start | bytes 491528 | tf_op jit(solution)/shard_map/ppermute | solution.py:76
  139.9 1.5 %fusion.14 = bf16[1,128,512]{2,1,0:T(8,128)(2,1)} fusion(bf16[256,576]{0,1:T(8,128)(2,1)S(1)} %copy-done.8, bf16[1024,576]{0,1:T(8,128)(2,1)S(1)} %bitcast.55, f32[1280,128]{1,0:T(8,128)S(1)} %get-tuple-element.82, f32[128]{0:T(128)S(1)} %get-tuple-element.81, pred[1280]{0:T(1024)(128)(4,1)S(1)} %pad_add_fusion, f32[128]{0:T(128)S(1)} %fusion.18), kind=kOutput, calls=%fused_computation.12 | convolution fusion | flops 171016192 | bytes 2263296 | tf_op jit(solution)/shard_map/dot_general | solution.py:38
  141.5 1.8 %collective-permute-done.23.refs_3_ = f32[32,1280]{1,0:T(8,128)S(1)} collective-permute-done((f32[32,1280]{1,0:T(8,128)S(1)}, f32[32,1280]{1,0:T(8,128)S(1)}, u32[]{:S(2)}, u32[]{:S(2)}) %collective-permute-start.23) | collective-permute-done | bytes 163872 | tf_op jit(solution)/shard_map/ppermute | solution.py:76
  (94 shorter events, 28.7 us)
Async XLA Ops:
  0.6 120.5 %copy-start = (bf16[1,128,576]{1,2,0:T(8,128)(2,1)S(1)}, bf16[1,128,576]{1,2,0:T(8,128)(2,1)}, u32[]{:S(2)}) copy-start(bf16[1,128,576]{1,2,0:T(8,128)(2,1)} %param.13) | copy-start | bytes 442372
  0.6 14.2 %collective-permute-start.2 = (bf16[512,3584]{1,0:T(8,128)(2,1)}, bf16[512,3584]{1,0:T(8,128)(2,1)}, u32[]{:S(2)}, u32[]{:S(2)}) collective-permute-start(bf16[512,3584]{1,0:T(8,128)(2,1)} %bitcast.19), channel_id=1, source_target_pairs={{0,1},{1,0},{2,3},{3,2},{4,5},{5,4},{6,7},{7,6},{8,9},{9,8},{10,11... | collective-permute-start | bytes 11010056 | tf_op jit(solution)/shard_map/ppermute | solution.py:80
  1.2 19.3 %collective-permute-start.6 = (bf16[3584,512]{1,0:T(8,128)(2,1)}, bf16[3584,512]{1,0:T(8,128)(2,1)}, u32[]{:S(2)}, u32[]{:S(2)}) collective-permute-start(bf16[3584,512]{1,0:T(8,128)(2,1)} %bitcast.48), channel_id=1, source_target_pairs={{0,1},{1,0},{2,3},{3,2},{4,5},{5,4},{6,7},{7,6},{8,9},{9,8},{10,11... | collective-permute-start | bytes 11010056 | tf_op jit(solution)/shard_map/ppermute | solution.py:80
  1.2 19.3 %collective-permute-start.7 = (bf16[3584,512]{1,0:T(8,128)(2,1)}, bf16[3584,512]{1,0:T(8,128)(2,1)}, u32[]{:S(2)}, u32[]{:S(2)}) collective-permute-start(bf16[3584,512]{1,0:T(8,128)(2,1)} %bitcast.51), channel_id=1, source_target_pairs={{0,1},{1,0},{2,3},{3,2},{4,5},{5,4},{6,7},{7,6},{8,9},{9,8},{10,11... | collective-permute-start | bytes 11010056 | tf_op jit(solution)/shard_map/ppermute | solution.py:80
  3.6 11.2 %collective-permute-start.1 = (bf16[32,2432]{1,0:T(8,128)(2,1)S(1)}, bf16[32,2432]{1,0:T(8,128)(2,1)S(1)}, u32[]{:S(2)}, u32[]{:S(2)}) collective-permute-start(bf16[32,2432]{1,0:T(8,128)(2,1)S(1)} %pad_maximum_fusion.refs_1_), channel_id=1, source_target_pairs={{0,24},{1,25},{2,26},{3,27},{4,28},{5,29},{6,30},{7,31},{8,16},{9,... | collective-permute-start | bytes 466952 | tf_op jit(solution)/shard_map/ppermute | solution.py:76
  9.2 5.6 %collective-permute-start = (bf16[32,1280]{1,0:T(8,128)(2,1)S(1)}, bf16[32,1280]{1,0:T(8,128)(2,1)S(1)}, u32[]{:S(2)}, u32[]{:S(2)}) collective-permute-start(bf16[32,1280]{1,0:T(8,128)(2,1)S(1)} %slice.47.refs_0_), channel_id=1, source_target_pairs={{0,8},{1,9},{2,10},{3,11},{4,12},{5,13},{6,14},{7,15},{8,0},{9,1},... | collective-permute-start | bytes 245768 | tf_op jit(solution)/shard_map/ppermute | solution.py:76
  14.9 9.3 %collective-permute-start.3 = (bf16[64,1280]{1,0:T(8,128)(2,1)S(1)}, bf16[64,1280]{1,0:T(8,128)(2,1)S(1)}, u32[]{:S(2)}, u32[]{:S(2)}) collective-permute-start(bf16[64,1280]{1,0:T(8,128)(2,1)S(1)} %get-tuple-element.46.refs_0_), channel_id=1, source_target_pairs={{0,24},{1,25},{2,26},{3,27},{4,28},{5,29},{6,30},{7,31},{8,16},{9,... | collective-permute-start | bytes 491528 | tf_op jit(solution)/shard_map/ppermute | solution.py:76
  17.5 6.7 %collective-permute-start.4 = (bf16[64,1280]{1,0:T(8,128)(2,1)S(1)}, bf16[64,1280]{1,0:T(8,128)(2,1)S(1)}, u32[]{:S(2)}, u32[]{:S(2)}) collective-permute-start(bf16[64,1280]{1,0:T(8,128)(2,1)S(1)} %get-tuple-element.47.refs_1_), channel_id=1, source_target_pairs={{0,4},{1,5},{2,6},{3,7},{4,0},{5,1},{6,2},{7,3},{8,12},{9,13},{10,... | collective-permute-start | bytes 491528 | tf_op jit(solution)/shard_map/ppermute | solution.py:76
  19.0 5.1 %collective-permute-start.5 = (bf16[64,1152]{1,0:T(8,128)(2,1)S(1)}, bf16[64,1152]{1,0:T(8,128)(2,1)S(1)}, u32[]{:S(2)}, u32[]{:S(2)}) collective-permute-start(bf16[64,1152]{1,0:T(8,128)(2,1)S(1)} %get-tuple-element.48.refs_2_), channel_id=1, source_target_pairs={{0,2},{1,3},{2,0},{3,1},{4,6},{5,7},{6,4},{7,5},{8,10},{9,11},{10,... | collective-permute-start | bytes 442376 | tf_op jit(solution)/shard_map/ppermute | solution.py:76
  24.2 14.6 %copy-start.10 = (s32[1,32,1]{1,2,0:T(1,128)S(1)}, s32[1,32,1]{1,2,0:T(1,128)}, u32[]{:S(2)}) copy-start(s32[1,32,1]{1,2,0:T(1,128)} %param.17) | copy-start | bytes 388
  24.2 10.6 %collective-permute-start.8 = (bf16[128,1280]{1,0:T(8,128)(2,1)S(1)}, bf16[128,1280]{1,0:T(8,128)(2,1)S(1)}, u32[]{:S(2)}, u32[]{:S(2)}) collective-permute-start(bf16[128,1280]{1,0:T(8,128)(2,1)S(1)} %get-tuple-element.49.refs_0_), channel_id=1, source_target_pairs={{0,2},{1,3},{2,0},{3,1},{4,6},{5,7},{6,4},{7,5},{8,10},{9,11},{10,... | collective-permute-start | bytes 983048 | tf_op jit(solution)/shard_map/ppermute | solution.py:76
  25.8 9.0 %collective-permute-start.9 = (bf16[128,1280]{1,0:T(8,128)(2,1)S(1)}, bf16[128,1280]{1,0:T(8,128)(2,1)S(1)}, u32[]{:S(2)}, u32[]{:S(2)}) collective-permute-start(bf16[128,1280]{1,0:T(8,128)(2,1)S(1)} %get-tuple-element.50.refs_1_), channel_id=1, source_target_pairs={{0,8},{1,9},{2,10},{3,11},{4,12},{5,13},{6,14},{7,15},{8,0},{9,1},... | collective-permute-start | bytes 983048 | tf_op jit(solution)/shard_map/ppermute | solution.py:76
  27.5 7.3 %collective-permute-start.10 = (bf16[128,1152]{1,0:T(8,128)(2,1)S(1)}, bf16[128,1152]{1,0:T(8,128)(2,1)S(1)}, u32[]{:S(2)}, u32[]{:S(2)}) collective-permute-start(bf16[128,1152]{1,0:T(8,128)(2,1)S(1)} %get-tuple-element.51.refs_2_), channel_id=1, source_target_pairs={{0,4},{1,5},{2,6},{3,7},{4,0},{5,1},{6,2},{7,3},{8,12},{9,13},{10,... | collective-permute-start | bytes 884744 | tf_op jit(solution)/shard_map/ppermute | solution.py:76
  35.8 14.6 %collective-permute-start.11 = (bf16[256,1280]{1,0:T(8,128)(2,1)S(1)}, bf16[256,1280]{1,0:T(8,128)(2,1)S(1)}, u32[]{:S(2)}, u32[]{:S(2)}) collective-permute-start(bf16[256,1280]{1,0:T(8,128)(2,1)S(1)} %get-tuple-element.52.refs_0_), channel_id=1, source_target_pairs={{0,4},{1,5},{2,6},{3,7},{4,0},{5,1},{6,2},{7,3},{8,12},{9,13},{10,... | collective-permute-start | bytes 1966088 | tf_op jit(solution)/shard_map/ppermute | solution.py:76
  37.3 13.8 %collective-permute-start.12 = (bf16[256,1280]{1,0:T(8,128)(2,1)S(1)}, bf16[256,1280]{1,0:T(8,128)(2,1)S(1)}, u32[]{:S(2)}, u32[]{:S(2)}) collective-permute-start(bf16[256,1280]{1,0:T(8,128)(2,1)S(1)} %get-tuple-element.53.refs_1_), channel_id=1, source_target_pairs={{0,2},{1,3},{2,0},{3,1},{4,6},{5,7},{6,4},{7,5},{8,10},{9,11},{10,... | collective-permute-start | bytes 1966088 | tf_op jit(solution)/shard_map/ppermute | solution.py:76
  37.8 12.6 %collective-permute-start.13 = (bf16[256,1152]{1,0:T(8,128)(2,1)}, bf16[256,1152]{1,0:T(8,128)(2,1)}, u32[]{:S(2)}, u32[]{:S(2)}) collective-permute-start(bf16[256,1152]{1,0:T(8,128)(2,1)} %get-tuple-element.54.refs_2_), channel_id=1, source_target_pairs={{0,8},{1,9},{2,10},{3,11},{4,12},{5,13},{6,14},{7,15},{8,0},{9,1},... | collective-permute-start | bytes 1769480 | tf_op jit(solution)/shard_map/ppermute | solution.py:76
  51.1 9.6 %copy-start.1 = (bf16[1,512,3584]{2,1,0:T(8,128)(2,1)S(1)}, bf16[1,512,3584]{2,1,0:T(8,128)(2,1)}, u32[]{:S(2)}) copy-start(bf16[1,512,3584]{2,1,0:T(8,128)(2,1)} %param.23) | copy-start | bytes 11010052
  64.0 27.3 %collective-permute-start.14 = (f32[256,1280]{1,0:T(8,128)}, f32[256,1280]{1,0:T(8,128)}, u32[]{:S(2)}, u32[]{:S(2)}) collective-permute-start(f32[256,1280]{1,0:T(8,128)} %expert_output.6.refs_10_), channel_id=1, source_target_pairs={{0,4},{1,5},{2,6},{3,7},{4,0},{5,1},{6,2},{7,3},{8,12},{9,13},{10,... | collective-permute-start | bytes 3932168 | tf_op jit(solution)/shard_map/ppermute | solution.py:76
  67.7 30.1 %collective-permute-start.16 = (f32[256,1280]{1,0:T(8,128)}, f32[256,1280]{1,0:T(8,128)}, u32[]{:S(2)}, u32[]{:S(2)}) collective-permute-start(f32[256,1280]{1,0:T(8,128)} %expert_output.7.refs_8_), channel_id=1, source_target_pairs={{0,2},{1,3},{2,0},{3,1},{4,6},{5,7},{6,4},{7,5},{8,10},{9,11},{10,... | collective-permute-start | bytes 3932168 | tf_op jit(solution)/shard_map/ppermute | solution.py:76
  71.5 23.6 %collective-permute-start.17 = (f32[256,1024]{1,0:T(8,128)}, f32[256,1024]{1,0:T(8,128)}, u32[]{:S(2)}, u32[]{:S(2)}) collective-permute-start(f32[256,1024]{1,0:T(8,128)} %expert_output.8.refs_10_), channel_id=1, source_target_pairs={{0,8},{1,9},{2,10},{3,11},{4,12},{5,13},{6,14},{7,15},{8,0},{9,1},... | collective-permute-start | bytes 3145736 | tf_op jit(solution)/shard_map/ppermute | solution.py:76
  84.4 19.1 %all-to-all-start = ((bf16[32,8,608]{2,1,0:T(8,128)(2,1)}), bf16[32,8,608]{2,1,0:T(8,128)(2,1)S(1)}, u32[]{:S(2)}, u32[]{:S(2)}) async-start(bf16[32,8,608]{2,1,0:T(8,128)(2,1)} %fusion.21), calls=%async_computation | async-start | bytes 655360 | tf_op jit(solution)/shard_map/all_to_all | solution.py:424
  89.9 5.2 %copy-start.6 = (f32[256,1024]{1,0:T(8,128)S(1)}, f32[256,1024]{1,0:T(8,128)}, u32[]{:S(2)}) copy-start(f32[256,1024]{1,0:T(8,128)} %copy-done.5) | copy-start | bytes 3145732
  93.7 4.2 %copy-start.4 = (f32[256,1280]{1,0:T(8,128)S(1)}, f32[256,1280]{1,0:T(8,128)}, u32[]{:S(2)}) copy-start(f32[256,1280]{1,0:T(8,128)} %copy-done.3) | copy-start | bytes 3932164
  93.7 18.8 %collective-permute-start.15 = (f32[128,1280]{1,0:T(8,128)}, f32[128,1280]{1,0:T(8,128)}, u32[]{:S(2)}, u32[]{:S(2)}) collective-permute-start(f32[128,1280]{1,0:T(8,128)} %get-tuple-element.61), channel_id=1, source_target_pairs={{0,2},{1,3},{2,0},{3,1},{4,6},{5,7},{6,4},{7,5},{8,10},{9,11},{10,... | collective-permute-start | bytes 1966088 | tf_op jit(solution)/shard_map/ppermute | solution.py:76
  100.2 19.3 %collective-permute-start.19 = (f32[128,1280]{1,0:T(8,128)}, f32[128,1280]{1,0:T(8,128)S(1)}, u32[]{:S(2)}, u32[]{:S(2)}) collective-permute-start(f32[128,1280]{1,0:T(8,128)} %get-tuple-element.66), channel_id=1, source_target_pairs={{0,8},{1,9},{2,10},{3,11},{4,12},{5,13},{6,14},{7,15},{8,0},{9,1},... | collective-permute-start | bytes 1966088 | tf_op jit(solution)/shard_map/ppermute | solution.py:76
  102.0 15.5 %collective-permute-start.20 = (f32[128,1024]{1,0:T(8,128)}, f32[128,1024]{1,0:T(8,128)}, u32[]{:S(2)}, u32[]{:S(2)}) collective-permute-start(f32[128,1024]{1,0:T(8,128)} %get-tuple-element.67), channel_id=1, source_target_pairs={{0,4},{1,5},{2,6},{3,7},{4,0},{5,1},{6,2},{7,3},{8,12},{9,13},{10,... | collective-permute-start | bytes 1572872 | tf_op jit(solution)/shard_map/ppermute | solution.py:76
  113.6 10.5 %collective-permute-start.18 = (f32[64,1280]{1,0:T(8,128)S(1)}, f32[64,1280]{1,0:T(8,128)S(1)}, u32[]{:S(2)}, u32[]{:S(2)}) collective-permute-start(f32[64,1280]{1,0:T(8,128)S(1)} %get-tuple-element.65), channel_id=1, source_target_pairs={{0,24},{1,25},{2,26},{3,27},{4,28},{5,29},{6,30},{7,31},{8,16},{9,... | collective-permute-start | bytes 983048 | tf_op jit(solution)/shard_map/ppermute | solution.py:76
  118.7 6.4 %collective-permute-start.22 = (f32[64,1024]{1,0:T(8,128)S(1)}, f32[64,1024]{1,0:T(8,128)S(1)}, u32[]{:S(2)}, u32[]{:S(2)}) collective-permute-start(f32[64,1024]{1,0:T(8,128)S(1)} %get-tuple-element.72), channel_id=1, source_target_pairs={{0,2},{1,3},{2,0},{3,1},{4,6},{5,7},{6,4},{7,5},{8,10},{9,11},{10,... | collective-permute-start | bytes 786440 | tf_op jit(solution)/shard_map/ppermute | solution.py:76
  119.6 7.9 %collective-permute-start.21 = (f32[64,1280]{1,0:T(8,128)S(1)}, f32[64,1280]{1,0:T(8,128)S(1)}, u32[]{:S(2)}, u32[]{:S(2)}) collective-permute-start(f32[64,1280]{1,0:T(8,128)S(1)} %get-tuple-element.71), channel_id=1, source_target_pairs={{0,4},{1,5},{2,6},{3,7},{4,0},{5,1},{6,2},{7,3},{8,12},{9,13},{10,... | collective-permute-start | bytes 983048 | tf_op jit(solution)/shard_map/ppermute | solution.py:76
  127.5 13.9 %collective-permute-start.24 = (f32[32,1280]{1,0:T(8,128)S(1)}, f32[32,1280]{1,0:T(8,128)S(1)}, u32[]{:S(2)}, u32[]{:S(2)}) collective-permute-start(f32[32,1280]{1,0:T(8,128)S(1)} %get-tuple-element.76), channel_id=1, source_target_pairs={{0,24},{1,25},{2,26},{3,27},{4,28},{5,29},{6,30},{7,31},{8,16},{9,... | collective-permute-start | bytes 491528 | tf_op jit(solution)/shard_map/ppermute | solution.py:76
  128.4 13.1 %collective-permute-start.25 = (f32[32,1024]{1,0:T(8,128)S(1)}, f32[32,1024]{1,0:T(8,128)S(1)}, u32[]{:S(2)}, u32[]{:S(2)}) collective-permute-start(f32[32,1024]{1,0:T(8,128)S(1)} %get-tuple-element.77), channel_id=1, source_target_pairs={{0,24},{1,25},{2,26},{3,27},{4,28},{5,29},{6,30},{7,31},{8,16},{9,... | collective-permute-start | bytes 393224 | tf_op jit(solution)/shard_map/ppermute | solution.py:76
  131.4 11.8 %collective-permute-start.23 = (f32[32,1280]{1,0:T(8,128)S(1)}, f32[32,1280]{1,0:T(8,128)S(1)}, u32[]{:S(2)}, u32[]{:S(2)}) collective-permute-start(f32[32,1280]{1,0:T(8,128)S(1)} %get-tuple-element.75), channel_id=1, source_target_pairs={{0,8},{1,9},{2,10},{3,11},{4,12},{5,13},{6,14},{7,15},{8,0},{9,1},... | collective-permute-start | bytes 491528 | tf_op jit(solution)/shard_map/ppermute | solution.py:76
  (6 other events, 15.5 us)

commit v13 on v11

--- a/solution.py
+++ b/solution.py
@@ -316,13 +316,27 @@
 
 def halved(keep, got, after):
     rows, width = keep.shape
+    tiles = 2 if rows * width >= 1 << 18 else 1
     half = jax.ShapeDtypeStruct((rows // 2, width), keep.dtype)
 
-    def kernel(keep_ref, got_ref, first_ref, second_ref):
+    def kernel(keep_ref, got_ref, *refs):
+        first_ref, second_ref = refs[-2:]
         second_ref[...] = keep_ref[rows // 2 :] + got_ref[rows // 2 :]
         first_ref[...] = keep_ref[: rows // 2] + got_ref[: rows // 2]
 
-    return whole_call(kernel, [keep, got], [half, half], "halved", after)
+    return pl.pallas_call(
+        kernel,
+        grid=(tiles,),
+        in_specs=[pl.BlockSpec((rows, width // tiles), lambda i: (0, i))] * 2
+        + [pl.BlockSpec(memory_space=pl.ANY)] * len(after),
+        out_specs=[pl.BlockSpec((rows // 2, width // tiles), lambda i: (0, i))] * 2,
+        out_shape=[half, half],
+        compiler_params=pltpu.CompilerParams(vmem_limit_bytes=12 * MIB),
+        cost_estimate=pl.CostEstimate(
+            flops=rows * width, bytes_accessed=12 * rows * width, transcendentals=0
+        ),
+        name="halved",
+    )(keep, got, *after)
 
 
 def finished(keep, got):

time: 142 us -> 142 us (level)
    pallas_call x14 -> x5, Pallas kernels: 10.2 us -> 1 us  [whole_call(): pl.pallas_call(body, in_specs=[pl.BlockSpec(memory_space=pltpu.VMEM)] * g...]
    pallas_call x0 -> x9, Pallas kernels: none -> 8.89 us  [halved(): pl.pallas_call(kernel, grid=(tiles,), in_specs=[pl.BlockSpec((rows, width...]
where the time goes in v13:
time: 142 us; the launch traced here: 141 us
  starting transfers between devices  43.1 us (30%)
  waiting for transfers between devices  42.2 us (30%)
  Pallas kernels  39.3 us (28%)
  local copies, waits for them, and re-layouts  8.86 us (6%)
  other arithmetic  3.21 us (2%)
  matrix products  2.63 us (2%)
  between operations  1.5 us (1%)
    ppermute x23, waiting for transfers between devices, across(): lax.ppermute(value, 'ep', [(i, i ^ 2 * LINKS[link]) for i in range(peers)])  42.2 us
    ppermute x23, starting transfers between devices, across(): lax.ppermute(value, 'ep', [(i, i ^ 2 * LINKS[link]) for i in range(peers)])  36.3 us
    pallas_call x2, Pallas kernels, expert_part(): pl.pallas_call(functools.partial(part_kernel, unit, last), grid=(2 * step...  19.6 us
    pallas_call x3, Pallas kernels, expert_output(): pl.pallas_call(functools.partial(output_kernel, unit, order, tiles), grid...  9.83 us
    pallas_call x9, Pallas kernels, halved(): pl.pallas_call(kernel, grid=(tiles,), in_specs=[pl.BlockSpec((rows, width...  8.89 us
    all_to_all x1, starting transfers between devices, per_device(): lax.all_to_all(leaving, 'ep', split_axis=0, concat_axis=0, tiled=True)  5.76 us
    unnamed x22, local copies, waits for them, and re-layouts  4.07 us
  transfers between devices with their start and end apart: 27, of which 14 were waited for; matrix products, arithmetic and copies ran while one was open for 8% of the time, Pallas kernels for 18%

profile of v13, /device:TPU:0, one launch (start us, length us, event | category | flops | bytes accessed | tf_op | source)
XLA Modules:
  0.0 140.8 jit_solution(16240793311199014941)
XLA Ops:
  3.6 4.7 %collective-permute-start.1 = (bf16[32,2432]{1,0:T(8,128)(2,1)S(1)}, bf16[32,2432]{1,0:T(8,128)(2,1)S(1)}, u32[]{:S(2)}, u32[]{:S(2)}) collective-permute-start(bf16[32,2432]{1,0:T(8,128)(2,1)S(1)} %pad_maximum_fusion.refs_1_), channel_id=1, source_target_pairs={{0,24},{1,25},{2,26},{3,27},{4,28},{5,29},{6,30},{7,31},{8,16},{9,... | collective-permute-start | bytes 466952 | tf_op jit(solution)/shard_map/ppermute | solution.py:76
  9.2 5.6 %collective-permute-done.refs_2_ = bf16[32,1280]{1,0:T(8,128)(2,1)S(1)} collective-permute-done((bf16[32,1280]{1,0:T(8,128)(2,1)S(1)}, bf16[32,1280]{1,0:T(8,128)(2,1)S(1)}, u32[]{:S(2)}, u32[]{:S(2)}) %collective-permute-start) | collective-permute-done | bytes 81952 | tf_op jit(solution)/shard_map/ppermute | solution.py:76
  14.9 2.6 %collective-permute-start.3 = (bf16[64,1280]{1,0:T(8,128)(2,1)S(1)}, bf16[64,1280]{1,0:T(8,128)(2,1)S(1)}, u32[]{:S(2)}, u32[]{:S(2)}) collective-permute-start(bf16[64,1280]{1,0:T(8,128)(2,1)S(1)} %get-tuple-element.52.refs_0_), channel_id=1, source_target_pairs={{0,24},{1,25},{2,26},{3,27},{4,28},{5,29},{6,30},{7,31},{8,16},{9,... | collective-permute-start | bytes 491528 | tf_op jit(solution)/shard_map/ppermute | solution.py:76
  17.5 1.5 %collective-permute-start.4 = (bf16[64,1280]{1,0:T(8,128)(2,1)S(1)}, bf16[64,1280]{1,0:T(8,128)(2,1)S(1)}, u32[]{:S(2)}, u32[]{:S(2)}) collective-permute-start(bf16[64,1280]{1,0:T(8,128)(2,1)S(1)} %get-tuple-element.53.refs_1_), channel_id=1, source_target_pairs={{0,4},{1,5},{2,6},{3,7},{4,0},{5,1},{6,2},{7,3},{8,12},{9,13},{10,... | collective-permute-start | bytes 491528 | tf_op jit(solution)/shard_map/ppermute | solution.py:76
  19.0 1.5 %collective-permute-start.5 = (bf16[64,1152]{1,0:T(8,128)(2,1)S(1)}, bf16[64,1152]{1,0:T(8,128)(2,1)S(1)}, u32[]{:S(2)}, u32[]{:S(2)}) collective-permute-start(bf16[64,1152]{1,0:T(8,128)(2,1)S(1)} %get-tuple-element.54.refs_2_), channel_id=1, source_target_pairs={{0,2},{1,3},{2,0},{3,1},{4,6},{5,7},{6,4},{7,5},{8,10},{9,11},{10,... | collective-permute-start | bytes 442376 | tf_op jit(solution)/shard_map/ppermute | solution.py:76
  20.5 3.6 %collective-permute-done.5.refs_5_ = bf16[64,1152]{1,0:T(8,128)(2,1)S(1)} collective-permute-done((bf16[64,1152]{1,0:T(8,128)(2,1)S(1)}, bf16[64,1152]{1,0:T(8,128)(2,1)S(1)}, u32[]{:S(2)}, u32[]{:S(2)}) %collective-permute-start.5) | collective-permute-done | bytes 147488 | tf_op jit(solution)/shard_map/ppermute | solution.py:76
  24.2 1.6 %collective-permute-start.8 = (bf16[128,1280]{1,0:T(8,128)(2,1)S(1)}, bf16[128,1280]{1,0:T(8,128)(2,1)S(1)}, u32[]{:S(2)}, u32[]{:S(2)}) collective-permute-start(bf16[128,1280]{1,0:T(8,128)(2,1)S(1)} %get-tuple-element.55.refs_0_), channel_id=1, source_target_pairs={{0,2},{1,3},{2,0},{3,1},{4,6},{5,7},{6,4},{7,5},{8,10},{9,11},{10,... | collective-permute-start | bytes 983048 | tf_op jit(solution)/shard_map/ppermute | solution.py:76
  25.8 1.7 %collective-permute-start.9 = (bf16[128,1280]{1,0:T(8,128)(2,1)S(1)}, bf16[128,1280]{1,0:T(8,128)(2,1)S(1)}, u32[]{:S(2)}, u32[]{:S(2)}) collective-permute-start(bf16[128,1280]{1,0:T(8,128)(2,1)S(1)} %get-tuple-element.56.refs_1_), channel_id=1, source_target_pairs={{0,8},{1,9},{2,10},{3,11},{4,12},{5,13},{6,14},{7,15},{8,0},{9,1},... | collective-permute-start | bytes 983048 | tf_op jit(solution)/shard_map/ppermute | solution.py:76
  27.5 1.5 %collective-permute-start.10 = (bf16[128,1152]{1,0:T(8,128)(2,1)S(1)}, bf16[128,1152]{1,0:T(8,128)(2,1)S(1)}, u32[]{:S(2)}, u32[]{:S(2)}) collective-permute-start(bf16[128,1152]{1,0:T(8,128)(2,1)S(1)} %get-tuple-element.57.refs_2_), channel_id=1, source_target_pairs={{0,4},{1,5},{2,6},{3,7},{4,0},{5,1},{6,2},{7,3},{8,12},{9,13},{10,... | collective-permute-start | bytes 884744 | tf_op jit(solution)/shard_map/ppermute | solution.py:76
  29.0 5.7 %collective-permute-done.10.refs_5_ = bf16[128,1152]{1,0:T(8,128)(2,1)S(1)} collective-permute-done((bf16[128,1152]{1,0:T(8,128)(2,1)S(1)}, bf16[128,1152]{1,0:T(8,128)(2,1)S(1)}, u32[]{:S(2)}, u32[]{:S(2)}) %collective-permute-start.10) | collective-permute-done | bytes 294944 | tf_op jit(solution)/shard_map/ppermute | solution.py:76
  34.9 1.6 %collective-permute-start.11 = (bf16[256,1280]{1,0:T(8,128)(2,1)S(1)}, bf16[256,1280]{1,0:T(8,128)(2,1)S(1)}, u32[]{:S(2)}, u32[]{:S(2)}) collective-permute-start(bf16[256,1280]{1,0:T(8,128)(2,1)S(1)} %get-tuple-element.58.refs_0_), channel_id=1, source_target_pairs={{0,4},{1,5},{2,6},{3,7},{4,0},{5,1},{6,2},{7,3},{8,12},{9,13},{10,... | collective-permute-start | bytes 1966088 | tf_op jit(solution)/shard_map/ppermute | solution.py:76
  38.0 10.0 %expert_part.2 = (f32[512,1024]{1,0:T(8,128)S(1)}, f32[512,1024]{1,0:T(8,128)}, f32[512,1]{1,0:T(8,128)S(1)}) custom-call(s32[1]{0:T(128)} %bitcast.2.chip_ref, bf16[256,1280]{1,0:T(8,128)(2,1)S(1)} %get-tuple-element.58.refs_0_, bf16[256,1280]{1,0:T(8,128)(2,1)S(1)} %get-tuple-element.59.refs_1_, bf16[256,1152]{1,0:T(8,128)(2,1)S(1)} %get-tuple-element.60.refs_2_, ...), custom_call_target="tpu_custom_call" | custom-call | flops 3758096384 | bytes 19660800 | tf_op jit(solution)/shard_map/expert_part/pallas_call | solution.py:249
  50.3 9.6 %expert_part.3 = (bf16[512,1024]{1,0:T(8,128)(2,1)S(1)}, f32[512,1]{1,0:T(8,128)S(1)}) custom-call(s32[1]{0:T(128)} %bitcast.2.chip_ref, bf16[256,1280]{1,0:T(8,128)(2,1)S(1)} %collective-permute-done.11.refs_0_, bf16[256,1280]{1,0:T(8,128)(2,1)S(1)} %collective-permute-done.12.refs_1_, bf16[256,1152]{1,0:T(8,128)(2,1)} %collective-permute-done.13.refs_2_, ...), custom_call_target="tpu_custom_call" | custom-call | flops 3758096384 | bytes 19660800 | tf_op jit(solution)/shard_map/expert_part/pallas_call | solution.py:249
  59.9 3.5 %expert_output.3 = (f32[256,1280]{1,0:T(8,128)S(1)}, f32[256,1280]{1,0:T(8,128)}) custom-call(f32[512,1]{1,0:T(8,128)S(1)} %get-tuple-element.64.scale_ref, bf16[512,1024]{1,0:T(8,128)(2,1)S(1)} %get-tuple-element.65.hidden_ref, bf16[512,3584]{1,0:T(8,128)(2,1)S(1)} %bitcast.20, bf16[512,3584]{1,0:T(8,128)(2,1)S(1)} %bitcast.21, ...), custom_call_target="tpu_custom_call" | custom-call | flops 1342177280 | bytes 6291456 | tf_op jit(solution)/shard_map/expert_output/pallas_call | solution.py:296
  63.9 3.4 %expert_output.4 = (f32[256,1280]{1,0:T(8,128)S(1)}, f32[256,1280]{1,0:T(8,128)}) custom-call(f32[512,1]{1,0:T(8,128)S(1)} %get-tuple-element.64.scale_ref, bf16[512,1024]{1,0:T(8,128)(2,1)S(1)} %get-tuple-element.65.hidden_ref, bf16[512,3584]{1,0:T(8,128)(2,1)S(1)} %bitcast.25, bf16[512,3584]{1,0:T(8,128)(2,1)S(1)} %bitcast.26, ...), custom_call_target="tpu_custom_call" | custom-call | flops 1342177280 | bytes 6291456 | tf_op jit(solution)/shard_map/expert_output/pallas_call | solution.py:296
  68.0 2.9 %expert_output.5 = (f32[256,1024]{1,0:T(8,128)S(1)}, f32[256,1024]{1,0:T(8,128)}) custom-call(f32[512,1]{1,0:T(8,128)S(1)} %get-tuple-element.64.scale_ref, bf16[512,1024]{1,0:T(8,128)(2,1)S(1)} %get-tuple-element.65.hidden_ref, bf16[512,3584]{1,0:T(8,128)(2,1)S(1)} %bitcast.30, bf16[512,3584]{1,0:T(8,128)(2,1)S(1)} %bitcast.31, ...), custom_call_target="tpu_custom_call" | custom-call | flops 1073741824 | bytes 5242880 | tf_op jit(solution)/shard_map/expert_output/pallas_call | solution.py:296
  76.5 5.8 %all-to-all-start = ((bf16[32,8,608]{2,1,0:T(8,128)(2,1)}), bf16[32,8,608]{2,1,0:T(8,128)(2,1)}, u32[]{:S(2)}, u32[]{:S(2)}) async-start(bf16[32,8,608]{2,1,0:T(8,128)(2,1)} %fusion.21), calls=%async_computation | async-start | bytes 655360 | tf_op jit(solution)/shard_map/all_to_all | solution.py:436
  82.2 10.1 %collective-permute-done.14.got_ref = f32[256,1280]{1,0:T(8,128)} collective-permute-done((f32[256,1280]{1,0:T(8,128)}, f32[256,1280]{1,0:T(8,128)}, u32[]{:S(2)}, u32[]{:S(2)}) %collective-permute-start.14) | collective-permute-done | bytes 1310752 | tf_op jit(solution)/shard_map/ppermute | solution.py:76
  92.3 2.2 %halved.9 = (f32[128,1280]{1,0:T(8,128)S(1)}, f32[128,1280]{1,0:T(8,128)}) custom-call(f32[256,1280]{1,0:T(8,128)S(1)} %get-tuple-element.66.refs_10_.keep_ref, f32[256,1280]{1,0:T(8,128)} %collective-permute-done.14.got_ref), custom_call_target="tpu_custom_call" | custom-call | flops 327680 | bytes 3932160 | tf_op jit(solution)/shard_map/halved/pallas_call | solution.py:327
  95.0 1.5 %collective-permute-done.17.got_ref = f32[256,1024]{1,0:T(8,128)} collective-permute-done((f32[256,1024]{1,0:T(8,128)}, f32[256,1024]{1,0:T(8,128)}, u32[]{:S(2)}, u32[]{:S(2)}) %collective-permute-start.17) | collective-permute-done | bytes 1048608 | tf_op jit(solution)/shard_map/ppermute | solution.py:76
  96.5 2.1 %halved.10 = (f32[128,1024]{1,0:T(8,128)S(1)}, f32[128,1024]{1,0:T(8,128)}) custom-call(f32[256,1024]{1,0:T(8,128)S(1)} %copy-done.4, f32[256,1024]{1,0:T(8,128)} %collective-permute-done.17.got_ref, f32[128,1280]{1,0:T(8,128)S(1)} %get-tuple-element.70.refs_0_.keep_ref), custom_call_target="tpu_custom_call" | custom-call | flops 262144 | bytes 3145728 | tf_op jit(solution)/shard_map/halved/pallas_call | solution.py:327
  98.5 3.3 %collective-permute-done.16.got_ref = f32[256,1280]{1,0:T(8,128)} collective-permute-done((f32[256,1280]{1,0:T(8,128)}, f32[256,1280]{1,0:T(8,128)}, u32[]{:S(2)}, u32[]{:S(2)}) %collective-permute-start.16) | collective-permute-done | bytes 1310752 | tf_op jit(solution)/shard_map/ppermute | solution.py:76
  101.9 2.2 %halved.11 = (f32[128,1280]{1,0:T(8,128)S(1)}, f32[128,1280]{1,0:T(8,128)}) custom-call(f32[256,1280]{1,0:T(8,128)S(1)} %get-tuple-element.67.refs_8_.keep_ref, f32[256,1280]{1,0:T(8,128)} %collective-permute-done.16.got_ref, f32[128,1024]{1,0:T(8,128)S(1)} %get-tuple-element.74.refs_0_.keep_ref), custom_call_target="tpu_custom_call" | custom-call | flops 327680 | bytes 3932160 | tf_op jit(solution)/shard_map/halved/pallas_call | solution.py:327
  106.0 1.5 %collective-permute-start.20 = (f32[128,1024]{1,0:T(8,128)}, f32[128,1024]{1,0:T(8,128)S(1)}, u32[]{:S(2)}, u32[]{:S(2)}) collective-permute-start(f32[128,1024]{1,0:T(8,128)} %get-tuple-element.79), channel_id=1, source_target_pairs={{0,4},{1,5},{2,6},{3,7},{4,0},{5,1},{6,2},{7,3},{8,12},{9,13},{10,... | collective-permute-start | bytes 1572872 | tf_op jit(solution)/shard_map/ppermute | solution.py:76
  113.2 4.0 %collective-permute-start.18 = (f32[64,1280]{1,0:T(8,128)S(1)}, f32[64,1280]{1,0:T(8,128)S(1)}, u32[]{:S(2)}, u32[]{:S(2)}) collective-permute-start(f32[64,1280]{1,0:T(8,128)S(1)} %get-tuple-element.77), channel_id=1, source_target_pairs={{0,24},{1,25},{2,26},{3,27},{4,28},{5,29},{6,30},{7,31},{8,16},{9,... | collective-permute-start | bytes 983048 | tf_op jit(solution)/shard_map/ppermute | solution.py:76
  120.8 1.5 %collective-permute-start.21 = (f32[64,1280]{1,0:T(8,128)S(1)}, f32[64,1280]{1,0:T(8,128)S(1)}, u32[]{:S(2)}, u32[]{:S(2)}) collective-permute-start(f32[64,1280]{1,0:T(8,128)S(1)} %get-tuple-element.83), channel_id=1, source_target_pairs={{0,4},{1,5},{2,6},{3,7},{4,0},{5,1},{6,2},{7,3},{8,12},{9,13},{10,... | collective-permute-start | bytes 983048 | tf_op jit(solution)/shard_map/ppermute | solution.py:76
  125.5 2.4 %collective-permute-done.21.got_ref = f32[64,1280]{1,0:T(8,128)S(1)} collective-permute-done((f32[64,1280]{1,0:T(8,128)S(1)}, f32[64,1280]{1,0:T(8,128)S(1)}, u32[]{:S(2)}, u32[]{:S(2)}) %collective-permute-start.21) | collective-permute-done | bytes 327712 | tf_op jit(solution)/shard_map/ppermute | solution.py:76
  128.0 1.7 %collective-permute-start.24 = (f32[32,1280]{1,0:T(8,128)S(1)}, f32[32,1280]{1,0:T(8,128)S(1)}, u32[]{:S(2)}, u32[]{:S(2)}) collective-permute-start(f32[32,1280]{1,0:T(8,128)S(1)} %get-tuple-element.88), channel_id=1, source_target_pairs={{0,24},{1,25},{2,26},{3,27},{4,28},{5,29},{6,30},{7,31},{8,16},{9,... | collective-permute-start | bytes 491528 | tf_op jit(solution)/shard_map/ppermute | solution.py:76
  129.7 2.1 %collective-permute-start.25 = (f32[32,1024]{1,0:T(8,128)S(1)}, f32[32,1024]{1,0:T(8,128)S(1)}, u32[]{:S(2)}, u32[]{:S(2)}) collective-permute-start(f32[32,1024]{1,0:T(8,128)S(1)} %get-tuple-element.89), channel_id=1, source_target_pairs={{0,24},{1,25},{2,26},{3,27},{4,28},{5,29},{6,30},{7,31},{8,16},{9,... | collective-permute-start | bytes 393224 | tf_op jit(solution)/shard_map/ppermute | solution.py:76
  131.8 2.5 %collective-permute-start.23 = (f32[32,1280]{1,0:T(8,128)S(1)}, f32[32,1280]{1,0:T(8,128)S(1)}, u32[]{:S(2)}, u32[]{:S(2)}) collective-permute-start(f32[32,1280]{1,0:T(8,128)S(1)} %get-tuple-element.87), channel_id=1, source_target_pairs={{0,8},{1,9},{2,10},{3,11},{4,12},{5,13},{6,14},{7,15},{8,0},{9,1},... | collective-permute-start | bytes 491528 | tf_op jit(solution)/shard_map/ppermute | solution.py:76
  134.3 1.5 %fusion.14 = bf16[1,128,512]{2,1,0:T(8,128)(2,1)} fusion(bf16[256,576]{0,1:T(8,128)(2,1)S(1)} %copy-done.8, bf16[1024,576]{0,1:T(8,128)(2,1)S(1)} %bitcast.41, f32[1280,128]{1,0:T(8,128)S(1)} %get-tuple-element.94, f32[128]{0:T(128)S(1)} %get-tuple-element.93, pred[1280]{0:T(1024)(128)(4,1)S(1)} %pad_add_fusion, f32[128]{0:T(128)S(1)} %fusion.18), kind=kOutput, calls=%fused_computation.12 | convolution fusion | flops 171016192 | bytes 2263296 | tf_op jit(solution)/shard_map/dot_general | solution.py:38
  136.9 3.2 %collective-permute-done.23.refs_3_ = f32[32,1280]{1,0:T(8,128)S(1)} collective-permute-done((f32[32,1280]{1,0:T(8,128)S(1)}, f32[32,1280]{1,0:T(8,128)S(1)}, u32[]{:S(2)}, u32[]{:S(2)}) %collective-permute-start.23) | collective-permute-done | bytes 163872 | tf_op jit(solution)/shard_map/ppermute | solution.py:76
  (91 shorter events, 30.6 us)
Async XLA Ops:
  0.6 121.7 %copy-start = (bf16[1,128,576]{1,2,0:T(8,128)(2,1)S(1)}, bf16[1,128,576]{1,2,0:T(8,128)(2,1)}, u32[]{:S(2)}) copy-start(bf16[1,128,576]{1,2,0:T(8,128)(2,1)} %param.13) | copy-start | bytes 442372
  0.6 14.2 %collective-permute-start.2 = (bf16[512,3584]{1,0:T(8,128)(2,1)}, bf16[512,3584]{1,0:T(8,128)(2,1)}, u32[]{:S(2)}, u32[]{:S(2)}) collective-permute-start(bf16[512,3584]{1,0:T(8,128)(2,1)} %bitcast.19), channel_id=1, source_target_pairs={{0,1},{1,0},{2,3},{3,2},{4,5},{5,4},{6,7},{7,6},{8,9},{9,8},{10,11... | collective-permute-start | bytes 11010056 | tf_op jit(solution)/shard_map/ppermute | solution.py:80
  1.2 19.3 %collective-permute-start.6 = (bf16[3584,512]{1,0:T(8,128)(2,1)}, bf16[3584,512]{1,0:T(8,128)(2,1)}, u32[]{:S(2)}, u32[]{:S(2)}) collective-permute-start(bf16[3584,512]{1,0:T(8,128)(2,1)} %bitcast.34), channel_id=1, source_target_pairs={{0,1},{1,0},{2,3},{3,2},{4,5},{5,4},{6,7},{7,6},{8,9},{9,8},{10,11... | collective-permute-start | bytes 11010056 | tf_op jit(solution)/shard_map/ppermute | solution.py:80
  1.2 19.3 %collective-permute-start.7 = (bf16[3584,512]{1,0:T(8,128)(2,1)}, bf16[3584,512]{1,0:T(8,128)(2,1)}, u32[]{:S(2)}, u32[]{:S(2)}) collective-permute-start(bf16[3584,512]{1,0:T(8,128)(2,1)} %bitcast.37), channel_id=1, source_target_pairs={{0,1},{1,0},{2,3},{3,2},{4,5},{5,4},{6,7},{7,6},{8,9},{9,8},{10,11... | collective-permute-start | bytes 11010056 | tf_op jit(solution)/shard_map/ppermute | solution.py:80
  3.6 11.2 %collective-permute-start.1 = (bf16[32,2432]{1,0:T(8,128)(2,1)S(1)}, bf16[32,2432]{1,0:T(8,128)(2,1)S(1)}, u32[]{:S(2)}, u32[]{:S(2)}) collective-permute-start(bf16[32,2432]{1,0:T(8,128)(2,1)S(1)} %pad_maximum_fusion.refs_1_), channel_id=1, source_target_pairs={{0,24},{1,25},{2,26},{3,27},{4,28},{5,29},{6,30},{7,31},{8,16},{9,... | collective-permute-start | bytes 466952 | tf_op jit(solution)/shard_map/ppermute | solution.py:76
  9.2 5.6 %collective-permute-start = (bf16[32,1280]{1,0:T(8,128)(2,1)S(1)}, bf16[32,1280]{1,0:T(8,128)(2,1)S(1)}, u32[]{:S(2)}, u32[]{:S(2)}) collective-permute-start(bf16[32,1280]{1,0:T(8,128)(2,1)S(1)} %slice.47.refs_0_), channel_id=1, source_target_pairs={{0,8},{1,9},{2,10},{3,11},{4,12},{5,13},{6,14},{7,15},{8,0},{9,1},... | collective-permute-start | bytes 245768 | tf_op jit(solution)/shard_map/ppermute | solution.py:76
  14.9 9.3 %collective-permute-start.3 = (bf16[64,1280]{1,0:T(8,128)(2,1)S(1)}, bf16[64,1280]{1,0:T(8,128)(2,1)S(1)}, u32[]{:S(2)}, u32[]{:S(2)}) collective-permute-start(bf16[64,1280]{1,0:T(8,128)(2,1)S(1)} %get-tuple-element.52.refs_0_), channel_id=1, source_target_pairs={{0,24},{1,25},{2,26},{3,27},{4,28},{5,29},{6,30},{7,31},{8,16},{9,... | collective-permute-start | bytes 491528 | tf_op jit(solution)/shard_map/ppermute | solution.py:76
  17.5 6.7 %collective-permute-start.4 = (bf16[64,1280]{1,0:T(8,128)(2,1)S(1)}, bf16[64,1280]{1,0:T(8,128)(2,1)S(1)}, u32[]{:S(2)}, u32[]{:S(2)}) collective-permute-start(bf16[64,1280]{1,0:T(8,128)(2,1)S(1)} %get-tuple-element.53.refs_1_), channel_id=1, source_target_pairs={{0,4},{1,5},{2,6},{3,7},{4,0},{5,1},{6,2},{7,3},{8,12},{9,13},{10,... | collective-permute-start | bytes 491528 | tf_op jit(solution)/shard_map/ppermute | solution.py:76
  19.0 5.1 %collective-permute-start.5 = (bf16[64,1152]{1,0:T(8,128)(2,1)S(1)}, bf16[64,1152]{1,0:T(8,128)(2,1)S(1)}, u32[]{:S(2)}, u32[]{:S(2)}) collective-permute-start(bf16[64,1152]{1,0:T(8,128)(2,1)S(1)} %get-tuple-element.54.refs_2_), channel_id=1, source_target_pairs={{0,2},{1,3},{2,0},{3,1},{4,6},{5,7},{6,4},{7,5},{8,10},{9,11},{10,... | collective-permute-start | bytes 442376 | tf_op jit(solution)/shard_map/ppermute | solution.py:76
  24.2 10.6 %collective-permute-start.8 = (bf16[128,1280]{1,0:T(8,128)(2,1)S(1)}, bf16[128,1280]{1,0:T(8,128)(2,1)S(1)}, u32[]{:S(2)}, u32[]{:S(2)}) collective-permute-start(bf16[128,1280]{1,0:T(8,128)(2,1)S(1)} %get-tuple-element.55.refs_0_), channel_id=1, source_target_pairs={{0,2},{1,3},{2,0},{3,1},{4,6},{5,7},{6,4},{7,5},{8,10},{9,11},{10,... | collective-permute-start | bytes 983048 | tf_op jit(solution)/shard_map/ppermute | solution.py:76
  25.8 9.0 %collective-permute-start.9 = (bf16[128,1280]{1,0:T(8,128)(2,1)S(1)}, bf16[128,1280]{1,0:T(8,128)(2,1)S(1)}, u32[]{:S(2)}, u32[]{:S(2)}) collective-permute-start(bf16[128,1280]{1,0:T(8,128)(2,1)S(1)} %get-tuple-element.56.refs_1_), channel_id=1, source_target_pairs={{0,8},{1,9},{2,10},{3,11},{4,12},{5,13},{6,14},{7,15},{8,0},{9,1},... | collective-permute-start | bytes 983048 | tf_op jit(solution)/shard_map/ppermute | solution.py:76
  27.5 7.3 %collective-permute-start.10 = (bf16[128,1152]{1,0:T(8,128)(2,1)S(1)}, bf16[128,1152]{1,0:T(8,128)(2,1)S(1)}, u32[]{:S(2)}, u32[]{:S(2)}) collective-permute-start(bf16[128,1152]{1,0:T(8,128)(2,1)S(1)} %get-tuple-element.57.refs_2_), channel_id=1, source_target_pairs={{0,4},{1,5},{2,6},{3,7},{4,0},{5,1},{6,2},{7,3},{8,12},{9,13},{10,... | collective-permute-start | bytes 884744 | tf_op jit(solution)/shard_map/ppermute | solution.py:76
  34.9 14.3 %collective-permute-start.11 = (bf16[256,1280]{1,0:T(8,128)(2,1)S(1)}, bf16[256,1280]{1,0:T(8,128)(2,1)S(1)}, u32[]{:S(2)}, u32[]{:S(2)}) collective-permute-start(bf16[256,1280]{1,0:T(8,128)(2,1)S(1)} %get-tuple-element.58.refs_0_), channel_id=1, source_target_pairs={{0,4},{1,5},{2,6},{3,7},{4,0},{5,1},{6,2},{7,3},{8,12},{9,13},{10,... | collective-permute-start | bytes 1966088 | tf_op jit(solution)/shard_map/ppermute | solution.py:76
  36.5 13.8 %collective-permute-start.12 = (bf16[256,1280]{1,0:T(8,128)(2,1)S(1)}, bf16[256,1280]{1,0:T(8,128)(2,1)S(1)}, u32[]{:S(2)}, u32[]{:S(2)}) collective-permute-start(bf16[256,1280]{1,0:T(8,128)(2,1)S(1)} %get-tuple-element.59.refs_1_), channel_id=1, source_target_pairs={{0,2},{1,3},{2,0},{3,1},{4,6},{5,7},{6,4},{7,5},{8,10},{9,11},{10,... | collective-permute-start | bytes 1966088 | tf_op jit(solution)/shard_map/ppermute | solution.py:76
  37.1 12.2 %collective-permute-start.13 = (bf16[256,1152]{1,0:T(8,128)(2,1)S(1)}, bf16[256,1152]{1,0:T(8,128)(2,1)}, u32[]{:S(2)}, u32[]{:S(2)}) collective-permute-start(bf16[256,1152]{1,0:T(8,128)(2,1)S(1)} %get-tuple-element.60.refs_2_), channel_id=1, source_target_pairs={{0,8},{1,9},{2,10},{3,11},{4,12},{5,13},{6,14},{7,15},{8,0},{9,1},... | collective-permute-start | bytes 1769480 | tf_op jit(solution)/shard_map/ppermute | solution.py:76
  50.3 9.6 %copy-start.1 = (bf16[1,512,3584]{2,1,0:T(8,128)(2,1)S(1)}, bf16[1,512,3584]{2,1,0:T(8,128)(2,1)}, u32[]{:S(2)}) copy-start(bf16[1,512,3584]{2,1,0:T(8,128)(2,1)} %param.23) | copy-start | bytes 11010052
  63.4 29.0 %collective-permute-start.14 = (f32[256,1280]{1,0:T(8,128)}, f32[256,1280]{1,0:T(8,128)}, u32[]{:S(2)}, u32[]{:S(2)}) collective-permute-start(f32[256,1280]{1,0:T(8,128)} %get-tuple-element.69), channel_id=1, source_target_pairs={{0,4},{1,5},{2,6},{3,7},{4,0},{5,1},{6,2},{7,3},{8,12},{9,13},{10,... | collective-permute-start | bytes 3932168 | tf_op jit(solution)/shard_map/ppermute | solution.py:76
  63.9 4.0 %copy-start.10 = (s32[1,32,1]{1,2,0:T(1,128)S(1)}, s32[1,32,1]{1,2,0:T(1,128)}, u32[]{:S(2)}) copy-start(s32[1,32,1]{1,2,0:T(1,128)} %param.17) | copy-start | bytes 388
  67.3 34.6 %collective-permute-start.16 = (f32[256,1280]{1,0:T(8,128)}, f32[256,1280]{1,0:T(8,128)}, u32[]{:S(2)}, u32[]{:S(2)}) collective-permute-start(f32[256,1280]{1,0:T(8,128)} %get-tuple-element.72), channel_id=1, source_target_pairs={{0,2},{1,3},{2,0},{3,1},{4,6},{5,7},{6,4},{7,5},{8,10},{9,11},{10,... | collective-permute-start | bytes 3932168 | tf_op jit(solution)/shard_map/ppermute | solution.py:76
  68.0 5.4 %copy-start.7 = (bf16[1,32,4,576]{3,2,1,0:T(4,128)(2,1)S(1)}, bf16[1,32,4,576]{3,2,1,0:T(4,128)(2,1)}, u32[]{:S(2)}) copy-start(bf16[1,32,4,576]{3,2,1,0:T(4,128)(2,1)} %refs_0_.1) | copy-start | bytes 442372
  71.9 24.5 %collective-permute-start.17 = (f32[256,1024]{1,0:T(8,128)}, f32[256,1024]{1,0:T(8,128)}, u32[]{:S(2)}, u32[]{:S(2)}) collective-permute-start(f32[256,1024]{1,0:T(8,128)} %get-tuple-element.73), channel_id=1, source_target_pairs={{0,8},{1,9},{2,10},{3,11},{4,12},{5,13},{6,14},{7,15},{8,0},{9,1},... | collective-permute-start | bytes 3145736 | tf_op jit(solution)/shard_map/ppermute | solution.py:76
  76.5 31.1 %all-to-all-start = ((bf16[32,8,608]{2,1,0:T(8,128)(2,1)}), bf16[32,8,608]{2,1,0:T(8,128)(2,1)}, u32[]{:S(2)}, u32[]{:S(2)}) async-start(bf16[32,8,608]{2,1,0:T(8,128)(2,1)} %fusion.21), calls=%async_computation | async-start | bytes 655360 | tf_op jit(solution)/shard_map/all_to_all | solution.py:436
  82.2 14.2 %copy-start.4 = (f32[256,1024]{1,0:T(8,128)S(1)}, f32[256,1024]{1,0:T(8,128)}, u32[]{:S(2)}) copy-start(f32[256,1024]{1,0:T(8,128)} %copy-done.2) | copy-start | bytes 3145732
  94.5 17.5 %collective-permute-start.15 = (f32[128,1280]{1,0:T(8,128)}, f32[128,1280]{1,0:T(8,128)}, u32[]{:S(2)}, u32[]{:S(2)}) collective-permute-start(f32[128,1280]{1,0:T(8,128)} %get-tuple-element.71), channel_id=1, source_target_pairs={{0,2},{1,3},{2,0},{3,1},{4,6},{5,7},{6,4},{7,5},{8,10},{9,11},{10,... | collective-permute-start | bytes 1966088 | tf_op jit(solution)/shard_map/ppermute | solution.py:76
  104.0 15.6 %collective-permute-start.19 = (f32[128,1280]{1,0:T(8,128)}, f32[128,1280]{1,0:T(8,128)}, u32[]{:S(2)}, u32[]{:S(2)}) collective-permute-start(f32[128,1280]{1,0:T(8,128)} %get-tuple-element.78), channel_id=1, source_target_pairs={{0,8},{1,9},{2,10},{3,11},{4,12},{5,13},{6,14},{7,15},{8,0},{9,1},... | collective-permute-start | bytes 1966088 | tf_op jit(solution)/shard_map/ppermute | solution.py:76
  106.0 11.1 %collective-permute-start.20 = (f32[128,1024]{1,0:T(8,128)}, f32[128,1024]{1,0:T(8,128)S(1)}, u32[]{:S(2)}, u32[]{:S(2)}) collective-permute-start(f32[128,1024]{1,0:T(8,128)} %get-tuple-element.79), channel_id=1, source_target_pairs={{0,4},{1,5},{2,6},{3,7},{4,0},{5,1},{6,2},{7,3},{8,12},{9,13},{10,... | collective-permute-start | bytes 1572872 | tf_op jit(solution)/shard_map/ppermute | solution.py:76
  113.2 11.1 %collective-permute-start.18 = (f32[64,1280]{1,0:T(8,128)S(1)}, f32[64,1280]{1,0:T(8,128)S(1)}, u32[]{:S(2)}, u32[]{:S(2)}) collective-permute-start(f32[64,1280]{1,0:T(8,128)S(1)} %get-tuple-element.77), channel_id=1, source_target_pairs={{0,24},{1,25},{2,26},{3,27},{4,28},{5,29},{6,30},{7,31},{8,16},{9,... | collective-permute-start | bytes 983048 | tf_op jit(solution)/shard_map/ppermute | solution.py:76
  119.0 6.4 %collective-permute-start.22 = (f32[64,1024]{1,0:T(8,128)S(1)}, f32[64,1024]{1,0:T(8,128)S(1)}, u32[]{:S(2)}, u32[]{:S(2)}) collective-permute-start(f32[64,1024]{1,0:T(8,128)S(1)} %get-tuple-element.84), channel_id=1, source_target_pairs={{0,2},{1,3},{2,0},{3,1},{4,6},{5,7},{6,4},{7,5},{8,10},{9,11},{10,... | collective-permute-start | bytes 786440 | tf_op jit(solution)/shard_map/ppermute | solution.py:76
  120.8 7.1 %collective-permute-start.21 = (f32[64,1280]{1,0:T(8,128)S(1)}, f32[64,1280]{1,0:T(8,128)S(1)}, u32[]{:S(2)}, u32[]{:S(2)}) collective-permute-start(f32[64,1280]{1,0:T(8,128)S(1)} %get-tuple-element.83), channel_id=1, source_target_pairs={{0,4},{1,5},{2,6},{3,7},{4,0},{5,1},{6,2},{7,3},{8,12},{9,13},{10,... | collective-permute-start | bytes 983048 | tf_op jit(solution)/shard_map/ppermute | solution.py:76
  128.0 9.0 %collective-permute-start.24 = (f32[32,1280]{1,0:T(8,128)S(1)}, f32[32,1280]{1,0:T(8,128)S(1)}, u32[]{:S(2)}, u32[]{:S(2)}) collective-permute-start(f32[32,1280]{1,0:T(8,128)S(1)} %get-tuple-element.88), channel_id=1, source_target_pairs={{0,24},{1,25},{2,26},{3,27},{4,28},{5,29},{6,30},{7,31},{8,16},{9,... | collective-permute-start | bytes 491528 | tf_op jit(solution)/shard_map/ppermute | solution.py:76
  129.7 7.2 %collective-permute-start.25 = (f32[32,1024]{1,0:T(8,128)S(1)}, f32[32,1024]{1,0:T(8,128)S(1)}, u32[]{:S(2)}, u32[]{:S(2)}) collective-permute-start(f32[32,1024]{1,0:T(8,128)S(1)} %get-tuple-element.89), channel_id=1, source_target_pairs={{0,24},{1,25},{2,26},{3,27},{4,28},{5,29},{6,30},{7,31},{8,16},{9,... | collective-permute-start | bytes 393224 | tf_op jit(solution)/shard_map/ppermute | solution.py:76
  131.8 8.2 %collective-permute-start.23 = (f32[32,1280]{1,0:T(8,128)S(1)}, f32[32,1280]{1,0:T(8,128)S(1)}, u32[]{:S(2)}, u32[]{:S(2)}) collective-permute-start(f32[32,1280]{1,0:T(8,128)S(1)} %get-tuple-element.87), channel_id=1, source_target_pairs={{0,8},{1,9},{2,10},{3,11},{4,12},{5,13},{6,14},{7,15},{8,0},{9,1},... | collective-permute-start | bytes 491528 | tf_op jit(solution)/shard_map/ppermute | solution.py:76
  (6 other events, 10.7 us)
